TPU v7x, 128 devices: a whole 4x4x4 slice. The times are simulated.
128 devices in a mesh: dp: 32 (over z_lo, y, x), tensor: 4 (over z_hi, core).
Axes of the slice: x: 4, y: 4, z: 4 (z_hi: 2, z_lo: 2; z = z_hi * 2 + z_lo), core: 2. Of those that a mesh axis runs over, the one named last changes fastest.
Arguments:
- hidden_in: bfloat16 [4096, 2048], P('dp'), may hold values from -6 to 6
- cotangent: bfloat16 [4096, 2048], P('dp'), may hold values from -6 to 6
- attn_gain: float32 [2048], replicated, may hold values from 0.1 to 1.9
- attn_router: bfloat16 [2048, 4], replicated, may hold values from -0.125 to 0.125
- qkv_weight: bfloat16 [2048, 6, 2048], P('dp', None, 'tensor'), may hold values from -0.125 to 0.125
- out_weight: bfloat16 [2048, 4, 2048], P('dp', None, 'tensor'), may hold values from -0.75 to 0.75
- mlp_gain: float32 [2048], replicated, may hold values from 0.1 to 1.9
- mlp_router: bfloat16 [2048, 4], replicated, may hold values from -0.125 to 0.125
- gate_up_weight: bfloat16 [2048, 4, 2, 5632], P('dp', None, None, 'tensor'), may hold values from -0.125 to 0.125
- down_weight: bfloat16 [2048, 4, 5632], P('dp', None, 'tensor'), may hold values from -0.15625 to 0.15625
- attn_route: int32 [4096, 2], P('dp'), may hold values from 0 to 3, as said below
- attn_slot: int32 [4096, 2], P('dp'), may hold values from 0 to 127, as said below
- mlp_route: int32 [4096, 2], P('dp'), may hold values from 0 to 3, as said below
- mlp_slot: int32 [4096, 2], P('dp'), may hold values from 0 to 127, as said below
Outputs:
- out_hidden: bfloat16 [4096, 2048], P('dp')
- grad_in: float32 [4096, 2048], P('dp')
- attn_gain_grad: float32 [2048], replicated
- attn_router_grad: float32 [2048, 4], replicated
- qkv_grad: float32 [2048, 6, 2048], P('dp', None, 'tensor')
- out_grad: float32 [2048, 4, 2048], P('dp', None, 'tensor')
- mlp_gain_grad: float32 [2048], replicated
- mlp_router_grad: float32 [2048, 4], replicated
- gate_up_grad: float32 [2048, 4, 2, 5632], P('dp', None, None, 'tensor')
- down_grad: float32 [2048, 4, 5632], P('dp', None, 'tensor')
Inputs may be any that keep to these rules, and one draw needn't show every extreme that they name: `attn_route`: each row names two different attention experts; among the rows of one sequence no expert is named more than 128 times, and in some sequence one expert is named by every row. `attn_slot`: within one sequence the pairs (expert, slot) of all rows and choices are distinct, and an expert named n times there holds slots 0 to n - 1. `mlp_route`: each row names two different feed-forward experts; among the rows of one sequence no expert is named more than 128 times, and in some sequence one expert is named by every row. `mlp_slot`: within one sequence the pairs (expert, slot) of all rows and choices are distinct, and an expert named n times there holds slots 0 to n - 1.
All inputs are finite; a program needn't handle non-finite values.
Results may differ from a plain program's by a relative error of at most 0.029.
Values may be sent and summed in bfloat16 or wider, within the bound.
A program may use at most 384 MiB of HBM per device.

v0:
```python
import jax
import jax.numpy as jnp
from jax import lax
from jax.sharding import PartitionSpec as P

HEAD_SIZE = 128


EPS = 1e-05
THETA = 10000.0
NEG = -1e30
HIGHEST = lax.Precision.HIGHEST


def rms_scale(values):
    return lax.rsqrt(jnp.mean(values * values, axis=-1, keepdims=True) + EPS)


def rope_tables(positions, head_dim):
    half_dim = head_dim // 2
    frequency = THETA ** (-(jnp.arange(half_dim).astype(jnp.float32) * 2.0 / head_dim))
    angles = positions[:, None] * frequency[None, :]
    return (jnp.cos(angles)[:, None, :], jnp.sin(angles)[:, None, :])


def apply_rotary(values, cosines, sines):
    half_dim = values.shape[-1] // 2
    first = values[..., :half_dim]
    second = values[..., half_dim:]
    return jnp.concatenate(
        [first * cosines - second * sines, second * cosines + first * sines], axis=-1
    )


def pair_gates(logits, route):
    chosen = jnp.take_along_axis(logits, route, axis=1)
    row_top = jnp.max(chosen, axis=1, keepdims=True)
    expon = jnp.exp(chosen - row_top)
    return expon / jnp.sum(expon, axis=1, keepdims=True)


def gate_back(gate_weights, grad_gates, route, experts):
    inner = jnp.sum(gate_weights * grad_gates, axis=1, keepdims=True)
    grad_chosen = gate_weights * (grad_gates - inner)
    columns = (route[:, :, None] == jnp.arange(experts)[None, None, :]).astype(jnp.float32)
    return jnp.sum(grad_chosen[:, :, None] * columns, axis=1)


def slot_table(route, slot, experts, capacity):
    token_rows = route.shape[0]
    flat_index = route * capacity + slot
    owners = jnp.broadcast_to(jnp.arange(token_rows)[:, None], route.shape)
    token_of = (
        jnp.zeros((experts * capacity,), jnp.int32)
        .at[flat_index.reshape(-1)]
        .set(owners.reshape(-1))
    )
    filled = jnp.zeros((experts * capacity,), jnp.float32).at[flat_index.reshape(-1)].set(1.0)
    return (token_of, filled, flat_index)


def slot_gates(gate_weights, flat_index, slots):
    return jnp.zeros((slots,), jnp.float32).at[flat_index.reshape(-1)].set(gate_weights.reshape(-1))


def dispatch(source, token_of, filled):
    select = (token_of[:, None] == jnp.arange(source.shape[0])[None, :]).astype(
        jnp.float32
    ) * filled[:, None]
    return jnp.dot(select.astype(jnp.bfloat16), source, preferred_element_type=jnp.float32).astype(
        jnp.bfloat16
    )


def pick_slots(branch, flat_index):
    width = branch.shape[-1]
    return jnp.take(branch.reshape(-1, width), flat_index.reshape(-1), axis=0).reshape(
        flat_index.shape + (width,)
    )


def norm_back(inputs, scale, gain, grad_normed):
    scaled = inputs * scale
    gain_grad = jnp.sum(grad_normed * scaled, axis=0)
    grad_scaled = grad_normed * gain
    grad_inputs = scale * (
        grad_scaled - scaled * jnp.mean(grad_scaled * scaled, axis=-1, keepdims=True)
    )
    return (grad_inputs, gain_grad)


def masked_scores(query_blk, pos_blk, rotated_key, positions, scale):
    scores = (
        jnp.einsum("rhk,thk->hrt", query_blk, rotated_key, preferred_element_type=jnp.float32)
        * scale
    )
    allowed = positions[None, None, :] <= pos_blk[None, :, None]
    return jnp.where(allowed, scores, NEG)


def attend(query_blk, pos_blk, rotated_key, value_block, positions, scale):
    scores = masked_scores(query_blk, pos_blk, rotated_key, positions, scale)
    row_top = jnp.max(scores, axis=2, keepdims=True)
    expon = jnp.exp(scores - row_top)
    totals = jnp.sum(expon, axis=2, keepdims=True)
    probs_b = (expon / totals).astype(jnp.bfloat16)
    attention_output = jnp.einsum(
        "hrt,thk->rhk", probs_b, value_block, preferred_element_type=jnp.float32
    )
    return (attention_output, (row_top + jnp.log(totals))[:, :, 0])


def attend_back(query_blk, pos_blk, lse_blk, grad_blk, rotated_key, value_block, positions, scale):
    scores = masked_scores(query_blk, pos_blk, rotated_key, positions, scale)
    probs = jnp.exp(scores - lse_blk[:, :, None])
    grad_probs = jnp.einsum(
        "rhk,thk->hrt", grad_blk, value_block, preferred_element_type=jnp.float32
    )
    inner = jnp.sum(probs * grad_probs, axis=2, keepdims=True)
    grad_scores = (probs * (grad_probs - inner) * scale).astype(jnp.bfloat16)
    grad_query = jnp.einsum(
        "hrt,thk->rhk", grad_scores, rotated_key, preferred_element_type=jnp.float32
    )
    grad_key = jnp.einsum(
        "hrt,rhk->thk", grad_scores, query_blk, preferred_element_type=jnp.float32
    )
    grad_value = jnp.einsum(
        "hrt,rhk->thk", probs.astype(jnp.bfloat16), grad_blk, preferred_element_type=jnp.float32
    )
    return (grad_query, grad_key, grad_value)


def local(
    hidden_in,
    cotangent,
    attn_gain,
    attn_router,
    qkv_weight,
    out_weight,
    mlp_gain,
    mlp_router,
    gate_up_weight,
    down_weight,
    attn_route,
    attn_slot,
    mlp_route,
    mlp_slot,
):
    token_rows, width = hidden_in.shape
    experts_a = out_weight.shape[1]
    experts_m = down_weight.shape[1]
    head_dim = HEAD_SIZE
    heads_local = qkv_weight.shape[2] // head_dim
    head_cols = heads_local * head_dim
    scale = head_dim ** (-0.5)
    positions = jnp.arange(token_rows).astype(jnp.float32)
    cosine_token, sine_token = rope_tables(positions, head_dim)
    qkv_full, out_full = (
        lax.all_gather(qkv_weight, "dp", axis=0, tiled=True),
        lax.all_gather(out_weight, "dp", axis=0, tiled=True),
    )
    inputs = hidden_in.astype(jnp.float32)
    scale_a = rms_scale(inputs)
    normed_a = (inputs * scale_a * attn_gain).astype(jnp.bfloat16)
    gates_a = pair_gates(
        jnp.dot(normed_a, attn_router, preferred_element_type=jnp.float32), attn_route
    )
    token_a, filled_a, flat_a = slot_table(attn_route, attn_slot, experts_a, token_rows)
    block_a = dispatch(normed_a, token_a, filled_a).reshape(experts_a, token_rows, width)
    query_rows = jnp.einsum(
        "ecd,dew->ecw", block_a, qkv_full[:, :experts_a], preferred_element_type=jnp.float32
    )
    key_value_pair = jnp.einsum(
        "td,dcw->tcw", normed_a, qkv_full[:, experts_a:], preferred_element_type=jnp.float32
    )
    pos_rows = jnp.take(positions, token_a)
    cosine_row, sine_row = rope_tables(pos_rows, head_dim)
    rows_total = experts_a * token_rows
    rotated_query = apply_rotary(
        query_rows.reshape(rows_total, heads_local, head_dim), cosine_row, sine_row
    ).astype(jnp.bfloat16)
    rotated_key = apply_rotary(
        key_value_pair[:, 0].reshape(token_rows, heads_local, head_dim), cosine_token, sine_token
    ).astype(jnp.bfloat16)
    value_block = (
        key_value_pair[:, 1].reshape(token_rows, heads_local, head_dim).astype(jnp.bfloat16)
    )
    block = min(512, rows_total)
    count_blocks = rows_total // block
    query_blocks = rotated_query.reshape(count_blocks, block, heads_local, head_dim)
    pos_blocks = pos_rows.reshape(count_blocks, block)

    def forward_block(members):
        return attend(members[0], members[1], rotated_key, value_block, positions, scale)

    attention_output, row_lse = lax.map(forward_block, (query_blocks, pos_blocks))
    attention_output_block = attention_output.reshape(experts_a, token_rows, head_cols).astype(
        jnp.bfloat16
    )
    branch_a = jnp.einsum(
        "ecw,dew->ecd", attention_output_block, out_full, preferred_element_type=jnp.float32
    )
    picked_a = pick_slots(branch_a, flat_a)
    attn_part = jnp.sum(gates_a[:, :, None] * picked_a, axis=1)
    after_attn = inputs + lax.psum(attn_part, "tensor")
    gu_full, down_full = (
        lax.all_gather(gate_up_weight, "dp", axis=0, tiled=True),
        lax.all_gather(down_weight, "dp", axis=0, tiled=True),
    )
    scale_m = rms_scale(after_attn)
    normed_m = (after_attn * scale_m * mlp_gain).astype(jnp.bfloat16)
    gates_m = pair_gates(
        jnp.dot(normed_m, mlp_router, preferred_element_type=jnp.float32), mlp_route
    )
    token_m, filled_m, flat_m = slot_table(mlp_route, mlp_slot, experts_m, token_rows)
    block_m = dispatch(normed_m, token_m, filled_m).reshape(experts_m, token_rows, width)
    gate_up = jnp.einsum("ecd,degf->ecgf", block_m, gu_full, preferred_element_type=jnp.float32)
    gate_part = gate_up[:, :, 0]
    up_part = gate_up[:, :, 1]
    sigma = jax.nn.sigmoid(gate_part)
    silu_value = gate_part * sigma
    activated = (silu_value * up_part).astype(jnp.bfloat16)
    branch_m = jnp.einsum("ecf,def->ecd", activated, down_full, preferred_element_type=jnp.float32)
    picked_m = pick_slots(branch_m, flat_m)
    mlp_part = jnp.sum(gates_m[:, :, None] * picked_m, axis=1)
    out_hidden = (
        after_attn + lax.psum(mlp_part.astype(jnp.bfloat16), "tensor").astype(jnp.float32)
    ).astype(jnp.bfloat16)
    grad_out = cotangent.astype(jnp.float32)
    gu_back, down_back = (gu_full, down_full)
    slot_gate_m = slot_gates(gates_m, flat_m, experts_m * token_rows)
    grad_branch_m = (
        (slot_gate_m[:, None] * jnp.take(grad_out, token_m, axis=0))
        .astype(jnp.bfloat16)
        .reshape(experts_m, token_rows, width)
    )
    dots_m = jnp.sum(grad_out[:, None, :] * picked_m, axis=2)
    grad_act = jnp.einsum(
        "ecd,def->ecf", grad_branch_m, down_back, preferred_element_type=jnp.float32
    )
    silu_slope = sigma * (1.0 + gate_part * (1.0 - sigma))
    grad_gate_up = jnp.stack(
        [grad_act * up_part * silu_slope, grad_act * silu_value], axis=2
    ).astype(jnp.bfloat16)
    grad_block_m = jnp.einsum(
        "ecgf,degf->ecd", grad_gate_up, gu_back, preferred_element_type=jnp.float32
    )
    grad_normed_m = jnp.sum(pick_slots(grad_block_m, flat_m), axis=1)
    rows_cols, grad_cols = (
        lax.all_to_all(block_m, "dp", split_axis=2, concat_axis=1, tiled=True),
        lax.all_to_all(grad_branch_m, "dp", split_axis=2, concat_axis=1, tiled=True),
    )
    gu_add = jnp.einsum(
        "ecd,ecgf->degf",
        rows_cols,
        lax.all_gather(grad_gate_up, "dp", axis=1, tiled=True),
        preferred_element_type=jnp.float32,
    )
    down_add = jnp.einsum(
        "ecd,ecf->def",
        grad_cols,
        lax.all_gather(activated, "dp", axis=1, tiled=True),
        preferred_element_type=jnp.float32,
    )
    mlp_sums = (
        lax.psum(grad_normed_m.astype(jnp.bfloat16), "tensor").astype(jnp.float32),
        lax.psum(dots_m.astype(jnp.bfloat16), "tensor").astype(jnp.float32),
    )
    grad_logits_m = gate_back(gates_m, mlp_sums[1], mlp_route, experts_m)
    router_grad_m = jnp.dot(normed_m.astype(jnp.float32).T, grad_logits_m, precision=HIGHEST)
    full_grad_m = mlp_sums[0] + jnp.dot(
        grad_logits_m, mlp_router.astype(jnp.float32).T, precision=HIGHEST
    )
    grad_inner_m, gain_grad_m = norm_back(after_attn, scale_m, mlp_gain, full_grad_m)
    grad_mid = grad_out + grad_inner_m
    qkv_back, out_back = (qkv_full, out_full)
    slot_gate_a = slot_gates(gates_a, flat_a, experts_a * token_rows)
    grad_branch_a = (
        (slot_gate_a[:, None] * jnp.take(grad_mid, token_a, axis=0))
        .astype(jnp.bfloat16)
        .reshape(experts_a, token_rows, width)
    )
    dots_a = jnp.sum(grad_mid[:, None, :] * picked_a, axis=2)
    grad_attended = jnp.einsum(
        "ecd,dew->ecw", grad_branch_a, out_back, preferred_element_type=jnp.float32
    ).astype(jnp.bfloat16)
    grad_blocks = grad_attended.reshape(count_blocks, block, heads_local, head_dim)

    def back_block(carry, members):
        grad_q, grad_k, grad_v = attend_back(
            members[0],
            members[1],
            members[2],
            members[3],
            rotated_key,
            value_block,
            positions,
            scale,
        )
        return ((carry[0] + grad_k, carry[1] + grad_v), grad_q)

    zero_keys = jnp.zeros((token_rows, heads_local, head_dim), jnp.float32)
    (grad_key, grad_value), grad_query = lax.scan(
        back_block, (zero_keys, zero_keys), (query_blocks, pos_blocks, row_lse, grad_blocks)
    )
    grad_query_b = (
        apply_rotary(grad_query.reshape(rows_total, heads_local, head_dim), cosine_row, -sine_row)
        .reshape(experts_a, token_rows, head_cols)
        .astype(jnp.bfloat16)
    )
    grad_key_plain = apply_rotary(grad_key, cosine_token, -sine_token).reshape(
        token_rows, head_cols
    )
    grad_kv_b = jnp.stack(
        [grad_key_plain, grad_value.reshape(token_rows, head_cols)], axis=1
    ).astype(jnp.bfloat16)
    grad_block_a = jnp.einsum(
        "ecw,dew->ecd", grad_query_b, qkv_back[:, :experts_a], preferred_element_type=jnp.float32
    )
    grad_norm_kv = jnp.einsum(
        "tcw,dcw->td", grad_kv_b, qkv_back[:, experts_a:], preferred_element_type=jnp.float32
    )
    grad_normed_a = grad_norm_kv + jnp.sum(pick_slots(grad_block_a, flat_a), axis=1)
    query_term = jnp.einsum(
        "ecd,ecw->dew", block_a, grad_query_b, preferred_element_type=jnp.float32
    )
    kv_term = jnp.einsum("td,tcw->dcw", normed_a, grad_kv_b, preferred_element_type=jnp.float32)
    out_term = jnp.einsum(
        "ecd,ecw->dew", grad_branch_a, attention_output_block, preferred_element_type=jnp.float32
    )
    attn_grads = lax.psum_scatter(
        jnp.concatenate([query_term, kv_term, out_term], axis=1).astype(jnp.bfloat16),
        "dp",
        scatter_dimension=0,
        tiled=True,
    ).astype(jnp.float32)
    qkv_grad = attn_grads[:, : experts_a + 2]
    out_grad = attn_grads[:, experts_a + 2 :]
    attn_sums = (
        lax.psum(grad_normed_a.astype(jnp.bfloat16), "tensor").astype(jnp.float32),
        lax.psum(dots_a.astype(jnp.bfloat16), "tensor").astype(jnp.float32),
    )
    grad_logits_a = gate_back(gates_a, attn_sums[1], attn_route, experts_a)
    router_grad_a = jnp.dot(normed_a.astype(jnp.float32).T, grad_logits_a, precision=HIGHEST)
    full_grad_a = attn_sums[0] + jnp.dot(
        grad_logits_a, attn_router.astype(jnp.float32).T, precision=HIGHEST
    )
    grad_inner_a, gain_grad_a = norm_back(inputs, scale_a, attn_gain, full_grad_a)
    grad_in = grad_mid + grad_inner_a
    summed = (
        lax.psum(gain_grad_a.astype(jnp.bfloat16), "dp").astype(jnp.float32),
        lax.psum(router_grad_a.astype(jnp.bfloat16), "dp").astype(jnp.float32),
        lax.psum(gain_grad_m.astype(jnp.bfloat16), "dp").astype(jnp.float32),
        lax.psum(router_grad_m.astype(jnp.bfloat16), "dp").astype(jnp.float32),
    )
    return (
        out_hidden,
        grad_in,
        summed[0],
        summed[1],
        qkv_grad,
        out_grad,
        summed[2],
        summed[3],
        gu_add,
        down_add,
    )


def solution(mesh):
    placed = (
        P("dp", None),
        P("dp", None),
        P(),
        P(),
        P("dp", None, "tensor"),
        P("dp", None, "tensor"),
        P(),
        P(),
        P("dp", None, None, "tensor"),
        P("dp", None, "tensor"),
        P("dp", None),
        P("dp", None),
        P("dp", None),
        P("dp", None),
    )
    return jax.shard_map(
        local,
        mesh=mesh,
        in_specs=placed,
        out_specs=(
            P("dp", None),
            P("dp", None),
            P(),
            P(),
            P("dp", None, "tensor"),
            P("dp", None, "tensor"),
            P(),
            P(),
            P("dp", None, None, "tensor"),
            P("dp", None, "tensor"),
        ),
        check_vma=False,
    )
```

profile of v0, /device:TPU:0, one launch (start us, length us, event | category | flops | bytes accessed | tf_op | source)
XLA Modules:
  0.0 3381.9 jit_solution(3626582533234228666)
XLA Ops:
  21.1 3.3 gather_fusion
  29.3 158.8 %all-gather.7.cloned.1.call-done = bf16[2048,6,512]{2,0,1:T(8,128)(2,1)} async-done(((bf16[64,6,512]{2,0,1:T(8,128)(2,1)}), bf16[2048,6,512]{2,0,1:T(8,128)(2,1)}) %all-gather.7.cloned.1.call-update) | async-done | bytes 12582928 | tf_op jit(solution)/shard_map/all_gather | solution.py:159
  188.2 3.0 fusion.13
  193.6 5.6 fusion.7
  206.2 150.3 %all-gather.9.cloned.1.call-done = bf16[2048,4,512]{2,0,1:T(8,128)(2,1)} async-done(((bf16[64,4,512]{2,0,1:T(8,128)(2,1)}), bf16[2048,4,512]{2,0,1:T(8,128)(2,1)}) %all-gather.9.cloned.1.call-update) | async-done | bytes 8388624 | tf_op jit(solution)/shard_map/all_gather | solution.py:160
  356.5 8.2 fusion.66
  364.7 4.6 gather_fusion.2
  371.0 3.7 reshape.451
  374.7 5.7 multiply_reduce_fusion.3
  380.5 2.7 copy.251
  390.2 3.7 mul.499
  395.6 4.1 gather_fusion.5
  399.7 27.5 all-reduce.6.cloned.1.call-done
  433.9 490.7 %all-gather.11.cloned.1.call-done = bf16[2048,4,2,1408]{3,0,2,1:T(8,128)(2,1)} async-done(((bf16[64,4,2,1408]{3,0,2,1:T(8,128)(2,1)}), bf16[2048,4,2,1408]{3,0,2,1:T(8,128)(2,1)}) %all-gather.11.cloned.1.call-update) | async-done | bytes 46137360 | tf_op jit(solution)/shard_map/all_gather | solution.py:207
  924.6 21.1 fusion.124
  945.6 4.7 multiply_convert_fusion.2
  950.3 229.0 %all-gather.13.cloned.1.call-done = bf16[2048,4,1408]{2,0,1:T(8,128)(2,1)} async-done(((bf16[64,4,1408]{2,0,1:T(8,128)(2,1)}), bf16[2048,4,1408]{2,0,1:T(8,128)(2,1)}) %all-gather.13.cloned.1.call-update) | async-done | bytes 23068688 | tf_op jit(solution)/shard_map/all_gather | solution.py:208
  1179.3 13.6 fusion.125
  1192.9 5.8 gather_fusion.4
  1198.6 3.8 multiply_reduce_fusion.1
  1202.7 9.9 psum.73
  1214.3 2.6 fusion.10
  1217.0 15.8 fusion.36
  1232.7 22.9 fusion.3
  1255.6 5.8 gather_fusion.6
  1261.4 3.1 broadcast_select_fusion.1
  1264.5 3.4 reshape.460
  1267.9 5.0 reduce_sum.189
  1273.0 3.5 reshape.456
  1276.5 5.6 multiply_reduce_fusion.2
  1282.1 27.9 all-reduce.8.cloned.1.call-done
  1313.4 4.0 gather_fusion.7
  1317.4 2.6 fusion.9
  1321.3 5.4 convolution_convert_fusion.5
  1335.6 4.1 convolution_bitcast_fusion.1
  1339.7 3.5 convolution_bitcast_fusion.2
  1343.3 7.3 convert_bitcast_fusion
  1353.8 7.3 convert_bitcast_fusion.1
  1361.1 8.1 fusion.5
  1369.2 6.1 gather_fusion.8
  1375.3 3.1 broadcast_select_fusion
  1378.4 3.5 reshape.464
  1382.0 5.1 reduce_sum.195
  1387.8 3.3 convolution_convert_fusion
  1391.1 4.5 fusion.25
  1395.6 17.5 pad_maximum_fusion
  1413.1 43.5 %copy.277 = bf16[2048,10,512]{2,1,0:T(8,128)(2,1)} copy(bf16[2048,10,512]{0,2,1:T(8,128)(2,1)} %pad_maximum_fusion) | data formatting | bytes 41943040 | tf_op jit(solution)/shard_map/concatenate | solution.py:332
  1457.4 3.7 pad_maximum_fusion.1
  1461.1 4.2 copy.278
  1465.3 377.8 %all_to_all.36 = bf16[4,128,2048]{1,0,2:T(4,128)(2,1)S(1)} all-to-all(bf16[4,128,2048]{1,0,2:T(4,128)(2,1)} %copy.278), channel_id=1, replica_groups=mesh['dp'=32,'tensor'=4] {'dp'}, dimensions={2} | all-to-all | bytes 4194304 | tf_op jit(solution)/shard_map/all_to_all | solution.py:250
  1843.4 2.6 copy.280
  1846.0 4.2 reshape.626
  1850.2 4.3 copy.282
  1854.5 5.1 all-to-all-start.1
  1862.4 3.7 mul.526
  1869.0 33.4 psum.75
  1903.0 2.9 fusion.48
  1905.9 157.8 %all-reduce = (bf16[2048]{0:T(1024)(128)(2,1)S(1)}, bf16[2048,4]{0,1:T(4,128)(2,1)S(1)}, bf16[2048]{0:T(1024)(128)(2,1)S(1)}, bf16[2048,4]{0,1:T(4,128)(2,1)S(1)}) all-reduce(bf16[2048]{0:T(1024)(128)(2,1)S(1)} %get-tuple-element.122, bf16[2048,4]{0,1:T(4,128)(2,1)S(1)} %convolution_convert_fusion.4, ...), channel_id=1, replica_groups=mesh['dp'=32,'tensor'=4] {'dp'}, use_global_device_ids=true, to_apply=%region_34.38 | all-reduce | flops 20480 | bytes 81920 | tf_op jit(solution)/shard_map/psum | solution.py:351
  2066.2 2.9 fusion.47
  2074.5 291.7 %all-gather.17.cloned.1.call-done = bf16[4,4096,1408]{2,1,0:T(8,128)(2,1)} async-done(((bf16[4,128,1408]{2,1,0:T(8,128)(2,1)}), bf16[4,4096,1408]{2,1,0:T(8,128)(2,1)}) %all-gather.17.cloned.1.call-update) | async-done | bytes 46137360 | tf_op jit(solution)/shard_map/all_gather | solution.py:262
  2366.3 19.1 convolution_bitcast_fusion
  2387.4 951.3 %all-gather.15.cloned.1.call-done = bf16[4,4096,2,1408]{3,1,0,2:T(8,128)(2,1)} async-done(((bf16[4,128,2,1408]{3,1,0,2:T(8,128)(2,1)}), bf16[4,4096,2,1408]{3,1,0,2:T(8,128)(2,1)}) %all-gather.15.cloned.1.call-update) | async-done | bytes 92274704 | tf_op jit(solution)/shard_map/all_gather | solution.py:256
  3338.7 32.3 fusion.15
  3371.1 3.8 copy.286
  (253 shorter events, 81.3 us)
Async XLA Ops:
  7.2 421.7 %copy-start = (bf16[2048,4]{0,1:T(4,128)(2,1)S(1)}, bf16[2048,4]{0,1:T(4,128)(2,1)}, u32[]{:S(2)}) copy-start(bf16[2048,4]{0,1:T(4,128)(2,1)} %param.27) | copy-start | bytes 49156
  7.2 181.0 %all-gather.7.cloned.1.call-start = ((), (), s32[]{:S(2)}) async-start(), calls=%async_computation.3 | async-start | bytes 12976128 | tf_op jit(solution)/shard_map/all_gather | solution.py:159
  7.9 348.6 %all-gather.9.cloned.1.call-start = ((), (), s32[]{:S(2)}) async-start(), calls=%async_computation.4 | async-start | bytes 8650752 | tf_op jit(solution)/shard_map/all_gather | solution.py:160
  9.7 417.5 %all-reduce.6.cloned.1.call-start = ((), (), s32[]{:S(2)}) async-start(), calls=%async_computation.5 | async-start | bytes 2097152 | tf_op jit(solution)/shard_map/psum | solution.py:205
  13.2 175.0 %copy-start.47 = (f32[128]{0:T(128)}, f32[128]{0:T(128)S(1)}, u32[]{:S(2)}) copy-start(f32[128]{0:T(128)S(1)} %add_rsqrt_fusion.1) | copy-start | bytes 1540
  14.6 2.6 copy-start.38
  17.0 11.5 copy-start.4
  17.0 11.5 copy-start.33
  17.2 8.5 copy-start.35
  17.2 8.5 copy-start.40
  17.3 3.7 copy-start.43
  24.5 340.3 %copy-start.42 = (s32[1024]{0:T(1024)}, s32[1024]{0:T(1024)S(1)}, u32[]{:S(2)}) copy-start(s32[1024]{0:T(1024)S(1)} %pad_clamp_fusion.2) | copy-start | bytes 12292
  24.5 344.8 %copy-start.45 = (pred[256]{0:T(512)(128)(4,1)}, pred[256]{0:T(512)(128)(4,1)S(1)}, u32[]{:S(2)}) copy-start(pred[256]{0:T(512)(128)(4,1)S(1)} %compare_and_fusion.2) | copy-start | bytes 772
  26.7 175.9 %copy-start.20 = (f32[128,64]{1,0:T(8,128)}, f32[128,64]{1,0:T(8,128)S(1)}, u32[]{:S(2)}) copy-start(f32[128,64]{1,0:T(8,128)S(1)} %get-tuple-element.161) | copy-start | bytes 98308
  28.5 174.8 %copy-start.12 = (f32[512,64]{1,0:T(8,128)}, f32[512,64]{1,0:T(8,128)S(1)}, u32[]{:S(2)}) copy-start(f32[512,64]{1,0:T(8,128)S(1)} %get-tuple-element.158) | copy-start | bytes 393220
  29.3 164.3 %copy-start.5 = (bf16[512,2048]{1,0:T(8,128)(2,1)}, bf16[512,2048]{1,0:T(8,128)(2,1)S(1)}, u32[]{:S(2)}) copy-start(bf16[512,2048]{1,0:T(8,128)(2,1)S(1)} %convolution_convert_fusion.2) | copy-start | bytes 6291460
  199.2 3.4 copy-start.30
  202.7 1.0 copy-start.23
  202.7 1.0 copy-start.25
  203.3 0.8 copy-start.31
  203.3 2.4 copy-start.27
  203.6 1.3 copy-start.15
  203.6 1.3 copy-start.16
  204.7 1.0 copy-start.6
  369.3 5.4 copy-start.3
  371.0 3.7 copy-start.22
  380.4 2.9 copy-start.19
  380.5 3.9 copy-start.37
  380.5 3.9 copy-start.50
  380.5 7.2 copy-start.10
  380.5 544.1 %all-gather.11.cloned.1.call-start = ((), (), s32[]{:S(2)}) async-start(), calls=%async_computation.6 | async-start | bytes 47579136 | tf_op jit(solution)/shard_map/all_gather | solution.py:207
  383.3 796.0 %all-gather.13.cloned.1.call-start = ((), (), s32[]{:S(2)}) async-start(), calls=%async_computation.7 | async-start | bytes 23789568 | tf_op jit(solution)/shard_map/all_gather | solution.py:208
  384.3 925.7 %all-reduce.8.cloned.1.call-start = ((), (), s32[]{:S(2)}) async-start(), calls=%async_computation.8 | async-start | bytes 1048576 | tf_op jit(solution)/shard_map/psum | solution.py:266
  395.6 33.1 copy-start.32
  428.9 2.9 copy-start.7
  1216.9 15.8 copy-start.9
  1272.9 630.0 %all-reduce.10.cloned.1.call-start = ((), (), s32[]{:S(2)}) async-start(), calls=%async_computation.12 | async-start | bytes 2097152 | tf_op jit(solution)/shard_map/psum | solution.py:227
  1313.4 4.0 copy-start.49
  1320.0 1.3 copy-start.2
  1326.8 8.9 copy-start.24
  1326.8 8.9 copy-start.26
  1343.2 7.4 copy-start.11
  1343.3 7.4 copy-start.13
  1343.3 7.4 copy-start.17
  1369.2 6.1 copy-start.46
  1378.4 8.7 copy-start.28
  1378.4 8.8 copy-start.21
  1378.4 8.8 copy-start.29
  1382.0 5.8 copy-start.34
  1382.0 5.8 copy-start.48
  1387.8 3.3 copy-start.18
  1395.6 675.4 %reduce-scatter.2.cloned.1.call-start = ((), (), s32[]{:S(2)}) async-start(), calls=%async_computation.9 | async-start | bytes 34603008 | tf_op jit(solution)/shard_map/reduce_scatter | solution.py:331
  1456.6 909.7 %all-gather.17.cloned.1.call-start = ((), (), s32[]{:S(2)}) async-start(), calls=%async_computation.11 | async-start | bytes 47579136 | tf_op jit(solution)/shard_map/all_gather | solution.py:262
  1457.3 1881.4 %all-gather.15.cloned.1.call-start = ((), (), s32[]{:S(2)}) async-start(), calls=%async_computation.10 | async-start | bytes 95158272 | tf_op jit(solution)/shard_map/all_gather | solution.py:256
  1854.4 5.1 copy-start.8
  1854.5 214.6 %all-to-all-start.1 = ((bf16[4,128,2048]{1,0,2:T(4,128)(2,1)}), bf16[4,128,2048]{1,0,2:T(4,128)(2,1)}, u32[]{:S(2)}, u32[]{:S(2)}) async-start(bf16[4,128,2048]{1,0,2:T(4,128)(2,1)} %copy.282), calls=%async_computation.2 | async-start | bytes 4194304 | tf_op jit(solution)/shard_map/all_to_all | solution.py:251
  1866.1 36.3 %copy-start.36 = (f32[128,2]{0,1:T(2,128)S(1)}, f32[128,2]{0,1:T(2,128)}, u32[]{:S(2)}) copy-start(f32[128,2]{0,1:T(2,128)} %copy-done.35) | copy-start | bytes 3076
  1866.1 36.3 %copy-start.41 = (f32[128]{0:T(128)S(1)}, f32[128]{0:T(128)}, u32[]{:S(2)}) copy-start(f32[128]{0:T(128)} %copy-done.40) | copy-start | bytes 1540
  1866.1 36.3 %copy-start.44 = (f32[128]{0:T(128)S(1)}, f32[128]{0:T(128)}, u32[]{:S(2)}) copy-start(f32[128]{0:T(128)} %copy-done.43) | copy-start | bytes 1540
  1866.1 36.3 %copy-start.39 = (s32[128,2]{0,1:T(2,128)S(1)}, s32[128,2]{0,1:T(2,128)}, u32[]{:S(2)}) copy-start(s32[128,2]{0,1:T(2,128)} %param.30) | copy-start | bytes 3076
  1866.1 36.8 %copy-start.51 = (bf16[2048,4]{0,1:T(4,128)(2,1)S(1)}, bf16[2048,4]{0,1:T(4,128)(2,1)}, u32[]{:S(2)}) copy-start(bf16[2048,4]{0,1:T(4,128)(2,1)} %param.23) | copy-start | bytes 49156
  2071.0 2.6 copy-start.14
  3338.7 36.1 %copy-start.1 = (bf16[2048,4]{0,1:T(4,128)(2,1)S(1)}, bf16[2048,4]{0,1:T(4,128)(2,1)}, u32[]{:S(2)}) copy-start(bf16[2048,4]{0,1:T(4,128)(2,1)} %param.27) | copy-start | bytes 49156
Sparse Core Ops, SparseCore 0:
  9.7 178.4 all-gather.6
  190.4 166.1 all-gather.8
  380.6 46.6 all-reduce.5
  429.4 495.0 all-gather.10
  926.7 252.4 all-gather.12
  1273.0 36.8 all-reduce.7
  1395.7 44.4 all-reduce.9
  1456.7 386.8 reduce-scatter.1
  1845.9 520.3 all-gather.16
  2368.3 970.3 all-gather.14
where the time goes:
time: 3390 us; the launch traced here: 3380 us
  waiting for transfers between devices  2330 us (69%)
  blocking collectives  579 us (17%)
  matrix products  201 us (6%)
  local copies, waits for them, and re-layouts  169 us (5%)
  other arithmetic  83.6 us (2%)
    all_gather x1, waiting for transfers between devices, local(): lax.all_gather(grad_gate_up, 'dp', axis=1, tiled=True)  951 us
    all_gather x1, waiting for transfers between devices, local(): lax.all_gather(gate_up_weight, 'dp', axis=0, tiled=True)  491 us
    all_to_all x1, blocking collectives, local(): lax.all_to_all(block_m, 'dp', split_axis=2, concat_axis=1, tiled=True)  378 us
    all_gather x1, waiting for transfers between devices, local(): lax.all_gather(activated, 'dp', axis=1, tiled=True)  292 us
    all_gather x1, waiting for transfers between devices, local(): lax.all_gather(down_weight, 'dp', axis=0, tiled=True)  229 us
    all_gather x1, waiting for transfers between devices, local(): lax.all_gather(qkv_weight, 'dp', axis=0, tiled=True)  159 us
    psum x1, blocking collectives, local(): lax.psum(gain_grad_a.astype(jnp.bfloat16), 'dp').astype(jnp.float32)  158 us
    all_gather x1, waiting for transfers between devices, local(): lax.all_gather(out_weight, 'dp', axis=0, tiled=True)  150 us
  transfers between devices with their start and end apart: 11, of which 8 were waited for; matrix products, arithmetic and copies ran while one was open for 7% of the time, Pallas kernels for 0%

commit v1 on v0

v1 whole, which is shorter than its diff:
```python
import jax
import jax.numpy as jnp
from jax import lax
from jax.sharding import Mesh, PartitionSpec as P

HEAD = 128
LANE = 128
EPS = 1e-05
THETA = 10000.0
NEG = -1e30
EXPERTS = 4
GROUP = ("zl", "x")
TEAM = ("zl", "x", "zh", "c")
ALL = ("zl", "y", "x", "zh", "c")
BF = jnp.bfloat16
F32 = jnp.float32


def dot(a, b, dims):
    return lax.dot_general(a, b, (dims, ((), ())), preferred_element_type=F32)


def mm(a, b):
    return dot(a, b, ((1,), (0,)))


def mm_nt(a, b):
    return dot(a, b, ((1,), (1,)))


def mm_tn(a, b):
    return dot(a, b, ((0,), (0,)))


def rms_scale(values):
    return lax.rsqrt(jnp.mean(values * values, axis=-1, keepdims=True) + EPS)


def chosen_mask(route):
    columns = jnp.arange(EXPERTS)[None, :]
    return (route[:, :1] == columns) | (route[:, 1:] == columns)


def dense_gates(logits, mask):
    top = jnp.max(jnp.where(mask, logits, NEG), axis=1, keepdims=True)
    expon = jnp.where(mask, jnp.exp(jnp.where(mask, logits - top, 0.0)), 0.0)
    return expon / jnp.sum(expon, axis=1, keepdims=True)


def gates_back(gates, dots):
    return gates * (dots - jnp.sum(gates * dots, axis=1, keepdims=True))


def rope_tables(count):
    frequency = THETA ** (-(jnp.arange(HEAD // 2).astype(F32) * 2.0 / HEAD))
    angles = jnp.arange(count).astype(F32)[:, None] * frequency[None, :]
    cosines, sines = jnp.cos(angles), jnp.sin(angles)
    return (
        jnp.concatenate([cosines, cosines], axis=1),
        jnp.concatenate([-sines, sines], axis=1),
    )


def rotate(values, cosines, sines):
    half = HEAD // 2
    swapped = jnp.concatenate([values[..., half:], values[..., :half]], axis=-1)
    return values * cosines + swapped * sines


def norm_back(inputs, scale, gain, grad_normed):
    scaled = inputs * scale
    grad_scaled = grad_normed * gain
    grad_inputs = scale * (
        grad_scaled - scaled * jnp.mean(grad_scaled * scaled, axis=-1, keepdims=True)
    )
    return grad_inputs, jnp.sum(grad_normed * scaled, axis=0)


def gather_rows(blocks):
    _, count, rows, cols = blocks.shape
    got = lax.all_to_all(blocks, GROUP, split_axis=0, concat_axis=0, tiled=True)
    got = lax.all_gather(got, "y", axis=0, tiled=False)
    got = got.reshape(4, 2, 4, count, rows, cols)
    return got.transpose(3, 1, 0, 2, 4, 5).reshape(count, 32 * rows, cols)


def scatter_rows(grads):
    count, all_rows, cols = grads.shape
    rows = all_rows // 32
    parts = grads.reshape(count, 2, 4, 4, rows, cols).transpose(2, 1, 3, 0, 4, 5)
    parts = parts.reshape(4, 8, count, rows, cols)
    mine = lax.psum_scatter(parts, "y", scatter_dimension=0, tiled=False)
    return lax.all_to_all(mine, GROUP, split_axis=0, concat_axis=0, tiled=True)


def local(
    hidden,
    cotangent,
    attn_gain,
    attn_router,
    qkv_weight,
    out_weight,
    mlp_gain,
    mlp_router,
    gate_up_weight,
    down_weight,
    attn_route,
    attn_slot,
    mlp_route,
    mlp_slot,
):
    seq, width = hidden.shape
    rows = qkv_weight.shape[0]
    features = down_weight.shape[2]
    tiles = features // LANE
    part = (tiles + 1) // 2 * LANE
    low = features - part
    zl, x = lax.axis_index("zl"), lax.axis_index("x")
    quarter = lax.axis_index("zh") * 2 + lax.axis_index("c")
    own = seq // 4
    scale = HEAD ** (-0.5)
    group = 8 * seq

    query_blocks = qkv_weight[:, :EXPERTS].reshape(rows, 2, 2, 4, HEAD).transpose(1, 3, 2, 0, 4)
    kv_blocks = qkv_weight[:, EXPERTS:].reshape(rows, 2, 4, HEAD).transpose(2, 1, 0, 3)
    kv_blocks = jnp.broadcast_to(kv_blocks[None], (2,) + kv_blocks.shape)
    out_blocks = out_weight.reshape(rows, 2, 2, 4, HEAD).transpose(1, 3, 2, 0, 4)
    attn_blocks = jnp.concatenate([query_blocks, kv_blocks, out_blocks], axis=2)
    attn_w = gather_rows(attn_blocks.reshape(8, 6, rows, HEAD))
    mlp_all = jnp.concatenate([gate_up_weight, down_weight[:, :, None]], axis=2)
    mlp_all = mlp_all.transpose(1, 2, 0, 3)
    mlp_blocks = jnp.stack([mlp_all[..., :part], mlp_all[..., low:]], axis=0)
    mlp_w = gather_rows(mlp_blocks.reshape(8, 3, rows, part))

    masks = jnp.concatenate([chosen_mask(attn_route), chosen_mask(mlp_route)], axis=1)
    packed = jnp.concatenate(
        [hidden, cotangent, jnp.pad(masks.astype(BF), ((0, 0), (0, LANE - 2 * EXPERTS)))], axis=1
    )
    packed = lax.all_gather(packed, GROUP, axis=0, tiled=True)
    group_in = packed[:, :width]
    group_cot = packed[:, width : 2 * width]
    mask_a = packed[:, 2 * width : 2 * width + EXPERTS] > 0.5
    mask_m = packed[:, 2 * width + EXPERTS : 2 * width + 2 * EXPERTS] > 0.5
    start = (zl * 4 + x) * seq + quarter * own

    def mine(array):
        return lax.dynamic_slice_in_dim(array, start, own, axis=0)

    inputs = group_in.astype(F32)
    scale_a = rms_scale(inputs)
    normed_a = (inputs * scale_a * attn_gain).astype(BF)
    gates_a = dense_gates(mm(normed_a, attn_router), mask_a)
    pair_a = lax.dynamic_slice_in_dim(gates_a, zl * 2, 2, axis=1)
    cosines, sines = rope_tables(seq)
    proj = jnp.einsum("td,ndw->ntw", normed_a, attn_w[:4], preferred_element_type=F32)
    proj = proj.reshape(4, 8, seq, HEAD)
    turned = rotate(proj[:3], cosines, sines).astype(BF)
    query, key, value = turned[:2], turned[2], proj[3].astype(BF)
    scores = jnp.einsum("nsrk,stk->nsrt", query, key, preferred_element_type=F32) * scale
    causal = jnp.arange(seq)[None, :] <= jnp.arange(seq)[:, None]
    scores = jnp.where(causal, scores, NEG)
    expon = jnp.exp(scores - jnp.max(scores, axis=-1, keepdims=True))
    probs = expon / jnp.sum(expon, axis=-1, keepdims=True)
    probs_b = probs.astype(BF)
    attended = jnp.einsum("nsrt,stk->nsrk", probs_b, value, preferred_element_type=F32)
    attended = attended.reshape(2, group, HEAD)
    gate_cols = pair_a.T[:, :, None]
    gated_att = (attended * gate_cols).astype(BF)
    branch_a = jnp.einsum("ntw,ndw->td", gated_att, attn_w[4:], preferred_element_type=F32)
    branch_a = lax.psum_scatter(branch_a.astype(BF), TEAM, scatter_dimension=0, tiled=True)
    own_in = mine(inputs)
    after_attn = own_in + branch_a.astype(F32)

    scale_m = rms_scale(after_attn)
    normed_own = (after_attn * scale_m * mlp_gain).astype(BF)
    normed_m = lax.all_gather(normed_own, TEAM, axis=0, tiled=True)
    gates_m = dense_gates(mm(normed_m, mlp_router), mask_m)
    col_ok = (jnp.arange(part)[None, :] >= zl * (2 * part - features)).astype(F32)
    gate_m = lax.dynamic_slice_in_dim(gates_m, x, 1, axis=1) * col_ok
    gate_part = mm(normed_m, mlp_w[0])
    up_part = mm(normed_m, mlp_w[1])
    sigma = jax.nn.sigmoid(gate_part)
    silu = gate_part * sigma
    activated = silu * up_part
    gated_act = (activated * gate_m).astype(BF)
    branch_m = mm_nt(gated_act, mlp_w[2])
    branch_m = lax.psum_scatter(branch_m.astype(BF), TEAM, scatter_dimension=0, tiled=True)
    out_own = (after_attn + branch_m.astype(F32)).astype(BF)

    cot_down = mm(group_cot, mlp_w[2])
    dots_m = jnp.sum(activated * col_ok * cot_down, axis=1, keepdims=True)
    grad_act = cot_down * gate_m
    grad_gate = (grad_act * up_part * sigma * (1.0 + gate_part * (1.0 - sigma))).astype(BF)
    grad_up = (grad_act * silu).astype(BF)
    grad_rows = mm_nt(grad_gate, mlp_w[0]) + mm_nt(grad_up, mlp_w[1])
    one_hot_x = (jnp.arange(LANE) == x).astype(F32)
    back_m = jnp.concatenate([grad_rows, dots_m * one_hot_x], axis=1).astype(BF)
    back_m = lax.psum_scatter(back_m, TEAM, scatter_dimension=0, tiled=True).astype(F32)
    mlp_grads = jnp.stack(
        [mm_tn(normed_m, grad_gate), mm_tn(normed_m, grad_up), mm_tn(group_cot, gated_act)]
    )
    mlp_grads = scatter_rows(mlp_grads.astype(BF)).astype(F32)
    own_gates_m = mine(gates_m)
    logits_back_m = gates_back(own_gates_m, back_m[:, width : width + EXPERTS])
    router_grad_m = mm_tn(normed_own.astype(F32), logits_back_m)
    full_m = back_m[:, :width] + mm_nt(logits_back_m, mlp_router.astype(F32))
    inner_m, gain_grad_m = norm_back(after_attn, scale_m, mlp_gain, full_m)
    grad_mid_own = mine(group_cot).astype(F32) + inner_m

    grad_mid = lax.all_gather(grad_mid_own.astype(BF), TEAM, axis=0, tiled=True)
    grad_att = jnp.einsum("td,ndw->ntw", grad_mid, attn_w[4:], preferred_element_type=F32)
    dots_a = jnp.sum(attended * grad_att, axis=2).T
    grad_att = (grad_att * gate_cols).astype(BF).reshape(2, 8, seq, HEAD)
    grad_probs = jnp.einsum("nsrk,stk->nsrt", grad_att, value, preferred_element_type=F32)
    inner = jnp.sum(probs * grad_probs, axis=-1, keepdims=True)
    grad_scores = (probs * (grad_probs - inner) * scale).astype(BF)
    grad_query = jnp.einsum("nsrt,stk->nsrk", grad_scores, key, preferred_element_type=F32)
    grad_key = jnp.einsum("nsrt,nsrk->stk", grad_scores, query, preferred_element_type=F32)
    grad_value = jnp.einsum("nsrt,nsrk->stk", probs_b, grad_att, preferred_element_type=F32)
    turned_back = rotate(
        jnp.concatenate([grad_query, grad_key[None]], axis=0), cosines, -sines
    )
    grad_proj = jnp.concatenate([turned_back, grad_value[None]], axis=0).astype(BF)
    grad_proj = grad_proj.reshape(4, group, HEAD)
    grad_rows_a = jnp.einsum("ntw,ndw->td", grad_proj, attn_w[:4], preferred_element_type=F32)
    pair_hot = (jnp.arange(LANE)[None, :] == (zl * 2 + jnp.arange(2))[:, None]).astype(F32)
    back_a = jnp.concatenate([grad_rows_a, mm(dots_a, pair_hot)], axis=1).astype(BF)
    back_a = lax.psum_scatter(back_a, TEAM, scatter_dimension=0, tiled=True).astype(F32)
    attn_grads = jnp.concatenate(
        [
            jnp.einsum("td,ntw->ndw", normed_a, grad_proj, preferred_element_type=F32),
            jnp.einsum("td,ntw->ndw", grad_mid, gated_att, preferred_element_type=F32),
        ],
        axis=0,
    )
    attn_grads = scatter_rows(attn_grads.astype(BF)).astype(F32)
    logits_back_a = gates_back(mine(gates_a), back_a[:, width : width + EXPERTS])
    own_normed_a = mine(normed_a).astype(F32)
    router_grad_a = mm_tn(own_normed_a, logits_back_a)
    full_a = back_a[:, :width] + mm_nt(logits_back_a, attn_router.astype(F32))
    inner_a, gain_grad_a = norm_back(own_in, mine(scale_a), attn_gain, full_a)
    grad_in_own = grad_mid_own + inner_a

    out_hidden = lax.all_gather(out_own, ("zh", "c"), axis=0, tiled=True)
    grad_in = lax.all_gather(grad_in_own, ("zh", "c"), axis=0, tiled=True)
    small = jnp.concatenate(
        [gain_grad_a[None], gain_grad_m[None], router_grad_a.T, router_grad_m.T], axis=0
    )
    small = lax.psum(small, ALL)

    attn_grads = attn_grads.reshape(2, 4, 6, rows, HEAD)
    query_grad = attn_grads[:, :, :2].transpose(3, 0, 2, 1, 4).reshape(rows, EXPERTS, 4 * HEAD)
    kv_grad = jnp.sum(attn_grads[:, :, 2:4], axis=0).transpose(2, 1, 0, 3).reshape(rows, 2, 4 * HEAD)
    qkv_grad = jnp.concatenate([query_grad, kv_grad], axis=1)
    out_grad = attn_grads[:, :, 4:].transpose(3, 0, 2, 1, 4).reshape(rows, EXPERTS, 4 * HEAD)
    mlp_grads = mlp_grads.reshape(2, EXPERTS, 3, rows, part)
    whole = jnp.concatenate([mlp_grads[0], mlp_grads[1][..., 2 * part - features :]], axis=-1)
    whole = whole.transpose(2, 0, 1, 3)
    return (
        out_hidden,
        grad_in,
        small[0],
        small[2 : 2 + EXPERTS].T,
        qkv_grad,
        out_grad,
        small[1],
        small[2 + EXPERTS :].T,
        whole[:, :, :2],
        whole[:, :, 2],
    )


def solution(mesh):
    fine = Mesh(mesh.devices.reshape(2, 4, 4, 2, 2), ALL)
    dp, tensor = ("zl", "y", "x"), ("zh", "c")
    placed = (
        P(dp, None),
        P(dp, None),
        P(),
        P(),
        P(dp, None, tensor),
        P(dp, None, tensor),
        P(),
        P(),
        P(dp, None, None, tensor),
        P(dp, None, tensor),
        P(dp, None),
        P(dp, None),
        P(dp, None),
        P(dp, None),
    )
    return jax.shard_map(
        local,
        mesh=fine,
        in_specs=placed,
        out_specs=(
            P(dp, None),
            P(dp, None),
            P(),
            P(),
            P(dp, None, tensor),
            P(dp, None, tensor),
            P(),
            P(),
            P(dp, None, None, tensor),
            P(dp, None, tensor),
        ),
        check_vma=False,
    )
```

time: 3390 us -> 1340 us (0.40)
  waiting for transfers between devices: 2330 us -> 1000 us
  blocking collectives: 579 us -> 63.3 us
  matrix products: 201 us -> 104 us
  local copies, waits for them, and re-layouts: 169 us -> 75.4 us
    all_gather x6, waiting for transfers between devices: 2270 us -> 299 us  [the longest x2 126 us: gather_rows(): got = lax.all_gather(got, 'y', axis=0, tiled=False)]
    reduce_scatter x1 -> x6, waiting for transfers between devices: 0.02 us -> 543 us  [the longest x1 142 us: local(): lax.psum_scatter(back_m, TEAM, scatter_dimension=0, tiled=True).astype(F32)]
    all_to_all x1 -> x2, blocking collectives: 378 us -> 55.3 us  [gather_rows(): got = lax.all_to_all(blocks, GROUP, split_axis=0, concat_axis=0, tiled=True)]
    psum x3 -> x0, blocking collectives: 201 us -> none  [the longest x1 158 us: local(): lax.psum(gain_grad_a.astype(jnp.bfloat16), 'dp').astype(jnp.float32)]
    dot_general x29 -> x27, matrix products: 201 us -> 101 us  [the longest x16 67.7 us: dot(): return lax.dot_general(a, b, (dims, ((), ())), preferred_element_type=F32)]
    psum x3 -> x1, waiting for transfers between devices: 55.5 us -> 128 us  [local(): small = lax.psum(small, ALL)]
    concatenate x3 -> x4, local copies, waits for them, and re-layouts: 44.8 us -> 3.58 us  [the longest x2 3.27 us: rotate(): swapped = jnp.concatenate([values[..., half:], values[..., :half]], axis=-1)]
    gather x17 -> x0, local copies, waits for them, and re-layouts: 39.3 us -> none  [the longest x4 22.2 us: pick_slots(): jnp.take(branch.reshape(-1, width), flat_index.reshape(-1), axis=0)]
  transfers between devices with their start and end apart: 11 -> 15, of which waited for: 8 -> 15; matrix products, arithmetic and copies ran while one was open for 7% -> 12% of each run, Pallas kernels for 0% -> 0%
where the time goes in v1:
time: 1340 us; the launch traced here: 1330 us
  waiting for transfers between devices  1000 us (75%)
  matrix products  104 us (8%)
  local copies, waits for them, and re-layouts  75.4 us (6%)
  blocking collectives  63.3 us (5%)
  other arithmetic  56.9 us (4%)
  between operations  15.4 us (1%)
    reduce_scatter x1, waiting for transfers between devices, local(): lax.psum_scatter(back_m, TEAM, scatter_dimension=0, tiled=True).astype(F32)  142 us
    reduce_scatter x1, waiting for transfers between devices, local(): lax.psum_scatter(branch_m.astype(BF), TEAM, scatter_dimension=0, tiled=True)  136 us
    psum x1, waiting for transfers between devices, local(): small = lax.psum(small, ALL)  128 us
    all_gather x2, waiting for transfers between devices, gather_rows(): got = lax.all_gather(got, 'y', axis=0, tiled=False)  126 us
    reduce_scatter x1, waiting for transfers between devices, local(): lax.psum_scatter(back_a, TEAM, scatter_dimension=0, tiled=True).astype(F32)  126 us
    reduce_scatter x1, waiting for transfers between devices, local(): lax.psum_scatter(branch_a.astype(BF), TEAM, scatter_dimension=0, tiled=True)  104 us
    all_gather x1, waiting for transfers between devices, local(): packed = lax.all_gather(packed, GROUP, axis=0, tiled=True)  91.2 us
    dot_general x16, matrix products, dot(): return lax.dot_general(a, b, (dims, ((), ())), preferred_element_type=F32)  67.7 us
  transfers between devices with their start and end apart: 15, of which 15 were waited for; matrix products, arithmetic and copies ran while one was open for 12% of the time, Pallas kernels for 0%

profile of v1, /device:TPU:0, one launch (start us, length us, event | category | flops | bytes accessed | tf_op | source)
XLA Modules:
  0.0 1328.0 jit_solution(5444929022276955170)
XLA Ops:
  11.3 18.5 %all_to_all.20 = bf16[8,6,64,128]{3,2,1,0:T(8,128)(2,1)} all-to-all(bf16[8,6,64,128]{3,2,1,0:T(8,128)(2,1)S(1)} %bitcast.273), channel_id=1, replica_groups=mesh['zl'=2,'y'=4,'x'=4,'zh'=2,'c'=2] {'zl','x'}, dimensions={0} | all-to-all | bytes 1572864 | tf_op jit(solution)/shard_map/all_to_all | solution.py:81
  32.9 36.7 %all-gather.17.cloned.1.call-done = bf16[32,6,64,128]{3,2,1,0:T(8,128)(2,1)} async-done(((bf16[8,6,64,128]{3,2,1,0:T(8,128)(2,1)}), bf16[32,6,64,128]{3,2,1,0:T(8,128)(2,1)}) %all-gather.17.cloned.1.call-update) | async-done | bytes 3145744 | tf_op jit(solution)/shard_map/all_gather | solution.py:82
  69.6 1.8 slice.187
  75.2 91.2 %all-gather.9.cloned.1.call-done = bf16[1024,4224]{1,0:T(8,128)(2,1)} async-done(((bf16[128,4224]{1,0:T(8,128)(2,1)}), bf16[1024,4224]{1,0:T(8,128)(2,1)}) %all-gather.9.cloned.1.call-update) | async-done | bytes 8650768 | tf_op jit(solution)/shard_map/all_gather | solution.py:139
  166.4 3.1 multiply_reduce_fusion
  169.5 3.0 multiply_convert_fusion
  172.6 2.4 fusion.24
  175.7 2.2 select_reduce_fusion.1
  183.4 1.7 fusion.100
  187.1 2.9 fusion.28
  189.9 2.6 fusion.102
  192.5 2.9 multiply_convert_fusion.5
  195.5 3.3 bitcast_convert_fusion.1
  201.1 36.8 %all_to_all.21 = bf16[8,3,64,768]{3,2,1,0:T(8,128)(2,1)} all-to-all(bf16[8,3,64,768]{3,2,1,0:T(8,128)(2,1)S(1)} %bitcast.252), channel_id=1, replica_groups=mesh['zl'=2,'y'=4,'x'=4,'zh'=2,'c'=2] {'zl','x'}, dimensions={0} | all-to-all | bytes 4718592 | tf_op jit(solution)/shard_map/all_to_all | solution.py:81
  238.0 7.8 fusion.99
  245.8 103.9 %reduce-scatter.19.cloned.1.call-done = bf16[32,2048]{1,0:T(8,128)(2,1)} async-done(((bf16[1024,2048]{1,0:T(8,128)(2,1)}), bf16[32,2048]{1,0:T(8,128)(2,1)}) %reduce-scatter.19.cloned.1.call-update) | async-done | bytes 131088 | tf_op jit(solution)/shard_map/reduce_scatter | solution.py:170
  351.7 89.6 %all-gather.19.cloned.1.call-done = bf16[32,3,64,768]{3,2,1,0:T(8,128)(2,1)} async-done(((bf16[8,3,64,768]{3,2,1,0:T(8,128)(2,1)}), bf16[32,3,64,768]{3,2,1,0:T(8,128)(2,1)}) %all-gather.19.cloned.1.call-update) | async-done | bytes 9437200 | tf_op jit(solution)/shard_map/all_gather | solution.py:82
  441.3 4.1 fusion.98
  445.4 1.9 copy.422
  447.6 2.0 copy.421
  450.3 7.3 fusion.87
  457.6 46.3 %all-gather.11.cloned.1.call-done = bf16[1024,2048]{1,0:T(8,128)(2,1)} async-done(((bf16[32,2048]{1,0:T(8,128)(2,1)}), bf16[1024,2048]{1,0:T(8,128)(2,1)}) %all-gather.11.cloned.1.call-update) | async-done | bytes 4194320 | tf_op jit(solution)/shard_map/all_gather | solution.py:176
  503.9 3.7 select_reduce_fusion
  510.8 5.3 fusion.107
  516.1 8.9 multiply_convert_fusion.2
  525.0 4.9 fusion.108
  529.9 5.2 add_convert_fusion
  535.4 2.5 pad_maximum_fusion
  537.9 141.8 %reduce-scatter.23.cloned.1.call-done = bf16[32,2176]{1,0:T(8,128)(2,1)} async-done(((bf16[1024,2176]{1,0:T(8,128)(2,1)}), bf16[32,2176]{1,0:T(8,128)(2,1)}) %reduce-scatter.23.cloned.1.call-update) | async-done | bytes 139280 | tf_op jit(solution)/shard_map/reduce_scatter | solution.py:198
  683.7 8.0 convolution_convert_fusion.3
  691.8 4.9 convolution_convert_fusion.2
  696.7 4.9 convolution_convert_fusion.1
  701.7 8.5 maximum_bitcast_fusion
  710.2 8.6 copy.458
  722.1 17.9 %all-gather.13.cloned.1.call-done = bf16[1024,2048]{1,0:T(8,128)(2,1)} async-done(((bf16[32,2048]{1,0:T(8,128)(2,1)}), bf16[1024,2048]{1,0:T(8,128)(2,1)}) %all-gather.13.cloned.1.call-update) | async-done | bytes 4194320 | tf_op jit(solution)/shard_map/all_gather | solution.py:210
  740.0 3.8 multiply_convert_fusion.4
  745.1 2.5 convolution_bitcast_fusion
  749.0 3.6 fusion.43
  758.2 2.7 fusion.42
  761.0 2.5 fusion.30
  764.3 3.8 fusion.15
  768.1 3.0 copy.451
  771.1 4.7 fusion.21
  775.9 2.3 copy.453
  779.6 2.3 copy.454
  783.5 3.6 bitcast_convert_fusion
  787.2 2.6 pad_maximum_fusion.1
  791.2 7.0 convolution_convert_fusion
  798.2 32.6 %reduce-scatter.17.cloned.1.call-done = bf16[1,8,3,64,768]{4,3,2,1,0:T(8,128)(2,1)} async-done(((bf16[4,8,3,64,768]{4,3,2,1,0:T(8,128)(2,1)}), bf16[1,8,3,64,768]{4,3,2,1,0:T(8,128)(2,1)}) %reduce-scatter.17.cloned.1.call-update) | async-done | bytes 2359312 | tf_op jit(solution)/shard_map/reduce_scatter | solution.py:92
  830.9 5.2 all-to-all-start.3
  839.0 26.9 %all-to-all-done.3 = bf16[8,3,64,768]{3,2,1,0:T(8,128)(2,1)S(1)} async-done(((bf16[8,3,64,768]{3,2,1,0:T(8,128)(2,1)}), bf16[8,3,64,768]{3,2,1,0:T(8,128)(2,1)S(1)}, u32[]{:S(2)}, u32[]{:S(2)}) %all-to-all-start.3) | async-done | bytes 2359328 | tf_op jit(solution)/shard_map/all_to_all | solution.py:93
  869.0 2.4 reduce-scatter.15.cloned.1.call-done
  871.4 5.3 all-to-all-start.2
  876.8 2.6 maximum_bitcast_fusion.1
  879.6 3.8 copy.460
  883.6 2.0 copy.461
  885.6 4.0 all-to-all-done.2
  889.8 126.0 %reduce-scatter.25.cloned.1.call-done = bf16[32,2176]{1,0:T(8,128)(2,1)} async-done(((bf16[1024,2176]{1,0:T(8,128)(2,1)}), bf16[32,2176]{1,0:T(8,128)(2,1)}) %reduce-scatter.25.cloned.1.call-update) | async-done | bytes 139280 | tf_op jit(solution)/shard_map/reduce_scatter | solution.py:228
  1020.2 136.0 %reduce-scatter.21.cloned.1.call-done = bf16[32,2048]{1,0:T(8,128)(2,1)} async-done(((bf16[1024,2048]{1,0:T(8,128)(2,1)}), bf16[32,2048]{1,0:T(8,128)(2,1)}) %reduce-scatter.21.cloned.1.call-update) | async-done | bytes 131088 | tf_op jit(solution)/shard_map/reduce_scatter | solution.py:187
  1156.2 1.9 multiply_add_fusion
  1161.2 8.0 all_gather.33
  1169.2 128.2 %all-reduce.3.cloned.1.call-done = f32[10,2048]{1,0:T(8,128)} async-done(((f32[10,2048]{1,0:T(8,128)}), f32[10,2048]{1,0:T(8,128)}) %all-reduce.3.cloned.1.call-update) | async-done | bytes 81936 | tf_op jit(solution)/shard_map/psum | solution.py:249
  1300.5 17.5 %all-gather.15.cloned.1.call-done = f32[128,2048]{1,0:T(8,128)} async-done(((f32[32,2048]{1,0:T(8,128)}), f32[128,2048]{1,0:T(8,128)}) %all-gather.15.cloned.1.call-update) | async-done | bytes 1048592 | tf_op jit(solution)/shard_map/all_gather | solution.py:245
  1318.8 2.3 copy.512
  (234 shorter events, 66.4 us)
Async XLA Ops:
  7.2 496.8 %copy-start = (bf16[2048,4]{0,1:T(4,128)(2,1)S(1)}, bf16[2048,4]{0,1:T(4,128)(2,1)}, u32[]{:S(2)}) copy-start(bf16[2048,4]{0,1:T(4,128)(2,1)} %param.21) | copy-start | bytes 49156
  7.2 62.4 %all-gather.17.cloned.1.call-start = ((), (), s32[]{:S(2)}) async-start(), calls=%async_computation.17 | async-start | bytes 3932160 | tf_op jit(solution)/shard_map/all_gather | solution.py:82
  10.4 19.5 %copy-start.40 = (s32[128,2]{0,1:T(2,128)S(1)}, s32[128,2]{0,1:T(2,128)}, u32[]{:S(2)}) copy-start(s32[128,2]{0,1:T(2,128)} %param.24) | copy-start | bytes 3076
  10.4 19.5 %copy-start.41 = (s32[128,2]{0,1:T(2,128)S(1)}, s32[128,2]{0,1:T(2,128)}, u32[]{:S(2)}) copy-start(s32[128,2]{0,1:T(2,128)} %param.25) | copy-start | bytes 3076
  10.4 19.7 %copy-start.23 = (bf16[128,2048]{1,0:T(8,128)(2,1)S(1)}, bf16[128,2048]{1,0:T(8,128)(2,1)}, u32[]{:S(2)}) copy-start(bf16[128,2048]{1,0:T(8,128)(2,1)} %param.15) | copy-start | bytes 1572868
  10.4 19.7 %copy-start.24 = (bf16[128,2048]{1,0:T(8,128)(2,1)S(1)}, bf16[128,2048]{1,0:T(8,128)(2,1)}, u32[]{:S(2)}) copy-start(bf16[128,2048]{1,0:T(8,128)(2,1)} %param.14) | copy-start | bytes 1572868
  29.8 136.6 %all-gather.9.cloned.1.call-start = ((), (), s32[]{:S(2)}) async-start(), calls=%async_computation.10 | async-start | bytes 9732096 | tf_op jit(solution)/shard_map/all_gather | solution.py:139
  31.2 318.4 %reduce-scatter.19.cloned.1.call-start = ((), (), s32[]{:S(2)}) async-start(), calls=%async_computation.19 | async-start | bytes 4325376 | tf_op jit(solution)/shard_map/reduce_scatter | solution.py:170
  74.2 95.3 %copy-start.30 = (f32[2048]{0:T(1024)S(1)}, f32[2048]{0:T(1024)}, u32[]{:S(2)}) copy-start(f32[2048]{0:T(1024)} %param.16) | copy-start | bytes 24580
  169.5 3.1 copy-start.33
  169.5 3.1 copy-start.13
  172.6 2.5 copy-start.5
  175.0 3.0 copy-start.2
  178.0 4.6 slice-start.3
  187.1 5.5 copy-start.19
  192.5 2.9 copy-start.7
  198.7 1.5 copy-start.22
  198.8 242.5 %all-gather.19.cloned.1.call-start = ((), (), s32[]{:S(2)}) async-start(), calls=%async_computation.18 | async-start | bytes 11796480 | tf_op jit(solution)/shard_map/all_gather | solution.py:82
  237.9 266.0 %all-gather.11.cloned.1.call-start = ((), (), s32[]{:S(2)}) async-start(), calls=%async_computation.11 | async-start | bytes 4325376 | tf_op jit(solution)/shard_map/all_gather | solution.py:176
  238.0 112.8 %copy-start.27 = (f32[2048]{0:T(1024)S(1)}, f32[2048]{0:T(1024)}, u32[]{:S(2)}) copy-start(f32[2048]{0:T(1024)} %param.20) | copy-start | bytes 24580
  350.8 330.9 %copy-start.34 = (f32[32]{0:T(128)}, f32[32]{0:T(128)S(1)}, u32[]{:S(2)}) copy-start(f32[32]{0:T(128)S(1)} %add_rsqrt_fusion.1) | copy-start | bytes 388
  351.6 328.1 %reduce-scatter.23.cloned.1.call-start = ((), (), s32[]{:S(2)}) async-start(), calls=%async_computation.21 | async-start | bytes 4595712 | tf_op jit(solution)/shard_map/reduce_scatter | solution.py:198
  447.6 2.7 copy-start.8
  503.9 6.8 copy-start.9
  503.9 6.8 copy-start.43
  510.4 170.4 %copy-start.11 = (f32[1024,4]{1,0:T(8,128)}, f32[1024,4]{1,0:T(8,128)S(1)}, u32[]{:S(2)}) copy-start(f32[1024,4]{1,0:T(8,128)S(1)} %fusion.56) | copy-start | bytes 49156
  510.8 5.3 copy-start.10
  510.8 5.3 copy-start.48
  537.9 202.1 %all-gather.13.cloned.1.call-start = ((), (), s32[]{:S(2)}) async-start(), calls=%async_computation.12 | async-start | bytes 4325376 | tf_op jit(solution)/shard_map/all_gather | solution.py:210
  680.7 11.0 copy-start.25
  680.8 10.9 copy-start.36
  681.7 10.0 copy-start.38
  683.4 147.5 %reduce-scatter.17.cloned.1.call-start = ((), (), s32[]{:S(2)}) async-start(), calls=%async_computation.16 | async-start | bytes 11796480 | tf_op jit(solution)/shard_map/reduce_scatter | solution.py:92
  683.6 8.1 copy-start.44
  683.6 8.1 copy-start.51
  683.6 13.1 slice-start
  683.7 13.1 slice-start.1
  691.7 5.0 slice-start.2
  691.8 5.0 copy-start.49
  718.8 2.9 copy-start.4
  718.8 152.6 %reduce-scatter.15.cloned.1.call-start = ((), (), s32[]{:S(2)}) async-start(), calls=%async_computation.15 | async-start | bytes 3932160 | tf_op jit(solution)/shard_map/reduce_scatter | solution.py:92
  722.1 22.2 %copy-start.20 = (bf16[8,128,128,1]{2,1,3,0:T(8,128)(2,1)S(1)}, bf16[8,128,128,1]{2,1,3,0:T(8,128)(2,1)}, u32[]{:S(2)}) copy-start(bf16[8,128,128,1]{2,1,3,0:T(8,128)(2,1)} %copy-done.19) | copy-start | bytes 786436
  745.1 2.5 copy-start.18
  758.2 2.7 copy-start.26
  760.9 3.4 copy-start.6
  761.0 3.4 copy-start.47
  782.0 1.6 copy-start.14
  782.0 233.8 %reduce-scatter.25.cloned.1.call-start = ((), (), s32[]{:S(2)}) async-start(), calls=%async_computation.22 | async-start | bytes 4595712 | tf_op jit(solution)/shard_map/reduce_scatter | solution.py:228
  789.8 366.4 %reduce-scatter.21.cloned.1.call-start = ((), (), s32[]{:S(2)}) async-start(), calls=%async_computation.20 | async-start | bytes 4325376 | tf_op jit(solution)/shard_map/reduce_scatter | solution.py:187
  798.2 39.2 %copy-start.17 = (bf16[32,2048]{1,0:T(8,128)(2,1)S(1)}, bf16[32,2048]{1,0:T(8,128)(2,1)}, u32[]{:S(2)}) copy-start(bf16[32,2048]{1,0:T(8,128)(2,1)} %multiply_convert_fusion.8) | copy-start | bytes 393220
  798.2 39.2 %copy-start.37 = (f32[32]{0:T(128)S(1)}, f32[32]{0:T(128)}, u32[]{:S(2)}) copy-start(f32[32]{0:T(128)} %copy-done.36) | copy-start | bytes 388
  830.9 35.0 %all-to-all-start.3 = ((bf16[8,3,64,768]{3,2,1,0:T(8,128)(2,1)}), bf16[8,3,64,768]{3,2,1,0:T(8,128)(2,1)S(1)}, u32[]{:S(2)}, u32[]{:S(2)}) async-start(bf16[8,3,64,768]{3,2,1,0:T(8,128)(2,1)} %bitcast.277), calls=%async_computation.5 | async-start | bytes 4718592 | tf_op jit(solution)/shard_map/all_to_all | solution.py:93
  871.4 18.2 %all-to-all-start.2 = ((bf16[8,6,64,128]{3,2,1,0:T(8,128)(2,1)}), bf16[8,6,64,128]{3,2,1,0:T(8,128)(2,1)S(1)}, u32[]{:S(2)}, u32[]{:S(2)}) async-start(bf16[8,6,64,128]{3,2,1,0:T(8,128)(2,1)} %bitcast.290), calls=%async_computation.3 | async-start | bytes 1572864 | tf_op jit(solution)/shard_map/all_to_all | solution.py:93
  876.8 420.7 %all-reduce.3.cloned.1.call-start = ((), (), s32[]{:S(2)}) async-start(), calls=%async_computation.14 | async-start | bytes 262144 | tf_op jit(solution)/shard_map/psum | solution.py:249
  883.5 133.3 %copy-start.31 = (f32[2048]{0:T(1024)S(1)}, f32[2048]{0:T(1024)}, u32[]{:S(2)}) copy-start(f32[2048]{0:T(1024)} %param.16) | copy-start | bytes 24580
  883.5 133.3 %copy-start.42 = (f32[32]{0:T(128)S(1)}, f32[32]{0:T(128)}, u32[]{:S(2)}) copy-start(f32[32]{0:T(128)} %dynamic-slice.3) | copy-start | bytes 388
  883.5 133.3 %copy-start.46 = (bf16[2048,4]{0,1:T(4,128)(2,1)S(1)}, bf16[2048,4]{0,1:T(4,128)(2,1)}, u32[]{:S(2)}) copy-start(bf16[2048,4]{0,1:T(4,128)(2,1)} %param.17) | copy-start | bytes 49156
  883.5 135.8 %copy-start.29 = (f32[4,2048]{1,0:T(4,128)S(1)}, f32[4,2048]{1,0:T(4,128)}, u32[]{:S(2)}) copy-start(f32[4,2048]{1,0:T(4,128)} %fusion.84) | copy-start | bytes 98308
  883.5 135.8 %copy-start.32 = (f32[2048]{0:T(1024)S(1)}, f32[2048]{0:T(1024)}, u32[]{:S(2)}) copy-start(f32[2048]{0:T(1024)} %get-tuple-element.92) | copy-start | bytes 24580
  883.6 272.6 %copy-start.28 = (f32[2048]{0:T(1024)S(1)}, f32[2048]{0:T(1024)}, u32[]{:S(2)}) copy-start(f32[2048]{0:T(1024)} %param.20) | copy-start | bytes 24580
  883.6 272.6 %copy-start.35 = (f32[32]{0:T(128)S(1)}, f32[32]{0:T(128)}, u32[]{:S(2)}) copy-start(f32[32]{0:T(128)} %copy-done.34) | copy-start | bytes 388
  883.6 272.6 %copy-start.39 = (f32[32]{0:T(128)S(1)}, f32[32]{0:T(128)}, u32[]{:S(2)}) copy-start(f32[32]{0:T(128)} %copy-done.38) | copy-start | bytes 388
  1020.1 297.8 %all-gather.15.cloned.1.call-start = ((), (), s32[]{:S(2)}) async-start(), calls=%async_computation.13 | async-start | bytes 1310720 | tf_op jit(solution)/shard_map/all_gather | solution.py:245
  1159.2 161.9 %copy-start.1 = (bf16[2048,4]{0,1:T(4,128)(2,1)S(1)}, bf16[2048,4]{0,1:T(4,128)(2,1)}, u32[]{:S(2)}) copy-start(bf16[2048,4]{0,1:T(4,128)(2,1)} %param.21) | copy-start | bytes 49156
  (7 other events, 7.1 us)
Sparse Core Ops, SparseCore 0:
  29.9 39.6 all-gather.16
  71.8 94.5 all-gather.8
  198.9 150.7 reduce-scatter.18
  351.1 90.0 all-gather.18
  442.8 61.0 all-gather.10
  538.0 141.7 reduce-scatter.22
  683.5 56.4 all-gather.12
  742.6 88.2 reduce-scatter.16
  833.4 37.9 reduce-scatter.14
  873.8 141.9 reduce-scatter.24
  1018.2 137.9 reduce-scatter.20
  1161.3 136.0 all-reduce.2
  1299.8 18.1 all-gather.14

commit v2 on v1

--- a/solution.py
+++ b/solution.py
@@ -1,6 +1,10 @@
+import itertools
+
 import jax
 import jax.numpy as jnp
 from jax import lax
+from jax.experimental import pallas as pl
+from jax.experimental.pallas import tpu as pltpu
 from jax.sharding import Mesh, PartitionSpec as P
 
 HEAD = 128
@@ -12,8 +16,12 @@
 GROUP = ("zl", "x")
 TEAM = ("zl", "x", "zh", "c")
 ALL = ("zl", "y", "x", "zh", "c")
+SIZES = dict(zl=2, y=4, x=4, zh=2, c=2)
 BF = jnp.bfloat16
 F32 = jnp.float32
+MESH = pl.DeviceIdType.MESH
+ANY = pl.BlockSpec(memory_space=pl.ANY)
+VMEM = pl.BlockSpec(memory_space=pltpu.VMEM)
 
 
 def dot(a, b, dims):
@@ -76,21 +84,389 @@
     return grad_inputs, jnp.sum(grad_normed * scaled, axis=0)
 
 
-def gather_rows(blocks):
-    _, count, rows, cols = blocks.shape
-    got = lax.all_to_all(blocks, GROUP, split_axis=0, concat_axis=0, tiled=True)
-    got = lax.all_gather(got, "y", axis=0, tiled=False)
-    got = got.reshape(4, 2, 4, count, rows, cols)
-    return got.transpose(3, 1, 0, 2, 4, 5).reshape(count, 32 * rows, cols)
-
-
-def scatter_rows(grads):
-    count, all_rows, cols = grads.shape
-    rows = all_rows // 32
-    parts = grads.reshape(count, 2, 4, 4, rows, cols).transpose(2, 1, 3, 0, 4, 5)
-    parts = parts.reshape(4, 8, count, rows, cols)
-    mine = lax.psum_scatter(parts, "y", scatter_dimension=0, tiled=False)
-    return lax.all_to_all(mine, GROUP, split_axis=0, concat_axis=0, tiled=True)
+def moves(*axes):
+    return [dict(zip(axes, steps)) for steps in itertools.product(*[range(SIZES[a]) for a in axes])]
+
+
+def place(move, sign=1):
+    return {a: lax.rem(lax.axis_index(a) + sign * v + SIZES[a], SIZES[a]) for a, v in move.items()}
+
+
+def number(coords):
+    total = 0
+    for axis, value in coords.items():
+        total = total * SIZES[axis] + value
+    return total
+
+
+def meet(partners):
+    barrier = pltpu.get_barrier_semaphore()
+    for partner in partners:
+        pl.semaphore_signal(barrier, inc=1, device_id=partner, device_id_type=MESH)
+    pl.semaphore_wait(barrier, len(partners))
+
+
+def push(src, dst, send, recv, to):
+    return pltpu.make_async_remote_copy(
+        src_ref=src, dst_ref=dst, send_sem=send, recv_sem=recv, device_id=to, device_id_type=MESH
+    )
+
+
+def settings(number, moved):
+    return dict(
+        compiler_params=pltpu.CompilerParams(
+            collective_id=number, has_side_effects=True, vmem_limit_bytes=32 << 20
+        ),
+        cost_estimate=pl.CostEstimate(flops=0, bytes_accessed=moved, transcendentals=0),
+    )
+
+
+GROUP_MOVES = moves("zl", "x")
+TEAM_MOVES = moves("zl", "x", "zh")
+Y_MOVES = moves("y")
+
+
+def sibling():
+    return {"c": 1 - lax.axis_index("c")}
+
+
+class Spread:
+    sems = [pltpu.SemaphoreType.DMA((8,))] * 4
+
+    def __init__(self, src, dst, sems):
+        self.src, self.dst = src, dst
+        self.send, self.recv, self.fsend, self.frecv = sems
+        rows = src.shape[0] // 2
+        self.half = pl.ds(pl.multiple_of(lax.axis_index("c") * rows, rows), rows)
+        self.me = number(place(GROUP_MOVES[0]))
+
+    def start(self):
+        self.copies = [pltpu.make_async_copy(self.src, self.dst.at[self.me], self.send.at[0])]
+        for k, move in enumerate(GROUP_MOVES):
+            if k:
+                self.copies.append(
+                    push(
+                        self.src.at[self.half],
+                        self.dst.at[self.me, self.half],
+                        self.send.at[k],
+                        self.recv.at[k],
+                        place(move),
+                    )
+                )
+        for copy in self.copies:
+            copy.start()
+
+    def finish(self):
+        forwards = []
+        for k, move in enumerate(GROUP_MOVES):
+            if k:
+                self.copies[k].wait_recv()
+                block = self.dst.at[number(place(move, -1)), self.half]
+                forwards.append(push(block, block, self.fsend.at[k], self.frecv.at[k], sibling()))
+                forwards[-1].start()
+        for forward in forwards:
+            forward.wait()
+        self.copies[0].wait()
+        for copy in self.copies[1:]:
+            copy.wait_send()
+
+
+class Swap:
+    sems = [pltpu.SemaphoreType.DMA((8,))] * 2
+
+    def __init__(self, src, dst, sems):
+        self.src, self.dst = src, dst
+        self.send, self.recv = sems
+
+    def start(self):
+        me = number(place(GROUP_MOVES[0]))
+        self.copies = [
+            pltpu.make_async_copy(self.src.at[me], self.dst.at[:, me], self.send.at[0])
+        ]
+        for k, move in enumerate(GROUP_MOVES):
+            if k:
+                to = place(move)
+                self.copies.append(
+                    push(
+                        self.src.at[number(to)],
+                        self.dst.at[:, me],
+                        self.send.at[k],
+                        self.recv.at[k],
+                        to,
+                    )
+                )
+        for copy in self.copies:
+            copy.start()
+
+    def finish(self):
+        for copy in self.copies:
+            copy.wait()
+
+
+def enter(collective, hidden, masks, blocks):
+    rows, width = hidden.shape
+    count, shard, cols = blocks.shape[1:]
+
+    def kernel(hidden_ref, mask_ref, block_ref, hidden_out, mask_out, block_out, *sems):
+        meet([place(m) for m in GROUP_MOVES[1:]] + [sibling()])
+        swap = Swap(block_ref, block_out, sems[0:2])
+        first = Spread(mask_ref, mask_out, sems[2:6])
+        second = Spread(hidden_ref, hidden_out, sems[6:10])
+        swap.start()
+        first.start()
+        second.start()
+        first.finish()
+        second.finish()
+        swap.finish()
+
+    return pl.pallas_call(
+        kernel,
+        out_shape=[
+            jax.ShapeDtypeStruct((8, rows, width), hidden.dtype),
+            jax.ShapeDtypeStruct((8,) + masks.shape, masks.dtype),
+            jax.ShapeDtypeStruct((count, 8, shard, cols), blocks.dtype),
+        ],
+        in_specs=[ANY] * 3,
+        out_specs=[ANY] * 3,
+        scratch_shapes=Swap.sems + Spread.sems * 2,
+        name="enter",
+        **settings(collective, 90 << 20),
+    )(hidden, masks, blocks)
+
+
+def along_y(collective, rows_a, blocks_m, cotangent):
+    count, all_rows, cols = rows_a.shape
+    count_m, shard, cols_m = blocks_m.shape[1:]
+
+    def kernel(a_ref, m_ref, cot_ref, a_out, m_out, cot_out, *sems):
+        meet([place(m) for m in GROUP_MOVES[1:] + Y_MOVES[1:]] + [sibling()])
+        y = lax.axis_index("y")
+        copies = [pltpu.make_async_copy(a_ref, a_out.at[:, y], sems[0].at[0])]
+        for k, move in enumerate(Y_MOVES):
+            if k:
+                copies.append(
+                    push(a_ref, a_out.at[:, y], sems[0].at[k], sems[1].at[k], place(move))
+                )
+        for copy in copies:
+            copy.start()
+        swap = Swap(m_ref, m_out, sems[2:4])
+        spread = Spread(cot_ref, cot_out, sems[4:8])
+        swap.start()
+        spread.start()
+        for copy in copies:
+            copy.wait()
+        swap.finish()
+        spread.finish()
+
+    return pl.pallas_call(
+        kernel,
+        out_shape=[
+            jax.ShapeDtypeStruct((count, 4, all_rows, cols), rows_a.dtype),
+            jax.ShapeDtypeStruct((count_m, 8, shard, cols_m), blocks_m.dtype),
+            jax.ShapeDtypeStruct((8,) + cotangent.shape, cotangent.dtype),
+        ],
+        in_specs=[ANY] * 3,
+        out_specs=[ANY] * 3,
+        scratch_shapes=[pltpu.SemaphoreType.DMA((4,))] * 2 + Swap.sems + Spread.sems,
+        name="along_y",
+        **settings(collective, 120 << 20),
+    )(rows_a, blocks_m, cotangent)
+
+
+def swap_back(collective, name, blocks):
+    count, shard, cols = blocks.shape[1:]
+
+    def kernel(m_ref, m_out, *sems):
+        meet([place(m) for m in GROUP_MOVES[1:]])
+        swap = Swap(m_ref, m_out, sems)
+        swap.start()
+        swap.finish()
+
+    return pl.pallas_call(
+        kernel,
+        out_shape=jax.ShapeDtypeStruct((count, 8, shard, cols), blocks.dtype),
+        in_specs=[ANY],
+        out_specs=ANY,
+        scratch_shapes=Swap.sems,
+        name=name,
+        **settings(collective, 80 << 20),
+    )(blocks)
+
+
+def team_sum(collective, name, parts):
+    width = parts.shape[1]
+    own = parts.shape[0] // 32
+    parts = parts.reshape(16, 2, own, width)
+
+    def kernel(part_ref, out_ref, held, other, got, lsem, ssem, rsem, dsend, drecv):
+        meet([place(m) for m in TEAM_MOVES[1:]] + [sibling()])
+        c = lax.axis_index("c")
+        loads, swaps = [], []
+        for k, move in enumerate(TEAM_MOVES):
+            tile = number(place(move))
+            loads.append(
+                pltpu.make_async_copy(part_ref.at[tile, c], held.at[k], lsem.at[k])
+            )
+            swaps.append(
+                push(part_ref.at[tile, 1 - c], other.at[k], ssem.at[k], rsem.at[k], sibling())
+            )
+        order = list(range(1, 16)) + [0]
+        for k in order:
+            swaps[k].start()
+            loads[k].start()
+        sends = []
+        for k in order:
+            loads[k].wait()
+            swaps[k].wait_recv()
+            total = held[k].astype(F32) + other[k].astype(F32)
+            if k:
+                held[k] = total.astype(BF)
+                sends.append(
+                    push(
+                        held.at[k],
+                        got.at[k - 1],
+                        dsend.at[k - 1],
+                        drecv.at[k - 1],
+                        place(TEAM_MOVES[k]),
+                    )
+                )
+                sends[-1].start()
+            else:
+                out_ref[...] = total
+        for k in range(15):
+            sends[k].wait_recv()
+            out_ref[...] += got[k].astype(F32)
+        for k in range(16):
+            swaps[k].wait_send()
+        for send in sends:
+            send.wait_send()
+
+    return pl.pallas_call(
+        kernel,
+        out_shape=jax.ShapeDtypeStruct((own, width), F32),
+        in_specs=[ANY],
+        out_specs=VMEM,
+        scratch_shapes=[
+            pltpu.VMEM((16, own, width), BF),
+            pltpu.VMEM((16, own, width), BF),
+            pltpu.VMEM((15, own, width), BF),
+        ]
+        + [pltpu.SemaphoreType.DMA((16,))] * 5,
+        name=name,
+        **settings(collective, 90 << 20),
+    )(parts)
+
+
+def team_spread(collective, name, rows):
+    own, width = rows.shape
+
+    def kernel(row_ref, out_ref, send, recv, fsend, frecv):
+        meet([place(m) for m in TEAM_MOVES[1:]] + [sibling()])
+        c = lax.axis_index("c")
+        mine = out_ref.at[number(place(TEAM_MOVES[0])), c]
+        stay = pltpu.make_async_copy(row_ref, mine, send.at[0])
+        stay.start()
+        pushes = [
+            push(row_ref, mine, send.at[k], recv.at[k], place(TEAM_MOVES[k])) for k in range(1, 16)
+        ]
+        for copy in pushes:
+            copy.start()
+        forwards = [push(row_ref, mine, fsend.at[0], frecv.at[0], sibling())]
+        forwards[0].start()
+        for k in range(1, 16):
+            pushes[k - 1].wait_recv()
+            tile = out_ref.at[number(place(TEAM_MOVES[k], -1)), c]
+            forwards.append(push(tile, tile, fsend.at[k], frecv.at[k], sibling()))
+            forwards[-1].start()
+        for copy in forwards:
+            copy.wait()
+        stay.wait()
+        for copy in pushes:
+            copy.wait_send()
+
+    return pl.pallas_call(
+        kernel,
+        out_shape=jax.ShapeDtypeStruct((16, 2, own, width), rows.dtype),
+        in_specs=[ANY],
+        out_specs=ANY,
+        scratch_shapes=[pltpu.SemaphoreType.DMA((16,))] * 4,
+        name=name,
+        **settings(collective, 90 << 20),
+    )(rows).reshape(32 * own, width)
+
+
+def leave(collective, out_own, grad_own, small):
+    own, width = out_own.shape
+    stages = [moves("c"), moves("x"), moves("y"), moves("zl", "zh")]
+    near = moves("zh", "c")
+
+    def kernel(out_ref, grad_ref, small_ref, out_all, grad_all, small_out, got, send, recv, ssend, srecv):
+        partners = [place(m) for m in near[1:]] + [place(m) for m in stages[1][1:] + stages[2][1:]]
+        partners += [place(m) for m in stages[3][1:] if m["zl"]]
+        meet(partners)
+        me = number(place(near[0]))
+        copies = []
+        for i, (src, dst) in enumerate(((out_ref, out_all), (grad_ref, grad_all))):
+            copies.append(pltpu.make_async_copy(src, dst.at[me], send.at[i, 0]))
+            for k in range(1, 4):
+                copies.append(
+                    push(src, dst.at[me], send.at[i, k], recv.at[i, k], place(near[k]))
+                )
+        for copy in copies:
+            copy.start()
+        small_out[...] = small_ref[...]
+        for s, stage in enumerate(stages):
+            swaps = [
+                push(small_out, got.at[s, k - 1], ssend.at[s, k], srecv.at[s, k], place(stage[k]))
+                for k in range(1, len(stage))
+            ]
+            for swap in swaps:
+                swap.start()
+            for swap in swaps:
+                swap.wait()
+            total = small_out[...]
+            for k in range(1, len(stage)):
+                total += got[s, k - 1]
+            small_out[...] = total
+        for copy in copies:
+            copy.wait()
+
+    return pl.pallas_call(
+        kernel,
+        out_shape=[
+            jax.ShapeDtypeStruct((4, own, width), out_own.dtype),
+            jax.ShapeDtypeStruct((4, own, width), grad_own.dtype),
+            jax.ShapeDtypeStruct(small.shape, F32),
+        ],
+        in_specs=[ANY, ANY, VMEM],
+        out_specs=[ANY, ANY, VMEM],
+        scratch_shapes=[pltpu.VMEM((4, 3) + small.shape, F32)]
+        + [pltpu.SemaphoreType.DMA((2, 4))] * 2
+        + [pltpu.SemaphoreType.DMA((4, 4))] * 2,
+        name="leave",
+        **settings(collective, 60 << 20),
+    )(out_own, grad_own, small)
+
+
+def reorder(array, axis):
+    shape = array.shape
+    split = shape[:axis] + (2, 4, shape[axis] // 8) + shape[axis + 1 :]
+    return jnp.swapaxes(array.reshape(split), axis, axis + 1).reshape(shape)
+
+
+def restore(array, axis):
+    shape = array.shape
+    split = shape[:axis] + (4, 2, shape[axis] // 8) + shape[axis + 1 :]
+    return jnp.swapaxes(array.reshape(split), axis, axis + 1).reshape(shape)
+
+
+def gather_y(blocks):
+    return [lax.all_gather(block, "y", axis=0, tiled=True) for block in blocks]
+
+
+def sum_y(grads):
+    summed = [lax.psum_scatter(g.astype(BF), "y", scatter_dimension=0, tiled=True) for g in grads]
+    return jnp.stack([s.reshape(8, s.shape[0] // 8, s.shape[1]) for s in summed], axis=1)
 
 
 def local(
@@ -126,21 +502,27 @@
     kv_blocks = jnp.broadcast_to(kv_blocks[None], (2,) + kv_blocks.shape)
     out_blocks = out_weight.reshape(rows, 2, 2, 4, HEAD).transpose(1, 3, 2, 0, 4)
     attn_blocks = jnp.concatenate([query_blocks, kv_blocks, out_blocks], axis=2)
-    attn_w = gather_rows(attn_blocks.reshape(8, 6, rows, HEAD))
+    attn_blocks = attn_blocks.reshape(8, 6, rows, HEAD)
     mlp_all = jnp.concatenate([gate_up_weight, down_weight[:, :, None]], axis=2)
     mlp_all = mlp_all.transpose(1, 2, 0, 3)
     mlp_blocks = jnp.stack([mlp_all[..., :part], mlp_all[..., low:]], axis=0)
-    mlp_w = gather_rows(mlp_blocks.reshape(8, 3, rows, part))
+    mlp_blocks = mlp_blocks.reshape(8, 3, rows, part)
 
     masks = jnp.concatenate([chosen_mask(attn_route), chosen_mask(mlp_route)], axis=1)
-    packed = jnp.concatenate(
-        [hidden, cotangent, jnp.pad(masks.astype(BF), ((0, 0), (0, LANE - 2 * EXPERTS)))], axis=1
-    )
-    packed = lax.all_gather(packed, GROUP, axis=0, tiled=True)
-    group_in = packed[:, :width]
-    group_cot = packed[:, width : 2 * width]
-    mask_a = packed[:, 2 * width : 2 * width + EXPERTS] > 0.5
-    mask_m = packed[:, 2 * width + EXPERTS : 2 * width + 2 * EXPERTS] > 0.5
+    masks = jnp.pad(masks.astype(BF), ((0, 0), (0, LANE - 2 * EXPERTS)))
+    attn_gain, mlp_gain = reorder(attn_gain, 0), reorder(mlp_gain, 0)
+    attn_router, mlp_router = reorder(attn_router, 0), reorder(mlp_router, 0)
+    group_in, masks, attn_rows = enter(1, reorder(hidden, 1), masks, attn_blocks)
+    attn_w, mlp_rows, group_cot = along_y(
+        2, attn_rows.reshape(6, 8 * rows, HEAD), mlp_blocks, reorder(cotangent, 1)
+    )
+    attn_w = attn_w.reshape(6, width, HEAD)
+    mlp_w = gather_y(mlp_rows.reshape(3, 8 * rows, part))
+    group_in = group_in.reshape(group, width)
+    group_cot = group_cot.reshape(group, width)
+    masks = masks.reshape(group, LANE)
+    mask_a = masks[:, :EXPERTS] > 0.5
+    mask_m = masks[:, EXPERTS : 2 * EXPERTS] > 0.5
     start = (zl * 4 + x) * seq + quarter * own
 
     def mine(array):
@@ -167,13 +549,13 @@
     gate_cols = pair_a.T[:, :, None]
     gated_att = (attended * gate_cols).astype(BF)
     branch_a = jnp.einsum("ntw,ndw->td", gated_att, attn_w[4:], preferred_element_type=F32)
-    branch_a = lax.psum_scatter(branch_a.astype(BF), TEAM, scatter_dimension=0, tiled=True)
+    branch_a = team_sum(3, "sum_attn", branch_a.astype(BF))
     own_in = mine(inputs)
-    after_attn = own_in + branch_a.astype(F32)
+    after_attn = own_in + branch_a
 
     scale_m = rms_scale(after_attn)
     normed_own = (after_attn * scale_m * mlp_gain).astype(BF)
-    normed_m = lax.all_gather(normed_own, TEAM, axis=0, tiled=True)
+    normed_m = team_spread(4, "spread_normed", normed_own)
     gates_m = dense_gates(mm(normed_m, mlp_router), mask_m)
     col_ok = (jnp.arange(part)[None, :] >= zl * (2 * part - features)).astype(F32)
     gate_m = lax.dynamic_slice_in_dim(gates_m, x, 1, axis=1) * col_ok
@@ -184,8 +566,8 @@
     activated = silu * up_part
     gated_act = (activated * gate_m).astype(BF)
     branch_m = mm_nt(gated_act, mlp_w[2])
-    branch_m = lax.psum_scatter(branch_m.astype(BF), TEAM, scatter_dimension=0, tiled=True)
-    out_own = (after_attn + branch_m.astype(F32)).astype(BF)
+    branch_m = team_sum(5, "sum_mlp", branch_m.astype(BF))
+    out_own = (after_attn + branch_m).astype(BF)
 
     cot_down = mm(group_cot, mlp_w[2])
     dots_m = jnp.sum(activated * col_ok * cot_down, axis=1, keepdims=True)
@@ -195,11 +577,11 @@
     grad_rows = mm_nt(grad_gate, mlp_w[0]) + mm_nt(grad_up, mlp_w[1])
     one_hot_x = (jnp.arange(LANE) == x).astype(F32)
     back_m = jnp.concatenate([grad_rows, dots_m * one_hot_x], axis=1).astype(BF)
-    back_m = lax.psum_scatter(back_m, TEAM, scatter_dimension=0, tiled=True).astype(F32)
-    mlp_grads = jnp.stack(
+    back_m = team_sum(6, "sum_mlp_back", back_m)
+    mlp_grads = sum_y(
         [mm_tn(normed_m, grad_gate), mm_tn(normed_m, grad_up), mm_tn(group_cot, gated_act)]
     )
-    mlp_grads = scatter_rows(mlp_grads.astype(BF)).astype(F32)
+    mlp_grads = swap_back(7, "swap_mlp", mlp_grads).astype(F32)
     own_gates_m = mine(gates_m)
     logits_back_m = gates_back(own_gates_m, back_m[:, width : width + EXPERTS])
     router_grad_m = mm_tn(normed_own.astype(F32), logits_back_m)
@@ -207,7 +589,7 @@
     inner_m, gain_grad_m = norm_back(after_attn, scale_m, mlp_gain, full_m)
     grad_mid_own = mine(group_cot).astype(F32) + inner_m
 
-    grad_mid = lax.all_gather(grad_mid_own.astype(BF), TEAM, axis=0, tiled=True)
+    grad_mid = team_spread(8, "spread_mid", grad_mid_own.astype(BF))
     grad_att = jnp.einsum("td,ndw->ntw", grad_mid, attn_w[4:], preferred_element_type=F32)
     dots_a = jnp.sum(attended * grad_att, axis=2).T
     grad_att = (grad_att * gate_cols).astype(BF).reshape(2, 8, seq, HEAD)
@@ -225,15 +607,14 @@
     grad_rows_a = jnp.einsum("ntw,ndw->td", grad_proj, attn_w[:4], preferred_element_type=F32)
     pair_hot = (jnp.arange(LANE)[None, :] == (zl * 2 + jnp.arange(2))[:, None]).astype(F32)
     back_a = jnp.concatenate([grad_rows_a, mm(dots_a, pair_hot)], axis=1).astype(BF)
-    back_a = lax.psum_scatter(back_a, TEAM, scatter_dimension=0, tiled=True).astype(F32)
+    back_a = team_sum(9, "sum_attn_back", back_a)
+    proj_grads = jnp.einsum("td,ntw->dnw", normed_a, grad_proj, preferred_element_type=F32)
+    back_grads = jnp.einsum("td,ntw->dnw", grad_mid, gated_att, preferred_element_type=F32)
     attn_grads = jnp.concatenate(
-        [
-            jnp.einsum("td,ntw->ndw", normed_a, grad_proj, preferred_element_type=F32),
-            jnp.einsum("td,ntw->ndw", grad_mid, gated_att, preferred_element_type=F32),
-        ],
-        axis=0,
-    )
-    attn_grads = scatter_rows(attn_grads.astype(BF)).astype(F32)
+        [proj_grads.reshape(width, 4 * HEAD), back_grads.reshape(width, 2 * HEAD)], axis=1
+    )
+    attn_grads = sum_y([attn_grads])
+    attn_grads = swap_back(10, "swap_attn", attn_grads).astype(F32)
     logits_back_a = gates_back(mine(gates_a), back_a[:, width : width + EXPERTS])
     own_normed_a = mine(normed_a).astype(F32)
     router_grad_a = mm_tn(own_normed_a, logits_back_a)
@@ -241,21 +622,24 @@
     inner_a, gain_grad_a = norm_back(own_in, mine(scale_a), attn_gain, full_a)
     grad_in_own = grad_mid_own + inner_a
 
-    out_hidden = lax.all_gather(out_own, ("zh", "c"), axis=0, tiled=True)
-    grad_in = lax.all_gather(grad_in_own, ("zh", "c"), axis=0, tiled=True)
     small = jnp.concatenate(
         [gain_grad_a[None], gain_grad_m[None], router_grad_a.T, router_grad_m.T], axis=0
     )
-    small = lax.psum(small, ALL)
-
-    attn_grads = attn_grads.reshape(2, 4, 6, rows, HEAD)
-    query_grad = attn_grads[:, :, :2].transpose(3, 0, 2, 1, 4).reshape(rows, EXPERTS, 4 * HEAD)
-    kv_grad = jnp.sum(attn_grads[:, :, 2:4], axis=0).transpose(2, 1, 0, 3).reshape(rows, 2, 4 * HEAD)
+    small = jnp.pad(small, ((0, 6), (0, 0)))
+    out_hidden, grad_in, small = leave(11, out_own, grad_in_own.astype(BF), small)
+    out_hidden = restore(out_hidden.reshape(seq, width), 1)
+    grad_in = restore(grad_in.reshape(seq, width), 1).astype(F32)
+    small = restore(small, 1)
+
+    attn_grads = attn_grads.reshape(2, 4, rows, 6, HEAD).transpose(2, 0, 3, 1, 4)
+    attn_grads = attn_grads.reshape(rows, 2, 6, 4 * HEAD)
+    query_grad = attn_grads[:, :, :2].reshape(rows, EXPERTS, 4 * HEAD)
+    kv_grad = attn_grads[:, 0, 2:4] + attn_grads[:, 1, 2:4]
     qkv_grad = jnp.concatenate([query_grad, kv_grad], axis=1)
-    out_grad = attn_grads[:, :, 4:].transpose(3, 0, 2, 1, 4).reshape(rows, EXPERTS, 4 * HEAD)
-    mlp_grads = mlp_grads.reshape(2, EXPERTS, 3, rows, part)
-    whole = jnp.concatenate([mlp_grads[0], mlp_grads[1][..., 2 * part - features :]], axis=-1)
-    whole = whole.transpose(2, 0, 1, 3)
+    out_grad = attn_grads[:, :, 4:].reshape(rows, EXPERTS, 4 * HEAD)
+    mlp_grads = mlp_grads.reshape(3, 2, EXPERTS, rows, part)
+    whole = jnp.concatenate([mlp_grads[:, 0], mlp_grads[:, 1, ..., 2 * part - features :]], axis=-1)
+    whole = whole.transpose(2, 1, 0, 3)
     return (
         out_hidden,
         grad_in,
@@ -264,7 +648,7 @@
         qkv_grad,
         out_grad,
         small[1],
-        small[2 + EXPERTS :].T,
+        small[2 + EXPERTS : 2 + 2 * EXPERTS].T,
         whole[:, :, :2],
         whole[:, :, 2],
     )

time: 1340 us -> 699 us (0.52)
  waiting for transfers between devices: 1000 us -> 1.49 us
  Pallas kernels: 0 us -> 421 us
  blocking collectives: 63.3 us -> 0 us
  other arithmetic: 56.9 us -> 33.5 us
  local copies, waits for them, and re-layouts: 75.4 us -> 96.3 us
    reduce_scatter x6 -> x4, waiting for transfers between devices: 543 us -> 0.01 us  [sum_y(): lax.psum_scatter(g.astype(BF), 'y', scatter_dimension=0, tiled=True)]
    pallas_call x0 -> x11, Pallas kernels: none -> 421 us  [the longest x4 165 us: team_sum(): pl.pallas_call(kernel, out_shape=jax.ShapeDtypeStruct((own, width), F32),...]
    all_gather x6 -> x3, waiting for transfers between devices: 299 us -> 0.02 us  [gather_y(): return [lax.all_gather(block, 'y', axis=0, tiled=True) for block in blocks]]
    psum x1 -> x0, waiting for transfers between devices: 128 us -> none  [local(): small = lax.psum(small, ALL)]
    all_to_all x2 -> x0, blocking collectives: 55.3 us -> none  [gather_rows(): got = lax.all_to_all(blocks, GROUP, split_axis=0, concat_axis=0, tiled=True)]
    all_to_all x2 -> x0, waiting for transfers between devices: 30.9 us -> none  [scatter_rows(): return lax.all_to_all(mine, GROUP, split_axis=0, concat_axis=0, tiled=True)]
    transpose x6 -> x5, local copies, waits for them, and re-layouts: 18.1 us -> 0.37 us  [the longest x1 0.21 us: restore(): return jnp.swapaxes(array.reshape(split), axis, axis + 1).reshape(shape)]
    dot_general x16, matrix products: 67.7 us -> 84.7 us  [dot(): return lax.dot_general(a, b, (dims, ((), ())), preferred_element_type=F32)]
  transfers between devices with their start and end apart: 15 -> 7, of which waited for: 15 -> 0; matrix products, arithmetic and copies ran while one was open for 12% -> 25% of each run, Pallas kernels for 0% -> 42%
where the time goes in v2:
time: 699 us; the launch traced here: 686 us
  Pallas kernels  421 us (60%)
  matrix products  117 us (17%)
  local copies, waits for them, and re-layouts  96.3 us (14%)
  other arithmetic  33.5 us (5%)
  between operations  15.6 us (2%)
    pallas_call x4, Pallas kernels, team_sum(): pl.pallas_call(kernel, out_shape=jax.ShapeDtypeStruct((own, width), F32),...  165 us
    dot_general x16, matrix products, dot(): return lax.dot_general(a, b, (dims, ((), ())), preferred_element_type=F32)  84.7 us
    pallas_call x1, Pallas kernels, along_y(): pl.pallas_call(kernel, out_shape=[jax.ShapeDtypeStruct((count, 4, all_row...  71.6 us
    pallas_call x2, Pallas kernels, team_spread(): pl.pallas_call(kernel, out_shape=jax.ShapeDtypeStruct((16, 2, own, width)...  63.7 us
    pallas_call x2, Pallas kernels, swap_back(): pl.pallas_call(kernel, out_shape=jax.ShapeDtypeStruct((count, 8, shard, c...  49.2 us
    pallas_call x1, Pallas kernels, enter(): pl.pallas_call(kernel, out_shape=[jax.ShapeDtypeStruct((8, rows, width),...  46.8 us
    unnamed x77, local copies, waits for them, and re-layouts  30.6 us
    pallas_call x1, Pallas kernels, leave(): pl.pallas_call(kernel, out_shape=[jax.ShapeDtypeStruct((4, own, width), o...  25.3 us
  transfers between devices with their start and end apart: 7, of which 0 were waited for; matrix products, arithmetic and copies ran while one was open for 25% of the time, Pallas kernels for 42%

profile of v2, /device:TPU:0, one launch (start us, length us, event | category | flops | bytes accessed | tf_op | source)
XLA Modules:
  0.0 685.6 jit_solution(4796574729156938536)
XLA Ops:
  10.9 1.8 reshape.352
  15.7 1.5 reshape.356
  18.7 2.2 copy.168
  21.0 3.0 maximum_bitcast_fusion.1
  25.1 2.2 pad_maximum_fusion.2
  28.6 46.8 %enter.1 = (bf16[8,128,2048]{2,1,0:T(8,128)(2,1)S(1)}, bf16[8,128,128]{2,1,0:T(8,128)(2,1)S(1)}, bf16[6,8,64,128]{3,2,1,0:T(8,128)(2,1)S(1)}) custom-call(bf16[128,2048]{1,0:T(8,128)(2,1)S(1)} %reshape.349.hidden_ref, bf16[128,128]{1,0:T(8,128)(2,1)S(1)} %pad_convert_fusion.mask_ref, bf16[8,6,64,128]{3,2,1,0:T(8,128)(2,1)S(1)} %bitcast.302), custom_call_target="tpu_custom_call" | custom-call | bytes 94371840 | tf_op jit(solution)/shard_map/enter/pallas_call | solution.py:222
  75.5 1.9 copy-done
  77.4 71.6 %along_y.1 = (bf16[6,4,512,128]{3,2,1,0:T(8,128)(2,1)S(1)}, bf16[3,8,64,768]{3,2,1,0:T(8,128)(2,1)S(1)}, bf16[8,128,2048]{2,1,0:T(8,128)(2,1)S(1)}) custom-call(bf16[6,512,128]{2,1,0:T(8,128)(2,1)S(1)} %bitcast.303, bf16[8,3,64,768]{3,2,1,0:T(8,128)(2,1)S(1)} %bitcast.286, bf16[128,2048]{1,0:T(8,128)(2,1)S(1)} %copy-done.4), custom_call_target="tpu_custom_call" | custom-call | bytes 125829120 | tf_op jit(solution)/shard_map/along_y/pallas_call | solution.py:261
  149.0 1.5 fusion.75
  153.9 3.1 multiply_reduce_fusion
  157.2 2.8 copy-done.1
  161.0 2.4 convolution_bitcast_fusion
  165.5 3.7 select_reduce_fusion.1
  170.8 2.0 constant_dynamic-slice_fusion.1
  172.8 1.8 copy.181
  174.6 2.9 copy.248
  177.5 3.1 copy.173
  180.6 1.7 copy.247
  182.3 1.8 copy.218
  184.1 2.6 fusion.77
  188.6 3.2 fusion.79
  191.7 3.0 multiply_convert_fusion.5
  198.4 2.5 bitcast_convert_fusion.1
  200.9 49.7 %sum_attn.1 = f32[32,2048]{1,0:T(8,128)S(1)} custom-call(bf16[16,2,32,2048]{3,2,1,0:T(8,128)(2,1)S(1)} %bitcast.283), custom_call_target="tpu_custom_call" | custom-call | bytes 94371840 | tf_op jit(solution)/shard_map/sum_attn/pallas_call | solution.py:344
  250.6 3.3 bitcast_convert_fusion.2
  254.1 3.1 copy-done.9
  257.2 30.8 %spread_normed.1 = bf16[16,2,32,2048]{3,2,1,0:T(8,128)(2,1)S(1)} custom-call(bf16[32,2048]{1,0:T(8,128)(2,1)S(1)} %multiply_convert_fusion.8.row_ref), custom_call_target="tpu_custom_call" | custom-call | bytes 94371840 | tf_op jit(solution)/shard_map/spread_normed/pallas_call | solution.py:387
  288.1 1.9 copy-done.2
  290.0 3.5 select_reduce_fusion
  294.8 8.3 %fusion.84 = f32[1024,768]{0,1:T(8,128)} fusion(bf16[1024,2048]{1,0:T(8,128)(2,1)} %bitcast.294, bf16[2048,768]{1,0:T(8,128)(2,1)} %all-gather.6.cloned.1.call-done), kind=kOutput, calls=%fused_computation.186 | convolution fusion | flops 3221225472 | bytes 10485760 | tf_op jit(solution)/shard_map/dot_general | solution.py:28
  303.1 8.4 %fusion.85 = f32[1024,768]{0,1:T(8,128)} fusion(bf16[1024,2048]{1,0:T(8,128)(2,1)} %bitcast.304, bf16[2048,768]{1,0:T(8,128)(2,1)} %all-gather.8.cloned.1.call-done), kind=kOutput, calls=%fused_computation.187 | convolution fusion | flops 3221225472 | bytes 10485760 | tf_op jit(solution)/shard_map/dot_general | solution.py:28
  311.5 12.5 %multiply_convert_fusion.2 = (bf16[1024,768]{0,1:T(8,128)(2,1)}, f32[1024]{0:T(1024)S(1)}, bf16[1024,768]{0,1:T(8,128)(2,1)}, bf16[1024,768]{0,1:T(8,128)(2,1)S(1)}) fusion(f32[1024,768]{0,1:T(8,128)} %fusion.84, f32[1024,768]{0,1:T(8,128)} %fusion.85, f32[768]{0:T(1024)S(1)} %fusion.44, f32[1024]{0:T(1024)S(1)} %dynamic-slice_reduce_fusion, ...), kind=kOutput, calls=%fused_computation.21 | convolution fusion | flops 3237739520 | bytes 18361344 | tf_op jit(solution)/shard_map/dot_general | solution.py:28
  325.1 4.9 convolution_convert_fusion.1
  330.1 7.9 %convolution_convert_fusion.2 = bf16[2048,768]{1,0:T(8,128)(2,1)} fusion(bf16[1024,2048]{1,0:T(8,128)(2,1)} %bitcast.296, bf16[1024,768]{0,1:T(8,128)(2,1)} %get-tuple-element.78), kind=kOutput, calls=%fused_computation.14 | convolution fusion | flops 3222798336 | bytes 8912896 | tf_op jit(solution)/shard_map/dot_general | solution.py:28
  342.3 8.0 %convolution_convert_fusion.3 = bf16[2048,768]{1,0:T(8,128)(2,1)} fusion(bf16[1024,2048]{1,0:T(8,128)(2,1)} %bitcast.297, bf16[1024,768]{0,1:T(8,128)(2,1)} %get-tuple-element.76), kind=kOutput, calls=%fused_computation.15 | convolution fusion | flops 3222798336 | bytes 8912896 | tf_op jit(solution)/shard_map/dot_general | solution.py:28
  350.3 9.1 %fusion.86 = f32[1024,2048]{1,0:T(8,128)} fusion(bf16[1024,768]{0,1:T(8,128)(2,1)} %get-tuple-element.76, bf16[2048,768]{1,0:T(8,128)(2,1)} %all-gather.4.cloned.1.call-done), kind=kOutput, calls=%fused_computation.188 | convolution fusion | flops 3221225472 | bytes 13107200 | tf_op jit(solution)/shard_map/dot_general | solution.py:28
  359.7 8.4 %add_convert_fusion = bf16[1024,2048]{1,0:T(8,128)(2,1)S(1)} fusion(f32[1024,2048]{1,0:T(8,128)} %fusion.86, bf16[1024,768]{0,1:T(8,128)(2,1)} %get-tuple-element.78, bf16[2048,768]{1,0:T(8,128)(2,1)} %all-gather.6.cloned.1.call-done), kind=kOutput, calls=%fused_computation.4 | convolution fusion | flops 3225419776 | bytes 17301504 | tf_op jit(solution)/shard_map/dot_general | solution.py:28
  368.7 39.2 %sum_mlp_back.1 = f32[32,2176]{1,0:T(8,128)S(1)} custom-call(bf16[16,2,32,2176]{3,2,1,0:T(8,128)(2,1)S(1)} %pad_maximum_fusion.part_ref), custom_call_target="tpu_custom_call" | custom-call | bytes 94371840 | tf_op jit(solution)/shard_map/sum_mlp_back/pallas_call | solution.py:344
  409.6 32.9 %spread_mid.1 = bf16[16,2,32,2048]{3,2,1,0:T(8,128)(2,1)S(1)} custom-call(bf16[32,2048]{1,0:T(8,128)(2,1)S(1)} %fusion.64.row_ref), custom_call_target="tpu_custom_call" | custom-call | bytes 94371840 | tf_op jit(solution)/shard_map/spread_mid/pallas_call | solution.py:387
  442.6 2.1 multiply_convert_fusion.3
  446.5 2.9 fusion.19
  450.4 2.8 convolution_bitcast_fusion.1
  455.8 1.6 copy.240
  457.4 2.8 copy.241
  460.2 1.9 fusion.16
  462.2 2.4 fusion.7
  467.1 3.6 convolution_convert_fusion.5
  470.8 2.4 convolution_convert_fusion.4
  473.2 1.9 pad_maximum_fusion.3
  476.5 5.8 convolution_convert_fusion
  482.3 36.6 %sum_mlp.1 = f32[32,2048]{1,0:T(8,128)S(1)} custom-call(bf16[16,2,32,2048]{3,2,1,0:T(8,128)(2,1)S(1)} %bitcast.300), custom_call_target="tpu_custom_call" | custom-call | bytes 94371840 | tf_op jit(solution)/shard_map/sum_mlp/pallas_call | solution.py:344
  519.0 4.0 fusion.17
  524.2 39.2 %sum_attn_back.1 = f32[32,2176]{1,0:T(8,128)S(1)} custom-call(bf16[16,2,32,2176]{3,2,1,0:T(8,128)(2,1)S(1)} %pad_maximum_fusion.1.part_ref), custom_call_target="tpu_custom_call" | custom-call | bytes 94371840 | tf_op jit(solution)/shard_map/sum_attn_back/pallas_call | solution.py:344
  568.4 25.3 %leave.1 = (bf16[4,32,2048]{2,1,0:T(8,128)(2,1)S(1)}, bf16[4,32,2048]{2,1,0:T(8,128)(2,1)S(1)}, f32[16,2048]{1,0:T(8,128)S(1)}) custom-call(bf16[32,2048]{1,0:T(8,128)(2,1)S(1)} %get-tuple-element.97.out_ref, bf16[32,2048]{1,0:T(8,128)(2,1)S(1)} %get-tuple-element.96.grad_ref, f32[16,2048]{1,0:T(8,128)S(1)} %select_maximum_fusion.small_ref), custom_call_target="tpu_custom_call" | custom-call | bytes 62914560 | tf_op jit(solution)/shard_map/leave/pallas_call | solution.py:434
  599.5 1.5 reshape.382
  601.0 1.9 pad_maximum_fusion.4.m_ref
  602.8 36.5 %swap_mlp.1 = bf16[3,8,64,768]{3,2,1,0:T(8,128)(2,1)S(1)} custom-call(bf16[8,3,64,768]{3,2,1,0:T(8,128)(2,1)S(1)} %pad_maximum_fusion.4.m_ref), custom_call_target="tpu_custom_call" | custom-call | bytes 83886080 | tf_op jit(solution)/shard_map/swap_mlp/pallas_call | solution.py:285
  639.7 1.5 copy.268
  643.5 2.0 copy-done.8
  648.1 12.7 %swap_attn.1 = bf16[1,8,64,768]{3,2,1,0:T(8,128)(2,1)S(1)} custom-call(bf16[8,1,64,768]{3,2,1,0:T(8,128)(2,1)S(1)} %bitcast.301), custom_call_target="tpu_custom_call" | custom-call | bytes 83886080 | tf_op jit(solution)/shard_map/swap_attn/pallas_call | solution.py:285
  660.9 2.1 reshape.390
  663.0 3.8 copy.211
  666.8 3.2 reshape.384
  672.4 3.8 copy.215
  (194 shorter events, 64.7 us)
Async XLA Ops:
  7.2 287.6 %all-gather.6.cloned.1.call-start = ((), (), s32[]{:S(2)}) async-start(), calls=%async_computation.5 | async-start | bytes 3932160 | tf_op jit(solution)/shard_map/all_gather | solution.py:464
  15.2 5.7 copy-start.17
  27.3 1.0 copy-start.22
  27.3 1.0 copy-start.23
  28.3 49.1 %copy-start.4 = (bf16[128,2048]{1,0:T(8,128)(2,1)S(1)}, bf16[128,2048]{1,0:T(8,128)(2,1)}, u32[]{:S(2)}) copy-start(bf16[128,2048]{1,0:T(8,128)(2,1)} %reshape.357.cot_ref) | copy-start | bytes 1572868
  75.5 1.9 copy-start
  149.0 2.6 copy-start.5
  149.0 4.8 copy-start.27
  151.7 151.4 %all-gather.8.cloned.1.call-start = ((), (), s32[]{:S(2)}) async-start(), calls=%async_computation.6 | async-start | bytes 3932160 | tf_op jit(solution)/shard_map/all_gather | solution.py:464
  152.4 159.1 %all-gather.4.cloned.1.call-start = ((), (), s32[]{:S(2)}) async-start(), calls=%async_computation.4 | async-start | bytes 3932160 | tf_op jit(solution)/shard_map/all_gather | solution.py:464
  153.2 447.8 %reduce-scatter.11.cloned.1.call-start = ((), (), s32[]{:S(2)}) async-start(), calls=%async_computation.10 | async-start | bytes 3932160 | tf_op jit(solution)/shard_map/reduce_scatter | solution.py:468
  157.0 2.9 copy-start.1
  157.1 3.8 copy-start.16
  160.9 2.4 copy-start.12
  163.4 2.0 copy-start.24
  165.4 3.7 copy-start.25
  184.1 3.0 copy-start.7
  253.9 3.2 copy-start.9
  288.1 2.0 copy-start.2
  294.4 113.7 %copy-start.14 = (f32[1024,4]{1,0:T(8,128)}, f32[1024,4]{1,0:T(8,128)S(1)}, u32[]{:S(2)}) copy-start(f32[1024,4]{1,0:T(8,128)S(1)} %fusion.31) | copy-start | bytes 49156
  311.5 13.6 %copy-start.6 = (bf16[8,128,2048]{2,1,0:T(8,128)(2,1)S(1)}, bf16[8,128,2048]{2,1,0:T(8,128)(2,1)}, u32[]{:S(2)}) copy-start(bf16[8,128,2048]{2,1,0:T(8,128)(2,1)} %copy-done.5) | copy-start | bytes 12582916
  324.0 1.1 copy-start.29
  330.1 270.9 %reduce-scatter.9.cloned.1.call-start = ((), (), s32[]{:S(2)}) async-start(), calls=%async_computation.9 | async-start | bytes 3932160 | tf_op jit(solution)/shard_map/reduce_scatter | solution.py:468
  338.0 1.2 copy-start.10
  338.1 262.9 %reduce-scatter.7.cloned.1.call-start = ((), (), s32[]{:S(2)}) async-start(), calls=%async_computation.8 | async-start | bytes 3932160 | tf_op jit(solution)/shard_map/reduce_scatter | solution.py:468
  350.2 296.5 %reduce-scatter.5.cloned.1.call-start = ((), (), s32[]{:S(2)}) async-start(), calls=%async_computation.7 | async-start | bytes 3932160 | tf_op jit(solution)/shard_map/reduce_scatter | solution.py:468
  407.9 34.6 %copy-start.11 = (bf16[2,4,512,128]{3,2,1,0:T(8,128)(2,1)S(1)}, bf16[2,4,512,128]{3,2,1,0:T(8,128)(2,1)}, u32[]{:S(2)}) copy-start(bf16[2,4,512,128]{3,2,1,0:T(8,128)(2,1)} %slice.150) | copy-start | bytes 3145732
  407.9 34.6 %copy-start.20 = (f32[2,1024,128]{1,2,0:T(8,128)S(1)}, f32[2,1024,128]{1,2,0:T(8,128)}, u32[]{:S(2)}) copy-start(f32[2,1024,128]{1,2,0:T(8,128)} %copy.203) | copy-start | bytes 3145732
  442.5 2.2 copy-start.3
  442.6 2.7 copy-start.19
  444.7 1.8 copy-start.31
  445.2 4.1 copy-start.15
  464.6 2.4 copy-start.28
  467.1 3.6 copy-start.13
  467.1 3.7 copy-start.21
  475.1 1.4 copy-start.30
  482.3 36.7 %copy-start.18 = (bf16[4,1024,128]{2,1,0:T(8,128)(2,1)S(1)}, bf16[4,1024,128]{2,1,0:T(8,128)(2,1)}, u32[]{:S(2)}) copy-start(bf16[4,1024,128]{2,1,0:T(8,128)(2,1)} %get-tuple-element.92) | copy-start | bytes 3145732
  524.2 39.4 %copy-start.26 = (bf16[2,4,256,4]{2,3,0,1:T(4,128)(2,1)S(1)}, bf16[2,4,256,4]{2,3,0,1:T(4,128)(2,1)}, u32[]{:S(2)}) copy-start(bf16[2,4,256,4]{2,3,0,1:T(4,128)(2,1)} %copy-done.25) | copy-start | bytes 49156
  643.5 2.0 copy-start.8
  666.8 5.6 slice-start
Sparse Core Ops, SparseCore 0:
  151.8 42.6 all-gather.5
  196.2 39.7 all-gather.7
  237.6 39.7 all-gather.3
  330.2 38.0 reduce-scatter.10
  370.6 37.9 reduce-scatter.8
  410.9 37.9 reduce-scatter.6
  475.2 35.7 reduce-scatter.4

commit v3 on v2

v3 whole, which is shorter than its diff:
```python
import itertools

import jax
import jax.numpy as jnp
import numpy as np
from jax import lax
from jax.experimental import pallas as pl
from jax.experimental.pallas import tpu as pltpu
from jax.sharding import Mesh, PartitionSpec as P

HEAD = 128
LANE = 128
EPS = 1e-05
THETA = 10000.0
NEG = -1e30
EXPERTS = 4
GROUP = ("zl", "x")
TEAM = ("zl", "x", "zh", "c")
ALL = ("zl", "y", "x", "zh", "c")
SIZES = dict(zl=2, y=4, x=4, zh=2, c=2)
BF = jnp.bfloat16
F32 = jnp.float32
MESH = pl.DeviceIdType.MESH
ANY = pl.BlockSpec(memory_space=pl.ANY)
VMEM = pl.BlockSpec(memory_space=pltpu.VMEM)


def dot(a, b, dims):
    return lax.dot_general(a, b, (dims, ((), ())), preferred_element_type=F32)


def mm(a, b):
    return dot(a, b, ((1,), (0,)))


def mm_nt(a, b):
    return dot(a, b, ((1,), (1,)))


def mm_tn(a, b):
    return dot(a, b, ((0,), (0,)))


def rms_scale(values):
    return lax.rsqrt(jnp.mean(values * values, axis=-1, keepdims=True) + EPS)


def chosen_mask(route):
    columns = jnp.arange(EXPERTS)[None, :]
    return (route[:, :1] == columns) | (route[:, 1:] == columns)


def lanes(rows):
    return lax.broadcasted_iota(jnp.int32, (rows, LANE), 1)


def dense_gates(logits, mask):
    top = jnp.max(jnp.where(mask, logits, NEG), axis=1, keepdims=True)
    expon = jnp.where(mask, jnp.exp(jnp.where(mask, logits - top, 0.0)), 0.0)
    return expon / jnp.sum(expon, axis=1, keepdims=True)


def pick(values, lane):
    return jnp.sum(jnp.where(lanes(values.shape[0]) == lane, values, 0.0), axis=1, keepdims=True)


def gates_back(gates, dots):
    return gates * (dots - jnp.sum(gates * dots, axis=1, keepdims=True))


def rope_tables(count):
    frequency = THETA ** (-(np.arange(HEAD // 2).astype(np.float32) * 2.0 / HEAD))
    angles = np.arange(count).astype(np.float32)[:, None] * frequency[None, :].astype(np.float32)
    cosines, sines = np.cos(angles), np.sin(angles)
    return (
        jnp.asarray(np.concatenate([cosines, cosines], axis=1), F32),
        jnp.asarray(np.concatenate([-sines, sines], axis=1), F32),
    )


def rotate(values, cosines, sines):
    return values * cosines + pltpu.roll(values, HEAD // 2, 1) * sines


def norm_back(inputs, gain, grad_normed):
    scale = rms_scale(inputs)
    scaled = inputs * scale
    grad_scaled = grad_normed * gain
    grad_inputs = scale * (
        grad_scaled - scaled * jnp.mean(grad_scaled * scaled, axis=-1, keepdims=True)
    )
    return grad_inputs, jnp.sum(grad_normed * scaled, axis=0, keepdims=True)


def moves(*axes):
    return [dict(zip(axes, steps)) for steps in itertools.product(*[range(SIZES[a]) for a in axes])]


def place(move, sign=1):
    return {a: lax.rem(lax.axis_index(a) + sign * v + SIZES[a], SIZES[a]) for a, v in move.items()}


def number(coords):
    total = 0
    for axis, value in coords.items():
        total = total * SIZES[axis] + value
    return total


def meet(partners):
    barrier = pltpu.get_barrier_semaphore()
    for partner in partners:
        pl.semaphore_signal(barrier, inc=1, device_id=partner, device_id_type=MESH)
    pl.semaphore_wait(barrier, len(partners))


def push(src, dst, send, recv, to):
    return pltpu.make_async_remote_copy(
        src_ref=src, dst_ref=dst, send_sem=send, recv_sem=recv, device_id=to, device_id_type=MESH
    )


def settings(number, moved, vmem=32):
    return dict(
        compiler_params=pltpu.CompilerParams(
            collective_id=number, has_side_effects=True, vmem_limit_bytes=vmem << 20
        ),
        cost_estimate=pl.CostEstimate(flops=0, bytes_accessed=moved, transcendentals=0),
    )


GROUP_MOVES = moves("zl", "x")
TEAM_MOVES = moves("zl", "x", "zh")
Y_MOVES = moves("y")


def sibling():
    return {"c": 1 - lax.axis_index("c")}


class Spread:
    sems = [pltpu.SemaphoreType.DMA((8,))] * 4

    def __init__(self, src, dst, sems):
        self.src, self.dst = src, dst
        self.send, self.recv, self.fsend, self.frecv = sems
        rows = src.shape[0] // 2
        self.half = pl.ds(pl.multiple_of(lax.axis_index("c") * rows, rows), rows)
        self.me = number(place(GROUP_MOVES[0]))

    def start(self):
        self.copies = [pltpu.make_async_copy(self.src, self.dst.at[self.me], self.send.at[0])]
        for k, move in enumerate(GROUP_MOVES):
            if k:
                self.copies.append(
                    push(
                        self.src.at[self.half],
                        self.dst.at[self.me, self.half],
                        self.send.at[k],
                        self.recv.at[k],
                        place(move),
                    )
                )
        for copy in self.copies:
            copy.start()

    def finish(self):
        forwards = []
        for k, move in enumerate(GROUP_MOVES):
            if k:
                self.copies[k].wait_recv()
                block = self.dst.at[number(place(move, -1)), self.half]
                forwards.append(push(block, block, self.fsend.at[k], self.frecv.at[k], sibling()))
                forwards[-1].start()
        for forward in forwards:
            forward.wait()
        self.copies[0].wait()
        for copy in self.copies[1:]:
            copy.wait_send()


class Swap:
    sems = [pltpu.SemaphoreType.DMA((8,))] * 2

    def __init__(self, src, dst, sems):
        self.src, self.dst = src, dst
        self.send, self.recv = sems

    def start(self):
        me = number(place(GROUP_MOVES[0]))
        self.copies = [
            pltpu.make_async_copy(self.src.at[me], self.dst.at[me], self.send.at[0])
        ]
        for k, move in enumerate(GROUP_MOVES):
            if k:
                to = place(move)
                self.copies.append(
                    push(
                        self.src.at[number(to)],
                        self.dst.at[me],
                        self.send.at[k],
                        self.recv.at[k],
                        to,
                    )
                )
        for copy in self.copies:
            copy.start()

    def finish(self):
        for copy in self.copies:
            copy.wait()


def enter(collective, hidden, masks, blocks):
    rows, width = hidden.shape

    def kernel(hidden_ref, mask_ref, block_ref, hidden_out, mask_out, block_out, *sems):
        meet([place(m) for m in GROUP_MOVES[1:]] + [sibling()])
        swap = Swap(block_ref, block_out, sems[0:2])
        first = Spread(mask_ref, mask_out, sems[2:6])
        second = Spread(hidden_ref, hidden_out, sems[6:10])
        swap.start()
        first.start()
        second.start()
        first.finish()
        second.finish()
        swap.finish()

    return pl.pallas_call(
        kernel,
        out_shape=[
            jax.ShapeDtypeStruct((8, rows, width), hidden.dtype),
            jax.ShapeDtypeStruct((8,) + masks.shape, masks.dtype),
            jax.ShapeDtypeStruct(blocks.shape, blocks.dtype),
        ],
        in_specs=[ANY] * 3,
        out_specs=[ANY] * 3,
        scratch_shapes=Swap.sems + Spread.sems * 2,
        name="enter",
        **settings(collective, 90 << 20),
    )(hidden, masks, blocks)


def along_y(collective, rows_a, blocks_m, cotangent):
    def kernel(a_ref, *refs):
        m_refs, cot_ref, a_out, m_outs, cot_out = refs[:3], refs[3], refs[4], refs[5:8], refs[8]
        sems = refs[9:]
        meet([place(m) for m in GROUP_MOVES[1:] + Y_MOVES[1:]] + [sibling()])
        y = lax.axis_index("y")
        copies = [pltpu.make_async_copy(a_ref, a_out.at[y], sems[0].at[0])]
        for k, move in enumerate(Y_MOVES):
            if k:
                copies.append(push(a_ref, a_out.at[y], sems[0].at[k], sems[1].at[k], place(move)))
        for copy in copies:
            copy.start()
        swaps = [Swap(m_refs[i], m_outs[i], sems[2 + 2 * i : 4 + 2 * i]) for i in range(3)]
        spread = Spread(cot_ref, cot_out, sems[8:12])
        for swap in swaps:
            swap.start()
        spread.start()
        for copy in copies:
            copy.wait()
        for swap in swaps:
            swap.finish()
        spread.finish()

    return pl.pallas_call(
        kernel,
        out_shape=[jax.ShapeDtypeStruct((4,) + rows_a.shape, rows_a.dtype)]
        + [jax.ShapeDtypeStruct(b.shape, b.dtype) for b in blocks_m]
        + [jax.ShapeDtypeStruct((8,) + cotangent.shape, cotangent.dtype)],
        in_specs=[ANY] * 5,
        out_specs=[ANY] * 5,
        scratch_shapes=[pltpu.SemaphoreType.DMA((4,))] * 2 + Swap.sems * 3 + Spread.sems,
        name="along_y",
        **settings(collective, 120 << 20),
    )(rows_a, *blocks_m, cotangent)


def swap_back(collective, name, blocks):
    count = len(blocks)

    def kernel(*refs):
        sems = refs[2 * count :]
        meet([place(m) for m in GROUP_MOVES[1:]])
        swaps = [Swap(refs[i], refs[count + i], sems[2 * i : 2 * i + 2]) for i in range(count)]
        for swap in swaps:
            swap.start()
        for swap in swaps:
            swap.finish()

    return pl.pallas_call(
        kernel,
        out_shape=[jax.ShapeDtypeStruct(b.shape, b.dtype) for b in blocks],
        in_specs=[ANY] * count,
        out_specs=[ANY] * count,
        scratch_shapes=Swap.sems * count,
        name=name,
        **settings(collective, 80 << 20),
    )(*blocks)


class TeamSum:
    @staticmethod
    def scratch(own, width):
        return [
            pltpu.VMEM((8, 2, own, width), BF),
            pltpu.VMEM((16, own, width), BF),
            pltpu.SemaphoreType.DMA((8,)),
            pltpu.SemaphoreType.DMA((8,)),
            pltpu.SemaphoreType.DMA((16,)),
            pltpu.SemaphoreType.DMA((16,)),
        ]

    def __init__(self, part, scratch):
        self.part = part
        self.other, self.got, self.ssem, self.rsem, self.dsend, self.drecv = scratch
        self.zl, self.x, self.zh, self.c = (lax.axis_index(a) for a in TEAM)
        self.seq = self.zl * 4 + self.x
        self.chip = self.seq * 2 + self.zh

    def swap(self, seq):
        return push(
            self.part.at[seq, :, 1 - self.c],
            self.other.at[seq],
            self.ssem.at[seq],
            self.rsem.at[seq],
            sibling(),
        )

    def send(self, seq, zh):
        chip = seq * 2 + zh
        return push(
            self.part.at[seq, zh, self.c],
            self.got.at[self.chip],
            self.dsend.at[chip],
            self.drecv.at[self.chip],
            {"zl": seq // 4, "x": lax.rem(seq, 4), "zh": zh},
        )

    def both(self, seq, zh):
        return self.part[seq, zh, self.c].astype(F32) + self.other[seq, zh].astype(F32)

    def forward(self, seq):
        self.swap(seq).wait_recv()
        for zh in range(2):
            self.part[seq, zh, self.c] = self.both(seq, zh).astype(BF)
            self.send(seq, zh).start()

    def pair(self, step):
        back = 3 - step
        return lax.rem(self.zl + back // 2, 2) * 2 + lax.rem(self.x // 2 + back, 2)

    def last(self):
        beside = self.seq + 1 - 2 * lax.rem(self.x, 2)
        self.forward(beside)
        self.swap(self.seq).wait_recv()
        away = 1 - self.zh
        self.part[self.seq, away, self.c] = self.both(self.seq, away).astype(BF)
        self.send(self.seq, away).start()

    def total(self, total_ref):
        total_ref[...] = self.both(self.seq, self.zh)
        for move in TEAM_MOVES[1:]:
            chip = number(place(move, -1))
            pltpu.make_async_copy(self.got.at[chip], self.got.at[chip], self.drecv.at[chip]).wait()
            total_ref[...] += self.got[chip].astype(F32)

    def close(self):
        for seq in range(8):
            self.swap(seq).wait_send()
        for move in TEAM_MOVES[1:]:
            to = place(move)
            self.send(to["zl"] * 4 + to["x"], to["zh"]).wait_send()

    def run(self):
        for step in range(4):
            for j in range(2):
                self.swap(self.pair(step) * 2 + j).start()
        for step in range(3):
            for j in range(2):
                self.forward(self.pair(step) * 2 + j)
        self.last()


class TeamSpread:
    sems = [pltpu.SemaphoreType.DMA((16,))] * 4

    def __init__(self, rows, out, sems):
        self.rows, self.out = rows, out
        self.send, self.recv, self.fsend, self.frecv = sems

    def run(self):
        c = lax.axis_index("c")
        mine = self.out.at[number(place(TEAM_MOVES[0])), c]
        stay = pltpu.make_async_copy(self.rows, mine, self.send.at[0])
        stay.start()
        pushes = [
            push(self.rows, mine, self.send.at[k], self.recv.at[k], place(TEAM_MOVES[k]))
            for k in range(1, 16)
        ]
        for copy in pushes:
            copy.start()
        forwards = [push(self.rows, mine, self.fsend.at[0], self.frecv.at[0], sibling())]
        forwards[0].start()
        for k in range(1, 16):
            pushes[k - 1].wait_recv()
            tile = self.out.at[number(place(TEAM_MOVES[k], -1)), c]
            forwards.append(push(tile, tile, self.fsend.at[k], self.frecv.at[k], sibling()))
            forwards[-1].start()
        for copy in forwards:
            copy.wait()
        stay.wait()
        for copy in pushes:
            copy.wait_send()


def meet_team():
    meet([place(m) for m in TEAM_MOVES[1:]] + [sibling()])


def soft(scores, causal):
    scores = jnp.where(causal, scores, NEG)
    expon = jnp.exp(scores - jnp.max(scores, axis=-1, keepdims=True))
    return expon / jnp.sum(expon, axis=-1, keepdims=True)


def causal_mask(copies, seq):
    rows = lax.rem(lax.broadcasted_iota(jnp.int32, (copies * seq, seq), 0), seq)
    return lax.broadcasted_iota(jnp.int32, (copies * seq, seq), 1) <= rows


def attn_forward(collective, hidden, masks, weights, gain, routers, cosines, sines, mlp_gain, hidden_own):
    _, seq, width = hidden.shape
    own = hidden_own.shape[0]
    scale = HEAD ** (-0.5)

    def kernel(
        hid, mask, w_ref, gain_ref, router_ref, cos_ref, sin_ref, gain_m_ref, own_ref,
        normed_out, qkv_out, gated_out, gates_out, after_out, spread_out,
        part, total, row, *rest,
    ):
        meet_team()
        team = TeamSum(part, rest[:6])
        first = 2 * team.zl
        causal = causal_mask(2, seq)

        def step(i, _):
            pair = team.pair(i)
            for j in range(2):
                values = hid[pair * 2 + j].astype(F32)
                normed_out[pair * 2 + j] = (values * rms_scale(values) * gain_ref[...]).astype(BF)
            normed = normed_out[pl.ds(pair * 2, 2)].reshape(2 * seq, width)
            logits = mm(normed, router_ref[...])
            proj = mm(normed, w_ref[:, : 4 * HEAD])
            allowed = mask[pl.ds(pair * 2, 2)].reshape(2 * seq, LANE).astype(F32) > 0.5
            gates = dense_gates(logits, allowed & (lanes(2 * seq) < EXPERTS))
            gates_out[pl.ds(pair * 2, 2)] = gates.reshape(2, seq, LANE)
            gated = []
            for j in range(2):
                rows = slice(j * seq, (j + 1) * seq)
                query = [
                    rotate(proj[rows, e * HEAD : (e + 1) * HEAD], cos_ref[...], sin_ref[...]).astype(BF)
                    for e in range(2)
                ]
                key = rotate(proj[rows, 2 * HEAD : 3 * HEAD], cos_ref[...], sin_ref[...]).astype(BF)
                value = proj[rows, 3 * HEAD :].astype(BF)
                probs = soft(mm_nt(jnp.concatenate(query, axis=0), key) * scale, causal)
                attended = mm(probs.astype(BF), value)
                out = [
                    (attended[e * seq : (e + 1) * seq] * pick(gates[rows], first + e)).astype(BF)
                    for e in range(2)
                ]
                qkv_out[pair * 2 + j] = jnp.concatenate(query + [key, value], axis=1)
                gated.append(jnp.concatenate(out, axis=1))
                gated_out[pair * 2 + j] = gated[-1]
            branch = mm_nt(jnp.concatenate(gated, axis=0), w_ref[:, 4 * HEAD :])
            part[pl.ds(pair * 2, 2)] = branch.astype(BF).reshape(2, 2, 2, own, width)
            for j in range(2):
                team.swap(pair * 2 + j).start()

            @pl.when(i > 0)
            def _():
                for j in range(2):
                    team.forward(team.pair(i - 1) * 2 + j)

            return 0

        lax.fori_loop(0, 4, step, 0)
        team.last()
        team.total(total)
        after = total[...] + own_ref[...].astype(F32)
        after_out[...] = after
        row[...] = (after * rms_scale(after) * gain_m_ref[...]).astype(BF)
        TeamSpread(row, spread_out, rest[6:]).run()
        team.close()

    return pl.pallas_call(
        kernel,
        out_shape=[
            jax.ShapeDtypeStruct((8, seq, width), BF),
            jax.ShapeDtypeStruct((8, seq, 4 * HEAD), BF),
            jax.ShapeDtypeStruct((8, seq, 2 * HEAD), BF),
            jax.ShapeDtypeStruct((8, seq, LANE), F32),
            jax.ShapeDtypeStruct((own, width), F32),
            jax.ShapeDtypeStruct((16, 2, own, width), BF),
        ],
        in_specs=[VMEM] * 9,
        out_specs=[VMEM] * 5 + [ANY],
        scratch_shapes=[
            pltpu.VMEM((8, 2, 2, own, width), BF),
            pltpu.VMEM((own, width), F32),
            pltpu.VMEM((own, width), BF),
        ]
        + TeamSum.scratch(own, width)
        + TeamSpread.sems,
        name="attn_forward",
        **settings(collective, 200 << 20, 48),
    )(hidden, masks, weights, gain, routers, cosines, sines, mlp_gain, hidden_own)


def experts(normed, cotangent, masks, routers, weights, extra):
    rows, width = normed.shape
    part = weights[0].shape[1]
    tile = rows // 4

    def kernel(x_ref, cot_ref, mask, router_ref, wg, wu, wd, h_out, dg_out, du_out, branch_out, back_out, gates_out):
        lane = EXPERTS + lax.axis_index("x")
        skip = lax.axis_index("zl") * extra
        x = x_ref[...]
        logits = mm(x, router_ref[...])
        index = lanes(tile)
        allowed = (mask[...].astype(F32) > 0.5) & (index >= EXPERTS) & (index < 2 * EXPERTS)
        gates = dense_gates(logits, allowed)
        gates_out[...] = gates
        valid = (lax.broadcasted_iota(jnp.int32, (1, part), 1) >= skip).astype(F32)
        gate = pick(gates, lane) * valid
        gate_part = mm(x, wg[...])
        up_part = mm(x, wu[...])
        sigma = 1.0 / (1.0 + jnp.exp(-gate_part))
        silu = gate_part * sigma
        activated = silu * up_part
        h = (activated * gate).astype(BF)
        h_out[...] = h
        branch_out[...] = mm_nt(h, wd[...]).astype(BF)
        cot_down = mm(cot_ref[...], wd[...])
        dots = jnp.sum(activated * valid * cot_down, axis=1, keepdims=True)
        grad_act = cot_down * gate
        grad_gate = (grad_act * up_part * sigma * (1.0 + gate_part * (1.0 - sigma))).astype(BF)
        grad_up = (grad_act * silu).astype(BF)
        dg_out[...] = grad_gate
        du_out[...] = grad_up
        back_out[:, :width] = (mm_nt(grad_gate, wg[...]) + mm_nt(grad_up, wu[...])).astype(BF)
        back_out[:, width:] = jnp.where(index == lane, dots, 0.0).astype(BF)

    def tiled(cols):
        return pl.BlockSpec((tile, cols), lambda i: (i, 0))

    def whole(array):
        return pl.BlockSpec(array.shape, lambda i: (0, 0), pipeline_mode=pl.Buffered(1))

    cols = [part, part, part, width, width + LANE]
    return pl.pallas_call(
        kernel,
        grid=(4,),
        out_shape=[jax.ShapeDtypeStruct((rows, c), BF) for c in cols]
        + [jax.ShapeDtypeStruct((rows, LANE), F32)],
        in_specs=[tiled(width), tiled(width), tiled(LANE), whole(routers)]
        + [whole(w) for w in weights],
        out_specs=[tiled(c) for c in cols] + [tiled(LANE)],
        compiler_params=pltpu.CompilerParams(vmem_limit_bytes=48 << 20),
        cost_estimate=pl.CostEstimate(
            flops=12 * rows * width * part, bytes_accessed=40 << 20, transcendentals=rows * part
        ),
        name="experts",
    )(normed, cotangent, masks, routers, *weights)


def attn_backward(grad_mid, qkv, gates, weights, cosines, sines):
    rows, width = grad_mid.shape
    tile = rows // 4
    seq = tile // 2
    scale = HEAD ** (-0.5)

    def kernel(gm_ref, qkv_ref, gates_ref, w_ref, cos_ref, sin_ref, proj_out, back_out):
        first = 2 * lax.axis_index("zl")
        causal = causal_mask(2, seq)
        grads = mm(gm_ref[...], w_ref[:, 4 * HEAD :])
        gates = gates_ref[...]
        index = lanes(tile)
        dots = jnp.zeros((tile, LANE), F32)
        for j in range(2):
            here = slice(j * seq, (j + 1) * seq)
            query = jnp.concatenate(
                [qkv_ref[here, e * HEAD : (e + 1) * HEAD] for e in range(2)], axis=0
            )
            key = qkv_ref[here, 2 * HEAD : 3 * HEAD]
            value = qkv_ref[here, 3 * HEAD :]
            probs = soft(mm_nt(query, key) * scale, causal)
            probs_b = probs.astype(BF)
            attended = mm(probs_b, value)
            grad = jnp.concatenate(
                [grads[here, e * HEAD : (e + 1) * HEAD] for e in range(2)], axis=0
            )
            gate = jnp.concatenate([pick(gates[here], first + e) for e in range(2)], axis=0)
            each = jnp.sum(attended * grad, axis=1, keepdims=True)
            spread = jnp.where(lanes(seq) == first, each[:seq], 0.0)
            spread += jnp.where(lanes(seq) == first + 1, each[seq:], 0.0)
            grad = (grad * gate).astype(BF)
            grad_probs = mm_nt(grad, value)
            inner = jnp.sum(probs * grad_probs, axis=1, keepdims=True)
            grad_scores = (probs * (grad_probs - inner) * scale).astype(BF)
            grad_query = mm(grad_scores, key)
            grad_key = mm_tn(grad_scores, query)
            grad_value = mm_tn(probs_b, grad)
            proj_out[here, :HEAD] = rotate(grad_query[:seq], cos_ref[...], -sin_ref[...]).astype(BF)
            proj_out[here, HEAD : 2 * HEAD] = rotate(
                grad_query[seq:], cos_ref[...], -sin_ref[...]
            ).astype(BF)
            proj_out[here, 2 * HEAD : 3 * HEAD] = rotate(
                grad_key, cos_ref[...], -sin_ref[...]
            ).astype(BF)
            proj_out[here, 3 * HEAD :] = grad_value.astype(BF)
            back_out[here, width:] = spread.astype(BF)
        back_out[:, :width] = mm_nt(proj_out[...], w_ref[:, : 4 * HEAD]).astype(BF)

    def tiled(cols):
        return pl.BlockSpec((tile, cols), lambda i: (i, 0))

    def whole(array):
        return pl.BlockSpec(array.shape, lambda i: (0, 0), pipeline_mode=pl.Buffered(1))

    return pl.pallas_call(
        kernel,
        grid=(4,),
        out_shape=[
            jax.ShapeDtypeStruct((rows, 4 * HEAD), BF),
            jax.ShapeDtypeStruct((rows, width + LANE), BF),
        ],
        in_specs=[tiled(width), tiled(4 * HEAD), tiled(LANE)]
        + [whole(a) for a in (weights, cosines, sines)],
        out_specs=[tiled(4 * HEAD), tiled(width + LANE)],
        compiler_params=pltpu.CompilerParams(vmem_limit_bytes=48 << 20),
        cost_estimate=pl.CostEstimate(
            flops=2 * rows * width * 6 * HEAD, bytes_accessed=20 << 20, transcendentals=0
        ),
        name="attn_backward",
    )(grad_mid, qkv, gates, weights, cosines, sines)


def back_through_norm(total, inputs, gain, gates, normed, routers):
    width = inputs.shape[1]
    logits_back = gates_back(gates, total[:, width:])
    full = total[:, :width] + mm_nt(logits_back.astype(BF), routers)
    inner, gain_grad = norm_back(inputs, gain, full)
    return inner, gain_grad, mm_tn(logits_back.astype(BF), normed)[:8]


def middle(collective, back, after, gain, gates_own, routers, cot_own):
    own, width = after.shape

    def kernel(part_ref, after_ref, gain_ref, gates_ref, router_ref, cot_ref, mid_out, small_out, spread_out, part, load, total, row, *rest):
        fetch = pltpu.make_async_copy(part_ref, part, load.at[0])
        fetch.start()
        meet_team()
        fetch.wait()
        team = TeamSum(part, rest[:6])
        team.run()
        after = after_ref[...]
        normed = (after * rms_scale(after) * gain_ref[...]).astype(BF)
        team.total(total)
        inner, gain_grad, router_grad = back_through_norm(
            total[...], after, gain_ref[...], gates_ref[...], normed, router_ref[...]
        )
        grad_mid = cot_ref[...].astype(F32) + inner
        mid_out[...] = grad_mid
        row[...] = grad_mid.astype(BF)
        small_out[:8] = jnp.zeros((8, width), F32)
        small_out[0:1] = gain_grad
        small_out[8:] = router_grad
        TeamSpread(row, spread_out, rest[6:]).run()
        team.close()

    return pl.pallas_call(
        kernel,
        out_shape=[
            jax.ShapeDtypeStruct((own, width), F32),
            jax.ShapeDtypeStruct((16, width), F32),
            jax.ShapeDtypeStruct((16, 2, own, width), BF),
        ],
        in_specs=[ANY] + [VMEM] * 5,
        out_specs=[VMEM] * 2 + [ANY],
        scratch_shapes=[
            pltpu.VMEM((8, 2, 2, own, width + LANE), BF),
            pltpu.SemaphoreType.DMA((1,)),
            pltpu.VMEM((own, width + LANE), F32),
            pltpu.VMEM((own, width), BF),
        ]
        + TeamSum.scratch(own, width + LANE)
        + TeamSpread.sems,
        name="middle",
        **settings(collective, 160 << 20, 48),
    )(back.reshape(8, 2, 2, own, width + LANE), after, gain, gates_own, routers, cot_own)


def leave(collective, back, branch, after, grad_mid, inputs, gain, gates_own, routers, small):
    own, width = after.shape
    stages = [moves("c"), moves("x"), moves("y"), moves("zl", "zh")]
    near = moves("zh", "c")

    def kernel(
        back_ref, branch_ref, after_ref, mid_ref, in_ref, gain_ref, gates_ref, router_ref, small_ref,
        out_all, grad_all, small_out,
        part_a, part_b, load, total_a, total_b, row_a, row_b, got, send, recv, ssend, srecv, *rest,
    ):
        fetches = [
            pltpu.make_async_copy(back_ref, part_a, load.at[0]),
            pltpu.make_async_copy(branch_ref, part_b, load.at[1]),
        ]
        for fetch in fetches:
            fetch.start()
        meet([place(m) for m in TEAM_MOVES[1:] + Y_MOVES[1:]] + [place(m) for m in near[1:] if m["c"]])
        team_a, team_b = TeamSum(part_a, rest[:6]), TeamSum(part_b, rest[6:])
        fetches[0].wait()
        team_a.run()
        fetches[1].wait()
        team_b.run()
        inputs = in_ref[...].astype(F32)
        normed = (inputs * rms_scale(inputs) * gain_ref[...]).astype(BF)
        team_a.total(total_a)
        inner, gain_grad, router_grad = back_through_norm(
            total_a[...], inputs, gain_ref[...], gates_ref[...], normed, router_ref[...]
        )
        row_a[...] = (mid_ref[...] + inner).astype(BF)
        small_out[...] = small_ref[...]
        small_out[1:2] = gain_grad
        small_out[8:] += router_grad
        me = number(place(near[0]))
        copies = []

        def spread(i, src, dst):
            new = [pltpu.make_async_copy(src, dst.at[me], send.at[i, 0])]
            for k in range(1, 4):
                new.append(push(src, dst.at[me], send.at[i, k], recv.at[i, k], place(near[k])))
            for copy in new:
                copy.start()
            copies.extend(new)

        spread(0, row_a, grad_all)
        for s, stage in enumerate(stages):
            swaps = [
                push(small_out, got.at[s, k - 1], ssend.at[s, k], srecv.at[s, k], place(stage[k]))
                for k in range(1, len(stage))
            ]
            for swap in swaps:
                swap.start()
            if s == 0:
                team_b.total(total_b)
                row_b[...] = (after_ref[...] + total_b[...]).astype(BF)
                spread(1, row_b, out_all)
            for swap in swaps:
                swap.wait()
            total = small_out[...]
            for k in range(1, len(stage)):
                total += got[s, k - 1]
            small_out[...] = total
        for copy in copies:
            copy.wait()
        team_a.close()
        team_b.close()

    return pl.pallas_call(
        kernel,
        out_shape=[jax.ShapeDtypeStruct((4, own, width), BF)] * 2
        + [jax.ShapeDtypeStruct((16, width), F32)],
        in_specs=[ANY, ANY] + [VMEM] * 7,
        out_specs=[ANY, ANY, VMEM],
        scratch_shapes=[
            pltpu.VMEM((8, 2, 2, own, width + LANE), BF),
            pltpu.VMEM((8, 2, 2, own, width), BF),
            pltpu.SemaphoreType.DMA((2,)),
            pltpu.VMEM((own, width + LANE), F32),
            pltpu.VMEM((own, width), F32),
            pltpu.VMEM((own, width), BF),
            pltpu.VMEM((own, width), BF),
            pltpu.VMEM((4, 3, 16, width), F32),
        ]
        + [pltpu.SemaphoreType.DMA((2, 4))] * 2
        + [pltpu.SemaphoreType.DMA((4, 4))] * 2
        + TeamSum.scratch(own, width + LANE)
        + TeamSum.scratch(own, width),
        name="leave",
        **settings(collective, 200 << 20, 48),
    )(
        back.reshape(8, 2, 2, own, width + LANE),
        branch.reshape(8, 2, 2, own, width),
        after, grad_mid, inputs, gain, gates_own, routers, small,
    )


def reorder(array, axis):
    shape = array.shape
    split = shape[:axis] + (2, 4, shape[axis] // 8) + shape[axis + 1 :]
    return jnp.swapaxes(array.reshape(split), axis, axis + 1).reshape(shape)


def restore(array, axis):
    shape = array.shape
    split = shape[:axis] + (4, 2, shape[axis] // 8) + shape[axis + 1 :]
    return jnp.swapaxes(array.reshape(split), axis, axis + 1).reshape(shape)


def gather_y(block):
    return lax.all_gather(block.reshape(-1, block.shape[2]), "y", axis=0, tiled=True)


def sum_y(grad):
    summed = lax.psum_scatter(grad.astype(BF), "y", scatter_dimension=0, tiled=True)
    return summed.reshape(8, -1, grad.shape[1])


def local(
    hidden,
    cotangent,
    attn_gain,
    attn_router,
    qkv_weight,
    out_weight,
    mlp_gain,
    mlp_router,
    gate_up_weight,
    down_weight,
    attn_route,
    attn_slot,
    mlp_route,
    mlp_slot,
):
    seq, width = hidden.shape
    rows = qkv_weight.shape[0]
    features = down_weight.shape[2]
    part = (features // LANE + 1) // 2 * LANE
    low = features - part
    zl, x = lax.axis_index("zl"), lax.axis_index("x")
    quarter = lax.axis_index("zh") * 2 + lax.axis_index("c")
    own = seq // 4
    group = 8 * seq
    cosines, sines = rope_tables(seq)

    query_blocks = qkv_weight[:, :EXPERTS].reshape(rows, 2, 2, 4, HEAD).transpose(1, 3, 0, 2, 4)
    kv_blocks = qkv_weight[:, EXPERTS:].reshape(rows, 2, 4, HEAD).transpose(2, 0, 1, 3)
    kv_blocks = jnp.broadcast_to(kv_blocks[None], (2,) + kv_blocks.shape)
    out_blocks = out_weight.reshape(rows, 2, 2, 4, HEAD).transpose(1, 3, 0, 2, 4)
    attn_blocks = jnp.concatenate([query_blocks, kv_blocks, out_blocks], axis=3)
    attn_blocks = attn_blocks.reshape(8, rows, 6 * HEAD)

    def by_target(weight):
        weight = weight.transpose(1, 0, 2)
        return jnp.stack([weight[..., :part], weight[..., low:]], axis=0).reshape(8, rows, part)

    mlp_blocks = [
        by_target(w) for w in (gate_up_weight[:, :, 0], gate_up_weight[:, :, 1], down_weight)
    ]

    masks = jnp.concatenate([chosen_mask(attn_route), chosen_mask(mlp_route)], axis=1)
    masks = jnp.pad(masks.astype(BF), ((0, 0), (0, LANE - 2 * EXPERTS)))
    attn_gain, mlp_gain = reorder(attn_gain, 0)[None], reorder(mlp_gain, 0)[None]
    routers = reorder(jnp.concatenate([attn_router, mlp_router], axis=1), 0)
    routers = jnp.pad(routers, ((0, 0), (0, LANE - 2 * EXPERTS)))
    hidden = reorder(hidden, 1)
    cotangent = reorder(cotangent, 1)
    hidden_own = lax.dynamic_slice_in_dim(hidden, quarter * own, own, axis=0)
    cot_own = lax.dynamic_slice_in_dim(cotangent, quarter * own, own, axis=0)
    start = (zl * 4 + x) * seq + quarter * own

    def mine(array):
        return lax.dynamic_slice_in_dim(array, start, own, axis=0)

    group_in, masks, attn_rows = enter(1, hidden, masks, attn_blocks)
    attn_w, *mlp_rows, group_cot = along_y(
        2, attn_rows.reshape(8 * rows, 6 * HEAD), mlp_blocks, cotangent
    )
    attn_w = attn_w.reshape(width, 6 * HEAD)
    mlp_w = [gather_y(block) for block in mlp_rows]
    group_cot = group_cot.reshape(group, width)

    normed_a, qkv, gated_att, gates_a, after, normed_m = attn_forward(
        3, group_in, masks, attn_w, attn_gain, routers, cosines, sines, mlp_gain, hidden_own
    )
    normed_a = normed_a.reshape(group, width)
    normed_m = normed_m.reshape(group, width)
    gates_a = gates_a.reshape(group, LANE)

    h, grad_gate, grad_up, branch_m, back_m, gates_m = experts(
        normed_m, group_cot, masks.reshape(group, LANE), routers, mlp_w, 2 * part - features
    )
    mlp_grads = [
        sum_y(mm_tn(normed_m, grad_gate)),
        sum_y(mm_tn(normed_m, grad_up)),
        sum_y(mm_tn(group_cot, h)),
    ]
    grad_mid_own, small_m, grad_mid = middle(
        4, back_m, after, mlp_gain, mine(gates_m), routers, cot_own
    )
    grad_mid = grad_mid.reshape(group, width)
    grad_proj, back_a = attn_backward(
        grad_mid, qkv.reshape(group, 4 * HEAD), gates_a, attn_w, cosines, sines
    )
    attn_grads = sum_y(
        jnp.concatenate(
            [
                mm_tn(normed_a, grad_proj).astype(BF),
                mm_tn(grad_mid, gated_att.reshape(group, 2 * HEAD)).astype(BF),
            ],
            axis=1,
        )
    )
    out_hidden, grad_in, small = leave(
        5, back_a, branch_m, after, grad_mid_own, hidden_own, attn_gain, mine(gates_a), routers, small_m
    )
    out_hidden = restore(out_hidden.reshape(seq, width), 1)
    grad_in = restore(grad_in.reshape(seq, width), 1).astype(F32)
    small = restore(small, 1)

    *mlp_grads, attn_grads = swap_back(6, "swap_back", mlp_grads + [attn_grads])
    attn_grads = attn_grads.astype(F32).reshape(2, 4, rows, 6, HEAD).transpose(2, 0, 3, 1, 4)
    attn_grads = attn_grads.reshape(rows, 2, 6, 4 * HEAD)
    query_grad = attn_grads[:, :, :2].reshape(rows, EXPERTS, 4 * HEAD)
    kv_grad = attn_grads[:, 0, 2:4] + attn_grads[:, 1, 2:4]
    qkv_grad = jnp.concatenate([query_grad, kv_grad], axis=1)
    out_grad = attn_grads[:, :, 4:].reshape(rows, EXPERTS, 4 * HEAD)

    def placed_back(grad):
        grad = grad.reshape(2, EXPERTS, rows, part)
        return jnp.concatenate([grad[0], grad[1, ..., 2 * part - features :]], axis=-1).transpose(1, 0, 2)

    gate_grad, up_grad, down_grad = [placed_back(g) for g in mlp_grads]
    return (
        out_hidden,
        grad_in,
        small[1],
        small[8 : 8 + EXPERTS].T,
        qkv_grad,
        out_grad,
        small[0],
        small[8 + EXPERTS :].T,
        jnp.stack([gate_grad, up_grad], axis=2).astype(F32),
        down_grad.astype(F32),
    )


def solution(mesh):
    fine = Mesh(mesh.devices.reshape(2, 4, 4, 2, 2), ALL)
    dp, tensor = ("zl", "y", "x"), ("zh", "c")
    placed = (
        P(dp, None),
        P(dp, None),
        P(),
        P(),
        P(dp, None, tensor),
        P(dp, None, tensor),
        P(),
        P(),
        P(dp, None, None, tensor),
        P(dp, None, tensor),
        P(dp, None),
        P(dp, None),
        P(dp, None),
        P(dp, None),
    )
    return jax.shard_map(
        local,
        mesh=fine,
        in_specs=placed,
        out_specs=(
            P(dp, None),
            P(dp, None),
            P(),
            P(),
            P(dp, None, tensor),
            P(dp, None, tensor),
            P(),
            P(),
            P(dp, None, None, tensor),
            P(dp, None, tensor),
        ),
        check_vma=False,
    )
```

time: 699 us -> 638 us (0.913)
  matrix products: 117 us -> 29.6 us
  waiting for transfers between devices: 1.49 us -> 80.4 us
  local copies, waits for them, and re-layouts: 96.3 us -> 54.3 us
  other arithmetic: 33.5 us -> 7.32 us
  Pallas kernels: 421 us -> 441 us
    dot_general x16 -> x5, matrix products: 84.7 us -> 29.6 us  [dot(): return lax.dot_general(a, b, (dims, ((), ())), preferred_element_type=F32)]
    all_gather x3, waiting for transfers between devices: 0.02 us -> 44.9 us  [gather_y(): lax.all_gather(block.reshape(-1, block.shape[2]), 'y', axis=0, tiled=True)]
    reduce_scatter x4, waiting for transfers between devices: 0.01 us -> 34.1 us  [sum_y(): lax.psum_scatter(grad.astype(BF), 'y', scatter_dimension=0, tiled=True)]
    dot_general x11 -> x0, matrix products: 28.8 us -> none  [the longest x1 3.96 us: local(): jnp.einsum('ntw,ndw->td', grad_proj, attn_w[:4], preferred_element_type=F32)]
    pallas_call x10 -> x7, Pallas kernels: 375 us -> 395 us  [the longest x1 94.2 us: leave(): pl.pallas_call(kernel, out_shape=[jax.ShapeDtypeStruct((4, own, width), B...]
    unnamed x77 -> x54, local copies, waits for them, and re-layouts: 30.6 us -> 22.6 us
    convert_element_type x9 -> x2, other arithmetic: 8.12 us -> 0.29 us  [the longest x1 0.19 us: local(): jnp.stack([gate_grad, up_grad], axis=2).astype(F32)]
  transfers between devices with their start and end apart: 7 -> 7, of which waited for: 0 -> 3; matrix products, arithmetic and copies ran while one was open for 25% -> 5% of each run, Pallas kernels for 42% -> 27%
where the time goes in v3:
time: 638 us; the launch traced here: 629 us
  Pallas kernels  441 us (69%)
  waiting for transfers between devices  80.4 us (13%)
  local copies, waits for them, and re-layouts  54.3 us (9%)
  matrix products  29.6 us (5%)
  between operations  15 us (2%)
  other arithmetic  7.32 us (1%)
    pallas_call x1, Pallas kernels, leave(): pl.pallas_call(kernel, out_shape=[jax.ShapeDtypeStruct((4, own, width), B...  94.2 us
    pallas_call x1, Pallas kernels, attn_forward(): pl.pallas_call(kernel, out_shape=[jax.ShapeDtypeStruct((8, seq, width), B...  74.8 us
    pallas_call x1, Pallas kernels, middle(): pl.pallas_call(kernel, out_shape=[jax.ShapeDtypeStruct((own, width), F32)...  74 us
    pallas_call x1, Pallas kernels, along_y(): pl.pallas_call(kernel, out_shape=[jax.ShapeDtypeStruct((4,) + rows_a.shap...  67.2 us
    pallas_call x1, Pallas kernels, enter(): pl.pallas_call(kernel, out_shape=[jax.ShapeDtypeStruct((8, rows, width),...  46.7 us
    all_gather x3, waiting for transfers between devices, gather_y(): lax.all_gather(block.reshape(-1, block.shape[2]), 'y', axis=0, tiled=True)  44.9 us
    pallas_call x1, Pallas kernels, swap_back(): pl.pallas_call(kernel, out_shape=[jax.ShapeDtypeStruct(b.shape, b.dtype)...  41.8 us
    reduce_scatter x4, waiting for transfers between devices, sum_y(): lax.psum_scatter(grad.astype(BF), 'y', scatter_dimension=0, tiled=True)  34.1 us
  transfers between devices with their start and end apart: 7, of which 3 were waited for; matrix products, arithmetic and copies ran while one was open for 5% of the time, Pallas kernels for 27%

profile of v3, /device:TPU:0, one launch (start us, length us, event | category | flops | bytes accessed | tf_op | source)
XLA Modules:
  0.0 628.8 jit_solution(14448407623813667277)
XLA Ops:
  7.2 1.0 slice.99
  8.2 0.9 slice.100
  9.1 0.8 slice_bitcast_fusion.14
  9.9 0.8 slice_bitcast_fusion.12
  10.9 1.1 reshape.180
  12.1 0.5 copy_bitcast_fusion.4
  12.8 0.9 pad_maximum_fusion.1
  13.7 0.9 reshape.181.block_ref
  15.0 0.4 copy.111
  15.4 0.4 reshape.177.hidden_ref
  15.8 4.4 fusion.4
  20.4 0.9 slice_bitcast_fusion.3
  21.4 0.9 slice_bitcast_fusion.5
  22.6 0.6 pad_maximum_fusion.4
  23.7 0.4 copy.110
  24.2 0.4 reshape.187.refs_3_
  24.5 1.2 pad_maximum_fusion.3
  25.7 1.2 pad_maximum_fusion.2
  26.9 46.7 %enter.1 = (bf16[8,128,2048]{2,1,0:T(8,128)(2,1)S(1)}, bf16[8,128,128]{2,1,0:T(8,128)(2,1)S(1)}, bf16[8,64,768]{2,1,0:T(8,128)(2,1)S(1)}) custom-call(bf16[128,2048]{1,0:T(8,128)(2,1)S(1)} %reshape.177.hidden_ref, bf16[128,128]{1,0:T(8,128)(2,1)S(1)} %pad_convert_fusion.mask_ref, bf16[8,64,768]{2,1,0:T(8,128)(2,1)S(1)} %reshape.181.block_ref), custom_call_target="tpu_custom_call" | custom-call | bytes 94371840 | tf_op jit(solution)/shard_map/enter/pallas_call | solution.py:229
  73.6 2.1 copy-done
  75.7 67.2 %along_y.1 = (bf16[4,512,768]{2,1,0:T(8,128)(2,1)S(1)}, bf16[8,64,768]{2,1,0:T(8,128)(2,1)}, bf16[8,64,768]{2,1,0:T(8,128)(2,1)}, bf16[8,64,768]{2,1,0:T(8,128)(2,1)}, bf16[8,128,2048]{2,1,0:T(8,128)(2,1)S(1)}) custom-call(bf16[512,768]{1,0:T(8,128)(2,1)S(1)} %bitcast.128, bf16[8,64,768]{2,1,0:T(8,128)(2,1)S(1)} %bitcast.124, ...), custom_call_target="tpu_custom_call" | custom-call | bytes 125829120 | tf_op jit(solution)/shard_map/along_y/pallas_call | solution.py:267
  142.9 1.6 copy-done.1
  144.5 2.0 copy-done.10
  146.6 0.7 all-gather.6.cloned.1.call-update
  147.3 0.7 all-gather.8.cloned.1.call-update
  148.7 74.8 %attn_forward.1 = (bf16[8,128,2048]{2,1,0:T(8,128)(2,1)}, bf16[8,128,512]{2,1,0:T(8,128)(2,1)S(1)}, bf16[8,128,256]{2,1,0:T(8,128)(2,1)S(1)}, f32[8,128,128]{2,1...) custom-call(bf16[8,128,2048]{2,1,0:T(8,128)(2,1)} %copy-done, ...), custom_call_target="tpu_custom_call" | custom-call | bytes 209715200 | tf_op jit(solution)/shard_map/attn_forward/pallas_call | solution.py:498
  223.5 1.0 copy-done.12
  224.5 3.5 all-gather.6.cloned.1.call-done.wu
  227.9 41.4 %all-gather.8.cloned.1.call-done.wd = bf16[2048,768]{1,0:T(8,128)(2,1)} async-done(((bf16[512,768]{1,0:T(8,128)(2,1)}), bf16[2048,768]{1,0:T(8,128)(2,1)}) %all-gather.8.cloned.1.call-update) | async-done | bytes 3145744 | tf_op jit(solution)/shard_map/all_gather | solution.py:814
  269.4 30.4 %experts.1 = (bf16[1024,768]{1,0:T(8,128)(2,1)S(1)}, bf16[1024,768]{1,0:T(8,128)(2,1)S(1)}, bf16[1024,768]{1,0:T(8,128)(2,1)S(1)}, bf16[1024,2048]{1,0:T(8,128)(...) custom-call(bf16[1024,2048]{1,0:T(8,128)(2,1)} %bitcast.166, bf16[1024,2048]{1,0:T(8,128)(2,1)} %bitcast.138, ...), custom_call_target="tpu_custom_call" | custom-call | flops 19327352832 | bytes 41943040 | tf_op jit(solution)/shard_map/experts/pallas_call | solution.py:563
  299.8 74.0 %middle.1 = (f32[32,2048]{1,0:T(8,128)S(1)}, f32[16,2048]{1,0:T(8,128)S(1)}, bf16[16,2,32,2048]{3,2,1,0:T(8,128)(2,1)S(1)}) custom-call(bf16[8,2,2,32,2176]{4,3,2,1,0:T(8,128)(2,1)} %bitcast.146, f32[32,2048]{1,0:T(8,128)S(1)} %get-tuple-element.52.after_ref, f32[1,2048]{1,0:T(1,128)S(1)} %broadcast_in_dim_reshape.7.gain_m_ref.gain_ref, ...), custom_call_target="tpu_custom_call" | custom-call | bytes 167772160 | tf_op jit(solution)/shard_map/middle/pallas_call | solution.py:684
  373.9 1.3 convolution_convert_fusion.4
  375.2 0.8 copy-done.11
  376.0 1.3 copy-done.2
  377.5 12.4 %attn_backward.1 = (bf16[1024,512]{1,0:T(8,128)(2,1)S(1)}, bf16[1024,2176]{1,0:T(8,128)(2,1)}) custom-call(bf16[1024,2048]{1,0:T(8,128)(2,1)} %bitcast.141, bf16[1024,512]{1,0:T(8,128)(2,1)S(1)} %bitcast.142, f32[1024,128]{1,0:T(8,128)S(1)} %bitcast.136, bf16[2048,768]{1,0:T(8,128)(2,1)S(1)} %bitcast.127, f32[128,128]{1,0:T(8,128)S(1)} %copy-done.8, ...), custom_call_target="tpu_custom_call" | custom-call | flops 3221225472 | bytes 20971520 | tf_op jit(solution)/shard_map/attn_backward/pallas_call | solution.py:633
  390.0 4.6 convolution_convert_fusion.3
  394.5 2.1 pad_maximum_fusion
  396.7 7.8 %convolution_convert_fusion = bf16[2048,768]{1,0:T(8,128)(2,1)} fusion(bf16[1024,2048]{1,0:T(8,128)(2,1)} %bitcast.139, bf16[1024,768]{1,0:T(8,128)(2,1)} %copy-done.16), kind=kOutput, calls=%fused_computation | convolution fusion | flops 3222798336 | bytes 8912896 | tf_op jit(solution)/shard_map/dot_general | solution.py:29
  404.6 7.9 %convolution_convert_fusion.1 = bf16[2048,768]{1,0:T(8,128)(2,1)} fusion(bf16[1024,2048]{1,0:T(8,128)(2,1)} %bitcast.167, bf16[1024,768]{1,0:T(8,128)(2,1)} %copy-done.15), kind=kOutput, calls=%fused_computation.1 | convolution fusion | flops 3222798336 | bytes 8912896 | tf_op jit(solution)/shard_map/dot_general | solution.py:29
  412.5 0.4 reduce-scatter.5.cloned.1.call-start
  412.9 8.0 %convolution_convert_fusion.2 = bf16[2048,768]{1,0:T(8,128)(2,1)} fusion(bf16[1024,2048]{1,0:T(8,128)(2,1)} %bitcast.168, bf16[1024,768]{1,0:T(8,128)(2,1)} %copy-done.14), kind=kOutput, calls=%fused_computation.2 | convolution fusion | flops 3222798336 | bytes 8912896 | tf_op jit(solution)/shard_map/dot_general | solution.py:29
  421.0 94.2 %leave.1 = (bf16[4,32,2048]{2,1,0:T(8,128)(2,1)S(1)}, bf16[4,32,2048]{2,1,0:T(8,128)(2,1)S(1)}, f32[16,2048]{1,0:T(8,128)S(1)}) custom-call(bf16[8,2,2,32,2176]{4,3,2,1,0:T(8,128)(2,1)} %bitcast.145, bf16[8,2,2,32,2048]{4,3,2,1,0:T(8,128)(2,1)} %bitcast.147, f32[32,2048]{1,0:T(8,128)S(1)} %get-tuple-element.52.after_ref, ...), custom_call_target="tpu_custom_call" | custom-call | bytes 209715200 | tf_op jit(solution)/shard_map/leave/pallas_call | solution.py:772
  515.2 1.0 reshape.225
  516.5 1.5 reshape.221
  518.6 1.2 reshape.205
  520.0 0.6 slice.111
  520.6 0.6 slice.118
  521.2 0.6 copy.101
  521.9 0.6 copy.102
  522.5 1.4 copy.94
  523.9 34.0 %reduce-scatter.5.cloned.1.call-done = bf16[512,768]{1,0:T(8,128)(2,1)} async-done(((bf16[2048,768]{1,0:T(8,128)(2,1)}), bf16[512,768]{1,0:T(8,128)(2,1)}) %reduce-scatter.5.cloned.1.call-update) | async-done | bytes 786448 | tf_op jit(solution)/shard_map/reduce_scatter | solution.py:818
  558.0 1.1 copy-done.3
  559.1 1.1 copy-done.4
  560.2 1.1 copy-done.5
  561.4 41.8 %swap_back.1 = (bf16[8,64,768]{2,1,0:T(8,128)(2,1)S(1)}, bf16[8,64,768]{2,1,0:T(8,128)(2,1)S(1)}, bf16[8,64,768]{2,1,0:T(8,128)(2,1)S(1)}, bf16[8,64,768]{2,1,0:T(8,128)(2,1)S(1)}) custom-call(bf16[8,64,768]{2,1,0:T(8,128)(2,1)S(1)} %bitcast.131, bf16[8,64,768]{2,1,0:T(8,128)(2,1)S(1)} %bitcast.130, bf16[8,64,768]{2,1,0:T(8,128)(2,1)S(1)} %bitcast.129, ...), custom_call_target="tpu_custom_call" | custom-call | bytes 83886080 | tf_op jit(solution)/shard_map/swap_back/pallas_call | solution.py:292
  603.2 0.9 copy-done.6
  604.0 2.1 reshape.227
  606.2 3.8 copy.95
  609.9 2.1 reshape.223
  612.2 1.0 copy-done.7
  613.4 2.0 copy.98
  615.9 3.8 copy.97
  619.7 1.1 copy.96
  620.8 0.9 pad_maximum_fusion.5
  (96 shorter events, 4.9 us)
Async XLA Ops:
  7.2 217.3 %all-gather.4.cloned.1.call-start = ((), (), s32[]{:S(2)}) async-start(), calls=%async_computation.4 | async-start | bytes 3932160 | tf_op jit(solution)/shard_map/all_gather | solution.py:814
  12.7 2.0 copy-start.18
  20.4 1.9 copy-start.17
  22.3 1.0 copy-start.19
  73.6 2.1 copy-start
  142.8 1.6 copy-start.1
  144.5 2.0 copy-start.10
  146.5 1.6 copy-start.20
  146.5 1.6 copy-start.21
  146.5 1.9 copy-start.22
  146.5 2.0 copy-start.23
  146.5 2.2 copy-start.8
  146.5 2.2 copy-start.9
  146.5 81.4 %all-gather.6.cloned.1.call-start = ((), (), s32[]{:S(2)}) async-start(), calls=%async_computation.5 | async-start | bytes 3932160 | tf_op jit(solution)/shard_map/all_gather | solution.py:814
  147.3 122.1 %all-gather.8.cloned.1.call-start = ((), (), s32[]{:S(2)}) async-start(), calls=%async_computation.6 | async-start | bytes 3932160 | tf_op jit(solution)/shard_map/all_gather | solution.py:814
  148.0 374.4 %reduce-scatter.11.cloned.1.call-start = ((), (), s32[]{:S(2)}) async-start(), calls=%async_computation.10 | async-start | bytes 3932160 | tf_op jit(solution)/shard_map/reduce_scatter | solution.py:818
  223.5 1.0 copy-start.12
  299.8 74.1 %copy-start.14 = (bf16[1024,768]{1,0:T(8,128)(2,1)}, bf16[1024,768]{1,0:T(8,128)(2,1)S(1)}, u32[]{:S(2)}) copy-start(bf16[1024,768]{1,0:T(8,128)(2,1)S(1)} %get-tuple-element.64) | copy-start | bytes 4718596
  299.8 74.1 %copy-start.15 = (bf16[1024,768]{1,0:T(8,128)(2,1)}, bf16[1024,768]{1,0:T(8,128)(2,1)S(1)}, u32[]{:S(2)}) copy-start(bf16[1024,768]{1,0:T(8,128)(2,1)S(1)} %get-tuple-element.65) | copy-start | bytes 4718596
  299.8 74.1 %copy-start.16 = (bf16[1024,768]{1,0:T(8,128)(2,1)}, bf16[1024,768]{1,0:T(8,128)(2,1)S(1)}, u32[]{:S(2)}) copy-start(bf16[1024,768]{1,0:T(8,128)(2,1)S(1)} %get-tuple-element.66) | copy-start | bytes 4718596
  373.8 2.1 copy-start.11
  373.9 3.4 copy-start.2
  373.9 3.7 copy-start.13
  396.6 127.2 %reduce-scatter.9.cloned.1.call-start = ((), (), s32[]{:S(2)}) async-start(), calls=%async_computation.9 | async-start | bytes 3932160 | tf_op jit(solution)/shard_map/reduce_scatter | solution.py:818
  404.5 119.4 %reduce-scatter.7.cloned.1.call-start = ((), (), s32[]{:S(2)}) async-start(), calls=%async_computation.8 | async-start | bytes 3932160 | tf_op jit(solution)/shard_map/reduce_scatter | solution.py:818
  412.5 145.5 %reduce-scatter.5.cloned.1.call-start = ((), (), s32[]{:S(2)}) async-start(), calls=%async_computation.7 | async-start | bytes 3932160 | tf_op jit(solution)/shard_map/reduce_scatter | solution.py:818
  558.0 1.1 copy-start.3
  559.1 1.1 copy-start.4
  560.2 1.1 copy-start.5
  603.1 0.9 copy-start.6
  612.1 1.1 copy-start.7
Sparse Core Ops, SparseCore 0:
  146.6 39.8 all-gather.3
  188.2 39.7 all-gather.5
  229.6 39.7 all-gather.7
  396.8 34.5 reduce-scatter.10
  433.7 37.9 reduce-scatter.8
  473.9 43.5 reduce-scatter.6
  519.9 37.9 reduce-scatter.4

commit v4 on v3

--- a/solution.py
+++ b/solution.py
@@ -211,70 +211,62 @@
             copy.wait()
 
 
-def enter(collective, hidden, masks, blocks):
-    rows, width = hidden.shape
-
-    def kernel(hidden_ref, mask_ref, block_ref, hidden_out, mask_out, block_out, *sems):
+def enter(collective, attn_blocks, blocks):
+    def kernel(a_ref, *refs):
+        m_refs, a_mid, a_out, m_outs, sems = refs[:3], refs[3], refs[4], refs[5:8], refs[8:]
+        meet([place(m) for m in GROUP_MOVES[1:] + Y_MOVES[1:]])
+        first = Swap(a_ref, a_mid, sems[2:4])
+        first.start()
+        swaps = [Swap(m_refs[i], m_outs[i], sems[4 + 2 * i : 6 + 2 * i]) for i in range(3)]
+        for swap in swaps:
+            swap.start()
+        first.finish()
+        mine = a_out.at[lax.axis_index("y")]
+        copies = [pltpu.make_async_copy(a_mid, mine, sems[0].at[0])]
+        for k in range(1, 4):
+            copies.append(push(a_mid, mine, sems[0].at[k], sems[1].at[k], place(Y_MOVES[k])))
+        for copy in copies:
+            copy.start()
+        for swap in swaps:
+            swap.finish()
+        for copy in copies:
+            copy.wait()
+
+    like = jax.ShapeDtypeStruct(attn_blocks.shape, attn_blocks.dtype)
+    return pl.pallas_call(
+        kernel,
+        out_shape=[like, jax.ShapeDtypeStruct((4,) + like.shape, like.dtype)]
+        + [jax.ShapeDtypeStruct(b.shape, b.dtype) for b in blocks],
+        in_specs=[ANY] * 4,
+        out_specs=[ANY] * 5,
+        scratch_shapes=[pltpu.SemaphoreType.DMA((4,))] * 2 + Swap.sems * 4,
+        name="enter",
+        **settings(collective, 120 << 20),
+    )(attn_blocks, *blocks)[1:]
+
+
+def spread_in(collective, hidden, masks):
+    def kernel(hidden_ref, mask_ref, hidden_out, mask_out, *sems):
         meet([place(m) for m in GROUP_MOVES[1:]] + [sibling()])
-        swap = Swap(block_ref, block_out, sems[0:2])
-        first = Spread(mask_ref, mask_out, sems[2:6])
-        second = Spread(hidden_ref, hidden_out, sems[6:10])
-        swap.start()
+        first = Spread(mask_ref, mask_out, sems[0:4])
+        second = Spread(hidden_ref, hidden_out, sems[4:8])
         first.start()
         second.start()
         first.finish()
         second.finish()
-        swap.finish()
 
     return pl.pallas_call(
         kernel,
         out_shape=[
-            jax.ShapeDtypeStruct((8, rows, width), hidden.dtype),
+            jax.ShapeDtypeStruct((8,) + hidden.shape, hidden.dtype),
             jax.ShapeDtypeStruct((8,) + masks.shape, masks.dtype),
-            jax.ShapeDtypeStruct(blocks.shape, blocks.dtype),
         ],
-        in_specs=[ANY] * 3,
-        out_specs=[ANY] * 3,
-        scratch_shapes=Swap.sems + Spread.sems * 2,
-        name="enter",
+        in_specs=[ANY] * 2,
+        out_specs=[ANY] * 2,
+        scratch_shapes=Spread.sems * 2,
+        name="spread_in",
         **settings(collective, 90 << 20),
-    )(hidden, masks, blocks)
-
-
-def along_y(collective, rows_a, blocks_m, cotangent):
-    def kernel(a_ref, *refs):
-        m_refs, cot_ref, a_out, m_outs, cot_out = refs[:3], refs[3], refs[4], refs[5:8], refs[8]
-        sems = refs[9:]
-        meet([place(m) for m in GROUP_MOVES[1:] + Y_MOVES[1:]] + [sibling()])
-        y = lax.axis_index("y")
-        copies = [pltpu.make_async_copy(a_ref, a_out.at[y], sems[0].at[0])]
-        for k, move in enumerate(Y_MOVES):
-            if k:
-                copies.append(push(a_ref, a_out.at[y], sems[0].at[k], sems[1].at[k], place(move)))
-        for copy in copies:
-            copy.start()
-        swaps = [Swap(m_refs[i], m_outs[i], sems[2 + 2 * i : 4 + 2 * i]) for i in range(3)]
-        spread = Spread(cot_ref, cot_out, sems[8:12])
-        for swap in swaps:
-            swap.start()
-        spread.start()
-        for copy in copies:
-            copy.wait()
-        for swap in swaps:
-            swap.finish()
-        spread.finish()
-
-    return pl.pallas_call(
-        kernel,
-        out_shape=[jax.ShapeDtypeStruct((4,) + rows_a.shape, rows_a.dtype)]
-        + [jax.ShapeDtypeStruct(b.shape, b.dtype) for b in blocks_m]
-        + [jax.ShapeDtypeStruct((8,) + cotangent.shape, cotangent.dtype)],
-        in_specs=[ANY] * 5,
-        out_specs=[ANY] * 5,
-        scratch_shapes=[pltpu.SemaphoreType.DMA((4,))] * 2 + Swap.sems * 3 + Spread.sems,
-        name="along_y",
-        **settings(collective, 120 << 20),
-    )(rows_a, *blocks_m, cotangent)
+    )(hidden, masks)
 
 
 def swap_back(collective, name, blocks):
@@ -430,18 +422,22 @@
     return lax.broadcasted_iota(jnp.int32, (copies * seq, seq), 1) <= rows
 
 
-def attn_forward(collective, hidden, masks, weights, gain, routers, cosines, sines, mlp_gain, hidden_own):
+def attn_forward(
+    collective, hidden, masks, weights, gain, routers, cosines, sines, mlp_gain, hidden_own, cotangent
+):
     _, seq, width = hidden.shape
     own = hidden_own.shape[0]
     scale = HEAD ** (-0.5)
 
     def kernel(
-        hid, mask, w_ref, gain_ref, router_ref, cos_ref, sin_ref, gain_m_ref, own_ref,
-        normed_out, qkv_out, gated_out, gates_out, after_out, spread_out,
+        hid, mask, w_ref, gain_ref, router_ref, cos_ref, sin_ref, gain_m_ref, own_ref, cot_ref,
+        normed_out, qkv_out, gated_out, gates_out, after_out, spread_out, cot_out,
         part, total, row, *rest,
     ):
         meet_team()
         team = TeamSum(part, rest[:6])
+        cot = Spread(cot_ref, cot_out, rest[10:])
+        cot.start()
         first = 2 * team.zl
         causal = causal_mask(2, seq)
 
@@ -488,11 +484,12 @@
 
         lax.fori_loop(0, 4, step, 0)
         team.last()
+        cot.finish()
         team.total(total)
         after = total[...] + own_ref[...].astype(F32)
         after_out[...] = after
         row[...] = (after * rms_scale(after) * gain_m_ref[...]).astype(BF)
-        TeamSpread(row, spread_out, rest[6:]).run()
+        TeamSpread(row, spread_out, rest[6:10]).run()
         team.close()
 
     return pl.pallas_call(
@@ -504,19 +501,21 @@
             jax.ShapeDtypeStruct((8, seq, LANE), F32),
             jax.ShapeDtypeStruct((own, width), F32),
             jax.ShapeDtypeStruct((16, 2, own, width), BF),
+            jax.ShapeDtypeStruct((8, seq, width), BF),
         ],
-        in_specs=[VMEM] * 9,
-        out_specs=[VMEM] * 5 + [ANY],
+        in_specs=[VMEM] * 9 + [ANY],
+        out_specs=[VMEM] * 5 + [ANY] * 2,
         scratch_shapes=[
             pltpu.VMEM((8, 2, 2, own, width), BF),
             pltpu.VMEM((own, width), F32),
             pltpu.VMEM((own, width), BF),
         ]
         + TeamSum.scratch(own, width)
-        + TeamSpread.sems,
+        + TeamSpread.sems
+        + Spread.sems,
         name="attn_forward",
         **settings(collective, 200 << 20, 48),
-    )(hidden, masks, weights, gain, routers, cosines, sines, mlp_gain, hidden_own)
+    )(hidden, masks, weights, gain, routers, cosines, sines, mlp_gain, hidden_own, cotangent)
 
 
 def experts(normed, cotangent, masks, routers, weights, extra):
@@ -703,14 +702,14 @@
     )(back.reshape(8, 2, 2, own, width + LANE), after, gain, gates_own, routers, cot_own)
 
 
-def leave(collective, back, branch, after, grad_mid, inputs, gain, gates_own, routers, small):
+def leave(collective, back, branch, after, grad_mid, inputs, gain, gates_own, routers, small, grads):
     own, width = after.shape
     stages = [moves("c"), moves("x"), moves("y"), moves("zl", "zh")]
     near = moves("zh", "c")
 
     def kernel(
         back_ref, branch_ref, after_ref, mid_ref, in_ref, gain_ref, gates_ref, router_ref, small_ref,
-        out_all, grad_all, small_out,
+        g0, g1, g2, out_all, grad_all, small_out, s0, s1, s2,
         part_a, part_b, load, total_a, total_b, row_a, row_b, got, send, recv, ssend, srecv, *rest,
     ):
         fetches = [
@@ -720,11 +719,17 @@
         for fetch in fetches:
             fetch.start()
         meet([place(m) for m in TEAM_MOVES[1:] + Y_MOVES[1:]] + [place(m) for m in near[1:] if m["c"]])
-        team_a, team_b = TeamSum(part_a, rest[:6]), TeamSum(part_b, rest[6:])
+        team_a, team_b = TeamSum(part_a, rest[:6]), TeamSum(part_b, rest[6:12])
         fetches[0].wait()
         team_a.run()
         fetches[1].wait()
         team_b.run()
+        grad_swaps = [
+            Swap(g, s, rest[12 + 2 * i : 14 + 2 * i])
+            for i, (g, s) in enumerate(((g0, s0), (g1, s1), (g2, s2)))
+        ]
+        for swap in grad_swaps:
+            swap.start()
         inputs = in_ref[...].astype(F32)
         normed = (inputs * rms_scale(inputs) * gain_ref[...]).astype(BF)
         team_a.total(total_a)
@@ -766,15 +771,18 @@
             small_out[...] = total
         for copy in copies:
             copy.wait()
+        for swap in grad_swaps:
+            swap.finish()
         team_a.close()
         team_b.close()
 
     return pl.pallas_call(
         kernel,
         out_shape=[jax.ShapeDtypeStruct((4, own, width), BF)] * 2
-        + [jax.ShapeDtypeStruct((16, width), F32)],
-        in_specs=[ANY, ANY] + [VMEM] * 7,
-        out_specs=[ANY, ANY, VMEM],
+        + [jax.ShapeDtypeStruct((16, width), F32)]
+        + [jax.ShapeDtypeStruct(g.shape, g.dtype) for g in grads],
+        in_specs=[ANY, ANY] + [VMEM] * 7 + [ANY] * 3,
+        out_specs=[ANY, ANY, VMEM] + [ANY] * 3,
         scratch_shapes=[
             pltpu.VMEM((8, 2, 2, own, width + LANE), BF),
             pltpu.VMEM((8, 2, 2, own, width), BF),
@@ -788,13 +796,14 @@
         + [pltpu.SemaphoreType.DMA((2, 4))] * 2
         + [pltpu.SemaphoreType.DMA((4, 4))] * 2
         + TeamSum.scratch(own, width + LANE)
-        + TeamSum.scratch(own, width),
+        + TeamSum.scratch(own, width)
+        + Swap.sems * 3,
         name="leave",
         **settings(collective, 200 << 20, 48),
     )(
         back.reshape(8, 2, 2, own, width + LANE),
         branch.reshape(8, 2, 2, own, width),
-        after, grad_mid, inputs, gain, gates_own, routers, small,
+        after, grad_mid, inputs, gain, gates_own, routers, small, *grads,
     )
 
 
@@ -875,17 +884,16 @@
     def mine(array):
         return lax.dynamic_slice_in_dim(array, start, own, axis=0)
 
-    group_in, masks, attn_rows = enter(1, hidden, masks, attn_blocks)
-    attn_w, *mlp_rows, group_cot = along_y(
-        2, attn_rows.reshape(8 * rows, 6 * HEAD), mlp_blocks, cotangent
-    )
+    attn_w, *mlp_rows = enter(1, attn_blocks, mlp_blocks)
     attn_w = attn_w.reshape(width, 6 * HEAD)
     mlp_w = [gather_y(block) for block in mlp_rows]
+    hidden, _ = lax.optimization_barrier((hidden, attn_w))
+    group_in, masks = spread_in(2, hidden, masks)
+
+    normed_a, qkv, gated_att, gates_a, after, normed_m, group_cot = attn_forward(
+        3, group_in, masks, attn_w, attn_gain, routers, cosines, sines, mlp_gain, hidden_own, cotangent
+    )
     group_cot = group_cot.reshape(group, width)
-
-    normed_a, qkv, gated_att, gates_a, after, normed_m = attn_forward(
-        3, group_in, masks, attn_w, attn_gain, routers, cosines, sines, mlp_gain, hidden_own
-    )
     normed_a = normed_a.reshape(group, width)
     normed_m = normed_m.reshape(group, width)
     gates_a = gates_a.reshape(group, LANE)
@@ -894,34 +902,38 @@
         normed_m, group_cot, masks.reshape(group, LANE), routers, mlp_w, 2 * part - features
     )
     mlp_grads = [
-        sum_y(mm_tn(normed_m, grad_gate)),
-        sum_y(mm_tn(normed_m, grad_up)),
-        sum_y(mm_tn(group_cot, h)),
+        mm_tn(normed_m, grad_gate).astype(BF),
+        mm_tn(normed_m, grad_up).astype(BF),
+        mm_tn(group_cot, h).astype(BF),
     ]
+    back_m = lax.optimization_barrier((back_m, *mlp_grads))[0]
+    mlp_grads = [sum_y(grad) for grad in mlp_grads]
     grad_mid_own, small_m, grad_mid = middle(
         4, back_m, after, mlp_gain, mine(gates_m), routers, cot_own
     )
+    grad_mid = lax.optimization_barrier((grad_mid, mlp_grads[0], mlp_grads[1]))[0]
     grad_mid = grad_mid.reshape(group, width)
     grad_proj, back_a = attn_backward(
         grad_mid, qkv.reshape(group, 4 * HEAD), gates_a, attn_w, cosines, sines
     )
-    attn_grads = sum_y(
-        jnp.concatenate(
-            [
-                mm_tn(normed_a, grad_proj).astype(BF),
-                mm_tn(grad_mid, gated_att.reshape(group, 2 * HEAD)).astype(BF),
-            ],
-            axis=1,
-        )
-    )
-    out_hidden, grad_in, small = leave(
-        5, back_a, branch_m, after, grad_mid_own, hidden_own, attn_gain, mine(gates_a), routers, small_m
+    attn_grads = jnp.concatenate(
+        [
+            mm_tn(normed_a, grad_proj).astype(BF),
+            mm_tn(grad_mid, gated_att.reshape(group, 2 * HEAD)).astype(BF),
+        ],
+        axis=1,
+    )
+    attn_grads = sum_y(lax.optimization_barrier((attn_grads, mlp_grads[2]))[0])
+    out_hidden, grad_in, small, *mlp_grads = leave(
+        5, back_a, branch_m, after, grad_mid_own, hidden_own, attn_gain, mine(gates_a), routers, small_m,
+        mlp_grads,
     )
     out_hidden = restore(out_hidden.reshape(seq, width), 1)
     grad_in = restore(grad_in.reshape(seq, width), 1).astype(F32)
     small = restore(small, 1)
 
-    *mlp_grads, attn_grads = swap_back(6, "swap_back", mlp_grads + [attn_grads])
+    attn_grads = lax.optimization_barrier((attn_grads, small))[0]
+    (attn_grads,) = swap_back(6, "swap_back", [attn_grads])
     attn_grads = attn_grads.astype(F32).reshape(2, 4, rows, 6, HEAD).transpose(2, 0, 3, 1, 4)
     attn_grads = attn_grads.reshape(rows, 2, 6, 4 * HEAD)
     query_grad = attn_grads[:, :, :2].reshape(rows, EXPERTS, 4 * HEAD)

time: 638 us -> 549 us (0.86)
  waiting for transfers between devices: 80.4 us -> 7.33 us
    all_gather x3, waiting for transfers between devices: 44.9 us -> 0.01 us  [gather_y(): lax.all_gather(block.reshape(-1, block.shape[2]), 'y', axis=0, tiled=True)]
    pallas_call x1, Pallas kernels: 74.8 us -> 103 us  [attn_forward(): pl.pallas_call(kernel, out_shape=[jax.ShapeDtypeStruct((8, seq, width), B...]
    reduce_scatter x4, waiting for transfers between devices: 34.1 us -> 5.87 us  [sum_y(): lax.psum_scatter(grad.astype(BF), 'y', scatter_dimension=0, tiled=True)]
    pallas_call x1, Pallas kernels: 41.8 us -> 15.1 us  [swap_back(): pl.pallas_call(kernel, out_shape=[jax.ShapeDtypeStruct(b.shape, b.dtype)...]
    pallas_call x2, Pallas kernels: 114 us -> 90.4 us  [the longest x1 52.6 us: enter(): pl.pallas_call(kernel, out_shape=[like, jax.ShapeDtypeStruct((4,) + like....]
    pallas_call x1, Pallas kernels: 94.2 us -> 116 us  [leave(): pl.pallas_call(kernel, out_shape=[jax.ShapeDtypeStruct((4, own, width), B...]
    unnamed x54 -> x56, local copies, waits for them, and re-layouts: 22.6 us -> 22 us
  transfers between devices with their start and end apart: 7 -> 7, of which waited for: 3 -> 1; matrix products, arithmetic and copies ran while one was open for 5% -> 7% of each run, Pallas kernels for 27% -> 63%
where the time goes in v4:
time: 549 us; the launch traced here: 541 us
  Pallas kernels  439 us (80%)
  local copies, waits for them, and re-layouts  49 us (9%)
  matrix products  24.5 us (4%)
  between operations  15.3 us (3%)
  waiting for transfers between devices  7.33 us (1%)
    pallas_call x1, Pallas kernels, leave(): pl.pallas_call(kernel, out_shape=[jax.ShapeDtypeStruct((4, own, width), B...  116 us
    pallas_call x1, Pallas kernels, attn_forward(): pl.pallas_call(kernel, out_shape=[jax.ShapeDtypeStruct((8, seq, width), B...  103 us
    pallas_call x1, Pallas kernels, middle(): pl.pallas_call(kernel, out_shape=[jax.ShapeDtypeStruct((own, width), F32)...  71.8 us
    pallas_call x1, Pallas kernels, enter(): pl.pallas_call(kernel, out_shape=[like, jax.ShapeDtypeStruct((4,) + like....  52.6 us
    pallas_call x1, Pallas kernels, spread_in(): pl.pallas_call(kernel, out_shape=[jax.ShapeDtypeStruct((8,) + hidden.shap...  37.7 us
    pallas_call x1, Pallas kernels, experts(): pl.pallas_call(kernel, grid=(4,), out_shape=[jax.ShapeDtypeStruct((rows,...  30.6 us
    dot_general x5, matrix products, dot(): return lax.dot_general(a, b, (dims, ((), ())), preferred_element_type=F32)  24.5 us
    unnamed x56, local copies, waits for them, and re-layouts  22 us
  transfers between devices with their start and end apart: 7, of which 1 were waited for; matrix products, arithmetic and copies ran while one was open for 7% of the time, Pallas kernels for 63%

profile of v4, /device:TPU:0, one launch (start us, length us, event | category | flops | bytes accessed | tf_op | source)
XLA Modules:
  0.0 540.9 jit_solution(16738417181835721383)
XLA Ops:
  7.2 4.4 fusion.4
  11.6 0.2 copy_bitcast_fusion
  12.0 0.8 slice-done
  13.2 0.5 copy_bitcast_fusion.4
  13.7 0.1 broadcast_in_dim.2
  13.9 0.9 pad_maximum_fusion.1
  14.7 0.9 reshape.178.a_ref
  15.7 1.4 slice_bitcast_fusion.1
  17.0 0.6 pad_maximum_fusion.4
  17.9 52.6 %enter.1 = (bf16[8,64,768]{2,1,0:T(8,128)(2,1)}, bf16[4,8,64,768]{3,2,1,0:T(8,128)(2,1)S(1)}, bf16[8,64,768]{2,1,0:T(8,128)(2,1)}, bf16[8,64,768]{2,1,0:T(8,128)(2,1)}, bf16[8,64,768]{2,1,0:T(8,128)(2,1)}) custom-call(bf16[8,64,768]{2,1,0:T(8,128)(2,1)S(1)} %reshape.178.a_ref, bf16[8,64,768]{2,1,0:T(8,128)(2,1)S(1)} %bitcast.126, ...), custom_call_target="tpu_custom_call" | custom-call | bytes 125829120 | tf_op jit(solution)/shard_map/enter/pallas_call | solution.py:236
  70.5 1.6 copy-done.1
  72.2 0.7 all-gather.6.cloned.1.call-update
  73.0 0.7 all-gather.8.cloned.1.call-update
  73.8 0.4 reshape.173
  74.2 0.4 copy.111
  74.6 0.4 reshape.174.hidden_ref
  75.2 0.4 reshape.187
  75.6 0.4 copy.110
  76.1 0.4 reshape.188.cot_ref
  76.5 0.3 copy.88
  76.9 37.7 %spread_in.1 = (bf16[8,128,2048]{2,1,0:T(8,128)(2,1)S(1)}, bf16[8,128,128]{2,1,0:T(8,128)(2,1)S(1)}) custom-call(bf16[128,2048]{1,0:T(8,128)(2,1)S(1)} %reshape.174.hidden_ref, bf16[128,128]{1,0:T(8,128)(2,1)S(1)} %pad_convert_fusion.mask_ref), custom_call_target="tpu_custom_call" | custom-call | bytes 94371840 | tf_op jit(solution)/shard_map/spread_in/pallas_call | solution.py:258
  114.7 2.1 copy-done
  116.9 103.1 %attn_forward.1 = (bf16[8,128,2048]{2,1,0:T(8,128)(2,1)}, bf16[8,128,512]{2,1,0:T(8,128)(2,1)S(1)}, bf16[8,128,256]{2,1,0:T(8,128)(2,1)S(1)}, f32[8,128,128]{2,1...) custom-call(bf16[8,128,2048]{2,1,0:T(8,128)(2,1)} %copy-done, ...), custom_call_target="tpu_custom_call" | custom-call | bytes 209715200 | tf_op jit(solution)/shard_map/attn_forward/pallas_call | solution.py:495
  220.0 1.0 copy-done.8
  221.0 0.8 copy-done.10
  221.8 30.6 %experts.1 = (bf16[1024,768]{1,0:T(8,128)(2,1)S(1)}, bf16[1024,768]{1,0:T(8,128)(2,1)S(1)}, bf16[1024,768]{1,0:T(8,128)(2,1)S(1)}, bf16[1024,2048]{1,0:T(8,128)(...) custom-call(bf16[1024,2048]{1,0:T(8,128)(2,1)} %bitcast.165, bf16[1024,2048]{1,0:T(8,128)(2,1)} %bitcast.163, ...), custom_call_target="tpu_custom_call" | custom-call | flops 19327352832 | bytes 41943040 | tf_op jit(solution)/shard_map/experts/pallas_call | solution.py:562
  252.4 1.2 copy-done.12
  253.5 1.1 copy-done.13
  254.7 4.9 convolution_convert_fusion.1
  259.6 0.2 reduce-scatter.5.cloned.1.call-start
  259.8 7.9 %convolution_convert_fusion.2 = bf16[2048,768]{1,0:T(8,128)(2,1)} fusion(bf16[1024,2048]{1,0:T(8,128)(2,1)} %bitcast.166, bf16[1024,768]{1,0:T(8,128)(2,1)} %copy-done.13), kind=kOutput, calls=%fused_computation.2 | convolution fusion | flops 3222798336 | bytes 8912896 | tf_op jit(solution)/shard_map/dot_general | solution.py:29
  267.8 8.0 %convolution_convert_fusion = bf16[2048,768]{1,0:T(8,128)(2,1)} fusion(bf16[1024,2048]{1,0:T(8,128)(2,1)} %bitcast.164, bf16[1024,768]{1,0:T(8,128)(2,1)} %copy-done.12), kind=kOutput, calls=%fused_computation | convolution fusion | flops 3222798336 | bytes 8912896 | tf_op jit(solution)/shard_map/dot_general | solution.py:29
  275.8 0.3 reduce-scatter.11.cloned.1.call-start
  276.1 71.8 %middle.1 = (f32[32,2048]{1,0:T(8,128)S(1)}, f32[16,2048]{1,0:T(8,128)S(1)}, bf16[16,2,32,2048]{3,2,1,0:T(8,128)(2,1)S(1)}) custom-call(bf16[8,2,2,32,2176]{4,3,2,1,0:T(8,128)(2,1)} %bitcast.139, f32[32,2048]{1,0:T(8,128)S(1)} %get-tuple-element.58.after_ref, f32[1,2048]{1,0:T(1,128)S(1)} %broadcast_in_dim_reshape.7.gain_m_ref.gain_ref, ...), custom_call_target="tpu_custom_call" | custom-call | bytes 167772160 | tf_op jit(solution)/shard_map/middle/pallas_call | solution.py:683
  348.0 1.9 copy-done.6
  349.9 1.9 copy-done.2
  351.8 1.2 copy-done.9
  353.0 12.3 %attn_backward.1 = (bf16[1024,512]{1,0:T(8,128)(2,1)S(1)}, bf16[1024,2176]{1,0:T(8,128)(2,1)}) custom-call(bf16[1024,2048]{1,0:T(8,128)(2,1)} %bitcast.134, bf16[1024,512]{1,0:T(8,128)(2,1)S(1)} %bitcast.136, f32[1024,128]{1,0:T(8,128)S(1)} %bitcast.132, bf16[2048,768]{1,0:T(8,128)(2,1)S(1)} %bitcast.122, f32[128,128]{1,0:T(8,128)S(1)} %copy-done.4, ...), custom_call_target="tpu_custom_call" | custom-call | flops 3221225472 | bytes 20971520 | tf_op jit(solution)/shard_map/attn_backward/pallas_call | solution.py:632
  365.3 1.3 convolution_convert_fusion.4
  366.6 0.9 copy-done.23
  367.5 2.4 convolution_convert_fusion.3
  369.9 2.1 pad_maximum_fusion
  372.0 5.9 %reduce-scatter.9.cloned.1.call-done = bf16[512,768]{1,0:T(8,128)(2,1)} async-done(((bf16[2048,768]{1,0:T(8,128)(2,1)}), bf16[512,768]{1,0:T(8,128)(2,1)}) %reduce-scatter.9.cloned.1.call-update) | async-done | bytes 786448 | tf_op jit(solution)/shard_map/reduce_scatter | solution.py:827
  377.9 115.7 %leave.1 = (bf16[4,32,2048]{2,1,0:T(8,128)(2,1)S(1)}, bf16[4,32,2048]{2,1,0:T(8,128)(2,1)S(1)}, f32[16,2048]{1,0:T(8,128)S(1)}, bf16[8,64,768]{2,1,0:T(8,128)(2,...) custom-call(bf16[8,2,2,32,2176]{4,3,2,1,0:T(8,128)(2,1)} %bitcast.140, ...), custom_call_target="tpu_custom_call" | custom-call | bytes 209715200 | tf_op jit(solution)/shard_map/leave/pallas_call | solution.py:779
  493.8 2.0 copy.98
  496.1 0.2 maximum_convert_fusion
  496.3 3.8 copy.97
  500.1 1.9 reshape.221
  502.0 1.5 copy.92
  503.5 1.5 reshape.217
  505.1 0.4 reshape_reshape.4
  505.4 0.2 copy.91
  505.6 1.2 reshape.204
  507.0 0.6 slice.111
  507.6 0.6 slice.118
  508.3 0.6 copy.101
  508.9 0.6 copy.102
  509.5 1.4 copy.94
  510.9 15.1 %swap_back.1 = bf16[8,64,768]{2,1,0:T(8,128)(2,1)S(1)} custom-call(bf16[8,64,768]{2,1,0:T(8,128)(2,1)S(1)} %bitcast.123), custom_call_target="tpu_custom_call" | custom-call | bytes 83886080 | tf_op jit(solution)/shard_map/swap_back/pallas_call | solution.py:284
  526.0 2.2 reshape.223
  528.2 2.6 copy.95
  530.8 0.6 reshape.219
  531.6 1.1 copy.96
  532.7 1.0 pad_maximum_fusion.5
  (100 shorter events, 2.2 us)
Async XLA Ops:
  7.2 214.6 %all-gather.4.cloned.1.call-start = ((), (), s32[]{:S(2)}) async-start(), calls=%async_computation.4 | async-start | bytes 3932160 | tf_op jit(solution)/shard_map/all_gather | solution.py:823
  11.8 1.0 slice-start
  11.8 1.0 copy-start.16
  11.9 1.1 slice-start.1
  17.9 55.9 %copy-start.14 = (bf16[128,2048]{1,0:T(8,128)(2,1)S(1)}, bf16[128,2048]{1,0:T(8,128)(2,1)}, u32[]{:S(2)}) copy-start(bf16[128,2048]{1,0:T(8,128)(2,1)} %param.16) | copy-start | bytes 1572868
  70.5 1.7 copy-start.1
  72.2 149.6 %all-gather.6.cloned.1.call-start = ((), (), s32[]{:S(2)}) async-start(), calls=%async_computation.5 | async-start | bytes 3932160 | tf_op jit(solution)/shard_map/all_gather | solution.py:823
  72.9 2.1 copy-start.21
  73.0 2.1 copy-start.22
  73.0 2.3 copy-start.15
  73.0 148.8 %all-gather.8.cloned.1.call-start = ((), (), s32[]{:S(2)}) async-start(), calls=%async_computation.6 | async-start | bytes 3932160 | tf_op jit(solution)/shard_map/all_gather | solution.py:823
  73.7 276.2 %reduce-scatter.7.cloned.1.call-start = ((), (), s32[]{:S(2)}) async-start(), calls=%async_computation.8 | async-start | bytes 3932160 | tf_op jit(solution)/shard_map/reduce_scatter | solution.py:827
  74.6 1.9 copy-start.17
  74.6 1.9 copy-start.18
  75.0 1.8 copy-start.19
  75.0 1.8 copy-start.20
  76.0 40.9 %copy-start.4 = (f32[128,128]{1,0:T(8,128)S(1)}, f32[128,128]{1,0:T(8,128)}, u32[]{:S(2)}) copy-start(f32[128,128]{1,0:T(8,128)} %constant.35.clone.cos_ref) | copy-start | bytes 196612
  76.0 40.9 %copy-start.5 = (f32[128,128]{1,0:T(8,128)S(1)}, f32[128,128]{1,0:T(8,128)}, u32[]{:S(2)}) copy-start(f32[128,128]{1,0:T(8,128)} %constant.36.clone.sin_ref) | copy-start | bytes 196612
  114.7 2.1 copy-start
  220.0 1.0 copy-start.8
  221.0 0.8 copy-start.10
  221.8 32.9 %copy-start.24 = (bf16[16,2,32,2048]{3,2,1,0:T(8,128)(2,1)S(1)}, bf16[16,2,32,2048]{3,2,1,0:T(8,128)(2,1)}, u32[]{:S(2)}) copy-start(bf16[16,2,32,2048]{3,2,1,0:T(8,128)(2,1)} %get-tuple-element.48) | copy-start | bytes 12582916
  252.4 1.2 copy-start.12
  253.5 1.1 copy-start.13
  259.6 90.3 %reduce-scatter.5.cloned.1.call-start = ((), (), s32[]{:S(2)}) async-start(), calls=%async_computation.7 | async-start | bytes 3932160 | tf_op jit(solution)/shard_map/reduce_scatter | solution.py:827
  267.7 110.1 %reduce-scatter.9.cloned.1.call-start = ((), (), s32[]{:S(2)}) async-start(), calls=%async_computation.9 | async-start | bytes 3932160 | tf_op jit(solution)/shard_map/reduce_scatter | solution.py:827
  275.8 233.7 %reduce-scatter.11.cloned.1.call-start = ((), (), s32[]{:S(2)}) async-start(), calls=%async_computation.10 | async-start | bytes 3932160 | tf_op jit(solution)/shard_map/reduce_scatter | solution.py:827
  348.0 1.9 copy-start.6
  349.9 1.9 copy-start.2
  351.8 1.2 copy-start.9
  353.0 12.3 %copy-start.7 = (bf16[16,2,32,2048]{3,2,1,0:T(8,128)(2,1)S(1)}, bf16[16,2,32,2048]{3,2,1,0:T(8,128)(2,1)}, u32[]{:S(2)}) copy-start(bf16[16,2,32,2048]{3,2,1,0:T(8,128)(2,1)} %copy-done.6) | copy-start | bytes 12582916
  353.0 12.3 %copy-start.11 = (bf16[8,128,256]{2,1,0:T(8,128)(2,1)S(1)}, bf16[8,128,256]{2,1,0:T(8,128)(2,1)}, u32[]{:S(2)}) copy-start(bf16[8,128,256]{2,1,0:T(8,128)(2,1)} %copy-done.10) | copy-start | bytes 1572868
  365.3 2.2 copy-start.23
  372.0 5.9 %copy-start.3 = (bf16[512,768]{1,0:T(8,128)(2,1)S(1)}, bf16[512,768]{1,0:T(8,128)(2,1)}, u32[]{:S(2)}) copy-start(bf16[512,768]{1,0:T(8,128)(2,1)} %reduce-scatter.5.cloned.1.call-done) | copy-start | bytes 2359300
Sparse Core Ops, SparseCore 0:
  72.3 40.2 all-gather.3
  114.3 39.7 all-gather.5
  155.7 39.7 all-gather.7
  259.7 37.6 reduce-scatter.6
  299.6 37.9 reduce-scatter.4
  339.9 37.9 reduce-scatter.8
  380.3 37.9 reduce-scatter.10

commit v5 on v4

--- a/solution.py
+++ b/solution.py
@@ -131,52 +131,54 @@
 
 GROUP_MOVES = moves("zl", "x")
 TEAM_MOVES = moves("zl", "x", "zh")
+X_MOVES = moves("x")
 Y_MOVES = moves("y")
+Z_MOVES = moves("zl", "zh")
 
 
 def sibling():
     return {"c": 1 - lax.axis_index("c")}
 
 
-class Spread:
-    sems = [pltpu.SemaphoreType.DMA((8,))] * 4
-
-    def __init__(self, src, dst, sems):
-        self.src, self.dst = src, dst
-        self.send, self.recv, self.fsend, self.frecv = sems
-        rows = src.shape[0] // 2
-        self.half = pl.ds(pl.multiple_of(lax.axis_index("c") * rows, rows), rows)
-        self.me = number(place(GROUP_MOVES[0]))
+class RingY:
+    sems = [pltpu.SemaphoreType.DMA((5,)), pltpu.SemaphoreType.DMA((5,))]
+
+    def __init__(self, src, out, sems):
+        self.src, self.out = src, out
+        self.send, self.recv = sems
+        self.y = lax.axis_index("y")
+        self.half = src.shape[0] // 2
+
+    def line(self, step):
+        return lax.rem(self.y + step, 4)
+
+    def copy(self, k):
+        y = self.y
+        if k < 2:
+            src, dst, to = self.src, self.out.at[y], self.line((1, 3)[k])
+        else:
+            half = pl.ds((k - 2) * self.half, self.half)
+            src = dst = self.out.at[self.line((3, 1)[k - 2]), half]
+            to = self.line((1, 3)[k - 2])
+        return push(src, dst, self.send.at[k], self.recv.at[k], {"y": to})
 
     def start(self):
-        self.copies = [pltpu.make_async_copy(self.src, self.dst.at[self.me], self.send.at[0])]
-        for k, move in enumerate(GROUP_MOVES):
-            if k:
-                self.copies.append(
-                    push(
-                        self.src.at[self.half],
-                        self.dst.at[self.me, self.half],
-                        self.send.at[k],
-                        self.recv.at[k],
-                        place(move),
-                    )
-                )
-        for copy in self.copies:
-            copy.start()
+        self.stay = pltpu.make_async_copy(self.src, self.out.at[self.y], self.send.at[4])
+        for k in range(2):
+            self.copy(k).start()
+        self.stay.start()
+
+    def forward(self):
+        for k in range(2):
+            self.copy(k).wait_recv()
+            self.copy(k + 2).start()
 
     def finish(self):
-        forwards = []
-        for k, move in enumerate(GROUP_MOVES):
-            if k:
-                self.copies[k].wait_recv()
-                block = self.dst.at[number(place(move, -1)), self.half]
-                forwards.append(push(block, block, self.fsend.at[k], self.frecv.at[k], sibling()))
-                forwards[-1].start()
-        for forward in forwards:
-            forward.wait()
-        self.copies[0].wait()
-        for copy in self.copies[1:]:
-            copy.wait_send()
+        for k in range(2):
+            self.copy(k + 2).wait_recv()
+        for k in range(4):
+            self.copy(k).wait_send()
+        self.stay.wait()
 
 
 class Swap:
@@ -214,23 +216,19 @@
 def enter(collective, attn_blocks, blocks):
     def kernel(a_ref, *refs):
         m_refs, a_mid, a_out, m_outs, sems = refs[:3], refs[3], refs[4], refs[5:8], refs[8:]
-        meet([place(m) for m in GROUP_MOVES[1:] + Y_MOVES[1:]])
+        meet([place(m) for m in GROUP_MOVES[1:] + [Y_MOVES[1], Y_MOVES[3]]])
         first = Swap(a_ref, a_mid, sems[2:4])
         first.start()
         swaps = [Swap(m_refs[i], m_outs[i], sems[4 + 2 * i : 6 + 2 * i]) for i in range(3)]
         for swap in swaps:
             swap.start()
         first.finish()
-        mine = a_out.at[lax.axis_index("y")]
-        copies = [pltpu.make_async_copy(a_mid, mine, sems[0].at[0])]
-        for k in range(1, 4):
-            copies.append(push(a_mid, mine, sems[0].at[k], sems[1].at[k], place(Y_MOVES[k])))
-        for copy in copies:
-            copy.start()
+        ring = RingY(a_mid, a_out, sems[0:2])
+        ring.start()
+        ring.forward()
         for swap in swaps:
             swap.finish()
-        for copy in copies:
-            copy.wait()
+        ring.finish()
 
     like = jax.ShapeDtypeStruct(attn_blocks.shape, attn_blocks.dtype)
     return pl.pallas_call(
@@ -239,34 +237,31 @@
         + [jax.ShapeDtypeStruct(b.shape, b.dtype) for b in blocks],
         in_specs=[ANY] * 4,
         out_specs=[ANY] * 5,
-        scratch_shapes=[pltpu.SemaphoreType.DMA((4,))] * 2 + Swap.sems * 4,
+        scratch_shapes=RingY.sems + Swap.sems * 4,
         name="enter",
         **settings(collective, 120 << 20),
     )(attn_blocks, *blocks)[1:]
 
 
-def spread_in(collective, hidden, masks):
-    def kernel(hidden_ref, mask_ref, hidden_out, mask_out, *sems):
-        meet([place(m) for m in GROUP_MOVES[1:]] + [sibling()])
-        first = Spread(mask_ref, mask_out, sems[0:4])
-        second = Spread(hidden_ref, hidden_out, sems[4:8])
-        first.start()
-        second.start()
-        first.finish()
-        second.finish()
+def spread_in(collective, rows):
+    own, width = rows.shape
+
+    def kernel(row_ref, out_ref, *sems):
+        meet_team()
+        spread = TeamSpread(row_ref, out_ref, sems)
+        spread.start()
+        spread.middle()
+        spread.finish()
 
     return pl.pallas_call(
         kernel,
-        out_shape=[
-            jax.ShapeDtypeStruct((8,) + hidden.shape, hidden.dtype),
-            jax.ShapeDtypeStruct((8,) + masks.shape, masks.dtype),
-        ],
-        in_specs=[ANY] * 2,
-        out_specs=[ANY] * 2,
-        scratch_shapes=Spread.sems * 2,
+        out_shape=jax.ShapeDtypeStruct((2, 4, 2, 2, own, width), rows.dtype),
+        in_specs=[ANY],
+        out_specs=ANY,
+        scratch_shapes=TeamSpread.sems,
         name="spread_in",
         **settings(collective, 90 << 20),
-    )(hidden, masks)
+    )(rows)
 
 
 def swap_back(collective, name, blocks):
@@ -295,116 +290,237 @@
 class TeamSum:
     @staticmethod
     def scratch(own, width):
+        half = own // 2
         return [
             pltpu.VMEM((8, 2, own, width), BF),
-            pltpu.VMEM((16, own, width), BF),
+            pltpu.VMEM((3, 2, 2, half, width), BF),
+            pltpu.VMEM((3, 4, half, width), BF),
+            pltpu.VMEM((6, half, width), BF),
             pltpu.SemaphoreType.DMA((8,)),
             pltpu.SemaphoreType.DMA((8,)),
-            pltpu.SemaphoreType.DMA((16,)),
-            pltpu.SemaphoreType.DMA((16,)),
+            pltpu.SemaphoreType.DMA((6,)),
+            pltpu.SemaphoreType.DMA((6,)),
+            pltpu.SemaphoreType.DMA((6,)),
+            pltpu.SemaphoreType.DMA((6,)),
         ]
+
+    count = 10
 
     def __init__(self, part, scratch):
         self.part = part
-        self.other, self.got, self.ssem, self.rsem, self.dsend, self.drecv = scratch
+        self.other, self.got_x, self.got_z, self.late = scratch[:4]
+        self.ssem, self.rsem, self.send1, self.recv1, self.send2, self.recv2 = scratch[4:]
         self.zl, self.x, self.zh, self.c = (lax.axis_index(a) for a in TEAM)
-        self.seq = self.zl * 4 + self.x
-        self.chip = self.seq * 2 + self.zh
+        self.half = part.shape[4] // 2
+        self.top, self.low = pl.ds(0, self.half), pl.ds(self.half, self.half)
 
     def swap(self, seq):
         return push(
-            self.part.at[seq, :, 1 - self.c],
+            self.part.at[seq // 4, lax.rem(seq, 4), :, 1 - self.c],
             self.other.at[seq],
             self.ssem.at[seq],
             self.rsem.at[seq],
             sibling(),
         )
 
-    def send(self, seq, zh):
-        chip = seq * 2 + zh
+    def send_x(self, x):
+        slot = lax.rem(x - self.x + 4, 4) - 1
         return push(
-            self.part.at[seq, zh, self.c],
-            self.got.at[self.chip],
-            self.dsend.at[chip],
-            self.drecv.at[self.chip],
-            {"zl": seq // 4, "x": lax.rem(seq, 4), "zh": zh},
+            self.part.at[:, x, :, self.c, self.top],
+            self.got_x.at[slot],
+            self.send1.at[slot],
+            self.recv1.at[slot],
+            {"x": x},
         )
 
-    def both(self, seq, zh):
-        return self.part[seq, zh, self.c].astype(F32) + self.other[seq, zh].astype(F32)
-
-    def forward(self, seq):
+    def send_z(self, zl, zh):
+        slot = lax.rem(zl - self.zl + 2, 2) * 2 + lax.rem(zh - self.zh + 2, 2) - 1
+        return push(
+            self.part.at[zl, :, zh, self.c, self.low],
+            self.got_z.at[slot],
+            self.send1.at[3 + slot],
+            self.recv1.at[3 + slot],
+            {"zl": zl, "zh": zh},
+        )
+
+    def late_z(self, k):
+        to = place(Z_MOVES[k])
+        return push(
+            self.part.at[to["zl"], self.x, to["zh"], self.c, self.top],
+            self.late.at[k - 1],
+            self.send2.at[k - 1],
+            self.recv2.at[k - 1],
+            to,
+        )
+
+    def late_x(self, k):
+        to = place(X_MOVES[k])
+        return push(
+            self.part.at[self.zl, to["x"], self.zh, self.c, self.low],
+            self.late.at[2 + k],
+            self.send2.at[2 + k],
+            self.recv2.at[2 + k],
+            to,
+        )
+
+    def add(self, seq):
         self.swap(seq).wait_recv()
+        zl, x = seq // 4, lax.rem(seq, 4)
         for zh in range(2):
-            self.part[seq, zh, self.c] = self.both(seq, zh).astype(BF)
-            self.send(seq, zh).start()
+            mine = self.part[zl, x, zh, self.c].astype(F32)
+            self.part[zl, x, zh, self.c] = (mine + self.other[seq, zh].astype(F32)).astype(BF)
 
     def pair(self, step):
         back = 3 - step
         return lax.rem(self.zl + back // 2, 2) * 2 + lax.rem(self.x // 2 + back, 2)
 
+    def add_pair(self, step):
+        for j in range(2):
+            self.add(self.pair(step) * 2 + j)
+
+    def send_far_z(self):
+        for zh in range(2):
+            self.send_z(1 - self.zl, zh).start()
+
+    def send_far_x(self):
+        for j in range(2):
+            self.send_x((1 - self.x // 2) * 2 + j).start()
+
     def last(self):
-        beside = self.seq + 1 - 2 * lax.rem(self.x, 2)
-        self.forward(beside)
-        self.swap(self.seq).wait_recv()
-        away = 1 - self.zh
-        self.part[self.seq, away, self.c] = self.both(self.seq, away).astype(BF)
-        self.send(self.seq, away).start()
+        self.add_pair(3)
+        self.send_x(self.x + 1 - 2 * lax.rem(self.x, 2)).start()
+        self.send_z(self.zl, 1 - self.zh).start()
+
+    def got(self, ref, sem):
+        pltpu.make_async_copy(ref, ref, sem).wait()
 
     def total(self, total_ref):
-        total_ref[...] = self.both(self.seq, self.zh)
-        for move in TEAM_MOVES[1:]:
-            chip = number(place(move, -1))
-            pltpu.make_async_copy(self.got.at[chip], self.got.at[chip], self.drecv.at[chip]).wait()
-            total_ref[...] += self.got[chip].astype(F32)
+        half, c = self.half, self.c
+        for k in range(3):
+            self.got(self.got_x.at[k], self.recv1.at[k])
+        for k, move in reversed(list(enumerate(Z_MOVES))):
+            at = place(move)
+            rows = self.part[at["zl"], self.x, at["zh"], c, :half].astype(F32)
+            for j in range(3):
+                rows += self.got_x[j, at["zl"], at["zh"]].astype(F32)
+            if k:
+                self.part[at["zl"], self.x, at["zh"], c, :half] = rows.astype(BF)
+                self.late_z(k).start()
+            else:
+                total_ref[:half] = rows
+        for k in range(3):
+            self.got(self.got_z.at[k], self.recv1.at[3 + k])
+        for k, move in reversed(list(enumerate(X_MOVES))):
+            at = place(move)
+            rows = self.part[self.zl, at["x"], self.zh, c, half:].astype(F32)
+            for j in range(3):
+                rows += self.got_z[j, at["x"]].astype(F32)
+            if k:
+                self.part[self.zl, at["x"], self.zh, c, half:] = rows.astype(BF)
+                self.late_x(k).start()
+            else:
+                total_ref[half:] = rows
+        for k in range(3):
+            self.got(self.late.at[k], self.recv2.at[k])
+            total_ref[:half] += self.late[k].astype(F32)
+        for k in range(3):
+            self.got(self.late.at[3 + k], self.recv2.at[3 + k])
+            total_ref[half:] += self.late[3 + k].astype(F32)
 
     def close(self):
         for seq in range(8):
             self.swap(seq).wait_send()
-        for move in TEAM_MOVES[1:]:
-            to = place(move)
-            self.send(to["zl"] * 4 + to["x"], to["zh"]).wait_send()
+        for k in range(1, 4):
+            x, z = place(X_MOVES[k])["x"], place(Z_MOVES[k])
+            self.send_x(x).wait_send()
+            self.send_z(z["zl"], z["zh"]).wait_send()
+            self.late_z(k).wait_send()
+            self.late_x(k).wait_send()
 
     def run(self):
         for step in range(4):
             for j in range(2):
                 self.swap(self.pair(step) * 2 + j).start()
-        for step in range(3):
-            for j in range(2):
-                self.forward(self.pair(step) * 2 + j)
+        self.add_pair(0)
+        self.add_pair(1)
+        self.send_far_z()
+        self.add_pair(2)
+        self.send_far_x()
         self.last()
 
 
 class TeamSpread:
-    sems = [pltpu.SemaphoreType.DMA((16,))] * 4
+    sems = [pltpu.SemaphoreType.DMA((12,))] * 2 + [pltpu.SemaphoreType.DMA((9,))] * 2
 
     def __init__(self, rows, out, sems):
         self.rows, self.out = rows, out
         self.send, self.recv, self.fsend, self.frecv = sems
-
-    def run(self):
-        c = lax.axis_index("c")
-        mine = self.out.at[number(place(TEAM_MOVES[0])), c]
-        stay = pltpu.make_async_copy(self.rows, mine, self.send.at[0])
-        stay.start()
-        pushes = [
-            push(self.rows, mine, self.send.at[k], self.recv.at[k], place(TEAM_MOVES[k]))
-            for k in range(1, 16)
-        ]
-        for copy in pushes:
-            copy.start()
-        forwards = [push(self.rows, mine, self.fsend.at[0], self.frecv.at[0], sibling())]
-        forwards[0].start()
-        for k in range(1, 16):
-            pushes[k - 1].wait_recv()
-            tile = self.out.at[number(place(TEAM_MOVES[k], -1)), c]
-            forwards.append(push(tile, tile, self.fsend.at[k], self.frecv.at[k], sibling()))
-            forwards[-1].start()
-        for copy in forwards:
-            copy.wait()
-        stay.wait()
-        for copy in pushes:
-            copy.wait_send()
+        self.zl, self.x, self.zh, self.c = (lax.axis_index(a) for a in TEAM)
+        self.half = rows.shape[0] // 2
+        self.top, self.low = pl.ds(0, self.half), pl.ds(self.half, self.half)
+
+    def tops(self, zl, zh):
+        return self.out.at[zl, :, zh, self.c, self.top]
+
+    def lows(self, x):
+        return self.out.at[:, x, :, self.c, self.low]
+
+    def hop(self, k, src, dst, to):
+        return push(src, dst, self.send.at[k], self.recv.at[k], to)
+
+    def first(self, k):
+        here = (self.zl, self.x, self.zh, self.c)
+        if k < 3:
+            return self.hop(k, self.rows.at[self.top], self.out.at[(*here, self.top)], place(X_MOVES[k + 1]))
+        return self.hop(k, self.rows.at[self.low], self.out.at[(*here, self.low)], place(Z_MOVES[k - 2]))
+
+    def second(self, k):
+        if k < 3:
+            block = self.tops(self.zl, self.zh)
+            return self.hop(6 + k, block, block, place(Z_MOVES[k + 1]))
+        block = self.lows(self.x)
+        return self.hop(6 + k, block, block, place(X_MOVES[k - 2]))
+
+    def forward(self, k, block):
+        return push(block, block, self.fsend.at[k], self.frecv.at[k], sibling())
+
+    def start(self):
+        self.stay = pltpu.make_async_copy(
+            self.rows, self.out.at[self.zl, self.x, self.zh, self.c], self.fsend.at[8]
+        )
+        for k in range(6):
+            self.first(k).start()
+        self.stay.start()
+
+    def middle(self):
+        self.stay.wait()
+        for k in range(3):
+            self.first(k).wait_recv()
+        for k in range(3):
+            self.second(k).start()
+        self.forward(0, self.tops(self.zl, self.zh)).start()
+        for k in range(3, 6):
+            self.first(k).wait_recv()
+        for k in range(3, 6):
+            self.second(k).start()
+        self.forward(1, self.lows(self.x)).start()
+
+    def block(self, k):
+        if k < 3:
+            at = place(Z_MOVES[k + 1], -1)
+            return self.tops(at["zl"], at["zh"])
+        return self.lows(place(X_MOVES[k - 2], -1)["x"])
+
+    def finish(self):
+        for k in range(6):
+            self.second(k).wait_recv()
+            self.forward(2 + k, self.block(k)).start()
+        blocks = [self.tops(self.zl, self.zh), self.lows(self.x)] + [self.block(k) for k in range(6)]
+        for k in range(8):
+            self.forward(k, blocks[k]).wait()
+        for k in range(6):
+            self.first(k).wait_send()
+            self.second(k).wait_send()
 
 
 def meet_team():
@@ -423,20 +539,20 @@
 
 
 def attn_forward(
-    collective, hidden, masks, weights, gain, routers, cosines, sines, mlp_gain, hidden_own, cotangent
+    collective, hidden, weights, gain, routers, cosines, sines, mlp_gain, hidden_own, cot_own
 ):
-    _, seq, width = hidden.shape
-    own = hidden_own.shape[0]
+    own, width = hidden_own.shape
+    seq = hidden.shape[1]
     scale = HEAD ** (-0.5)
 
     def kernel(
-        hid, mask, w_ref, gain_ref, router_ref, cos_ref, sin_ref, gain_m_ref, own_ref, cot_ref,
+        hid, w_ref, gain_ref, router_ref, cos_ref, sin_ref, gain_m_ref, own_ref, cot_ref,
         normed_out, qkv_out, gated_out, gates_out, after_out, spread_out, cot_out,
         part, total, row, *rest,
     ):
         meet_team()
-        team = TeamSum(part, rest[:6])
-        cot = Spread(cot_ref, cot_out, rest[10:])
+        team = TeamSum(part, rest[: TeamSum.count])
+        cot = TeamSpread(cot_ref, cot_out, rest[TeamSum.count : TeamSum.count + 4])
         cot.start()
         first = 2 * team.zl
         causal = causal_mask(2, seq)
@@ -444,12 +560,12 @@
         def step(i, _):
             pair = team.pair(i)
             for j in range(2):
-                values = hid[pair * 2 + j].astype(F32)
+                values = hid[pair * 2 + j, :, :width].astype(F32)
                 normed_out[pair * 2 + j] = (values * rms_scale(values) * gain_ref[...]).astype(BF)
             normed = normed_out[pl.ds(pair * 2, 2)].reshape(2 * seq, width)
             logits = mm(normed, router_ref[...])
             proj = mm(normed, w_ref[:, : 4 * HEAD])
-            allowed = mask[pl.ds(pair * 2, 2)].reshape(2 * seq, LANE).astype(F32) > 0.5
+            allowed = hid[pl.ds(pair * 2, 2), :, width:].reshape(2 * seq, LANE).astype(F32) > 0.5
             gates = dense_gates(logits, allowed & (lanes(2 * seq) < EXPERTS))
             gates_out[pl.ds(pair * 2, 2)] = gates.reshape(2, seq, LANE)
             gated = []
@@ -471,14 +587,27 @@
                 gated.append(jnp.concatenate(out, axis=1))
                 gated_out[pair * 2 + j] = gated[-1]
             branch = mm_nt(jnp.concatenate(gated, axis=0), w_ref[:, 4 * HEAD :])
-            part[pl.ds(pair * 2, 2)] = branch.astype(BF).reshape(2, 2, 2, own, width)
+            part[pair // 2, pl.ds(lax.rem(pair, 2) * 2, 2)] = branch.astype(BF).reshape(
+                2, 2, 2, own, width
+            )
             for j in range(2):
                 team.swap(pair * 2 + j).start()
 
+            @pl.when(i == 0)
+            def _():
+                cot.middle()
+
             @pl.when(i > 0)
             def _():
-                for j in range(2):
-                    team.forward(team.pair(i - 1) * 2 + j)
+                team.add_pair(i - 1)
+
+            @pl.when(i == 2)
+            def _():
+                team.send_far_z()
+
+            @pl.when(i == 3)
+            def _():
+                team.send_far_x()
 
             return 0
 
@@ -489,7 +618,10 @@
         after = total[...] + own_ref[...].astype(F32)
         after_out[...] = after
         row[...] = (after * rms_scale(after) * gain_m_ref[...]).astype(BF)
-        TeamSpread(row, spread_out, rest[6:10]).run()
+        spread = TeamSpread(row, spread_out, rest[TeamSum.count + 4 :])
+        spread.start()
+        spread.middle()
+        spread.finish()
         team.close()
 
     return pl.pallas_call(
@@ -500,22 +632,21 @@
             jax.ShapeDtypeStruct((8, seq, 2 * HEAD), BF),
             jax.ShapeDtypeStruct((8, seq, LANE), F32),
             jax.ShapeDtypeStruct((own, width), F32),
-            jax.ShapeDtypeStruct((16, 2, own, width), BF),
-            jax.ShapeDtypeStruct((8, seq, width), BF),
+            jax.ShapeDtypeStruct((2, 4, 2, 2, own, width), BF),
+            jax.ShapeDtypeStruct((2, 4, 2, 2, own, width), BF),
         ],
-        in_specs=[VMEM] * 9 + [ANY],
+        in_specs=[VMEM] * 8 + [ANY],
         out_specs=[VMEM] * 5 + [ANY] * 2,
         scratch_shapes=[
-            pltpu.VMEM((8, 2, 2, own, width), BF),
+            pltpu.VMEM((2, 4, 2, 2, own, width), BF),
             pltpu.VMEM((own, width), F32),
             pltpu.VMEM((own, width), BF),
         ]
         + TeamSum.scratch(own, width)
-        + TeamSpread.sems
-        + Spread.sems,
+        + TeamSpread.sems * 2,
         name="attn_forward",
         **settings(collective, 200 << 20, 48),
-    )(hidden, masks, weights, gain, routers, cosines, sines, mlp_gain, hidden_own, cotangent)
+    )(hidden, weights, gain, routers, cosines, sines, mlp_gain, hidden_own, cot_own)
 
 
 def experts(normed, cotangent, masks, routers, weights, extra):
@@ -564,7 +695,8 @@
         grid=(4,),
         out_shape=[jax.ShapeDtypeStruct((rows, c), BF) for c in cols]
         + [jax.ShapeDtypeStruct((rows, LANE), F32)],
-        in_specs=[tiled(width), tiled(width), tiled(LANE), whole(routers)]
+        in_specs=[tiled(width), tiled(width)]
+        + [pl.BlockSpec((tile, LANE), lambda i: (i, width // LANE)), whole(routers)]
         + [whole(w) for w in weights],
         out_specs=[tiled(c) for c in cols] + [tiled(LANE)],
         compiler_params=pltpu.CompilerParams(vmem_limit_bytes=48 << 20),
@@ -663,7 +795,7 @@
         fetch.start()
         meet_team()
         fetch.wait()
-        team = TeamSum(part, rest[:6])
+        team = TeamSum(part, rest[: TeamSum.count])
         team.run()
         after = after_ref[...]
         normed = (after * rms_scale(after) * gain_ref[...]).astype(BF)
@@ -677,7 +809,10 @@
         small_out[:8] = jnp.zeros((8, width), F32)
         small_out[0:1] = gain_grad
         small_out[8:] = router_grad
-        TeamSpread(row, spread_out, rest[6:]).run()
+        spread = TeamSpread(row, spread_out, rest[TeamSum.count :])
+        spread.start()
+        spread.middle()
+        spread.finish()
         team.close()
 
     return pl.pallas_call(
@@ -685,12 +820,12 @@
         out_shape=[
             jax.ShapeDtypeStruct((own, width), F32),
             jax.ShapeDtypeStruct((16, width), F32),
-            jax.ShapeDtypeStruct((16, 2, own, width), BF),
+            jax.ShapeDtypeStruct((2, 4, 2, 2, own, width), BF),
         ],
         in_specs=[ANY] + [VMEM] * 5,
         out_specs=[VMEM] * 2 + [ANY],
         scratch_shapes=[
-            pltpu.VMEM((8, 2, 2, own, width + LANE), BF),
+            pltpu.VMEM((2, 4, 2, 2, own, width + LANE), BF),
             pltpu.SemaphoreType.DMA((1,)),
             pltpu.VMEM((own, width + LANE), F32),
             pltpu.VMEM((own, width), BF),
@@ -699,18 +834,17 @@
         + TeamSpread.sems,
         name="middle",
         **settings(collective, 160 << 20, 48),
-    )(back.reshape(8, 2, 2, own, width + LANE), after, gain, gates_own, routers, cot_own)
+    )(back.reshape(2, 4, 2, 2, own, width + LANE), after, gain, gates_own, routers, cot_own)
 
 
 def leave(collective, back, branch, after, grad_mid, inputs, gain, gates_own, routers, small, grads):
     own, width = after.shape
-    stages = [moves("c"), moves("x"), moves("y"), moves("zl", "zh")]
-    near = moves("zh", "c")
+    stages = [X_MOVES, Y_MOVES, Z_MOVES]
 
     def kernel(
         back_ref, branch_ref, after_ref, mid_ref, in_ref, gain_ref, gates_ref, router_ref, small_ref,
         g0, g1, g2, out_all, grad_all, small_out, s0, s1, s2,
-        part_a, part_b, load, total_a, total_b, row_a, row_b, got, send, recv, ssend, srecv, *rest,
+        part_a, part_b, load, total_a, total_b, row_a, row_b, got, other, rest_rows, csem, send, recv, ssend, srecv, *rest,
     ):
         fetches = [
             pltpu.make_async_copy(back_ref, part_a, load.at[0]),
@@ -718,14 +852,15 @@
         ]
         for fetch in fetches:
             fetch.start()
-        meet([place(m) for m in TEAM_MOVES[1:] + Y_MOVES[1:]] + [place(m) for m in near[1:] if m["c"]])
-        team_a, team_b = TeamSum(part_a, rest[:6]), TeamSum(part_b, rest[6:12])
+        meet([place(m) for m in TEAM_MOVES[1:] + Y_MOVES[1:]] + [sibling()])
+        count = TeamSum.count
+        team_a, team_b = TeamSum(part_a, rest[:count]), TeamSum(part_b, rest[count : 2 * count])
         fetches[0].wait()
         team_a.run()
         fetches[1].wait()
         team_b.run()
         grad_swaps = [
-            Swap(g, s, rest[12 + 2 * i : 14 + 2 * i])
+            Swap(g, s, rest[2 * count + 2 * i : 2 * count + 2 * i + 2])
             for i, (g, s) in enumerate(((g0, s0), (g1, s1), (g2, s2)))
         ]
         for swap in grad_swaps:
@@ -740,37 +875,54 @@
         small_out[...] = small_ref[...]
         small_out[1:2] = gain_grad
         small_out[8:] += router_grad
-        me = number(place(near[0]))
-        copies = []
+        zh, c = lax.axis_index("zh"), lax.axis_index("c")
 
         def spread(i, src, dst):
-            new = [pltpu.make_async_copy(src, dst.at[me], send.at[i, 0])]
-            for k in range(1, 4):
-                new.append(push(src, dst.at[me], send.at[i, k], recv.at[i, k], place(near[k])))
-            for copy in new:
+            mine, far = dst.at[zh, c], dst.at[1 - zh, c]
+            copies = [
+                pltpu.make_async_copy(src, mine, send.at[i, 0]),
+                push(src, mine, send.at[i, 1], recv.at[i, 1], {"zh": 1 - zh}),
+                push(src, mine, send.at[i, 2], recv.at[i, 2], sibling()),
+                push(far, far, send.at[i, 3], recv.at[i, 3], sibling()),
+            ]
+            for copy in copies[:3]:
                 copy.start()
-            copies.extend(new)
-
-        spread(0, row_a, grad_all)
+            return copies
+
+        def settle(copies):
+            copies[1].wait_recv()
+            copies[3].start()
+            copies[0].wait()
+            copies[1].wait_send()
+            copies[2].wait()
+            copies[3].wait()
+
+        first = spread(0, row_a, grad_all)
+        half = pl.ds(pl.multiple_of(c * 8, 8), 8)
+        rest_half = pl.ds(pl.multiple_of((1 - c) * 8, 8), 8)
+        over = push(small_out.at[rest_half], other, csem.at[0], csem.at[1], sibling())
+        over.start()
+        team_b.total(total_b)
+        row_b[...] = (after_ref[...] + total_b[...]).astype(BF)
+        second = spread(1, row_b, out_all)
+        over.wait()
+        small_out[half] = small_out[half] + other[...]
         for s, stage in enumerate(stages):
             swaps = [
-                push(small_out, got.at[s, k - 1], ssend.at[s, k], srecv.at[s, k], place(stage[k]))
-                for k in range(1, len(stage))
+                push(small_out.at[half], got.at[s, k - 1], ssend.at[s, k], srecv.at[s, k], place(stage[k]))
+                for k in range(1, 4)
             ]
             for swap in swaps:
                 swap.start()
-            if s == 0:
-                team_b.total(total_b)
-                row_b[...] = (after_ref[...] + total_b[...]).astype(BF)
-                spread(1, row_b, out_all)
             for swap in swaps:
                 swap.wait()
-            total = small_out[...]
-            for k in range(1, len(stage)):
-                total += got[s, k - 1]
-            small_out[...] = total
-        for copy in copies:
-            copy.wait()
+            small_out[half] = small_out[half] + got[s, 0] + got[s, 1] + got[s, 2]
+        back_over = push(small_out.at[half], rest_rows, csem.at[2], csem.at[3], sibling())
+        back_over.start()
+        settle(first)
+        settle(second)
+        back_over.wait()
+        small_out[rest_half] = rest_rows[...]
         for swap in grad_swaps:
             swap.finish()
         team_a.close()
@@ -778,20 +930,23 @@
 
     return pl.pallas_call(
         kernel,
-        out_shape=[jax.ShapeDtypeStruct((4, own, width), BF)] * 2
+        out_shape=[jax.ShapeDtypeStruct((2, 2, own, width), BF)] * 2
         + [jax.ShapeDtypeStruct((16, width), F32)]
         + [jax.ShapeDtypeStruct(g.shape, g.dtype) for g in grads],
         in_specs=[ANY, ANY] + [VMEM] * 7 + [ANY] * 3,
         out_specs=[ANY, ANY, VMEM] + [ANY] * 3,
         scratch_shapes=[
-            pltpu.VMEM((8, 2, 2, own, width + LANE), BF),
-            pltpu.VMEM((8, 2, 2, own, width), BF),
+            pltpu.VMEM((2, 4, 2, 2, own, width + LANE), BF),
+            pltpu.VMEM((2, 4, 2, 2, own, width), BF),
             pltpu.SemaphoreType.DMA((2,)),
             pltpu.VMEM((own, width + LANE), F32),
             pltpu.VMEM((own, width), F32),
             pltpu.VMEM((own, width), BF),
             pltpu.VMEM((own, width), BF),
-            pltpu.VMEM((4, 3, 16, width), F32),
+            pltpu.VMEM((3, 3, 8, width), F32),
+            pltpu.VMEM((8, width), F32),
+            pltpu.VMEM((8, width), F32),
+            pltpu.SemaphoreType.DMA((4,)),
         ]
         + [pltpu.SemaphoreType.DMA((2, 4))] * 2
         + [pltpu.SemaphoreType.DMA((4, 4))] * 2
@@ -801,8 +956,8 @@
         name="leave",
         **settings(collective, 200 << 20, 48),
     )(
-        back.reshape(8, 2, 2, own, width + LANE),
-        branch.reshape(8, 2, 2, own, width),
+        back.reshape(2, 4, 2, 2, own, width + LANE),
+        branch.reshape(2, 4, 2, 2, own, width),
         after, grad_mid, inputs, gain, gates_own, routers, small, *grads,
     )
 
@@ -875,10 +1030,12 @@
     attn_gain, mlp_gain = reorder(attn_gain, 0)[None], reorder(mlp_gain, 0)[None]
     routers = reorder(jnp.concatenate([attn_router, mlp_router], axis=1), 0)
     routers = jnp.pad(routers, ((0, 0), (0, LANE - 2 * EXPERTS)))
-    hidden = reorder(hidden, 1)
-    cotangent = reorder(cotangent, 1)
-    hidden_own = lax.dynamic_slice_in_dim(hidden, quarter * own, own, axis=0)
-    cot_own = lax.dynamic_slice_in_dim(cotangent, quarter * own, own, axis=0)
+
+    def quarter_of(array):
+        return lax.dynamic_slice_in_dim(array, quarter * own, own, axis=0)
+
+    hidden_own = reorder(quarter_of(hidden), 1)
+    cot_own = reorder(quarter_of(cotangent), 1)
     start = (zl * 4 + x) * seq + quarter * own
 
     def mine(array):
@@ -887,11 +1044,12 @@
     attn_w, *mlp_rows = enter(1, attn_blocks, mlp_blocks)
     attn_w = attn_w.reshape(width, 6 * HEAD)
     mlp_w = [gather_y(block) for block in mlp_rows]
-    hidden, _ = lax.optimization_barrier((hidden, attn_w))
-    group_in, masks = spread_in(2, hidden, masks)
+    entering = jnp.concatenate([hidden_own, quarter_of(masks)], axis=1)
+    entering = lax.optimization_barrier((entering, attn_w))[0]
+    group_in = spread_in(2, entering).reshape(8, seq, width + LANE)
 
     normed_a, qkv, gated_att, gates_a, after, normed_m, group_cot = attn_forward(
-        3, group_in, masks, attn_w, attn_gain, routers, cosines, sines, mlp_gain, hidden_own, cotangent
+        3, group_in, attn_w, attn_gain, routers, cosines, sines, mlp_gain, hidden_own, cot_own
     )
     group_cot = group_cot.reshape(group, width)
     normed_a = normed_a.reshape(group, width)
@@ -899,7 +1057,7 @@
     gates_a = gates_a.reshape(group, LANE)
 
     h, grad_gate, grad_up, branch_m, back_m, gates_m = experts(
-        normed_m, group_cot, masks.reshape(group, LANE), routers, mlp_w, 2 * part - features
+        normed_m, group_cot, group_in.reshape(group, width + LANE), routers, mlp_w, 2 * part - features
     )
     mlp_grads = [
         mm_tn(normed_m, grad_gate).astype(BF),

time: 549 us -> 502 us (0.914)
  Pallas kernels: 439 us -> 342 us
  waiting for transfers between devices: 7.33 us -> 51.4 us
  local copies, waits for them, and re-layouts: 49 us -> 55.8 us
    pallas_call x1, Pallas kernels: 103 us -> 68.2 us  [attn_forward(): pl.pallas_call(kernel, out_shape=[jax.ShapeDtypeStruct((8, seq, width), B...]
    pallas_call x2, Pallas kernels: 153 us -> 121 us  [the longest x1 93.2 us: leave(): pl.pallas_call(kernel, out_shape=[jax.ShapeDtypeStruct((2, 2, own, width)...]
    reduce_scatter x4, waiting for transfers between devices: 5.87 us -> 28.6 us  [sum_y(): lax.psum_scatter(grad.astype(BF), 'y', scatter_dimension=0, tiled=True)]
    pallas_call x1, Pallas kernels: 71.8 us -> 50.2 us  [middle(): pl.pallas_call(kernel, out_shape=[jax.ShapeDtypeStruct((own, width), F32)...]
    all_gather x3, waiting for transfers between devices: 0.01 us -> 21.4 us  [gather_y(): lax.all_gather(block.reshape(-1, block.shape[2]), 'y', axis=0, tiled=True)]
    pallas_call x1, Pallas kernels: 52.6 us -> 43.9 us  [enter(): pl.pallas_call(kernel, out_shape=[like, jax.ShapeDtypeStruct((4,) + like....]
    unnamed x56 -> x72, local copies, waits for them, and re-layouts: 22 us -> 26 us
  transfers between devices with their start and end apart: 7 -> 7, of which waited for: 1 -> 3; matrix products, arithmetic and copies ran while one was open for 7% -> 9% of each run, Pallas kernels for 63% -> 51%
where the time goes in v5:
time: 502 us; the launch traced here: 495 us
  Pallas kernels  342 us (68%)
  local copies, waits for them, and re-layouts  55.8 us (11%)
  waiting for transfers between devices  51.4 us (10%)
  matrix products  24.9 us (5%)
  between operations  15.3 us (3%)
  other arithmetic  5.1 us (1%)
    pallas_call x1, Pallas kernels, leave(): pl.pallas_call(kernel, out_shape=[jax.ShapeDtypeStruct((2, 2, own, width)...  93.2 us
    pallas_call x1, Pallas kernels, attn_forward(): pl.pallas_call(kernel, out_shape=[jax.ShapeDtypeStruct((8, seq, width), B...  68.2 us
    pallas_call x1, Pallas kernels, middle(): pl.pallas_call(kernel, out_shape=[jax.ShapeDtypeStruct((own, width), F32)...  50.2 us
    pallas_call x1, Pallas kernels, enter(): pl.pallas_call(kernel, out_shape=[like, jax.ShapeDtypeStruct((4,) + like....  43.9 us
    pallas_call x1, Pallas kernels, experts(): pl.pallas_call(kernel, grid=(4,), out_shape=[jax.ShapeDtypeStruct((rows,...  30.9 us
    reduce_scatter x4, waiting for transfers between devices, sum_y(): lax.psum_scatter(grad.astype(BF), 'y', scatter_dimension=0, tiled=True)  28.6 us
    pallas_call x1, Pallas kernels, spread_in(): pl.pallas_call(kernel, out_shape=jax.ShapeDtypeStruct((2, 4, 2, 2, own, w...  28 us
    unnamed x72, local copies, waits for them, and re-layouts  26 us
  transfers between devices with their start and end apart: 7, of which 3 were waited for; matrix products, arithmetic and copies ran while one was open for 9% of the time, Pallas kernels for 51%

profile of v5, /device:TPU:0, one launch (start us, length us, event | category | flops | bytes accessed | tf_op | source)
XLA Modules:
  0.0 495.2 jit_solution(17239682778720832737)
XLA Ops:
  7.2 0.9 slice.100
  8.1 1.0 slice.99
  9.3 1.1 reshape.177
  10.4 0.5 copy_bitcast_fusion.2
  11.1 0.9 pad_maximum_fusion.1
  12.0 0.9 reshape.178.a_ref
  12.9 0.3 slice_bitcast_fusion.1
  13.2 0.6 pad_maximum_fusion.4
  13.9 0.4 copy-done.23
  14.3 2.0 fusion.5
  16.8 43.9 %enter.1 = (bf16[8,64,768]{2,1,0:T(8,128)(2,1)}, bf16[4,8,64,768]{3,2,1,0:T(8,128)(2,1)S(1)}, bf16[8,64,768]{2,1,0:T(8,128)(2,1)}, bf16[8,64,768]{2,1,0:T(8,128)(2,1)}, bf16[8,64,768]{2,1,0:T(8,128)(2,1)}) custom-call(bf16[8,64,768]{2,1,0:T(8,128)(2,1)S(1)} %reshape.178.a_ref, bf16[8,64,768]{2,1,0:T(8,128)(2,1)S(1)} %bitcast.129, ...), custom_call_target="tpu_custom_call" | custom-call | bytes 125829120 | tf_op jit(solution)/shard_map/enter/pallas_call | solution.py:234
  60.7 1.7 copy-done.1
  62.5 0.7 all-gather.6.cloned.1.call-update
  63.2 0.7 all-gather.8.cloned.1.call-update
  64.3 1.0 constant_dynamic-slice_fusion.2
  65.9 0.3 copy.86
  66.2 28.0 %spread_in.1 = bf16[2,4,2,2,32,2176]{5,4,3,2,1,0:T(8,128)(2,1)S(1)} custom-call(bf16[32,2176]{1,0:T(8,128)(2,1)S(1)} %pad_maximum_fusion.6.row_ref), custom_call_target="tpu_custom_call" | custom-call | bytes 94371840 | tf_op jit(solution)/shard_map/spread_in/pallas_call | solution.py:256
  94.2 2.1 copy-done
  96.4 68.2 %attn_forward.1 = (bf16[8,128,2048]{2,1,0:T(8,128)(2,1)}, bf16[8,128,512]{2,1,0:T(8,128)(2,1)S(1)}, bf16[8,128,256]{2,1,0:T(8,128)(2,1)S(1)}, f32[8,128,128]{2,1...) custom-call(bf16[8,128,2176]{2,1,0:T(8,128)(2,1)} %bitcast.122, ...), custom_call_target="tpu_custom_call" | custom-call | bytes 209715200 | tf_op jit(solution)/shard_map/attn_forward/pallas_call | solution.py:627
  164.6 1.0 copy-done.17
  165.6 0.8 copy-done.19
  166.4 21.4 %all-gather.8.cloned.1.call-done.wd = bf16[2048,768]{1,0:T(8,128)(2,1)} async-done(((bf16[512,768]{1,0:T(8,128)(2,1)}), bf16[2048,768]{1,0:T(8,128)(2,1)}) %all-gather.8.cloned.1.call-update) | async-done | bytes 3145744 | tf_op jit(solution)/shard_map/all_gather | solution.py:978
  187.8 30.9 %experts.1 = (bf16[1024,768]{1,0:T(8,128)(2,1)S(1)}, bf16[1024,768]{1,0:T(8,128)(2,1)S(1)}, bf16[1024,768]{1,0:T(8,128)(2,1)S(1)}, bf16[1024,2048]{1,0:T(8,128)(...) custom-call(bf16[1024,2048]{1,0:T(8,128)(2,1)} %bitcast.167, bf16[1024,2048]{1,0:T(8,128)(2,1)} %bitcast.165, ...), custom_call_target="tpu_custom_call" | custom-call | flops 19327352832 | bytes 41943040 | tf_op jit(solution)/shard_map/experts/pallas_call | solution.py:693
  218.8 1.2 copy-done.21
  220.0 1.1 copy-done.22
  221.1 4.9 convolution_convert_fusion.1
  226.3 7.8 %convolution_convert_fusion.2 = bf16[2048,768]{1,0:T(8,128)(2,1)} fusion(bf16[1024,2048]{1,0:T(8,128)(2,1)} %bitcast.168, bf16[1024,768]{1,0:T(8,128)(2,1)} %copy-done.22), kind=kOutput, calls=%fused_computation.2 | convolution fusion | flops 3222798336 | bytes 8912896 | tf_op jit(solution)/shard_map/dot_general | solution.py:29
  234.1 8.5 %convolution_convert_fusion = bf16[2048,768]{1,0:T(8,128)(2,1)} fusion(bf16[1024,2048]{1,0:T(8,128)(2,1)} %bitcast.166, bf16[1024,768]{1,0:T(8,128)(2,1)} %copy-done.21), kind=kOutput, calls=%fused_computation | convolution fusion | flops 3222798336 | bytes 8912896 | tf_op jit(solution)/shard_map/dot_general | solution.py:29
  242.9 50.2 %middle.1 = (f32[32,2048]{1,0:T(8,128)S(1)}, f32[16,2048]{1,0:T(8,128)S(1)}, bf16[2,4,2,2,32,2048]{5,4,3,2,1,0:T(8,128)(2,1)S(1)}) custom-call(bf16[2,4,2,2,32,2176]{5,4,3,2,1,0:T(8,128)(2,1)} %bitcast.141, f32[32,2048]{1,0:T(8,128)S(1)} %get-tuple-element.54.after_ref, f32[1,2048]{1,0:T(1,128)S(1)} %broadcast_in_dim_reshape.7.gain_m_ref.gain_ref, ...), custom_call_target="tpu_custom_call" | custom-call | bytes 167772160 | tf_op jit(solution)/shard_map/middle/pallas_call | solution.py:818
  293.2 0.6 copy-done.9
  293.8 2.0 copy-done.15
  295.9 9.0 %reduce-scatter.5.cloned.1.call-done = bf16[512,768]{1,0:T(8,128)(2,1)} async-done(((bf16[2048,768]{1,0:T(8,128)(2,1)}), bf16[512,768]{1,0:T(8,128)(2,1)}) %reduce-scatter.5.cloned.1.call-update) | async-done | bytes 786448 | tf_op jit(solution)/shard_map/reduce_scatter | solution.py:982
  304.9 1.9 copy-done.2
  306.8 12.3 %attn_backward.1 = (bf16[1024,512]{1,0:T(8,128)(2,1)S(1)}, bf16[1024,2176]{1,0:T(8,128)(2,1)}) custom-call(bf16[1024,2048]{1,0:T(8,128)(2,1)} %bitcast.136, bf16[1024,512]{1,0:T(8,128)(2,1)S(1)} %bitcast.138, f32[1024,128]{1,0:T(8,128)S(1)} %bitcast.134, bf16[2048,768]{1,0:T(8,128)(2,1)S(1)} %bitcast.125, f32[128,128]{1,0:T(8,128)S(1)} %copy-done.14, ...), custom_call_target="tpu_custom_call" | custom-call | flops 3221225472 | bytes 20971520 | tf_op jit(solution)/shard_map/attn_backward/pallas_call | solution.py:764
  319.1 1.3 convolution_convert_fusion.4
  320.4 0.9 copy-done.31
  321.3 2.4 convolution_convert_fusion.3
  323.7 2.0 pad_maximum_fusion
  325.7 19.5 %reduce-scatter.9.cloned.1.call-done = bf16[512,768]{1,0:T(8,128)(2,1)} async-done(((bf16[2048,768]{1,0:T(8,128)(2,1)}), bf16[512,768]{1,0:T(8,128)(2,1)}) %reduce-scatter.9.cloned.1.call-update) | async-done | bytes 786448 | tf_op jit(solution)/shard_map/reduce_scatter | solution.py:982
  345.3 0.9 copy-done.10
  346.2 93.2 %leave.1 = (bf16[2,2,32,2048]{3,2,1,0:T(8,128)(2,1)S(1)}, bf16[2,2,32,2048]{3,2,1,0:T(8,128)(2,1)S(1)}, f32[16,2048]{1,0:T(8,128)S(1)}, bf16[8,64,768]{2,1,0:T(8...) custom-call(bf16[2,4,2,2,32,2176]{5,4,3,2,1,0:T(8,128)(2,1)} %bitcast.142, ...), custom_call_target="tpu_custom_call" | custom-call | bytes 209715200 | tf_op jit(solution)/shard_map/leave/pallas_call | solution.py:931
  439.5 0.9 copy-done.4
  440.3 0.8 copy-done.6
  441.1 0.8 copy-done.8
  441.9 0.7 copy-done.11
  442.6 1.5 reshape_reshape.8
  444.0 1.0 copy.89
  445.0 2.2 reshape.204
  447.4 0.6 slice.118
  448.1 0.6 copy.100
  448.7 0.6 copy.99
  449.3 0.6 slice.111
  450.2 2.0 copy.96
  452.2 1.9 reshape.221
  454.1 2.5 copy.90
  456.6 2.7 reshape.217
  459.7 3.8 copy.95
  463.5 1.4 copy.92
  464.9 15.3 %swap_back.1 = bf16[8,64,768]{2,1,0:T(8,128)(2,1)S(1)} custom-call(bf16[8,64,768]{2,1,0:T(8,128)(2,1)S(1)} %bitcast.126), custom_call_target="tpu_custom_call" | custom-call | bytes 83886080 | tf_op jit(solution)/shard_map/swap_back/pallas_call | solution.py:279
  480.3 2.2 reshape.223
  482.4 2.6 copy.93
  485.0 0.6 reshape.219
  485.8 1.1 copy.94
  487.0 1.0 pad_maximum_fusion.5
  (115 shorter events, 3.6 us)
Async XLA Ops:
  7.2 159.2 %all-gather.4.cloned.1.call-start = ((), (), s32[]{:S(2)}) async-start(), calls=%async_computation.4 | async-start | bytes 3932160 | tf_op jit(solution)/shard_map/all_gather | solution.py:978
  11.0 2.0 copy-start.24
  12.9 1.4 copy-start.23
  16.8 47.2 %copy-start.27 = (f32[2048]{0:T(1024)S(1)}, f32[2048]{0:T(1024)}, u32[]{:S(2)}) copy-start(f32[2048]{0:T(1024)} %param.18) | copy-start | bytes 24580
  16.8 47.2 %copy-start.28 = (f32[2048]{0:T(1024)S(1)}, f32[2048]{0:T(1024)}, u32[]{:S(2)}) copy-start(f32[2048]{0:T(1024)} %param.22) | copy-start | bytes 24580
  16.8 47.3 %copy-start.29 = (s32[128,2]{0,1:T(2,128)S(1)}, s32[128,2]{0,1:T(2,128)}, u32[]{:S(2)}) copy-start(s32[128,2]{0,1:T(2,128)} %param.26) | copy-start | bytes 3076
  16.8 47.3 %copy-start.30 = (s32[128,2]{0,1:T(2,128)S(1)}, s32[128,2]{0,1:T(2,128)}, u32[]{:S(2)}) copy-start(s32[128,2]{0,1:T(2,128)} %param.27) | copy-start | bytes 3076
  60.7 1.7 copy-start.1
  62.4 3.4 copy-start.25
  62.4 3.4 copy-start.26
  62.4 104.0 %all-gather.6.cloned.1.call-start = ((), (), s32[]{:S(2)}) async-start(), calls=%async_computation.5 | async-start | bytes 3932160 | tf_op jit(solution)/shard_map/all_gather | solution.py:978
  63.2 124.6 %all-gather.8.cloned.1.call-start = ((), (), s32[]{:S(2)}) async-start(), calls=%async_computation.6 | async-start | bytes 3932160 | tf_op jit(solution)/shard_map/all_gather | solution.py:978
  63.9 232.0 %reduce-scatter.7.cloned.1.call-start = ((), (), s32[]{:S(2)}) async-start(), calls=%async_computation.8 | async-start | bytes 3932160 | tf_op jit(solution)/shard_map/reduce_scatter | solution.py:982
  66.2 30.2 %copy-start.13 = (f32[128,128]{1,0:T(8,128)S(1)}, f32[128,128]{1,0:T(8,128)}, u32[]{:S(2)}) copy-start(f32[128,128]{1,0:T(8,128)} %constant.36.clone.sin_ref) | copy-start | bytes 196612
  66.2 30.2 %copy-start.14 = (f32[128,128]{1,0:T(8,128)S(1)}, f32[128,128]{1,0:T(8,128)}, u32[]{:S(2)}) copy-start(f32[128,128]{1,0:T(8,128)} %constant.35.clone.cos_ref) | copy-start | bytes 196612
  94.2 2.1 copy-start
  164.6 1.0 copy-start.17
  165.6 0.8 copy-start.19
  187.8 33.3 %copy-start.32 = (bf16[2,4,2,2,32,2048]{5,4,3,2,1,0:T(8,128)(2,1)S(1)}, bf16[2,4,2,2,32,2048]{5,4,3,2,1,0:T(8,128)(2,1)}, u32[]{:S(2)}) copy-start(bf16[2,4,2,2,32,2048]{5,4,3,2,1,0:T(8,128)(2,1)} %get-tuple-element.44) | copy-start | bytes 12582916
  218.8 1.2 copy-start.21
  220.0 1.1 copy-start.22
  226.0 78.9 %reduce-scatter.5.cloned.1.call-start = ((), (), s32[]{:S(2)}) async-start(), calls=%async_computation.7 | async-start | bytes 3932160 | tf_op jit(solution)/shard_map/reduce_scatter | solution.py:982
  234.1 111.1 %reduce-scatter.9.cloned.1.call-start = ((), (), s32[]{:S(2)}) async-start(), calls=%async_computation.9 | async-start | bytes 3932160 | tf_op jit(solution)/shard_map/reduce_scatter | solution.py:982
  242.6 220.9 %reduce-scatter.11.cloned.1.call-start = ((), (), s32[]{:S(2)}) async-start(), calls=%async_computation.10 | async-start | bytes 3932160 | tf_op jit(solution)/shard_map/reduce_scatter | solution.py:982
  242.9 62.0 %copy-start.18 = (bf16[8,128,512]{2,1,0:T(8,128)(2,1)S(1)}, bf16[8,128,512]{2,1,0:T(8,128)(2,1)}, u32[]{:S(2)}) copy-start(bf16[8,128,512]{2,1,0:T(8,128)(2,1)} %copy-done.17) | copy-start | bytes 3145732
  293.2 0.7 copy-start.9
  293.8 2.0 copy-start.15
  304.9 1.9 copy-start.2
  306.8 12.3 %copy-start.16 = (bf16[2,4,2,2,32,2048]{5,4,3,2,1,0:T(8,128)(2,1)S(1)}, bf16[2,4,2,2,32,2048]{5,4,3,2,1,0:T(8,128)(2,1)}, u32[]{:S(2)}) copy-start(bf16[2,4,2,2,32,2048]{5,4,3,2,1,0:T(8,128)(2,1)} %copy-done.15) | copy-start | bytes 12582916
  306.8 12.3 %copy-start.20 = (bf16[8,128,256]{2,1,0:T(8,128)(2,1)S(1)}, bf16[8,128,256]{2,1,0:T(8,128)(2,1)}, u32[]{:S(2)}) copy-start(bf16[8,128,256]{2,1,0:T(8,128)(2,1)} %copy-done.19) | copy-start | bytes 1572868
  319.1 2.2 copy-start.31
  325.7 19.6 %copy-start.3 = (bf16[512,768]{1,0:T(8,128)(2,1)S(1)}, bf16[512,768]{1,0:T(8,128)(2,1)}, u32[]{:S(2)}) copy-start(bf16[512,768]{1,0:T(8,128)(2,1)} %reduce-scatter.5.cloned.1.call-done) | copy-start | bytes 2359300
  345.3 0.9 copy-start.10
  439.4 0.9 copy-start.4
  440.3 0.8 copy-start.6
  441.1 0.8 copy-start.8
  441.9 0.7 copy-start.11
  442.6 4.7 copy-start.12
  444.0 6.0 %copy-start.5 = (bf16[8,64,768]{2,1,0:T(8,128)(2,1)S(1)}, bf16[8,64,768]{2,1,0:T(8,128)(2,1)}, u32[]{:S(2)}) copy-start(bf16[8,64,768]{2,1,0:T(8,128)(2,1)} %copy-done.4) | copy-start | bytes 2359300
  450.1 2.1 copy-start.7
Sparse Core Ops, SparseCore 0:
  62.5 42.3 all-gather.3
  106.6 39.7 all-gather.5
  148.1 39.7 all-gather.7
  226.2 38.4 reduce-scatter.6
  266.9 37.9 reduce-scatter.4
  307.2 38.0 reduce-scatter.8
  347.6 37.9 reduce-scatter.10

commit v6 on v5

--- a/solution.py
+++ b/solution.py
@@ -213,18 +213,26 @@
             copy.wait()
 
 
-def enter(collective, attn_blocks, blocks):
+def enter(collective, attn_blocks, blocks, rows):
+    own, width = rows.shape
+
     def kernel(a_ref, *refs):
-        m_refs, a_mid, a_out, m_outs, sems = refs[:3], refs[3], refs[4], refs[5:8], refs[8:]
-        meet([place(m) for m in GROUP_MOVES[1:] + [Y_MOVES[1], Y_MOVES[3]]])
+        m_refs, row_ref, a_mid, a_out, m_outs, row_out, sems = (
+            refs[:3], refs[3], refs[4], refs[5], refs[6:9], refs[9], refs[10:],
+        )
+        meet([place(m) for m in TEAM_MOVES[1:] + [Y_MOVES[1], Y_MOVES[3]]] + [sibling()])
         first = Swap(a_ref, a_mid, sems[2:4])
         first.start()
+        spread = TeamSpread(row_ref, row_out, sems[10:14])
+        spread.start()
+        first.finish()
+        ring = RingY(a_mid, a_out, sems[0:2])
+        ring.start()
+        spread.middle()
         swaps = [Swap(m_refs[i], m_outs[i], sems[4 + 2 * i : 6 + 2 * i]) for i in range(3)]
         for swap in swaps:
             swap.start()
-        first.finish()
-        ring = RingY(a_mid, a_out, sems[0:2])
-        ring.start()
+        spread.finish()
         ring.forward()
         for swap in swaps:
             swap.finish()
@@ -234,57 +242,69 @@
     return pl.pallas_call(
         kernel,
         out_shape=[like, jax.ShapeDtypeStruct((4,) + like.shape, like.dtype)]
-        + [jax.ShapeDtypeStruct(b.shape, b.dtype) for b in blocks],
-        in_specs=[ANY] * 4,
-        out_specs=[ANY] * 5,
-        scratch_shapes=RingY.sems + Swap.sems * 4,
+        + [jax.ShapeDtypeStruct(b.shape, b.dtype) for b in blocks]
+        + [jax.ShapeDtypeStruct((2, 4, 2, 2, own, width), rows.dtype)],
+        in_specs=[ANY] * 5,
+        out_specs=[ANY] * 6,
+        scratch_shapes=RingY.sems + Swap.sems * 4 + TeamSpread.sems,
         name="enter",
         **settings(collective, 120 << 20),
-    )(attn_blocks, *blocks)[1:]
-
-
-def spread_in(collective, rows):
-    own, width = rows.shape
-
-    def kernel(row_ref, out_ref, *sems):
-        meet_team()
-        spread = TeamSpread(row_ref, out_ref, sems)
-        spread.start()
-        spread.middle()
-        spread.finish()
-
-    return pl.pallas_call(
-        kernel,
-        out_shape=jax.ShapeDtypeStruct((2, 4, 2, 2, own, width), rows.dtype),
-        in_specs=[ANY],
-        out_specs=ANY,
-        scratch_shapes=TeamSpread.sems,
-        name="spread_in",
-        **settings(collective, 90 << 20),
-    )(rows)
-
-
-def swap_back(collective, name, blocks):
-    count = len(blocks)
-
-    def kernel(*refs):
-        sems = refs[2 * count :]
-        meet([place(m) for m in GROUP_MOVES[1:]])
-        swaps = [Swap(refs[i], refs[count + i], sems[2 * i : 2 * i + 2]) for i in range(count)]
-        for swap in swaps:
-            swap.start()
-        for swap in swaps:
-            swap.finish()
-
-    return pl.pallas_call(
-        kernel,
-        out_shape=[jax.ShapeDtypeStruct(b.shape, b.dtype) for b in blocks],
-        in_specs=[ANY] * count,
-        out_specs=[ANY] * count,
-        scratch_shapes=Swap.sems * count,
-        name=name,
-        **settings(collective, 80 << 20),
-    )(*blocks)
+    )(attn_blocks, *blocks, rows)[1:]
+
+
+class RingSum:
+    @staticmethod
+    def scratch(rows, cols):
+        return [
+            pltpu.VMEM((2, rows // 2, cols), BF),
+            pltpu.VMEM((2, rows // 2, cols), BF),
+            pltpu.VMEM((2, rows, cols), BF),
+            pltpu.SemaphoreType.DMA((6,)),
+            pltpu.SemaphoreType.DMA((6,)),
+        ]
+
+    count = 5
+
+    def __init__(self, part, scratch):
+        self.part = part
+        self.got, self.mix, self.sums, self.send, self.recv = scratch
+        self.y = lax.axis_index("y")
+        half = part.shape[1] // 2
+        self.halves = [pl.ds(0, half), pl.ds(half, half)]
+
+    def line(self, step):
+        return lax.rem(self.y + step, 4)
+
+    def copy(self, k):
+        kind, way = k // 2, k % 2
+        step = (1, 3)[way]
+        top, low = self.halves[way], self.halves[1 - way]
+        if kind == 0:
+            src, dst = self.part.at[self.line(2), top], self.got.at[way]
+        elif kind == 1:
+            src, dst = self.part.at[self.line(step), low], self.sums.at[way, low]
+        else:
+            src, dst = self.mix.at[way], self.sums.at[way, top]
+        return push(src, dst, self.send.at[k], self.recv.at[k], {"y": self.line(step)})
+
+    def start(self):
+        for k in range(4):
+            self.copy(k).start()
+
+    def middle(self):
+        for way in range(2):
+            self.copy(way).wait_recv()
+            mine = self.part[self.line((1, 3)[way]), self.halves[way]].astype(F32)
+            self.mix[way] = (mine + self.got[way].astype(F32)).astype(BF)
+            self.copy(4 + way).start()
+
+    def finish(self, out):
+        for k in range(2, 6):
+            self.copy(k).wait_recv()
+        total = self.part[self.y].astype(F32) + self.sums[0].astype(F32) + self.sums[1].astype(F32)
+        out[...] = total.astype(BF).reshape(out.shape)
+        for k in range(6):
+            self.copy(k).wait_send()
 
 
 class TeamSum:
@@ -539,21 +559,28 @@
 
 
 def attn_forward(
-    collective, hidden, weights, gain, routers, cosines, sines, mlp_gain, hidden_own, cot_own
+    collective, hidden, weights, gain, routers, cosines, sines, mlp_gain, hidden_own, cot_own, blocks
 ):
     own, width = hidden_own.shape
     seq = hidden.shape[1]
     scale = HEAD ** (-0.5)
 
     def kernel(
-        hid, w_ref, gain_ref, router_ref, cos_ref, sin_ref, gain_m_ref, own_ref, cot_ref,
-        normed_out, qkv_out, gated_out, gates_out, after_out, spread_out, cot_out,
+        hid, w_ref, gain_ref, router_ref, cos_ref, sin_ref, gain_m_ref, own_ref, cot_ref, b0, b1, b2,
+        normed_out, qkv_out, gated_out, gates_out, after_out, spread_out, cot_out, w0, w1, w2,
         part, total, row, *rest,
     ):
-        meet_team()
-        team = TeamSum(part, rest[: TeamSum.count])
-        cot = TeamSpread(cot_ref, cot_out, rest[TeamSum.count : TeamSum.count + 4])
+        meet([place(m) for m in TEAM_MOVES[1:] + [Y_MOVES[1], Y_MOVES[3]]] + [sibling()])
+        count = TeamSum.count
+        team = TeamSum(part, rest[:count])
+        cot = TeamSpread(cot_ref, cot_out, rest[count : count + 4])
         cot.start()
+        rings = [
+            RingY(b, w, rest[count + 8 + 2 * k : count + 10 + 2 * k])
+            for k, (b, w) in enumerate(((b0, w0), (b1, w1), (b2, w2)))
+        ]
+        for ring in rings:
+            ring.start()
         first = 2 * team.zl
         causal = causal_mask(2, seq)
 
@@ -618,11 +645,16 @@
         after = total[...] + own_ref[...].astype(F32)
         after_out[...] = after
         row[...] = (after * rms_scale(after) * gain_m_ref[...]).astype(BF)
-        spread = TeamSpread(row, spread_out, rest[TeamSum.count + 4 :])
+        spread = TeamSpread(row, spread_out, rest[count + 4 : count + 8])
         spread.start()
+        rings[0].forward()
         spread.middle()
+        rings[1].forward()
         spread.finish()
+        rings[2].forward()
         team.close()
+        for ring in rings:
+            ring.finish()
 
     return pl.pallas_call(
         kernel,
@@ -634,19 +666,21 @@
             jax.ShapeDtypeStruct((own, width), F32),
             jax.ShapeDtypeStruct((2, 4, 2, 2, own, width), BF),
             jax.ShapeDtypeStruct((2, 4, 2, 2, own, width), BF),
-        ],
-        in_specs=[VMEM] * 8 + [ANY],
-        out_specs=[VMEM] * 5 + [ANY] * 2,
+        ]
+        + [jax.ShapeDtypeStruct((4,) + b.shape, b.dtype) for b in blocks],
+        in_specs=[VMEM] * 8 + [ANY] * 4,
+        out_specs=[VMEM] * 5 + [ANY] * 5,
         scratch_shapes=[
             pltpu.VMEM((2, 4, 2, 2, own, width), BF),
             pltpu.VMEM((own, width), F32),
             pltpu.VMEM((own, width), BF),
         ]
         + TeamSum.scratch(own, width)
-        + TeamSpread.sems * 2,
+        + TeamSpread.sems * 2
+        + RingY.sems * 3,
         name="attn_forward",
         **settings(collective, 200 << 20, 48),
-    )(hidden, weights, gain, routers, cosines, sines, mlp_gain, hidden_own, cot_own)
+    )(hidden, weights, gain, routers, cosines, sines, mlp_gain, hidden_own, cot_own, *blocks)
 
 
 def experts(normed, cotangent, masks, routers, weights, extra):
@@ -787,16 +821,29 @@
     return inner, gain_grad, mm_tn(logits_back.astype(BF), normed)[:8]
 
 
-def middle(collective, back, after, gain, gates_own, routers, cot_own):
+def middle(collective, back, after, gain, gates_own, routers, cot_own, grads):
     own, width = after.shape
-
-    def kernel(part_ref, after_ref, gain_ref, gates_ref, router_ref, cot_ref, mid_out, small_out, spread_out, part, load, total, row, *rest):
+    rows, cols = grads[0].shape[0] // 4, grads[0].shape[1]
+
+    def kernel(
+        part_ref, after_ref, gain_ref, gates_ref, router_ref, cot_ref, g0, g1,
+        mid_out, small_out, spread_out, s0, s1,
+        part, load, total, row, *rest,
+    ):
         fetch = pltpu.make_async_copy(part_ref, part, load.at[0])
         fetch.start()
-        meet_team()
+        meet([place(m) for m in TEAM_MOVES[1:] + [Y_MOVES[1], Y_MOVES[3]]] + [sibling()])
+        count = TeamSum.count
+        team = TeamSum(part, rest[:count])
+        rings = [
+            RingSum(g, rest[count + 4 + RingSum.count * k : count + 4 + RingSum.count * (k + 1)])
+            for k, g in enumerate((g0, g1))
+        ]
+        for ring in rings:
+            ring.start()
         fetch.wait()
-        team = TeamSum(part, rest[: TeamSum.count])
         team.run()
+        rings[0].middle()
         after = after_ref[...]
         normed = (after * rms_scale(after) * gain_ref[...]).astype(BF)
         team.total(total)
@@ -809,10 +856,13 @@
         small_out[:8] = jnp.zeros((8, width), F32)
         small_out[0:1] = gain_grad
         small_out[8:] = router_grad
-        spread = TeamSpread(row, spread_out, rest[TeamSum.count :])
+        spread = TeamSpread(row, spread_out, rest[count : count + 4])
         spread.start()
+        rings[1].middle()
         spread.middle()
         spread.finish()
+        rings[0].finish(s0)
+        rings[1].finish(s1)
         team.close()
 
     return pl.pallas_call(
@@ -821,9 +871,10 @@
             jax.ShapeDtypeStruct((own, width), F32),
             jax.ShapeDtypeStruct((16, width), F32),
             jax.ShapeDtypeStruct((2, 4, 2, 2, own, width), BF),
-        ],
-        in_specs=[ANY] + [VMEM] * 5,
-        out_specs=[VMEM] * 2 + [ANY],
+        ]
+        + [jax.ShapeDtypeStruct((8, rows // 8, cols), BF)] * 2,
+        in_specs=[ANY] + [VMEM] * 7,
+        out_specs=[VMEM] * 2 + [ANY] + [VMEM] * 2,
         scratch_shapes=[
             pltpu.VMEM((2, 4, 2, 2, own, width + LANE), BF),
             pltpu.SemaphoreType.DMA((1,)),
@@ -831,19 +882,23 @@
             pltpu.VMEM((own, width), BF),
         ]
         + TeamSum.scratch(own, width + LANE)
-        + TeamSpread.sems,
+        + TeamSpread.sems
+        + RingSum.scratch(rows, cols) * 2,
         name="middle",
         **settings(collective, 160 << 20, 48),
-    )(back.reshape(2, 4, 2, 2, own, width + LANE), after, gain, gates_own, routers, cot_own)
-
-
-def leave(collective, back, branch, after, grad_mid, inputs, gain, gates_own, routers, small, grads):
+    )(back.reshape(2, 4, 2, 2, own, width + LANE), after, gain, gates_own, routers, cot_own, *[
+        g.reshape(4, rows, cols) for g in grads
+    ])
+
+
+def leave(collective, back, branch, after, grad_mid, inputs, gain, gates_own, routers, small, summed, grads):
     own, width = after.shape
+    rows, cols = grads[0].shape[0] // 4, grads[0].shape[1]
     stages = [X_MOVES, Y_MOVES, Z_MOVES]
 
     def kernel(
         back_ref, branch_ref, after_ref, mid_ref, in_ref, gain_ref, gates_ref, router_ref, small_ref,
-        g0, g1, g2, out_all, grad_all, small_out, s0, s1, s2,
+        y0, y1, g2, g3, out_all, grad_all, small_out, s0, s1, s2, s3, y2, y3,
         part_a, part_b, load, total_a, total_b, row_a, row_b, got, other, rest_rows, csem, send, recv, ssend, srecv, *rest,
     ):
         fetches = [
@@ -855,16 +910,25 @@
         meet([place(m) for m in TEAM_MOVES[1:] + Y_MOVES[1:]] + [sibling()])
         count = TeamSum.count
         team_a, team_b = TeamSum(part_a, rest[:count]), TeamSum(part_b, rest[count : 2 * count])
+        count = 2 * count
+        swaps_back = [
+            Swap(y, s, rest[count + 2 * k : count + 2 * k + 2])
+            for k, (y, s) in enumerate(((y0, s0), (y1, s1), (y2, s2), (y3, s3)))
+        ]
+        count += 8
+        rings = [
+            RingSum(g, rest[count + RingSum.count * k : count + RingSum.count * (k + 1)])
+            for k, g in enumerate((g2, g3))
+        ]
+        for ring in rings:
+            ring.start()
         fetches[0].wait()
         team_a.run()
         fetches[1].wait()
         team_b.run()
-        grad_swaps = [
-            Swap(g, s, rest[2 * count + 2 * i : 2 * count + 2 * i + 2])
-            for i, (g, s) in enumerate(((g0, s0), (g1, s1), (g2, s2)))
-        ]
-        for swap in grad_swaps:
-            swap.start()
+        rings[0].middle()
+        swaps_back[0].start()
+        swaps_back[1].start()
         inputs = in_ref[...].astype(F32)
         normed = (inputs * rms_scale(inputs) * gain_ref[...]).astype(BF)
         team_a.total(total_a)
@@ -905,8 +969,11 @@
         team_b.total(total_b)
         row_b[...] = (after_ref[...] + total_b[...]).astype(BF)
         second = spread(1, row_b, out_all)
+        rings[1].middle()
         over.wait()
         small_out[half] = small_out[half] + other[...]
+        rings[0].finish(y2)
+        swaps_back[2].start()
         for s, stage in enumerate(stages):
             swaps = [
                 push(small_out.at[half], got.at[s, k - 1], ssend.at[s, k], srecv.at[s, k], place(stage[k]))
@@ -917,13 +984,16 @@
             for swap in swaps:
                 swap.wait()
             small_out[half] = small_out[half] + got[s, 0] + got[s, 1] + got[s, 2]
+            if s == 0:
+                rings[1].finish(y3)
+                swaps_back[3].start()
         back_over = push(small_out.at[half], rest_rows, csem.at[2], csem.at[3], sibling())
         back_over.start()
         settle(first)
         settle(second)
         back_over.wait()
         small_out[rest_half] = rest_rows[...]
-        for swap in grad_swaps:
+        for swap in swaps_back:
             swap.finish()
         team_a.close()
         team_b.close()
@@ -932,10 +1002,11 @@
         kernel,
         out_shape=[jax.ShapeDtypeStruct((2, 2, own, width), BF)] * 2
         + [jax.ShapeDtypeStruct((16, width), F32)]
-        + [jax.ShapeDtypeStruct(g.shape, g.dtype) for g in grads],
-        in_specs=[ANY, ANY] + [VMEM] * 7 + [ANY] * 3,
-        out_specs=[ANY, ANY, VMEM] + [ANY] * 3,
-        scratch_shapes=[
+        + [jax.ShapeDtypeStruct((8, rows // 8, cols), BF)] * 4,
+        in_specs=[ANY, ANY] + [VMEM] * 7 + [ANY] * 2 + [VMEM] * 2,
+        out_specs=[ANY, ANY, VMEM] + [ANY] * 4,
+        scratch_shapes=[pltpu.VMEM((8, rows // 8, cols), BF)] * 2
+        + [
             pltpu.VMEM((2, 4, 2, 2, own, width + LANE), BF),
             pltpu.VMEM((2, 4, 2, 2, own, width), BF),
             pltpu.SemaphoreType.DMA((2,)),
@@ -952,13 +1023,15 @@
         + [pltpu.SemaphoreType.DMA((4, 4))] * 2
         + TeamSum.scratch(own, width + LANE)
         + TeamSum.scratch(own, width)
-        + Swap.sems * 3,
+        + Swap.sems * 4
+        + RingSum.scratch(rows, cols) * 2,
         name="leave",
         **settings(collective, 200 << 20, 48),
     )(
         back.reshape(2, 4, 2, 2, own, width + LANE),
         branch.reshape(2, 4, 2, 2, own, width),
-        after, grad_mid, inputs, gain, gates_own, routers, small, *grads,
+        after, grad_mid, inputs, gain, gates_own, routers, small, *summed,
+        *[g.reshape(4, rows, cols) for g in grads],
     )
 
 
@@ -972,15 +1045,6 @@
     shape = array.shape
     split = shape[:axis] + (4, 2, shape[axis] // 8) + shape[axis + 1 :]
     return jnp.swapaxes(array.reshape(split), axis, axis + 1).reshape(shape)
-
-
-def gather_y(block):
-    return lax.all_gather(block.reshape(-1, block.shape[2]), "y", axis=0, tiled=True)
-
-
-def sum_y(grad):
-    summed = lax.psum_scatter(grad.astype(BF), "y", scatter_dimension=0, tiled=True)
-    return summed.reshape(8, -1, grad.shape[1])
 
 
 def local(
@@ -1041,16 +1105,15 @@
     def mine(array):
         return lax.dynamic_slice_in_dim(array, start, own, axis=0)
 
-    attn_w, *mlp_rows = enter(1, attn_blocks, mlp_blocks)
+    entering = jnp.concatenate([hidden_own, quarter_of(masks)], axis=1)
+    attn_w, *mlp_rows, group_in = enter(1, attn_blocks, mlp_blocks, entering)
     attn_w = attn_w.reshape(width, 6 * HEAD)
-    mlp_w = [gather_y(block) for block in mlp_rows]
-    entering = jnp.concatenate([hidden_own, quarter_of(masks)], axis=1)
-    entering = lax.optimization_barrier((entering, attn_w))[0]
-    group_in = spread_in(2, entering).reshape(8, seq, width + LANE)
-
-    normed_a, qkv, gated_att, gates_a, after, normed_m, group_cot = attn_forward(
-        3, group_in, attn_w, attn_gain, routers, cosines, sines, mlp_gain, hidden_own, cot_own
-    )
+    group_in = group_in.reshape(8, seq, width + LANE)
+
+    normed_a, qkv, gated_att, gates_a, after, normed_m, group_cot, *mlp_w = attn_forward(
+        2, group_in, attn_w, attn_gain, routers, cosines, sines, mlp_gain, hidden_own, cot_own, mlp_rows
+    )
+    mlp_w = [w.reshape(width, part) for w in mlp_w]
     group_cot = group_cot.reshape(group, width)
     normed_a = normed_a.reshape(group, width)
     normed_m = normed_m.reshape(group, width)
@@ -1059,17 +1122,10 @@
     h, grad_gate, grad_up, branch_m, back_m, gates_m = experts(
         normed_m, group_cot, group_in.reshape(group, width + LANE), routers, mlp_w, 2 * part - features
     )
-    mlp_grads = [
-        mm_tn(normed_m, grad_gate).astype(BF),
-        mm_tn(normed_m, grad_up).astype(BF),
-        mm_tn(group_cot, h).astype(BF),
-    ]
-    back_m = lax.optimization_barrier((back_m, *mlp_grads))[0]
-    mlp_grads = [sum_y(grad) for grad in mlp_grads]
-    grad_mid_own, small_m, grad_mid = middle(
-        4, back_m, after, mlp_gain, mine(gates_m), routers, cot_own
-    )
-    grad_mid = lax.optimization_barrier((grad_mid, mlp_grads[0], mlp_grads[1]))[0]
+    grad_mid_own, small_m, grad_mid, *summed = middle(
+        3, back_m, after, mlp_gain, mine(gates_m), routers, cot_own,
+        [mm_tn(normed_m, grad_gate).astype(BF), mm_tn(normed_m, grad_up).astype(BF)],
+    )
     grad_mid = grad_mid.reshape(group, width)
     grad_proj, back_a = attn_backward(
         grad_mid, qkv.reshape(group, 4 * HEAD), gates_a, attn_w, cosines, sines
@@ -1081,17 +1137,14 @@
         ],
         axis=1,
     )
-    attn_grads = sum_y(lax.optimization_barrier((attn_grads, mlp_grads[2]))[0])
-    out_hidden, grad_in, small, *mlp_grads = leave(
-        5, back_a, branch_m, after, grad_mid_own, hidden_own, attn_gain, mine(gates_a), routers, small_m,
-        mlp_grads,
+    out_hidden, grad_in, small, *mlp_grads, attn_grads = leave(
+        4, back_a, branch_m, after, grad_mid_own, hidden_own, attn_gain, mine(gates_a), routers, small_m,
+        summed, [mm_tn(group_cot, h).astype(BF), attn_grads],
     )
     out_hidden = restore(out_hidden.reshape(seq, width), 1)
     grad_in = restore(grad_in.reshape(seq, width), 1).astype(F32)
     small = restore(small, 1)
 
-    attn_grads = lax.optimization_barrier((attn_grads, small))[0]
-    (attn_grads,) = swap_back(6, "swap_back", [attn_grads])
     attn_grads = attn_grads.astype(F32).reshape(2, 4, rows, 6, HEAD).transpose(2, 0, 3, 1, 4)
     attn_grads = attn_grads.reshape(rows, 2, 6, 4 * HEAD)
     query_grad = attn_grads[:, :, :2].reshape(rows, EXPERTS, 4 * HEAD)

time: 502 us -> 435 us (0.87)
  waiting for transfers between devices: 51.4 us -> 0 us
  between operations: 15.3 us -> 1.65 us
    pallas_call x2 -> x0, Pallas kernels: 43.3 us -> none  [the longest x1 28 us: spread_in(): pl.pallas_call(kernel, out_shape=jax.ShapeDtypeStruct((2, 4, 2, 2, own, w...]
    reduce_scatter x4 -> x0, waiting for transfers between devices: 28.6 us -> none  [sum_y(): lax.psum_scatter(grad.astype(BF), 'y', scatter_dimension=0, tiled=True)]
    all_gather x3 -> x0, waiting for transfers between devices: 21.4 us -> none  [gather_y(): lax.all_gather(block.reshape(-1, block.shape[2]), 'y', axis=0, tiled=True)]
    pallas_call x1, Pallas kernels: 68.2 us -> 87.9 us  [attn_forward(): pl.pallas_call(kernel, out_shape=[jax.ShapeDtypeStruct((8, seq, width), B...]
    pallas_call x1, Pallas kernels: 43.9 us -> 62 us  [enter(): pl.pallas_call(kernel, out_shape=[like, jax.ShapeDtypeStruct((4,) + like....]
    unnamed x72 -> x54, local copies, waits for them, and re-layouts: 26 us -> 18.9 us
    pallas_call x1, Pallas kernels: 50.2 us -> 56.6 us  [middle(): pl.pallas_call(kernel, out_shape=[jax.ShapeDtypeStruct((own, width), F32)...]
  transfers between devices with their start and end apart: 7 -> 0, of which waited for: 3 -> 0; matrix products, arithmetic and copies ran while one was open for 9% -> 0% of each run, Pallas kernels for 51% -> 0%
where the time goes in v6:
time: 435 us; the launch traced here: 427 us
  Pallas kernels  345 us (79%)
  local copies, waits for them, and re-layouts  51.1 us (12%)
  matrix products  22.2 us (5%)
  other arithmetic  7.45 us (2%)
    pallas_call x1, Pallas kernels, leave(): pl.pallas_call(kernel, out_shape=[jax.ShapeDtypeStruct((2, 2, own, width)...  94.8 us
    pallas_call x1, Pallas kernels, attn_forward(): pl.pallas_call(kernel, out_shape=[jax.ShapeDtypeStruct((8, seq, width), B...  87.9 us
    pallas_call x1, Pallas kernels, enter(): pl.pallas_call(kernel, out_shape=[like, jax.ShapeDtypeStruct((4,) + like....  62 us
    pallas_call x1, Pallas kernels, middle(): pl.pallas_call(kernel, out_shape=[jax.ShapeDtypeStruct((own, width), F32)...  56.6 us
    pallas_call x1, Pallas kernels, experts(): pl.pallas_call(kernel, grid=(4,), out_shape=[jax.ShapeDtypeStruct((rows,...  31 us
    dot_general x5, matrix products, dot(): return lax.dot_general(a, b, (dims, ((), ())), preferred_element_type=F32)  22.2 us
    unnamed x54, local copies, waits for them, and re-layouts  18.9 us
    pallas_call x1, Pallas kernels, attn_backward(): pl.pallas_call(kernel, grid=(4,), out_shape=[jax.ShapeDtypeStruct((rows,...  12.5 us

profile of v6, /device:TPU:0, one launch (start us, length us, event | category | flops | bytes accessed | tf_op | source)
XLA Modules:
  0.0 427.3 jit_solution(1500078922431855183)
XLA Ops:
  0.7 0.8 slice_bitcast_fusion.14
  1.4 0.8 slice_bitcast_fusion.12
  2.2 0.7 reshape.184
  2.9 0.7 reshape.187
  3.7 0.1 copy.84
  3.8 0.8 pad_maximum_fusion.7
  4.6 0.9 slice.96
  5.6 0.1 copy.78
  5.7 0.1 broadcast_in_dim.2
  5.9 1.0 constant_dynamic-slice_fusion.2
  7.6 0.5 copy_bitcast_fusion.2
  8.1 0.9 pad_maximum_fusion.1
  9.0 0.9 reshape.176.a_ref
  9.9 0.3 copy.86
  10.3 0.3 slice_bitcast_fusion.1
  10.6 0.6 pad_maximum_fusion.4
  11.3 0.4 copy-done.17
  11.7 2.0 fusion.5
  13.7 0.2 copy_bitcast_fusion
  14.2 62.0 %enter.1 = (bf16[8,64,768]{2,1,0:T(8,128)(2,1)}, bf16[4,8,64,768]{3,2,1,0:T(8,128)(2,1)S(1)}, bf16[8,64,768]{2,1,0:T(8,128)(2,1)S(1)}, bf16[8,64,768]{2,1,0:T(8,...) custom-call(bf16[8,64,768]{2,1,0:T(8,128)(2,1)S(1)} %reshape.176.a_ref, ...), custom_call_target="tpu_custom_call" | custom-call | bytes 125829120 | tf_op jit(solution)/shard_map/enter/pallas_call | solution.py:242
  76.2 2.1 copy-done
  78.3 1.6 copy-done.1
  80.0 87.9 %attn_forward.1 = (bf16[8,128,2048]{2,1,0:T(8,128)(2,1)}, bf16[8,128,512]{2,1,0:T(8,128)(2,1)S(1)}, bf16[8,128,256]{2,1,0:T(8,128)(2,1)S(1)}, f32[8,128,128]{2,1...) custom-call(bf16[8,128,2176]{2,1,0:T(8,128)(2,1)} %bitcast.122, ...), custom_call_target="tpu_custom_call" | custom-call | bytes 209715200 | tf_op jit(solution)/shard_map/attn_forward/pallas_call | solution.py:659
  167.9 31.0 %experts.1 = (bf16[1024,768]{1,0:T(8,128)(2,1)S(1)}, bf16[1024,768]{1,0:T(8,128)(2,1)S(1)}, bf16[1024,768]{1,0:T(8,128)(2,1)S(1)}, bf16[1024,2048]{1,0:T(8,128)(...) custom-call(bf16[1024,2048]{1,0:T(8,128)(2,1)} %bitcast.163, bf16[1024,2048]{1,0:T(8,128)(2,1)} %bitcast.166, ...), custom_call_target="tpu_custom_call" | custom-call | flops 19327352832 | bytes 41943040 | tf_op jit(solution)/shard_map/experts/pallas_call | solution.py:727
  198.9 7.5 %convolution_convert_fusion = bf16[2048,768]{1,0:T(8,128)(2,1)} fusion(bf16[1024,2048]{1,0:T(8,128)(2,1)} %bitcast.167, bf16[1024,768]{1,0:T(8,128)(2,1)S(1)} %get-tuple-element.69), kind=kOutput, calls=%fused_computation | convolution fusion | flops 3222798336 | bytes 8912896 | tf_op jit(solution)/shard_map/dot_general | solution.py:29
  206.4 0.6 constant_dynamic-slice_fusion.gates_ref
  207.0 3.7 convolution_convert_fusion.2
  210.8 4.9 %convolution_convert_fusion.1 = bf16[2048,768]{1,0:T(8,128)(2,1)} fusion(bf16[1024,2048]{1,0:T(8,128)(2,1)S(1)} %bitcast.165, bf16[1024,768]{1,0:T(8,128)(2,1)S(1)} %get-tuple-element.59), kind=kOutput, calls=%fused_computation.1 | convolution fusion | flops 3222798336 | bytes 8912896 | tf_op jit(solution)/shard_map/dot_general | solution.py:29
  215.7 56.6 %middle.1 = (f32[32,2048]{1,0:T(8,128)S(1)}, f32[16,2048]{1,0:T(8,128)S(1)}, bf16[2,4,2,2,32,2048]{5,4,3,2,1,0:T(8,128)(2,1)}, bf16[8,64,768]{2,1,0:T(8,128)(2,1)S(1)}, bf16[8,64,768]{2,1,0:T(8,128)(2,1)S(1)}) custom-call(bf16[2,4,2,2,32,2176]{5,4,3,2,1,0:T(8,128)(2,1)} %bitcast.140, f32[32,2048]{1,0:T(8,128)S(1)} %get-tuple-element.56.after_ref, ...), custom_call_target="tpu_custom_call" | custom-call | bytes 167772160 | tf_op jit(solution)/shard_map/middle/pallas_call | solution.py:868
  272.3 0.9 copy-done.3
  273.2 0.9 copy-done.4
  274.1 0.7 copy-done.10
  274.8 3.6 convolution_convert_fusion.4
  278.4 12.5 %attn_backward.1 = (bf16[1024,512]{1,0:T(8,128)(2,1)S(1)}, bf16[1024,2176]{1,0:T(8,128)(2,1)}) custom-call(bf16[1024,2048]{1,0:T(8,128)(2,1)} %bitcast.169, bf16[1024,512]{1,0:T(8,128)(2,1)S(1)} %bitcast.135, f32[1024,128]{1,0:T(8,128)S(1)} %bitcast.134, bf16[2048,768]{1,0:T(8,128)(2,1)S(1)} %bitcast.128, f32[128,128]{1,0:T(8,128)S(1)} %copy-done.15, ...), custom_call_target="tpu_custom_call" | custom-call | flops 3221225472 | bytes 20971520 | tf_op jit(solution)/shard_map/attn_backward/pallas_call | solution.py:798
  291.0 2.4 convolution_convert_fusion.3
  293.4 1.9 pad_maximum_fusion
  295.3 4.7 %copy.89 = bf16[2048,768]{1,0:T(8,128)(2,1)} copy(bf16[2048,768]{0,1:T(8,128)(2,1)} %pad_maximum_fusion) | data formatting | bytes 6291456 | tf_op jit(solution)/shard_map/concatenate | solution.py:1133
  300.0 0.9 copy-done.11
  301.0 94.8 %leave.1 = (bf16[2,2,32,2048]{3,2,1,0:T(8,128)(2,1)S(1)}, bf16[2,2,32,2048]{3,2,1,0:T(8,128)(2,1)S(1)}, f32[16,2048]{1,0:T(8,128)S(1)}, bf16[8,64,768]{2,1,0:T(8...) custom-call(bf16[2,4,2,2,32,2176]{5,4,3,2,1,0:T(8,128)(2,1)} %bitcas, ...), custom_call_target="tpu_custom_call" | custom-call | bytes 209715200 | tf_op jit(solution)/shard_map/leave/pallas_call | solution.py:1001
  395.8 0.9 copy-done.5
  396.7 0.8 copy-done.7
  397.5 0.8 copy-done.9
  398.2 0.7 copy-done.12
  398.9 2.3 reshape_reshape.8
  401.2 2.0 copy.90
  403.2 2.2 reshape.207
  405.4 0.1 reshape.208
  405.6 0.6 slice.118
  406.3 0.6 copy.100
  406.9 0.6 copy.99
  407.5 0.6 slice.111
  408.3 0.9 maximum_bitcast_fusion
  409.2 0.9 maximum_bitcast_fusion.1
  410.3 2.0 copy.96
  412.3 1.0 reshape.221
  413.4 0.3 copy.91
  413.7 1.5 reshape.217
  415.2 0.2 maximum_convert_fusion
  415.4 3.8 copy.95
  419.2 2.2 reshape.223
  421.4 2.6 copy.93
  424.0 0.6 reshape.219
  424.8 1.1 copy.94
  425.9 1.0 pad_maximum_fusion.5
  (75 shorter events, 1.8 us)
Async XLA Ops:
  0.6 6.8 %copy-start.21 = (bf16[64,4,512]{2,1,0:T(4,128)(2,1)S(1)}, bf16[64,4,512]{2,1,0:T(4,128)(2,1)}, u32[]{:S(2)}) copy-start(bf16[64,4,512]{2,1,0:T(4,128)(2,1)} %param.21) | copy-start | bytes 786436
  5.6 2.0 slice-start
  9.0 1.3 copy-start.20
  10.3 1.4 copy-start.17
  14.1 65.9 %copy-start.14 = (f32[128,128]{1,0:T(8,128)S(1)}, f32[128,128]{1,0:T(8,128)}, u32[]{:S(2)}) copy-start(f32[128,128]{1,0:T(8,128)} %constant.36.clone.sin_ref) | copy-start | bytes 196612
  14.1 65.9 %copy-start.15 = (f32[128,128]{1,0:T(8,128)S(1)}, f32[128,128]{1,0:T(8,128)}, u32[]{:S(2)}) copy-start(f32[128,128]{1,0:T(8,128)} %constant.35.clone.cos_ref) | copy-start | bytes 196612
  76.2 2.1 copy-start
  78.3 1.6 copy-start.1
  198.9 8.1 %copy-start.23 = (bf16[2,4,2,2,32,2048]{5,4,3,2,1,0:T(8,128)(2,1)S(1)}, bf16[2,4,2,2,32,2048]{5,4,3,2,1,0:T(8,128)(2,1)}, u32[]{:S(2)}) copy-start(bf16[2,4,2,2,32,2048]{5,4,3,2,1,0:T(8,128)(2,1)} %get-tuple-element.50) | copy-start | bytes 12582916
  272.3 0.9 copy-start.3
  273.2 0.9 copy-start.4
  274.1 0.7 copy-start.10
  274.8 3.6 copy-start.2
  278.4 12.5 %copy-start.22 = (bf16[8,128,2048]{2,1,0:T(8,128)(2,1)S(1)}, bf16[8,128,2048]{2,1,0:T(8,128)(2,1)}, u32[]{:S(2)}) copy-start(bf16[8,128,2048]{2,1,0:T(8,128)(2,1)} %get-tuple-element.70) | copy-start | bytes 12582916
  295.3 4.7 %copy-start.16 = (f32[32,128]{1,0:T(8,128)S(1)}, f32[32,128]{1,0:T(8,128)}, u32[]{:S(2)}) copy-start(f32[32,128]{1,0:T(8,128)} %constant_dynamic-slice_fusion.gates_ref) | copy-start | bytes 49156
  300.0 1.0 copy-start.11
  395.8 0.9 copy-start.5
  396.7 0.8 copy-start.7
  397.4 0.8 copy-start.9
  398.2 0.7 copy-start.12
  398.9 6.5 %copy-start.13 = (f32[16,2048]{1,0:T(8,128)S(1)}, f32[16,2048]{1,0:T(8,128)}, u32[]{:S(2)}) copy-start(f32[16,2048]{1,0:T(8,128)} %copy-done.12) | copy-start | bytes 393220
  398.9 9.3 %copy-start.6 = (bf16[8,64,768]{2,1,0:T(8,128)(2,1)S(1)}, bf16[8,64,768]{2,1,0:T(8,128)(2,1)}, u32[]{:S(2)}) copy-start(bf16[8,64,768]{2,1,0:T(8,128)(2,1)} %copy-done.5) | copy-start | bytes 2359300
  410.2 2.1 copy-start.8
  413.6 1.5 copy-start.18
  413.7 1.5 copy-start.19

commit v7 on v6

--- a/solution.py
+++ b/solution.py
@@ -45,13 +45,14 @@
     return lax.rsqrt(jnp.mean(values * values, axis=-1, keepdims=True) + EPS)
 
 
-def chosen_mask(route):
-    columns = jnp.arange(EXPERTS)[None, :]
-    return (route[:, :1] == columns) | (route[:, 1:] == columns)
-
-
 def lanes(rows):
     return lax.broadcasted_iota(jnp.int32, (rows, LANE), 1)
+
+
+def chosen(routes, first):
+    lane = lanes(routes.shape[0])
+    named = [pick(routes, first + c).astype(jnp.int32) + first for c in range(2)]
+    return (lane == named[0]) | (lane == named[1])
 
 
 def dense_gates(logits, mask):
@@ -213,12 +214,28 @@
             copy.wait()
 
 
+class ColumnSwap(Swap):
+    def start(self):
+        zl, x = lax.axis_index("zl"), lax.axis_index("x")
+        mine = self.dst.at[zl, :, :, pl.ds(pl.multiple_of(x * HEAD, HEAD), HEAD)]
+        self.copies = [
+            pltpu.make_async_copy(self.src.at[zl * 4 + x], mine, self.send.at[0])
+        ]
+        for k, move in enumerate(GROUP_MOVES):
+            if k:
+                to = place(move)
+                block = self.src.at[number(to)]
+                self.copies.append(push(block, mine, self.send.at[k], self.recv.at[k], to))
+        for copy in self.copies:
+            copy.start()
+
+
 def enter(collective, attn_blocks, blocks, rows):
     own, width = rows.shape
 
     def kernel(a_ref, *refs):
-        m_refs, row_ref, a_mid, a_out, m_outs, row_out, sems = (
-            refs[:3], refs[3], refs[4], refs[5], refs[6:9], refs[9], refs[10:],
+        m_refs, row_ref, a_mid, a_out, m_outs, row_out, g_out, sems = (
+            refs[:3], refs[3], refs[4], refs[5], refs[6:9], refs[9], refs[10], refs[11:],
         )
         meet([place(m) for m in TEAM_MOVES[1:] + [Y_MOVES[1], Y_MOVES[3]]] + [sibling()])
         first = Swap(a_ref, a_mid, sems[2:4])
@@ -228,25 +245,32 @@
         first.finish()
         ring = RingY(a_mid, a_out, sems[0:2])
         ring.start()
+        swaps = [Swap(m_refs[i], m_outs[i], sems[4 + 2 * i : 6 + 2 * i]) for i in range(3)]
+        swaps[0].start()
         spread.middle()
-        swaps = [Swap(m_refs[i], m_outs[i], sems[4 + 2 * i : 6 + 2 * i]) for i in range(3)]
-        for swap in swaps:
-            swap.start()
+        swaps[1].start()
+        ring.forward()
+        swaps[0].finish()
+        second = RingY(m_outs[0], g_out, sems[14:16])
+        second.start()
+        swaps[2].start()
         spread.finish()
-        ring.forward()
-        for swap in swaps:
-            swap.finish()
+        swaps[1].finish()
+        second.forward()
+        swaps[2].finish()
         ring.finish()
+        second.finish()
 
     like = jax.ShapeDtypeStruct(attn_blocks.shape, attn_blocks.dtype)
     return pl.pallas_call(
         kernel,
         out_shape=[like, jax.ShapeDtypeStruct((4,) + like.shape, like.dtype)]
         + [jax.ShapeDtypeStruct(b.shape, b.dtype) for b in blocks]
-        + [jax.ShapeDtypeStruct((2, 4, 2, 2, own, width), rows.dtype)],
+        + [jax.ShapeDtypeStruct((2, 4, 2, 2, own, width), rows.dtype)]
+        + [jax.ShapeDtypeStruct((4,) + blocks[0].shape, blocks[0].dtype)],
         in_specs=[ANY] * 5,
-        out_specs=[ANY] * 6,
-        scratch_shapes=RingY.sems + Swap.sems * 4 + TeamSpread.sems,
+        out_specs=[ANY] * 7,
+        scratch_shapes=RingY.sems + Swap.sems * 4 + TeamSpread.sems + RingY.sems,
         name="enter",
         **settings(collective, 120 << 20),
     )(attn_blocks, *blocks, rows)[1:]
@@ -302,7 +326,14 @@
         for k in range(2, 6):
             self.copy(k).wait_recv()
         total = self.part[self.y].astype(F32) + self.sums[0].astype(F32) + self.sums[1].astype(F32)
-        out[...] = total.astype(BF).reshape(out.shape)
+        total = total.astype(BF)
+        if len(out.shape) == 3:
+            out[...] = total.reshape(out.shape)
+        else:
+            targets, count, rows, cols = out.shape
+            for t in range(targets):
+                for n in range(count):
+                    out[t, n] = total[t * rows : (t + 1) * rows, n * cols : (n + 1) * cols]
         for k in range(6):
             self.copy(k).wait_send()
 
@@ -415,6 +446,10 @@
         pltpu.make_async_copy(ref, ref, sem).wait()
 
     def total(self, total_ref):
+        self.total1(total_ref)
+        self.total2(total_ref)
+
+    def total1(self, total_ref):
         half, c = self.half, self.c
         for k in range(3):
             self.got(self.got_x.at[k], self.recv1.at[k])
@@ -440,6 +475,9 @@
                 self.late_x(k).start()
             else:
                 total_ref[half:] = rows
+
+    def total2(self, total_ref):
+        half = self.half
         for k in range(3):
             self.got(self.late.at[k], self.recv2.at[k])
             total_ref[:half] += self.late[k].astype(F32)
@@ -566,10 +604,16 @@
     scale = HEAD ** (-0.5)
 
     def kernel(
-        hid, w_ref, gain_ref, router_ref, cos_ref, sin_ref, gain_m_ref, own_ref, cot_ref, b0, b1, b2,
-        normed_out, qkv_out, gated_out, gates_out, after_out, spread_out, cot_out, w0, w1, w2,
-        part, total, row, *rest,
+        hid_ref, weight_ref, gain_ref, router_ref, cos_ref, sin_ref, gain_m_ref, own_ref, cot_ref, b0, b1,
+        normed_out, qkv_out, gated_out, gates_out, after_out, spread_out, cot_out, w0, w1,
+        hid, w_ref, load, part, total, row, *rest,
     ):
+        fetches = [
+            pltpu.make_async_copy(hid_ref, hid, load.at[0]),
+            pltpu.make_async_copy(weight_ref, w_ref, load.at[1]),
+        ]
+        for fetch in fetches:
+            fetch.start()
         meet([place(m) for m in TEAM_MOVES[1:] + [Y_MOVES[1], Y_MOVES[3]]] + [sibling()])
         count = TeamSum.count
         team = TeamSum(part, rest[:count])
@@ -577,10 +621,12 @@
         cot.start()
         rings = [
             RingY(b, w, rest[count + 8 + 2 * k : count + 10 + 2 * k])
-            for k, (b, w) in enumerate(((b0, w0), (b1, w1), (b2, w2)))
+            for k, (b, w) in enumerate(((b0, w0), (b1, w1)))
         ]
         for ring in rings:
             ring.start()
+        for fetch in fetches:
+            fetch.wait()
         first = 2 * team.zl
         causal = causal_mask(2, seq)
 
@@ -592,8 +638,8 @@
             normed = normed_out[pl.ds(pair * 2, 2)].reshape(2 * seq, width)
             logits = mm(normed, router_ref[...])
             proj = mm(normed, w_ref[:, : 4 * HEAD])
-            allowed = hid[pl.ds(pair * 2, 2), :, width:].reshape(2 * seq, LANE).astype(F32) > 0.5
-            gates = dense_gates(logits, allowed & (lanes(2 * seq) < EXPERTS))
+            routes = hid[pl.ds(pair * 2, 2), :, width:].reshape(2 * seq, LANE).astype(F32)
+            gates = dense_gates(logits, chosen(routes, 0))
             gates_out[pl.ds(pair * 2, 2)] = gates.reshape(2, seq, LANE)
             gated = []
             for j in range(2):
@@ -640,6 +686,7 @@
 
         lax.fori_loop(0, 4, step, 0)
         team.last()
+        rings[0].forward()
         cot.finish()
         team.total(total)
         after = total[...] + own_ref[...].astype(F32)
@@ -647,11 +694,9 @@
         row[...] = (after * rms_scale(after) * gain_m_ref[...]).astype(BF)
         spread = TeamSpread(row, spread_out, rest[count + 4 : count + 8])
         spread.start()
-        rings[0].forward()
+        rings[1].forward()
         spread.middle()
-        rings[1].forward()
         spread.finish()
-        rings[2].forward()
         team.close()
         for ring in rings:
             ring.finish()
@@ -668,34 +713,36 @@
             jax.ShapeDtypeStruct((2, 4, 2, 2, own, width), BF),
         ]
         + [jax.ShapeDtypeStruct((4,) + b.shape, b.dtype) for b in blocks],
-        in_specs=[VMEM] * 8 + [ANY] * 4,
-        out_specs=[VMEM] * 5 + [ANY] * 5,
+        in_specs=[ANY] * 2 + [VMEM] * 6 + [ANY] * 3,
+        out_specs=[VMEM] * 5 + [ANY] * 4,
         scratch_shapes=[
+            pltpu.VMEM(hidden.shape, BF),
+            pltpu.VMEM(weights.shape, BF),
+            pltpu.SemaphoreType.DMA((2,)),
             pltpu.VMEM((2, 4, 2, 2, own, width), BF),
             pltpu.VMEM((own, width), F32),
             pltpu.VMEM((own, width), BF),
         ]
         + TeamSum.scratch(own, width)
         + TeamSpread.sems * 2
-        + RingY.sems * 3,
+        + RingY.sems * 2,
         name="attn_forward",
         **settings(collective, 200 << 20, 48),
     )(hidden, weights, gain, routers, cosines, sines, mlp_gain, hidden_own, cot_own, *blocks)
 
 
-def experts(normed, cotangent, masks, routers, weights, extra):
+def experts(normed, cotangent, entered, routers, weights, extra):
     rows, width = normed.shape
     part = weights[0].shape[1]
     tile = rows // 4
 
-    def kernel(x_ref, cot_ref, mask, router_ref, wg, wu, wd, h_out, dg_out, du_out, branch_out, back_out, gates_out):
+    def kernel(x_ref, cot_ref, route_ref, router_ref, wg, wu, wd, h_out, dg_out, du_out, branch_out, back_out, gates_out):
         lane = EXPERTS + lax.axis_index("x")
         skip = lax.axis_index("zl") * extra
         x = x_ref[...]
         logits = mm(x, router_ref[...])
         index = lanes(tile)
-        allowed = (mask[...].astype(F32) > 0.5) & (index >= EXPERTS) & (index < 2 * EXPERTS)
-        gates = dense_gates(logits, allowed)
+        gates = dense_gates(logits, chosen(route_ref[...].astype(F32), EXPERTS))
         gates_out[...] = gates
         valid = (lax.broadcasted_iota(jnp.int32, (1, part), 1) >= skip).astype(F32)
         gate = pick(gates, lane) * valid
@@ -738,7 +785,7 @@
             flops=12 * rows * width * part, bytes_accessed=40 << 20, transcendentals=rows * part
         ),
         name="experts",
-    )(normed, cotangent, masks, routers, *weights)
+    )(normed, cotangent, entered, routers, *weights)
 
 
 def attn_backward(grad_mid, qkv, gates, weights, cosines, sines):
@@ -846,7 +893,9 @@
         rings[0].middle()
         after = after_ref[...]
         normed = (after * rms_scale(after) * gain_ref[...]).astype(BF)
-        team.total(total)
+        team.total1(total)
+        rings[1].middle()
+        team.total2(total)
         inner, gain_grad, router_grad = back_through_norm(
             total[...], after, gain_ref[...], gates_ref[...], normed, router_ref[...]
         )
@@ -858,7 +907,6 @@
         small_out[8:] = router_grad
         spread = TeamSpread(row, spread_out, rest[count : count + 4])
         spread.start()
-        rings[1].middle()
         spread.middle()
         spread.finish()
         rings[0].finish(s0)
@@ -891,20 +939,31 @@
     ])
 
 
-def leave(collective, back, branch, after, grad_mid, inputs, gain, gates_own, routers, small, summed, grads):
+def in_order(values):
+    block = values.shape[1] // 8
+    order = [(b % 4) * 2 + b // 4 for b in range(8)]
+    return jnp.concatenate([values[:, k * block : (k + 1) * block] for k in order], axis=1)
+
+
+def leave(
+    collective, back, branch, after, grad_mid, inputs, gain, gates_own, routers, small, summed, grads, attn_grads
+):
     own, width = after.shape
-    rows, cols = grads[0].shape[0] // 4, grads[0].shape[1]
+    rows, cols = grads.shape[0] // 4, grads.shape[1]
+    shard = rows // 8
+    cuts = [a.shape[1] for a in attn_grads]
     stages = [X_MOVES, Y_MOVES, Z_MOVES]
 
     def kernel(
         back_ref, branch_ref, after_ref, mid_ref, in_ref, gain_ref, gates_ref, router_ref, small_ref,
-        y0, y1, g2, g3, out_all, grad_all, small_out, s0, s1, s2, s3, y2, y3,
-        part_a, part_b, load, total_a, total_b, row_a, row_b, got, other, rest_rows, csem, send, recv, ssend, srecv, *rest,
+        y0, y1, g2, a0, a1, out_all, grad_all, small_out, s0, s1, s2, s3,
+        y2, y3, g3, part_a, part_b, load, total_a, total_b, row_a, row_b,
+        acc, got, other, rest_rows, csem, send, recv, ssend, srecv, *rest,
     ):
-        fetches = [
-            pltpu.make_async_copy(back_ref, part_a, load.at[0]),
-            pltpu.make_async_copy(branch_ref, part_b, load.at[1]),
-        ]
+        loads = [
+            (a0, g3.at[:, :, : cuts[0]]), (a1, g3.at[:, :, cuts[0] :]), (back_ref, part_a), (branch_ref, part_b)
+        ]
+        fetches = [pltpu.make_async_copy(a, b, load.at[k]) for k, (a, b) in enumerate(loads)]
         for fetch in fetches:
             fetch.start()
         meet([place(m) for m in TEAM_MOVES[1:] + Y_MOVES[1:]] + [sibling()])
@@ -913,32 +972,37 @@
         count = 2 * count
         swaps_back = [
             Swap(y, s, rest[count + 2 * k : count + 2 * k + 2])
-            for k, (y, s) in enumerate(((y0, s0), (y1, s1), (y2, s2), (y3, s3)))
-        ]
+            for k, (y, s) in enumerate(((y0, s0), (y1, s1), (y2, s2)))
+        ]
+        last_swap = ColumnSwap(y3, s3, rest[count + 6 : count + 8])
         count += 8
         rings = [
             RingSum(g, rest[count + RingSum.count * k : count + RingSum.count * (k + 1)])
             for k, g in enumerate((g2, g3))
         ]
-        for ring in rings:
-            ring.start()
+        rings[0].start()
         fetches[0].wait()
+        fetches[1].wait()
+        rings[1].start()
+        fetches[2].wait()
         team_a.run()
-        fetches[1].wait()
+        fetches[3].wait()
         team_b.run()
         rings[0].middle()
         swaps_back[0].start()
         swaps_back[1].start()
         inputs = in_ref[...].astype(F32)
         normed = (inputs * rms_scale(inputs) * gain_ref[...]).astype(BF)
-        team_a.total(total_a)
+        team_a.total1(total_a)
+        rings[1].middle()
+        team_a.total2(total_a)
         inner, gain_grad, router_grad = back_through_norm(
             total_a[...], inputs, gain_ref[...], gates_ref[...], normed, router_ref[...]
         )
-        row_a[...] = (mid_ref[...] + inner).astype(BF)
-        small_out[...] = small_ref[...]
-        small_out[1:2] = gain_grad
-        small_out[8:] += router_grad
+        row_a[...] = in_order((mid_ref[...] + inner).astype(BF))
+        acc[...] = small_ref[...]
+        acc[1:2] = gain_grad
+        acc[8:] += router_grad
         zh, c = lax.axis_index("zh"), lax.axis_index("c")
 
         def spread(i, src, dst):
@@ -964,56 +1028,63 @@
         first = spread(0, row_a, grad_all)
         half = pl.ds(pl.multiple_of(c * 8, 8), 8)
         rest_half = pl.ds(pl.multiple_of((1 - c) * 8, 8), 8)
-        over = push(small_out.at[rest_half], other, csem.at[0], csem.at[1], sibling())
+        over = push(acc.at[rest_half], other, csem.at[0], csem.at[1], sibling())
         over.start()
         team_b.total(total_b)
-        row_b[...] = (after_ref[...] + total_b[...]).astype(BF)
+        row_b[...] = in_order((after_ref[...] + total_b[...]).astype(BF))
         second = spread(1, row_b, out_all)
-        rings[1].middle()
         over.wait()
-        small_out[half] = small_out[half] + other[...]
-        rings[0].finish(y2)
-        swaps_back[2].start()
+        acc[half] = acc[half] + other[...]
         for s, stage in enumerate(stages):
             swaps = [
-                push(small_out.at[half], got.at[s, k - 1], ssend.at[s, k], srecv.at[s, k], place(stage[k]))
+                push(acc.at[half], got.at[s, k - 1], ssend.at[s, k], srecv.at[s, k], place(stage[k]))
                 for k in range(1, 4)
             ]
             for swap in swaps:
                 swap.start()
+            if s == 0:
+                rings[0].finish(y2)
+                swaps_back[2].start()
+            if s == 1:
+                rings[1].finish(y3)
+                last_swap.start()
             for swap in swaps:
                 swap.wait()
-            small_out[half] = small_out[half] + got[s, 0] + got[s, 1] + got[s, 2]
-            if s == 0:
-                rings[1].finish(y3)
-                swaps_back[3].start()
-        back_over = push(small_out.at[half], rest_rows, csem.at[2], csem.at[3], sibling())
+            acc[half] = acc[half] + got[s, 0] + got[s, 1] + got[s, 2]
+        back_over = push(acc.at[half], rest_rows, csem.at[2], csem.at[3], sibling())
         back_over.start()
+        small_out[half] = in_order(acc[half])
         settle(first)
         settle(second)
         back_over.wait()
-        small_out[rest_half] = rest_rows[...]
-        for swap in swaps_back:
+        small_out[rest_half] = in_order(rest_rows[...])
+        for swap in swaps_back + [last_swap]:
             swap.finish()
         team_a.close()
         team_b.close()
 
+    block = jax.ShapeDtypeStruct((8, shard, cols), BF)
+    count = cols // HEAD
     return pl.pallas_call(
         kernel,
         out_shape=[jax.ShapeDtypeStruct((2, 2, own, width), BF)] * 2
         + [jax.ShapeDtypeStruct((16, width), F32)]
-        + [jax.ShapeDtypeStruct((8, rows // 8, cols), BF)] * 4,
-        in_specs=[ANY, ANY] + [VMEM] * 7 + [ANY] * 2 + [VMEM] * 2,
+        + [block] * 3
+        + [jax.ShapeDtypeStruct((2, count, shard, 4 * HEAD), BF)],
+        in_specs=[ANY, ANY] + [VMEM] * 7 + [ANY] * 2 + [VMEM] + [ANY] * 2,
         out_specs=[ANY, ANY, VMEM] + [ANY] * 4,
-        scratch_shapes=[pltpu.VMEM((8, rows // 8, cols), BF)] * 2
-        + [
+        scratch_shapes=[
+            pltpu.VMEM((8, shard, cols), BF),
+            pltpu.VMEM((8, count, shard, HEAD), BF),
+            pltpu.VMEM((4, rows, cols), BF),
             pltpu.VMEM((2, 4, 2, 2, own, width + LANE), BF),
             pltpu.VMEM((2, 4, 2, 2, own, width), BF),
-            pltpu.SemaphoreType.DMA((2,)),
+            pltpu.SemaphoreType.DMA((4,)),
             pltpu.VMEM((own, width + LANE), F32),
             pltpu.VMEM((own, width), F32),
             pltpu.VMEM((own, width), BF),
             pltpu.VMEM((own, width), BF),
+            pltpu.VMEM((16, width), F32),
             pltpu.VMEM((3, 3, 8, width), F32),
             pltpu.VMEM((8, width), F32),
             pltpu.VMEM((8, width), F32),
@@ -1026,24 +1097,18 @@
         + Swap.sems * 4
         + RingSum.scratch(rows, cols) * 2,
         name="leave",
-        **settings(collective, 200 << 20, 48),
+        **settings(collective, 200 << 20, 56),
     )(
         back.reshape(2, 4, 2, 2, own, width + LANE),
         branch.reshape(2, 4, 2, 2, own, width),
         after, grad_mid, inputs, gain, gates_own, routers, small, *summed,
-        *[g.reshape(4, rows, cols) for g in grads],
+        grads.reshape(4, rows, cols), *[a.reshape(4, rows, a.shape[1]) for a in attn_grads],
     )
 
 
 def reorder(array, axis):
     shape = array.shape
     split = shape[:axis] + (2, 4, shape[axis] // 8) + shape[axis + 1 :]
-    return jnp.swapaxes(array.reshape(split), axis, axis + 1).reshape(shape)
-
-
-def restore(array, axis):
-    shape = array.shape
-    split = shape[:axis] + (4, 2, shape[axis] // 8) + shape[axis + 1 :]
     return jnp.swapaxes(array.reshape(split), axis, axis + 1).reshape(shape)
 
 
@@ -1089,8 +1154,6 @@
         by_target(w) for w in (gate_up_weight[:, :, 0], gate_up_weight[:, :, 1], down_weight)
     ]
 
-    masks = jnp.concatenate([chosen_mask(attn_route), chosen_mask(mlp_route)], axis=1)
-    masks = jnp.pad(masks.astype(BF), ((0, 0), (0, LANE - 2 * EXPERTS)))
     attn_gain, mlp_gain = reorder(attn_gain, 0)[None], reorder(mlp_gain, 0)[None]
     routers = reorder(jnp.concatenate([attn_router, mlp_router], axis=1), 0)
     routers = jnp.pad(routers, ((0, 0), (0, LANE - 2 * EXPERTS)))
@@ -1105,15 +1168,18 @@
     def mine(array):
         return lax.dynamic_slice_in_dim(array, start, own, axis=0)
 
-    entering = jnp.concatenate([hidden_own, quarter_of(masks)], axis=1)
-    attn_w, *mlp_rows, group_in = enter(1, attn_blocks, mlp_blocks, entering)
+    no_routes = jnp.zeros((own, 2), jnp.int32)
+    routes = [quarter_of(attn_route), no_routes, quarter_of(mlp_route)]
+    routes = jnp.pad(jnp.concatenate(routes, axis=1), ((0, 0), (0, LANE - 6)))
+    entering = jnp.concatenate([hidden_own, routes.astype(BF)], axis=1)
+    attn_w, _, *mlp_rows, group_in, gate_w = enter(1, attn_blocks, mlp_blocks, entering)
     attn_w = attn_w.reshape(width, 6 * HEAD)
     group_in = group_in.reshape(8, seq, width + LANE)
 
     normed_a, qkv, gated_att, gates_a, after, normed_m, group_cot, *mlp_w = attn_forward(
         2, group_in, attn_w, attn_gain, routers, cosines, sines, mlp_gain, hidden_own, cot_own, mlp_rows
     )
-    mlp_w = [w.reshape(width, part) for w in mlp_w]
+    mlp_w = [w.reshape(width, part) for w in [gate_w] + mlp_w]
     group_cot = group_cot.reshape(group, width)
     normed_a = normed_a.reshape(group, width)
     normed_m = normed_m.reshape(group, width)
@@ -1130,27 +1196,22 @@
     grad_proj, back_a = attn_backward(
         grad_mid, qkv.reshape(group, 4 * HEAD), gates_a, attn_w, cosines, sines
     )
-    attn_grads = jnp.concatenate(
-        [
-            mm_tn(normed_a, grad_proj).astype(BF),
-            mm_tn(grad_mid, gated_att.reshape(group, 2 * HEAD)).astype(BF),
-        ],
-        axis=1,
-    )
+    attn_grads = [
+        mm_tn(normed_a, grad_proj).astype(BF),
+        mm_tn(grad_mid, gated_att.reshape(group, 2 * HEAD)).astype(BF),
+    ]
     out_hidden, grad_in, small, *mlp_grads, attn_grads = leave(
         4, back_a, branch_m, after, grad_mid_own, hidden_own, attn_gain, mine(gates_a), routers, small_m,
-        summed, [mm_tn(group_cot, h).astype(BF), attn_grads],
+        summed, mm_tn(group_cot, h).astype(BF), attn_grads,
     )
-    out_hidden = restore(out_hidden.reshape(seq, width), 1)
-    grad_in = restore(grad_in.reshape(seq, width), 1).astype(F32)
-    small = restore(small, 1)
-
-    attn_grads = attn_grads.astype(F32).reshape(2, 4, rows, 6, HEAD).transpose(2, 0, 3, 1, 4)
-    attn_grads = attn_grads.reshape(rows, 2, 6, 4 * HEAD)
-    query_grad = attn_grads[:, :, :2].reshape(rows, EXPERTS, 4 * HEAD)
-    kv_grad = attn_grads[:, 0, 2:4] + attn_grads[:, 1, 2:4]
-    qkv_grad = jnp.concatenate([query_grad, kv_grad], axis=1)
-    out_grad = attn_grads[:, :, 4:].reshape(rows, EXPERTS, 4 * HEAD)
+    out_hidden = out_hidden.reshape(seq, width)
+    grad_in = grad_in.reshape(seq, width).astype(F32)
+
+    attn_grads = attn_grads.astype(F32)
+    query_grad = attn_grads[:, :2].reshape(EXPERTS, rows, 4 * HEAD)
+    kv_grad = attn_grads[0, 2:4] + attn_grads[1, 2:4]
+    qkv_grad = jnp.concatenate([query_grad, kv_grad], axis=0).transpose(1, 0, 2)
+    out_grad = attn_grads[:, 4:].reshape(EXPERTS, rows, 4 * HEAD).transpose(1, 0, 2)
 
     def placed_back(grad):
         grad = grad.reshape(2, EXPERTS, rows, part)

time: 435 us -> 410 us (0.943)
  local copies, waits for them, and re-layouts: 51.1 us -> 33.9 us
  Pallas kernels: 345 us -> 337 us
    pallas_call x1, Pallas kernels: 87.9 us -> 65.5 us  [attn_forward(): pl.pallas_call(kernel, out_shape=[jax.ShapeDtypeStruct((8, seq, width), B...]
    pallas_call x1, Pallas kernels: 62 us -> 72.1 us  [enter(): pl.pallas_call(kernel, out_shape=[like, jax.ShapeDtypeStruct((4,) + like....]
    reshape x6 -> x1, local copies, waits for them, and re-layouts: 7.76 us -> 1.13 us  [local(): attn_grads[:, 4:].reshape(EXPERTS, rows, 4 * HEAD).transpose(1, 0, 2)]
    concatenate x2, local copies, waits for them, and re-layouts: 4.83 us -> 0.18 us  [local(): routes = jnp.pad(jnp.concatenate(routes, axis=1), ((0, 0), (0, LANE - 6)))]
    unnamed x54 -> x53, local copies, waits for them, and re-layouts: 18.9 us -> 16.8 us
where the time goes in v7:
time: 410 us; the launch traced here: 403 us
  Pallas kernels  337 us (82%)
  local copies, waits for them, and re-layouts  33.9 us (8%)
  matrix products  24.7 us (6%)
  other arithmetic  5.92 us (1%)
    pallas_call x1, Pallas kernels, leave(): pl.pallas_call(kernel, out_shape=[jax.ShapeDtypeStruct((2, 2, own, width)...  96.4 us
    pallas_call x1, Pallas kernels, enter(): pl.pallas_call(kernel, out_shape=[like, jax.ShapeDtypeStruct((4,) + like....  72.1 us
    pallas_call x1, Pallas kernels, attn_forward(): pl.pallas_call(kernel, out_shape=[jax.ShapeDtypeStruct((8, seq, width), B...  65.5 us
    pallas_call x1, Pallas kernels, middle(): pl.pallas_call(kernel, out_shape=[jax.ShapeDtypeStruct((own, width), F32)...  59 us
    pallas_call x1, Pallas kernels, experts(): pl.pallas_call(kernel, grid=(4,), out_shape=[jax.ShapeDtypeStruct((rows,...  31 us
    dot_general x5, matrix products, dot(): return lax.dot_general(a, b, (dims, ((), ())), preferred_element_type=F32)  24.7 us
    unnamed x53, local copies, waits for them, and re-layouts  16.8 us
    pallas_call x1, Pallas kernels, attn_backward(): pl.pallas_call(kernel, grid=(4,), out_shape=[jax.ShapeDtypeStruct((rows,...  12.6 us

profile of v7, /device:TPU:0, one launch (start us, length us, event | category | flops | bytes accessed | tf_op | source)
XLA Modules:
  0.0 402.7 jit_solution(10039948687152751053)
XLA Ops:
  0.7 0.1 pad.26.clone
  0.8 0.8 fusion.3
  1.5 0.1 pad_maximum_fusion.5
  1.6 0.1 copy.59
  1.7 0.7 reshape.165
  2.5 0.7 reshape.168
  3.2 0.8 pad_maximum_fusion.4
  4.0 0.9 slice.76
  4.9 0.1 copy.53
  5.1 0.1 broadcast_in_dim.4
  5.2 1.0 constant_dynamic-slice_fusion.2
  6.2 0.1 reshape.169
  6.3 0.1 copy.63
  6.4 0.1 reshape.170.cot_ref
  6.5 0.1 reshape.161
  6.6 0.1 copy.58
  6.7 0.1 reshape.162.own_ref.in_ref
  6.8 0.1 reshape.156
  7.0 0.5 copy_bitcast_fusion.3
  7.5 0.9 pad_maximum_fusion
  8.4 0.9 reshape.157.a_ref
  9.3 0.3 copy.61
  9.6 0.1 pad.10.router_ref
  9.8 0.3 slice_bitcast_fusion.1
  10.0 0.6 pad_maximum_fusion.3
  10.6 0.1 copy.57
  10.7 0.6 copy-done.14
  11.3 2.0 fusion.5
  13.3 0.2 copy_bitcast_fusion
  13.7 0.1 pad_maximum_fusion.1
  13.8 72.1 %enter.1 = (bf16[8,64,768]{2,1,0:T(8,128)(2,1)}, bf16[4,8,64,768]{3,2,1,0:T(8,128)(2,1)S(1)}, bf16[8,64,768]{2,1,0:T(8,128)(2,1)}, bf16[8,64,768]{2,1,0:T(8,128)...) custom-call(bf16[8,64,768]{2,1,0:T(8,128)(2,1)S(1)} %reshape.157.a_r, ...), custom_call_target="tpu_custom_call" | custom-call | bytes 125829120 | tf_op jit(solution)/shard_map/enter/pallas_call | solution.py:265
  85.9 2.1 copy-done.1
  88.0 1.6 copy-done.2
  89.6 1.7 copy-done.13
  91.4 65.5 %attn_forward.1 = (bf16[8,128,2048]{2,1,0:T(8,128)(2,1)}, bf16[8,128,512]{2,1,0:T(8,128)(2,1)S(1)}, bf16[8,128,256]{2,1,0:T(8,128)(2,1)S(1)}, f32[8,128,128]{2,1...) custom-call(bf16[8,128,2176]{2,1,0:T(8,128)(2,1)} %bitcast.110, ...), custom_call_target="tpu_custom_call" | custom-call | bytes 209715200 | tf_op jit(solution)/shard_map/attn_forward/pallas_call | solution.py:704
  156.9 31.0 %experts.1 = (bf16[1024,768]{1,0:T(8,128)(2,1)S(1)}, bf16[1024,768]{1,0:T(8,128)(2,1)S(1)}, bf16[1024,768]{1,0:T(8,128)(2,1)S(1)}, bf16[1024,2048]{1,0:T(8,128)(...) custom-call(bf16[1024,2048]{1,0:T(8,128)(2,1)} %bitcast.148, bf16[1024,2048]{1,0:T(8,128)(2,1)} %bitcast.151, ...), custom_call_target="tpu_custom_call" | custom-call | flops 19327352832 | bytes 41943040 | tf_op jit(solution)/shard_map/experts/pallas_call | solution.py:774
  188.0 7.5 %convolution_convert_fusion = bf16[2048,768]{1,0:T(8,128)(2,1)} fusion(bf16[1024,2048]{1,0:T(8,128)(2,1)} %bitcast.152, bf16[1024,768]{1,0:T(8,128)(2,1)S(1)} %get-tuple-element.67), kind=kOutput, calls=%fused_computation | convolution fusion | flops 3222798336 | bytes 8912896 | tf_op jit(solution)/shard_map/dot_general | solution.py:29
  195.5 0.6 constant_dynamic-slice_fusion.gates_ref
  196.1 3.7 convolution_convert_fusion.2
  199.9 5.0 %convolution_convert_fusion.1 = bf16[2048,768]{1,0:T(8,128)(2,1)} fusion(bf16[1024,2048]{1,0:T(8,128)(2,1)S(1)} %bitcast.150, bf16[1024,768]{1,0:T(8,128)(2,1)S(1)} %get-tuple-element.57), kind=kOutput, calls=%fused_computation.1 | convolution fusion | flops 3222798336 | bytes 8912896 | tf_op jit(solution)/shard_map/dot_general | solution.py:29
  204.9 59.0 %middle.1 = (f32[32,2048]{1,0:T(8,128)S(1)}, f32[16,2048]{1,0:T(8,128)S(1)}, bf16[2,4,2,2,32,2048]{5,4,3,2,1,0:T(8,128)(2,1)}, bf16[8,64,768]{2,1,0:T(8,128)(2,1)S(1)}, bf16[8,64,768]{2,1,0:T(8,128)(2,1)S(1)}) custom-call(bf16[2,4,2,2,32,2176]{5,4,3,2,1,0:T(8,128)(2,1)} %bitcast.124, f32[32,2048]{1,0:T(8,128)S(1)} %get-tuple-element.54.after_ref, ...), custom_call_target="tpu_custom_call" | custom-call | bytes 167772160 | tf_op jit(solution)/shard_map/middle/pallas_call | solution.py:916
  263.9 0.9 copy-done.6
  264.7 0.9 copy-done.7
  265.6 0.7 copy-done.8
  266.3 0.6 copy-done.9
  266.9 4.7 %convolution_convert_fusion.4 = bf16[2048,256]{1,0:T(8,128)(2,1)} fusion(bf16[1024,2048]{1,0:T(8,128)(2,1)} %bitcast.153, bf16[1024,256]{1,0:T(8,128)(2,1)S(1)} %bitcast.122), kind=kOutput, calls=%fused_computation.4 | convolution fusion | flops 1074266112 | bytes 5767168 | tf_op jit(solution)/shard_map/dot_general | solution.py:29
  271.6 12.6 %attn_backward.1 = (bf16[1024,512]{1,0:T(8,128)(2,1)S(1)}, bf16[1024,2176]{1,0:T(8,128)(2,1)}) custom-call(bf16[1024,2048]{1,0:T(8,128)(2,1)} %bitcast.154, bf16[1024,512]{1,0:T(8,128)(2,1)S(1)} %bitcast.121, f32[1024,128]{1,0:T(8,128)S(1)} %bitcast.119, bf16[2048,768]{1,0:T(8,128)(2,1)S(1)} %bitcast.113, f32[128,128]{1,0:T(8,128)S(1)} %copy-done.12, ...), custom_call_target="tpu_custom_call" | custom-call | flops 3221225472 | bytes 20971520 | tf_op jit(solution)/shard_map/attn_backward/pallas_call | solution.py:845
  284.2 3.8 convolution_convert_fusion.3
  288.0 96.4 %leave.1 = (bf16[2,2,32,2048]{3,2,1,0:T(8,128)(2,1)}, bf16[2,2,32,2048]{3,2,1,0:T(8,128)(2,1)}, f32[16,2048]{1,0:T(8,128)}, bf16[8,64,768]{2,1,0:T(8,128)(2,1)},...) custom-call(bf16[2,4,2,2,32,2176]{5,4,3,2,1,0:T(8,128)(2,1)} %bitcast.123, ...), custom_call_target="tpu_custom_call" | custom-call | bytes 209715200 | tf_op jit(solution)/shard_map/leave/pallas_call | solution.py:1068
  384.4 1.6 fusion.7
  386.0 1.5 slice_bitcast_fusion.9
  387.5 1.1 slice_bitcast_fusion.6
  388.6 1.0 slice_bitcast_fusion.7
  389.6 1.0 slice_bitcast_fusion.8
  390.8 0.9 copy-done.17
  391.8 0.1 convert_bitcast_fusion
  391.9 2.0 copy.66
  394.0 1.1 bitcast_convert_fusion
  395.2 1.1 copy.74
  396.3 0.2 convert_element_type.43
  396.5 1.0 maximum_bitcast_fusion
  397.5 0.2 maximum_convert_fusion
  397.7 3.8 copy.65
  401.5 0.8 copy.76
  (62 shorter events, 0.8 us)
Async XLA Ops:
  0.6 6.2 %copy-start.22 = (bf16[64,4,512]{2,1,0:T(4,128)(2,1)S(1)}, bf16[64,4,512]{2,1,0:T(4,128)(2,1)}, u32[]{:S(2)}) copy-start(bf16[64,4,512]{2,1,0:T(4,128)(2,1)} %param.21) | copy-start | bytes 786436
  2.4 88.9 %copy-start.10 = (f32[1,2048]{1,0:T(1,128)}, f32[1,2048]{1,0:T(1,128)S(1)}, u32[]{:S(2)}) copy-start(f32[1,2048]{1,0:T(1,128)S(1)} %broadcast_in_dim_reshape.6.gain_ref) | copy-start | bytes 24580
  4.9 2.0 slice-start
  6.8 84.6 %copy-start.4 = (bf16[32,2048]{1,0:T(8,128)(2,1)}, bf16[32,2048]{1,0:T(8,128)(2,1)S(1)}, u32[]{:S(2)}) copy-start(bf16[32,2048]{1,0:T(8,128)(2,1)S(1)} %reshape.162.own_ref.in_ref) | copy-start | bytes 393220
  8.4 1.3 copy-start.16
  9.7 195.1 %copy-start = (bf16[2048,128]{1,0:T(8,128)(2,1)}, bf16[2048,128]{1,0:T(8,128)(2,1)S(1)}, u32[]{:S(2)}) copy-start(bf16[2048,128]{1,0:T(8,128)(2,1)S(1)} %pad.10.router_ref) | copy-start | bytes 1572868
  9.8 1.6 copy-start.14
  13.7 77.6 %copy-start.11 = (f32[128,128]{1,0:T(8,128)S(1)}, f32[128,128]{1,0:T(8,128)}, u32[]{:S(2)}) copy-start(f32[128,128]{1,0:T(8,128)} %constant.36.clone.sin_ref) | copy-start | bytes 196612
  13.7 77.6 %copy-start.12 = (f32[128,128]{1,0:T(8,128)S(1)}, f32[128,128]{1,0:T(8,128)}, u32[]{:S(2)}) copy-start(f32[128,128]{1,0:T(8,128)} %constant.35.clone.cos_ref) | copy-start | bytes 196612
  85.9 2.1 copy-start.1
  88.0 1.6 copy-start.2
  89.6 1.7 copy-start.13
  156.9 47.9 %copy-start.5 = (f32[32,2048]{1,0:T(8,128)}, f32[32,2048]{1,0:T(8,128)S(1)}, u32[]{:S(2)}) copy-start(f32[32,2048]{1,0:T(8,128)S(1)} %get-tuple-element.54.after_ref) | copy-start | bytes 786436
  188.0 8.1 %copy-start.24 = (bf16[2,4,2,2,32,2048]{5,4,3,2,1,0:T(8,128)(2,1)S(1)}, bf16[2,4,2,2,32,2048]{5,4,3,2,1,0:T(8,128)(2,1)}, u32[]{:S(2)}) copy-start(bf16[2,4,2,2,32,2048]{5,4,3,2,1,0:T(8,128)(2,1)} %get-tuple-element.48) | copy-start | bytes 12582916
  263.8 0.9 copy-start.6
  264.7 0.9 copy-start.7
  265.6 0.7 copy-start.8
  266.3 0.6 copy-start.9
  266.9 4.7 %copy-start.3 = (bf16[4,8,64,768]{3,2,1,0:T(8,128)(2,1)S(1)}, bf16[4,8,64,768]{3,2,1,0:T(8,128)(2,1)}, u32[]{:S(2)}) copy-start(bf16[4,8,64,768]{3,2,1,0:T(8,128)(2,1)} %copy-done.2) | copy-start | bytes 9437188
  271.6 12.6 %copy-start.23 = (bf16[8,128,2048]{2,1,0:T(8,128)(2,1)S(1)}, bf16[8,128,2048]{2,1,0:T(8,128)(2,1)}, u32[]{:S(2)}) copy-start(bf16[8,128,2048]{2,1,0:T(8,128)(2,1)} %get-tuple-element.68) | copy-start | bytes 12582916
  384.4 6.2 %copy-start.19 = (bf16[8,64,768]{2,1,0:T(8,128)(2,1)S(1)}, bf16[8,64,768]{2,1,0:T(8,128)(2,1)}, u32[]{:S(2)}) copy-start(bf16[8,64,768]{2,1,0:T(8,128)(2,1)} %get-tuple-element.75) | copy-start | bytes 2359300
  387.5 3.2 copy-start.18
  390.6 1.1 copy-start.17
  391.8 2.2 copy-start.20
  391.9 3.2 copy-start.15
  397.7 3.8 copy-start.21

commit v8 on v7

--- a/solution.py
+++ b/solution.py
@@ -315,6 +315,16 @@
         for k in range(4):
             self.copy(k).start()
 
+    def start_with(self, product):
+        product(self.line(2))
+        self.copy(0).start()
+        self.copy(1).start()
+        product(self.line(1))
+        self.copy(2).start()
+        product(self.line(3))
+        self.copy(3).start()
+        product(self.y)
+
     def middle(self):
         for way in range(2):
             self.copy(way).wait_recv()
@@ -495,10 +505,12 @@
             self.late_z(k).wait_send()
             self.late_x(k).wait_send()
 
-    def run(self):
+    def swap_all(self):
         for step in range(4):
             for j in range(2):
                 self.swap(self.pair(step) * 2 + j).start()
+
+    def add_all(self):
         self.add_pair(0)
         self.add_pair(1)
         self.send_far_z()
@@ -788,78 +800,6 @@
     )(normed, cotangent, entered, routers, *weights)
 
 
-def attn_backward(grad_mid, qkv, gates, weights, cosines, sines):
-    rows, width = grad_mid.shape
-    tile = rows // 4
-    seq = tile // 2
-    scale = HEAD ** (-0.5)
-
-    def kernel(gm_ref, qkv_ref, gates_ref, w_ref, cos_ref, sin_ref, proj_out, back_out):
-        first = 2 * lax.axis_index("zl")
-        causal = causal_mask(2, seq)
-        grads = mm(gm_ref[...], w_ref[:, 4 * HEAD :])
-        gates = gates_ref[...]
-        index = lanes(tile)
-        dots = jnp.zeros((tile, LANE), F32)
-        for j in range(2):
-            here = slice(j * seq, (j + 1) * seq)
-            query = jnp.concatenate(
-                [qkv_ref[here, e * HEAD : (e + 1) * HEAD] for e in range(2)], axis=0
-            )
-            key = qkv_ref[here, 2 * HEAD : 3 * HEAD]
-            value = qkv_ref[here, 3 * HEAD :]
-            probs = soft(mm_nt(query, key) * scale, causal)
-            probs_b = probs.astype(BF)
-            attended = mm(probs_b, value)
-            grad = jnp.concatenate(
-                [grads[here, e * HEAD : (e + 1) * HEAD] for e in range(2)], axis=0
-            )
-            gate = jnp.concatenate([pick(gates[here], first + e) for e in range(2)], axis=0)
-            each = jnp.sum(attended * grad, axis=1, keepdims=True)
-            spread = jnp.where(lanes(seq) == first, each[:seq], 0.0)
-            spread += jnp.where(lanes(seq) == first + 1, each[seq:], 0.0)
-            grad = (grad * gate).astype(BF)
-            grad_probs = mm_nt(grad, value)
-            inner = jnp.sum(probs * grad_probs, axis=1, keepdims=True)
-            grad_scores = (probs * (grad_probs - inner) * scale).astype(BF)
-            grad_query = mm(grad_scores, key)
-            grad_key = mm_tn(grad_scores, query)
-            grad_value = mm_tn(probs_b, grad)
-            proj_out[here, :HEAD] = rotate(grad_query[:seq], cos_ref[...], -sin_ref[...]).astype(BF)
-            proj_out[here, HEAD : 2 * HEAD] = rotate(
-                grad_query[seq:], cos_ref[...], -sin_ref[...]
-            ).astype(BF)
-            proj_out[here, 2 * HEAD : 3 * HEAD] = rotate(
-                grad_key, cos_ref[...], -sin_ref[...]
-            ).astype(BF)
-            proj_out[here, 3 * HEAD :] = grad_value.astype(BF)
-            back_out[here, width:] = spread.astype(BF)
-        back_out[:, :width] = mm_nt(proj_out[...], w_ref[:, : 4 * HEAD]).astype(BF)
-
-    def tiled(cols):
-        return pl.BlockSpec((tile, cols), lambda i: (i, 0))
-
-    def whole(array):
-        return pl.BlockSpec(array.shape, lambda i: (0, 0), pipeline_mode=pl.Buffered(1))
-
-    return pl.pallas_call(
-        kernel,
-        grid=(4,),
-        out_shape=[
-            jax.ShapeDtypeStruct((rows, 4 * HEAD), BF),
-            jax.ShapeDtypeStruct((rows, width + LANE), BF),
-        ],
-        in_specs=[tiled(width), tiled(4 * HEAD), tiled(LANE)]
-        + [whole(a) for a in (weights, cosines, sines)],
-        out_specs=[tiled(4 * HEAD), tiled(width + LANE)],
-        compiler_params=pltpu.CompilerParams(vmem_limit_bytes=48 << 20),
-        cost_estimate=pl.CostEstimate(
-            flops=2 * rows * width * 6 * HEAD, bytes_accessed=20 << 20, transcendentals=0
-        ),
-        name="attn_backward",
-    )(grad_mid, qkv, gates, weights, cosines, sines)
-
-
 def back_through_norm(total, inputs, gain, gates, normed, routers):
     width = inputs.shape[1]
     logits_back = gates_back(gates, total[:, width:])
@@ -868,50 +808,123 @@
     return inner, gain_grad, mm_tn(logits_back.astype(BF), normed)[:8]
 
 
-def middle(collective, back, after, gain, gates_own, routers, cot_own, grads):
+def row_block(array, block, count):
+    cols = array.shape[-1] // 4
+    part = array[..., pl.ds(pl.multiple_of(block * cols, cols), cols)]
+    return part.reshape(count, cols)
+
+
+class Pass:
+    sems = [pltpu.SemaphoreType.DMA((4,))] * 2
+
+    def __init__(self, src, dst, sems):
+        send, recv = sems
+        zh, c = lax.axis_index("zh"), lax.axis_index("c")
+        mine, far = dst.at[zh, c], dst.at[1 - zh, c]
+        self.copies = [
+            pltpu.make_async_copy(src, mine, send.at[0]),
+            push(src, mine, send.at[1], recv.at[1], {"zh": 1 - zh}),
+            push(src, mine, send.at[2], recv.at[2], sibling()),
+            push(far, far, send.at[3], recv.at[3], sibling()),
+        ]
+
+    def start(self):
+        for copy in self.copies[:3]:
+            copy.start()
+
+    def finish(self):
+        self.copies[1].wait_recv()
+        self.copies[3].start()
+        self.copies[0].wait()
+        self.copies[1].wait_send()
+        self.copies[2].wait()
+        self.copies[3].wait()
+
+
+def own_tile():
+    zl, x, zh, c = (lax.axis_index(a) for a in TEAM)
+    return zl * 4 + x, zh * 2 + c
+
+
+def middle(collective, back, branch, normed, cotangent, grads, after, gain, gates, routers, cot_own):
     own, width = after.shape
-    rows, cols = grads[0].shape[0] // 4, grads[0].shape[1]
+    count, cols = grads[0].shape
+    rows = width // 4
 
     def kernel(
-        part_ref, after_ref, gain_ref, gates_ref, router_ref, cot_ref, g0, g1,
-        mid_out, small_out, spread_out, s0, s1,
-        part, load, total, row, *rest,
+        part_ref, branch_ref, x_ref, cot_ref, d0_ref, d1_ref, d2_ref,
+        after_ref, gain_ref, gates_ref, router_ref, own_ref,
+        mid_out, small_out, spread_out, s0, s1, g2, out_all,
+        x, cot, d0, d1, d2, g0, g1, part_a, part_b, load, total_a, total_b, row_a, row_b, *rest,
     ):
-        fetch = pltpu.make_async_copy(part_ref, part, load.at[0])
-        fetch.start()
+        loads = [
+            (part_ref, part_a), (x_ref, x), (d0_ref, d0), (d1_ref, d1), (cot_ref, cot), (d2_ref, d2), (branch_ref, part_b)
+        ]
+        fetches = [pltpu.make_async_copy(a, b, load.at[k]) for k, (a, b) in enumerate(loads)]
+        for fetch in fetches:
+            fetch.start()
         meet([place(m) for m in TEAM_MOVES[1:] + [Y_MOVES[1], Y_MOVES[3]]] + [sibling()])
-        count = TeamSum.count
-        team = TeamSum(part, rest[:count])
-        rings = [
-            RingSum(g, rest[count + 4 + RingSum.count * k : count + 4 + RingSum.count * (k + 1)])
-            for k, g in enumerate((g0, g1))
-        ]
-        for ring in rings:
-            ring.start()
-        fetch.wait()
-        team.run()
+        n = TeamSum.count
+        team_a, team_b = TeamSum(part_a, rest[:n]), TeamSum(part_b, rest[n : 2 * n])
+        rest = rest[2 * n :]
+        n = RingSum.count
+        rings = [RingSum(g0, rest[:n]), RingSum(g1, rest[n : 2 * n])]
+        rest = rest[2 * n :]
+        spread = TeamSpread(row_a, spread_out, rest[:4])
+        out = Pass(row_b, out_all, rest[4:6])
+
+        def product(left, right, dst):
+            def one(block):
+                dst[block] = mm_tn(row_block(left, block, count), right[...]).astype(BF)
+
+            return one
+
+        fetches[0].wait()
+        team_a.swap_all()
+        fetches[1].wait()
+        fetches[2].wait()
+        team_a.add_all()
+        rings[0].start_with(product(x, d0, g0))
+        fetches[3].wait()
         rings[0].middle()
+        rings[1].start_with(product(x, d1, g1))
+        team_a.total1(total_a)
+        rings[1].middle()
         after = after_ref[...]
-        normed = (after * rms_scale(after) * gain_ref[...]).astype(BF)
-        team.total1(total)
-        rings[1].middle()
-        team.total2(total)
+        normed_own = (after * rms_scale(after) * gain_ref[...]).astype(BF)
+        seq, quarter = own_tile()
+        team_a.total2(total_a)
         inner, gain_grad, router_grad = back_through_norm(
-            total[...], after, gain_ref[...], gates_ref[...], normed, router_ref[...]
+            total_a[...], after, gain_ref[...], gates_ref[seq * 4 + quarter], normed_own, router_ref[...]
         )
-        grad_mid = cot_ref[...].astype(F32) + inner
+        grad_mid = own_ref[...].astype(F32) + inner
         mid_out[...] = grad_mid
-        row[...] = grad_mid.astype(BF)
+        row_a[...] = grad_mid.astype(BF)
+        spread.start()
         small_out[:8] = jnp.zeros((8, width), F32)
         small_out[0:1] = gain_grad
         small_out[8:] = router_grad
-        spread = TeamSpread(row, spread_out, rest[count : count + 4])
-        spread.start()
+        fetches[6].wait()
+        team_b.swap_all()
         spread.middle()
+        team_b.add_all()
+        fetches[4].wait()
+        fetches[5].wait()
+
+        def down(block, _):
+            product(cot, d2, g2)(block)
+            return 0
+
+        lax.fori_loop(0, 4, down, 0)
         spread.finish()
+        team_b.total(total_b)
+        row_b[...] = in_order((after + total_b[...]).astype(BF))
+        out.start()
         rings[0].finish(s0)
         rings[1].finish(s1)
-        team.close()
+        out.finish()
+        team_a.close()
+        team_b.close()
 
     return pl.pallas_call(
         kernel,
@@ -919,24 +932,40 @@
             jax.ShapeDtypeStruct((own, width), F32),
             jax.ShapeDtypeStruct((16, width), F32),
             jax.ShapeDtypeStruct((2, 4, 2, 2, own, width), BF),
-        ]
-        + [jax.ShapeDtypeStruct((8, rows // 8, cols), BF)] * 2,
-        in_specs=[ANY] + [VMEM] * 7,
-        out_specs=[VMEM] * 2 + [ANY] + [VMEM] * 2,
+            jax.ShapeDtypeStruct((8, rows // 8, cols), BF),
+            jax.ShapeDtypeStruct((8, rows // 8, cols), BF),
+            jax.ShapeDtypeStruct((4, rows, cols), BF),
+            jax.ShapeDtypeStruct((2, 2, own, width), BF),
+        ],
+        in_specs=[ANY] * 7 + [VMEM] * 5,
+        out_specs=[VMEM] * 2 + [ANY] + [VMEM] * 3 + [ANY],
         scratch_shapes=[
+            pltpu.VMEM((count, width), BF),
+            pltpu.VMEM((count, width), BF),
+            pltpu.VMEM((count, cols), BF),
+            pltpu.VMEM((count, cols), BF),
+            pltpu.VMEM((count, cols), BF),
+            pltpu.VMEM((4, rows, cols), BF),
+            pltpu.VMEM((4, rows, cols), BF),
             pltpu.VMEM((2, 4, 2, 2, own, width + LANE), BF),
-            pltpu.SemaphoreType.DMA((1,)),
+            pltpu.VMEM((2, 4, 2, 2, own, width), BF),
+            pltpu.SemaphoreType.DMA((7,)),
             pltpu.VMEM((own, width + LANE), F32),
+            pltpu.VMEM((own, width), F32),
+            pltpu.VMEM((own, width), BF),
             pltpu.VMEM((own, width), BF),
         ]
         + TeamSum.scratch(own, width + LANE)
+        + TeamSum.scratch(own, width)
+        + RingSum.scratch(rows, cols) * 2
         + TeamSpread.sems
-        + RingSum.scratch(rows, cols) * 2,
+        + Pass.sems,
         name="middle",
-        **settings(collective, 160 << 20, 48),
-    )(back.reshape(2, 4, 2, 2, own, width + LANE), after, gain, gates_own, routers, cot_own, *[
-        g.reshape(4, rows, cols) for g in grads
-    ])
+        **settings(collective, 200 << 20, 58),
+    )(
+        back.reshape(2, 4, 2, 2, own, width + LANE), branch.reshape(2, 4, 2, 2, own, width),
+        normed, cotangent, *grads, after, gain, gates.reshape(-1, own, LANE), routers, cot_own,
+    )
 
 
 def in_order(values):
@@ -945,94 +974,140 @@
     return jnp.concatenate([values[:, k * block : (k + 1) * block] for k in order], axis=1)
 
 
-def leave(
-    collective, back, branch, after, grad_mid, inputs, gain, gates_own, routers, small, summed, grads, attn_grads
+def attn_backward(
+    collective, grad_mid, qkv, gated, normed, gates, weights, cosines, sines, mid_own, inputs, gain, routers, small, summed, grads
 ):
-    own, width = after.shape
-    rows, cols = grads.shape[0] // 4, grads.shape[1]
+    own, width = inputs.shape
+    seq = qkv.shape[1]
+    rows, cols = grads.shape[1:]
     shard = rows // 8
-    cuts = [a.shape[1] for a in attn_grads]
+    scale = HEAD ** (-0.5)
     stages = [X_MOVES, Y_MOVES, Z_MOVES]
 
     def kernel(
-        back_ref, branch_ref, after_ref, mid_ref, in_ref, gain_ref, gates_ref, router_ref, small_ref,
-        y0, y1, g2, a0, a1, out_all, grad_all, small_out, s0, s1, s2, s3,
-        y2, y3, g3, part_a, part_b, load, total_a, total_b, row_a, row_b,
-        acc, got, other, rest_rows, csem, send, recv, ssend, srecv, *rest,
+        gm_ref, w_ref, x_ref, g2_ref, y0, y1, qkv_ref, gated_ref, gates_ref, cos_ref, sin_ref,
+        mid_ref, in_ref, gain_ref, router_ref, small_ref,
+        grad_all, small_out, s0, s1, s2, s3,
+        gm, w, x, g2, g3, y2, y3, proj, part, load, total, row,
+        acc, got, other, rest_rows, csem, ssend, srecv, *rest,
     ):
-        loads = [
-            (a0, g3.at[:, :, : cuts[0]]), (a1, g3.at[:, :, cuts[0] :]), (back_ref, part_a), (branch_ref, part_b)
-        ]
+        loads = [(gm_ref, gm), (w_ref, w), (g2_ref, g2), (x_ref, x)]
         fetches = [pltpu.make_async_copy(a, b, load.at[k]) for k, (a, b) in enumerate(loads)]
         for fetch in fetches:
             fetch.start()
         meet([place(m) for m in TEAM_MOVES[1:] + Y_MOVES[1:]] + [sibling()])
-        count = TeamSum.count
-        team_a, team_b = TeamSum(part_a, rest[:count]), TeamSum(part_b, rest[count : 2 * count])
-        count = 2 * count
+        n = TeamSum.count
+        team, rest = TeamSum(part, rest[:n]), rest[n:]
+        n = RingSum.count
+        rings, rest = [RingSum(g2, rest[:n]), RingSum(g3, rest[n : 2 * n])], rest[2 * n :]
         swaps_back = [
-            Swap(y, s, rest[count + 2 * k : count + 2 * k + 2])
-            for k, (y, s) in enumerate(((y0, s0), (y1, s1), (y2, s2)))
+            Swap(y, s, rest[2 * k : 2 * k + 2]) for k, (y, s) in enumerate(((y0, s0), (y1, s1), (y2, s2)))
         ]
-        last_swap = ColumnSwap(y3, s3, rest[count + 6 : count + 8])
-        count += 8
-        rings = [
-            RingSum(g, rest[count + RingSum.count * k : count + RingSum.count * (k + 1)])
-            for k, g in enumerate((g2, g3))
-        ]
-        rings[0].start()
+        last_swap = ColumnSwap(y3, s3, rest[6:8])
+        out = Pass(row, grad_all, rest[8:10])
+        first = 2 * team.zl
+        causal = causal_mask(2, seq)
+        swaps_back[0].start()
+        swaps_back[1].start()
         fetches[0].wait()
         fetches[1].wait()
-        rings[1].start()
-        fetches[2].wait()
-        team_a.run()
+
+        def step(i, _):
+            pair = team.pair(i)
+            grads = mm(gm[pl.ds(pair * 2, 2)].reshape(2 * seq, width), w[:, 4 * HEAD :])
+            both = []
+            for j in range(2):
+                at = pair * 2 + j
+                here = slice(j * seq, (j + 1) * seq)
+                query = jnp.concatenate(
+                    [qkv_ref[at, :, e * HEAD : (e + 1) * HEAD] for e in range(2)], axis=0
+                )
+                key = qkv_ref[at, :, 2 * HEAD : 3 * HEAD]
+                value = qkv_ref[at, :, 3 * HEAD :]
+                probs = soft(mm_nt(query, key) * scale, causal)
+                probs_b = probs.astype(BF)
+                attended = mm(probs_b, value)
+                grad = jnp.concatenate(
+                    [grads[here, e * HEAD : (e + 1) * HEAD] for e in range(2)], axis=0
+                )
+                gates = gates_ref[at]
+                gate = jnp.concatenate([pick(gates, first + e) for e in range(2)], axis=0)
+                each = jnp.sum(attended * grad, axis=1, keepdims=True)
+                dots = jnp.where(lanes(seq) == first, each[:seq], 0.0)
+                dots += jnp.where(lanes(seq) == first + 1, each[seq:], 0.0)
+                grad = (grad * gate).astype(BF)
+                grad_probs = mm_nt(grad, value)
+                inner = jnp.sum(probs * grad_probs, axis=1, keepdims=True)
+                grad_scores = (probs * (grad_probs - inner) * scale).astype(BF)
+                turned = [mm(grad_scores, key), mm_tn(grad_scores, query)]
+                turned = [turned[0][:seq], turned[0][seq:], turned[1]]
+                turned = [rotate(t, cos_ref[...], -sin_ref[...]).astype(BF) for t in turned]
+                grad_value = mm_tn(probs_b, grad).astype(BF)
+                both.append(jnp.concatenate(turned + [grad_value], axis=1))
+                proj[at] = both[-1]
+                part[pair // 2, lax.rem(pair, 2) * 2 + j, :, :, :, width:] = dots.astype(BF).reshape(
+                    2, 2, own, LANE
+                )
+            back = mm_nt(jnp.concatenate(both, axis=0), w[:, : 4 * HEAD])
+            part[pair // 2, pl.ds(lax.rem(pair, 2) * 2, 2), :, :, :, :width] = back.astype(BF).reshape(
+                2, 2, 2, own, width
+            )
+            for j in range(2):
+                team.swap(pair * 2 + j).start()
+
+            @pl.when(i == 0)
+            def _():
+                fetches[2].wait()
+                rings[0].start()
+
+            @pl.when(i > 0)
+            def _():
+                team.add_pair(i - 1)
+
+            @pl.when(i == 2)
+            def _():
+                team.send_far_z()
+
+            @pl.when(i == 3)
+            def _():
+                team.send_far_x()
+
+            return 0
+
+        lax.fori_loop(0, 4, step, 0)
+        team.last()
         fetches[3].wait()
-        team_b.run()
+
+        def product(block):
+            g3[block, :, : 4 * HEAD] = mm_tn(
+                row_block(x, block, 8 * seq), proj[...].reshape(8 * seq, 4 * HEAD)
+            ).astype(BF)
+            g3[block, :, 4 * HEAD :] = mm_tn(
+                row_block(gm, block, 8 * seq), gated_ref[...].reshape(8 * seq, 2 * HEAD)
+            ).astype(BF)
+
+        rings[1].start_with(product)
         rings[0].middle()
-        swaps_back[0].start()
-        swaps_back[1].start()
         inputs = in_ref[...].astype(F32)
-        normed = (inputs * rms_scale(inputs) * gain_ref[...]).astype(BF)
-        team_a.total1(total_a)
+        normed_own = (inputs * rms_scale(inputs) * gain_ref[...]).astype(BF)
+        own_seq, quarter = own_tile()
+        gates_own = gates_ref[own_seq, pl.ds(pl.multiple_of(quarter * own, own), own)]
+        team.total1(total)
         rings[1].middle()
-        team_a.total2(total_a)
+        team.total2(total)
         inner, gain_grad, router_grad = back_through_norm(
-            total_a[...], inputs, gain_ref[...], gates_ref[...], normed, router_ref[...]
+            total[...], inputs, gain_ref[...], gates_own, normed_own, router_ref[...]
         )
-        row_a[...] = in_order((mid_ref[...] + inner).astype(BF))
+        row[...] = in_order((mid_ref[...] + inner).astype(BF))
+        out.start()
         acc[...] = small_ref[...]
         acc[1:2] = gain_grad
         acc[8:] += router_grad
-        zh, c = lax.axis_index("zh"), lax.axis_index("c")
-
-        def spread(i, src, dst):
-            mine, far = dst.at[zh, c], dst.at[1 - zh, c]
-            copies = [
-                pltpu.make_async_copy(src, mine, send.at[i, 0]),
-                push(src, mine, send.at[i, 1], recv.at[i, 1], {"zh": 1 - zh}),
-                push(src, mine, send.at[i, 2], recv.at[i, 2], sibling()),
-                push(far, far, send.at[i, 3], recv.at[i, 3], sibling()),
-            ]
-            for copy in copies[:3]:
-                copy.start()
-            return copies
-
-        def settle(copies):
-            copies[1].wait_recv()
-            copies[3].start()
-            copies[0].wait()
-            copies[1].wait_send()
-            copies[2].wait()
-            copies[3].wait()
-
-        first = spread(0, row_a, grad_all)
+        c = lax.axis_index("c")
         half = pl.ds(pl.multiple_of(c * 8, 8), 8)
         rest_half = pl.ds(pl.multiple_of((1 - c) * 8, 8), 8)
         over = push(acc.at[rest_half], other, csem.at[0], csem.at[1], sibling())
         over.start()
-        team_b.total(total_b)
-        row_b[...] = in_order((after_ref[...] + total_b[...]).astype(BF))
-        second = spread(1, row_b, out_all)
         over.wait()
         acc[half] = acc[half] + other[...]
         for s, stage in enumerate(stages):
@@ -1045,44 +1120,45 @@
             if s == 0:
                 rings[0].finish(y2)
                 swaps_back[2].start()
-            if s == 1:
-                rings[1].finish(y3)
-                last_swap.start()
             for swap in swaps:
                 swap.wait()
             acc[half] = acc[half] + got[s, 0] + got[s, 1] + got[s, 2]
         back_over = push(acc.at[half], rest_rows, csem.at[2], csem.at[3], sibling())
         back_over.start()
         small_out[half] = in_order(acc[half])
-        settle(first)
-        settle(second)
+        rings[1].finish(y3)
+        last_swap.start()
+        out.finish()
         back_over.wait()
         small_out[rest_half] = in_order(rest_rows[...])
         for swap in swaps_back + [last_swap]:
             swap.finish()
-        team_a.close()
-        team_b.close()
+        team.close()
 
     block = jax.ShapeDtypeStruct((8, shard, cols), BF)
-    count = cols // HEAD
+    heads = cols // HEAD
     return pl.pallas_call(
         kernel,
-        out_shape=[jax.ShapeDtypeStruct((2, 2, own, width), BF)] * 2
-        + [jax.ShapeDtypeStruct((16, width), F32)]
-        + [block] * 3
-        + [jax.ShapeDtypeStruct((2, count, shard, 4 * HEAD), BF)],
-        in_specs=[ANY, ANY] + [VMEM] * 7 + [ANY] * 2 + [VMEM] + [ANY] * 2,
-        out_specs=[ANY, ANY, VMEM] + [ANY] * 4,
+        out_shape=[
+            jax.ShapeDtypeStruct((2, 2, own, width), BF),
+            jax.ShapeDtypeStruct((16, width), F32),
+            block, block, block,
+            jax.ShapeDtypeStruct((2, heads, shard, 4 * HEAD), BF),
+        ],
+        in_specs=[ANY] * 6 + [VMEM] * 10,
+        out_specs=[ANY, VMEM] + [ANY] * 4,
         scratch_shapes=[
+            pltpu.VMEM((8, seq, width), BF),
+            pltpu.VMEM(weights.shape, BF),
+            pltpu.VMEM((8, seq, width), BF),
+            pltpu.VMEM((4, rows, cols), BF),
+            pltpu.VMEM((4, rows, cols), BF),
             pltpu.VMEM((8, shard, cols), BF),
-            pltpu.VMEM((8, count, shard, HEAD), BF),
-            pltpu.VMEM((4, rows, cols), BF),
+            pltpu.VMEM((8, heads, shard, HEAD), BF),
+            pltpu.VMEM((8, seq, 4 * HEAD), BF),
             pltpu.VMEM((2, 4, 2, 2, own, width + LANE), BF),
-            pltpu.VMEM((2, 4, 2, 2, own, width), BF),
             pltpu.SemaphoreType.DMA((4,)),
             pltpu.VMEM((own, width + LANE), F32),
-            pltpu.VMEM((own, width), F32),
-            pltpu.VMEM((own, width), BF),
             pltpu.VMEM((own, width), BF),
             pltpu.VMEM((16, width), F32),
             pltpu.VMEM((3, 3, 8, width), F32),
@@ -1090,19 +1166,16 @@
             pltpu.VMEM((8, width), F32),
             pltpu.SemaphoreType.DMA((4,)),
         ]
-        + [pltpu.SemaphoreType.DMA((2, 4))] * 2
         + [pltpu.SemaphoreType.DMA((4, 4))] * 2
         + TeamSum.scratch(own, width + LANE)
-        + TeamSum.scratch(own, width)
+        + RingSum.scratch(rows, cols) * 2
         + Swap.sems * 4
-        + RingSum.scratch(rows, cols) * 2,
-        name="leave",
-        **settings(collective, 200 << 20, 56),
+        + Pass.sems,
+        name="attn_backward",
+        **settings(collective, 200 << 20, 58),
     )(
-        back.reshape(2, 4, 2, 2, own, width + LANE),
-        branch.reshape(2, 4, 2, 2, own, width),
-        after, grad_mid, inputs, gain, gates_own, routers, small, *summed,
-        grads.reshape(4, rows, cols), *[a.reshape(4, rows, a.shape[1]) for a in attn_grads],
+        grad_mid.reshape(8, seq, width), weights, normed, grads, *summed, qkv, gated, gates, cosines, sines,
+        mid_own, inputs, gain, routers, small,
     )
 
 
@@ -1133,7 +1206,6 @@
     features = down_weight.shape[2]
     part = (features // LANE + 1) // 2 * LANE
     low = features - part
-    zl, x = lax.axis_index("zl"), lax.axis_index("x")
     quarter = lax.axis_index("zh") * 2 + lax.axis_index("c")
     own = seq // 4
     group = 8 * seq
@@ -1163,11 +1235,6 @@
 
     hidden_own = reorder(quarter_of(hidden), 1)
     cot_own = reorder(quarter_of(cotangent), 1)
-    start = (zl * 4 + x) * seq + quarter * own
-
-    def mine(array):
-        return lax.dynamic_slice_in_dim(array, start, own, axis=0)
-
     no_routes = jnp.zeros((own, 2), jnp.int32)
     routes = [quarter_of(attn_route), no_routes, quarter_of(mlp_route)]
     routes = jnp.pad(jnp.concatenate(routes, axis=1), ((0, 0), (0, LANE - 6)))
@@ -1181,28 +1248,17 @@
     )
     mlp_w = [w.reshape(width, part) for w in [gate_w] + mlp_w]
     group_cot = group_cot.reshape(group, width)
-    normed_a = normed_a.reshape(group, width)
     normed_m = normed_m.reshape(group, width)
-    gates_a = gates_a.reshape(group, LANE)
 
     h, grad_gate, grad_up, branch_m, back_m, gates_m = experts(
         normed_m, group_cot, group_in.reshape(group, width + LANE), routers, mlp_w, 2 * part - features
     )
-    grad_mid_own, small_m, grad_mid, *summed = middle(
-        3, back_m, after, mlp_gain, mine(gates_m), routers, cot_own,
-        [mm_tn(normed_m, grad_gate).astype(BF), mm_tn(normed_m, grad_up).astype(BF)],
+    grad_mid_own, small_m, grad_mid, gate_sum, up_sum, down_part, out_hidden = middle(
+        3, back_m, branch_m, normed_m, group_cot, [grad_gate, grad_up, h], after, mlp_gain, gates_m, routers, cot_own
     )
-    grad_mid = grad_mid.reshape(group, width)
-    grad_proj, back_a = attn_backward(
-        grad_mid, qkv.reshape(group, 4 * HEAD), gates_a, attn_w, cosines, sines
-    )
-    attn_grads = [
-        mm_tn(normed_a, grad_proj).astype(BF),
-        mm_tn(grad_mid, gated_att.reshape(group, 2 * HEAD)).astype(BF),
-    ]
-    out_hidden, grad_in, small, *mlp_grads, attn_grads = leave(
-        4, back_a, branch_m, after, grad_mid_own, hidden_own, attn_gain, mine(gates_a), routers, small_m,
-        summed, mm_tn(group_cot, h).astype(BF), attn_grads,
+    grad_in, small, *mlp_grads, attn_grads = attn_backward(
+        4, grad_mid, qkv, gated_att, normed_a, gates_a, attn_w, cosines, sines, grad_mid_own, hidden_own, attn_gain,
+        routers, small_m, [gate_sum, up_sum], down_part,
     )
     out_hidden = out_hidden.reshape(seq, width)
     grad_in = grad_in.reshape(seq, width).astype(F32)

time: 410 us -> 396 us (0.966)
  matrix products: 24.7 us -> 0 us
  Pallas kernels: 337 us -> 345 us
  local copies, waits for them, and re-layouts: 33.9 us -> 38 us
    pallas_call x1, Pallas kernels: 59 us -> 92.2 us  [middle(): pl.pallas_call(kernel, out_shape=[jax.ShapeDtypeStruct((own, width), F32)...]
    pallas_call x2 -> x1, Pallas kernels: 109 us -> 83.6 us  [attn_backward(): pl.pallas_call(kernel, out_shape=[jax.ShapeDtypeStruct((2, 2, own, width)...]
    dot_general x5 -> x0, matrix products: 24.7 us -> none  [dot(): return lax.dot_general(a, b, (dims, ((), ())), preferred_element_type=F32)]
    unnamed x53 -> x57, local copies, waits for them, and re-layouts: 16.8 us -> 22.3 us
where the time goes in v8:
time: 396 us; the launch traced here: 390 us
  Pallas kernels  345 us (87%)
  local copies, waits for them, and re-layouts  38 us (10%)
  other arithmetic  5.91 us (1%)
    pallas_call x1, Pallas kernels, middle(): pl.pallas_call(kernel, out_shape=[jax.ShapeDtypeStruct((own, width), F32)...  92.2 us
    pallas_call x1, Pallas kernels, attn_backward(): pl.pallas_call(kernel, out_shape=[jax.ShapeDtypeStruct((2, 2, own, width)...  83.6 us
    pallas_call x1, Pallas kernels, enter(): pl.pallas_call(kernel, out_shape=[like, jax.ShapeDtypeStruct((4,) + like....  72.1 us
    pallas_call x1, Pallas kernels, attn_forward(): pl.pallas_call(kernel, out_shape=[jax.ShapeDtypeStruct((8, seq, width), B...  65.7 us
    pallas_call x1, Pallas kernels, experts(): pl.pallas_call(kernel, grid=(4,), out_shape=[jax.ShapeDtypeStruct((rows,...  31 us
    unnamed x57, local copies, waits for them, and re-layouts  22.3 us

profile of v8, /device:TPU:0, one launch (start us, length us, event | category | flops | bytes accessed | tf_op | source)
XLA Modules:
  0.0 390.1 jit_solution(6268001340406890418)
XLA Ops:
  0.7 0.1 pad.26.clone
  0.7 0.8 dynamic-slice_convert_fusion
  1.6 0.1 copy.59
  1.7 0.7 reshape.138
  2.4 0.7 reshape.141
  3.2 0.8 pad_maximum_fusion.4
  4.0 0.9 slice.76
  4.9 0.1 copy.53
  5.1 0.1 broadcast_in_dim.4
  5.2 1.0 constant_dynamic-slice_fusion
  6.2 0.1 reshape.142
  6.3 0.1 copy.63
  6.4 0.1 reshape.143.cot_ref.own_ref
  6.5 0.1 reshape.134
  6.6 0.1 copy.58
  6.7 0.1 reshape.135.own_ref.in_ref
  6.8 0.1 reshape.129
  6.9 0.2 slice-done
  7.2 0.5 copy_bitcast_fusion.3
  7.8 0.9 pad_maximum_fusion
  8.7 0.9 reshape.130.a_ref
  9.6 0.3 copy.61
  9.9 0.1 pad.10.router_ref
  10.0 0.3 slice_bitcast_fusion.1
  10.3 0.6 pad_maximum_fusion.3
  10.9 0.1 copy.57
  10.9 0.7 copy-done.18
  11.6 2.0 fusion.3
  13.6 0.2 copy_bitcast_fusion
  13.9 0.1 pad_maximum_fusion.2
  14.1 0.1 pad_maximum_fusion.1
  14.2 72.1 %enter.1 = (bf16[8,64,768]{2,1,0:T(8,128)(2,1)}, bf16[4,8,64,768]{3,2,1,0:T(8,128)(2,1)S(1)}, bf16[8,64,768]{2,1,0:T(8,128)(2,1)}, bf16[8,64,768]{2,1,0:T(8,128)...) custom-call(bf16[8,64,768]{2,1,0:T(8,128)(2,1)S(1)} %reshape.130.a_r, ...), custom_call_target="tpu_custom_call" | custom-call | bytes 125829120 | tf_op jit(solution)/shard_map/enter/pallas_call | solution.py:265
  86.2 1.6 copy-done
  87.9 2.1 copy-done.2
  90.0 1.7 copy-done.17
  91.7 65.7 %attn_forward.1 = (bf16[8,128,2048]{2,1,0:T(8,128)(2,1)}, bf16[8,128,512]{2,1,0:T(8,128)(2,1)S(1)}, bf16[8,128,256]{2,1,0:T(8,128)(2,1)S(1)}, f32[8,128,128]{2,1...) custom-call(bf16[8,128,2176]{2,1,0:T(8,128)(2,1)} %bitcast.93, ...), custom_call_target="tpu_custom_call" | custom-call | bytes 209715200 | tf_op jit(solution)/shard_map/attn_forward/pallas_call | solution.py:716
  157.4 1.0 copy-done.8
  158.4 0.8 copy-done.9
  159.2 0.8 copy-done.10
  159.9 0.7 copy-done.12
  160.6 31.0 %experts.1 = (bf16[1024,768]{1,0:T(8,128)(2,1)S(1)}, bf16[1024,768]{1,0:T(8,128)(2,1)S(1)}, bf16[1024,768]{1,0:T(8,128)(2,1)S(1)}, bf16[1024,2048]{1,0:T(8,128)(...) custom-call(bf16[1024,2048]{1,0:T(8,128)(2,1)} %bitcast.102, bf16[1024,2048]{1,0:T(8,128)(2,1)} %bitcast.104, ...), custom_call_target="tpu_custom_call" | custom-call | flops 19327352832 | bytes 41943040 | tf_op jit(solution)/shard_map/experts/pallas_call | solution.py:786
  191.6 1.2 copy-done.4
  192.8 1.1 copy-done.5
  193.9 1.2 copy-done.6
  195.1 0.8 copy-done.11
  195.9 92.2 %middle.1 = (f32[32,2048]{1,0:T(8,128)}, f32[16,2048]{1,0:T(8,128)}, bf16[2,4,2,2,32,2048]{5,4,3,2,1,0:T(8,128)(2,1)}, bf16[8,64,768]{2,1,0:T(8,128)(2,1)}, bf16...) custom-call(bf16[2,4,2,2,32,2176]{5,4,3,2,1,0:T(8,128)(2,1)} %bitcast.100, ...), custom_call_target="tpu_custom_call" | custom-call | bytes 209715200 | tf_op jit(solution)/shard_map/middle/pallas_call | solution.py:929
  288.2 83.6 %attn_backward.1 = (bf16[2,2,32,2048]{3,2,1,0:T(8,128)(2,1)}, f32[16,2048]{1,0:T(8,128)}, bf16[8,64,768]{2,1,0:T(8,128)(2,1)}, bf16[8,64,768]{2,1,0:T(8,128)(2,1...) custom-call(bf16[8,128,2048]{2,1,0:T(8,128)(2,1)} %bitcast.101, bf16[2048,768]{1,0:T(8,128)(2,1)} %bitcast.92, ...), custom_call_target="tpu_custom_call" | custom-call | bytes 209715200 | tf_op jit(solution)/shard_map/attn_backward/pallas_call | solution.py:1140
  371.8 1.6 fusion.5
  373.4 1.5 slice_bitcast_fusion.9
  374.9 1.0 slice_bitcast_fusion.6
  375.9 1.0 slice_bitcast_fusion.7
  377.1 1.0 copy-done.22
  378.2 0.2 copy-done.21
  378.4 0.8 copy-done.24
  379.2 1.1 bitcast_convert_fusion
  380.3 0.1 convert_bitcast_fusion
  380.4 2.0 copy.66
  382.4 0.1 fusion.4
  382.5 1.1 copy.74
  383.6 0.2 convert_element_type.23
  383.9 1.0 maximum_bitcast_fusion
  384.9 0.2 maximum_convert_fusion
  385.1 3.8 copy.65
  388.9 0.8 copy.76
  (58 shorter events, 0.7 us)
Async XLA Ops:
  2.4 89.3 %copy-start.15 = (f32[1,2048]{1,0:T(1,128)}, f32[1,2048]{1,0:T(1,128)S(1)}, u32[]{:S(2)}) copy-start(f32[1,2048]{1,0:T(1,128)S(1)} %broadcast_in_dim_reshape.6.gain_ref) | copy-start | bytes 24580
  3.2 88.5 %copy-start.16 = (f32[1,2048]{1,0:T(1,128)}, f32[1,2048]{1,0:T(1,128)S(1)}, u32[]{:S(2)}) copy-start(f32[1,2048]{1,0:T(1,128)S(1)} %broadcast_in_dim_reshape.7.gain_m_ref.gain_ref) | copy-start | bytes 24580
  4.9 1.9 copy-start.26
  6.2 1.0 slice-start
  6.5 85.2 %copy-start.7 = (bf16[32,2048]{1,0:T(8,128)(2,1)}, bf16[32,2048]{1,0:T(8,128)(2,1)S(1)}, u32[]{:S(2)}) copy-start(bf16[32,2048]{1,0:T(8,128)(2,1)S(1)} %reshape.143.cot_ref.own_ref) | copy-start | bytes 393220
  6.8 84.9 %copy-start.3 = (bf16[32,2048]{1,0:T(8,128)(2,1)}, bf16[32,2048]{1,0:T(8,128)(2,1)S(1)}, u32[]{:S(2)}) copy-start(bf16[32,2048]{1,0:T(8,128)(2,1)S(1)} %reshape.135.own_ref.in_ref) | copy-start | bytes 393220
  8.7 1.3 copy-start.20
  10.0 150.7 %copy-start.1 = (bf16[2048,128]{1,0:T(8,128)(2,1)}, bf16[2048,128]{1,0:T(8,128)(2,1)S(1)}, u32[]{:S(2)}) copy-start(bf16[2048,128]{1,0:T(8,128)(2,1)S(1)} %pad.10.router_ref) | copy-start | bytes 1572868
  10.3 1.4 copy-start.18
  14.1 77.6 %copy-start.13 = (f32[128,128]{1,0:T(8,128)S(1)}, f32[128,128]{1,0:T(8,128)}, u32[]{:S(2)}) copy-start(f32[128,128]{1,0:T(8,128)} %constant.23.clone.sin_ref) | copy-start | bytes 196612
  14.2 77.6 %copy-start.14 = (f32[128,128]{1,0:T(8,128)S(1)}, f32[128,128]{1,0:T(8,128)}, u32[]{:S(2)}) copy-start(f32[128,128]{1,0:T(8,128)} %constant.22.clone.cos_ref) | copy-start | bytes 196612
  86.2 1.6 copy-start
  87.9 2.1 copy-start.2
  90.0 1.7 copy-start.17
  157.4 1.0 copy-start.8
  158.4 0.8 copy-start.9
  159.1 0.8 copy-start.10
  159.9 0.7 copy-start.12
  191.6 1.2 copy-start.4
  192.8 1.1 copy-start.5
  193.9 1.2 copy-start.6
  195.1 0.8 copy-start.11
  371.8 5.1 %copy-start.23 = (bf16[8,64,768]{2,1,0:T(8,128)(2,1)S(1)}, bf16[8,64,768]{2,1,0:T(8,128)(2,1)}, u32[]{:S(2)}) copy-start(bf16[8,64,768]{2,1,0:T(8,128)(2,1)} %get-tuple-element.73) | copy-start | bytes 2359300
  376.9 1.1 copy-start.22
  377.0 1.3 copy-start.21
  378.1 1.1 copy-start.24
  380.4 2.0 copy-start.19
  385.1 3.8 copy-start.25

commit v9 on v8

--- a/solution.py
+++ b/solution.py
@@ -228,52 +228,6 @@
                 self.copies.append(push(block, mine, self.send.at[k], self.recv.at[k], to))
         for copy in self.copies:
             copy.start()
-
-
-def enter(collective, attn_blocks, blocks, rows):
-    own, width = rows.shape
-
-    def kernel(a_ref, *refs):
-        m_refs, row_ref, a_mid, a_out, m_outs, row_out, g_out, sems = (
-            refs[:3], refs[3], refs[4], refs[5], refs[6:9], refs[9], refs[10], refs[11:],
-        )
-        meet([place(m) for m in TEAM_MOVES[1:] + [Y_MOVES[1], Y_MOVES[3]]] + [sibling()])
-        first = Swap(a_ref, a_mid, sems[2:4])
-        first.start()
-        spread = TeamSpread(row_ref, row_out, sems[10:14])
-        spread.start()
-        first.finish()
-        ring = RingY(a_mid, a_out, sems[0:2])
-        ring.start()
-        swaps = [Swap(m_refs[i], m_outs[i], sems[4 + 2 * i : 6 + 2 * i]) for i in range(3)]
-        swaps[0].start()
-        spread.middle()
-        swaps[1].start()
-        ring.forward()
-        swaps[0].finish()
-        second = RingY(m_outs[0], g_out, sems[14:16])
-        second.start()
-        swaps[2].start()
-        spread.finish()
-        swaps[1].finish()
-        second.forward()
-        swaps[2].finish()
-        ring.finish()
-        second.finish()
-
-    like = jax.ShapeDtypeStruct(attn_blocks.shape, attn_blocks.dtype)
-    return pl.pallas_call(
-        kernel,
-        out_shape=[like, jax.ShapeDtypeStruct((4,) + like.shape, like.dtype)]
-        + [jax.ShapeDtypeStruct(b.shape, b.dtype) for b in blocks]
-        + [jax.ShapeDtypeStruct((2, 4, 2, 2, own, width), rows.dtype)]
-        + [jax.ShapeDtypeStruct((4,) + blocks[0].shape, blocks[0].dtype)],
-        in_specs=[ANY] * 5,
-        out_specs=[ANY] * 7,
-        scratch_shapes=RingY.sems + Swap.sems * 4 + TeamSpread.sems + RingY.sems,
-        name="enter",
-        **settings(collective, 120 << 20),
-    )(attn_blocks, *blocks, rows)[1:]
 
 
 class RingSum:
@@ -593,10 +547,6 @@
             self.second(k).wait_send()
 
 
-def meet_team():
-    meet([place(m) for m in TEAM_MOVES[1:]] + [sibling()])
-
-
 def soft(scores, causal):
     scores = jnp.where(causal, scores, NEG)
     expon = jnp.exp(scores - jnp.max(scores, axis=-1, keepdims=True))
@@ -609,49 +559,64 @@
 
 
 def attn_forward(
-    collective, hidden, weights, gain, routers, cosines, sines, mlp_gain, hidden_own, cot_own, blocks
+    collective, attn_blocks, blocks, entering, cot_own, gain, routers, cosines, sines, mlp_gain, hidden_own
 ):
     own, width = hidden_own.shape
-    seq = hidden.shape[1]
+    seq = 4 * own
     scale = HEAD ** (-0.5)
 
     def kernel(
-        hid_ref, weight_ref, gain_ref, router_ref, cos_ref, sin_ref, gain_m_ref, own_ref, cot_ref, b0, b1,
-        normed_out, qkv_out, gated_out, gates_out, after_out, spread_out, cot_out, w0, w1,
-        hid, w_ref, load, part, total, row, *rest,
+        a_ref, b0, b1, b2, enter_ref, cot_ref, gain_ref, router_ref, cos_ref, sin_ref, gain_m_ref, own_ref,
+        w_out, normed_out, qkv_out, gated_out, gates_out, routes_out, after_out,
+        spread_out, cot_out, w0, w1, w2, a_mid, m0, m1, m2,
+        hid, part, total, row, *rest,
     ):
-        fetches = [
-            pltpu.make_async_copy(hid_ref, hid, load.at[0]),
-            pltpu.make_async_copy(weight_ref, w_ref, load.at[1]),
+        meet([place(m) for m in TEAM_MOVES[1:] + [Y_MOVES[1], Y_MOVES[3]]] + [sibling()])
+        n = TeamSum.count
+        team, rest = TeamSum(part, rest[:n]), rest[n:]
+        enters = TeamSpread(enter_ref, hid, rest[:4])
+        cot = TeamSpread(cot_ref, cot_out, rest[4:8])
+        spread = TeamSpread(row, spread_out, rest[8:12])
+        rest = rest[12:]
+        swaps = [
+            Swap(b, m, rest[2 * k : 2 * k + 2])
+            for k, (b, m) in enumerate(((a_ref, a_mid), (b0, m0), (b1, m1), (b2, m2)))
         ]
-        for fetch in fetches:
-            fetch.start()
-        meet([place(m) for m in TEAM_MOVES[1:] + [Y_MOVES[1], Y_MOVES[3]]] + [sibling()])
-        count = TeamSum.count
-        team = TeamSum(part, rest[:count])
-        cot = TeamSpread(cot_ref, cot_out, rest[count : count + 4])
-        cot.start()
         rings = [
-            RingY(b, w, rest[count + 8 + 2 * k : count + 10 + 2 * k])
-            for k, (b, w) in enumerate(((b0, w0), (b1, w1)))
+            RingY(m, w, rest[8 + 2 * k : 10 + 2 * k])
+            for k, (m, w) in enumerate(((a_mid, w_out), (m0, w0), (m1, w1), (m2, w2)))
         ]
-        for ring in rings:
-            ring.start()
-        for fetch in fetches:
-            fetch.wait()
+        swaps[0].start()
+        enters.start()
+        swaps[0].finish()
+        rings[0].start()
+        swaps[1].start()
+        enters.middle()
+        swaps[2].start()
+        rings[0].forward()
+        swaps[1].finish()
+        rings[1].start()
+        swaps[3].start()
+        enters.finish()
+        rings[0].finish()
         first = 2 * team.zl
         causal = causal_mask(2, seq)
 
         def step(i, _):
             pair = team.pair(i)
+            zl, x = pair // 2, lax.rem(pair, 2) * 2
+            routes = []
             for j in range(2):
-                values = hid[pair * 2 + j, :, :width].astype(F32)
+                entered = hid[zl, x + j].reshape(seq, width + LANE)
+                values = entered[:, :width].astype(F32)
                 normed_out[pair * 2 + j] = (values * rms_scale(values) * gain_ref[...]).astype(BF)
+                routes.append(entered[:, width:])
+                routes_out[pair * 2 + j] = routes[j]
             normed = normed_out[pl.ds(pair * 2, 2)].reshape(2 * seq, width)
+            weights = w_out.reshape(width, 6 * HEAD)
             logits = mm(normed, router_ref[...])
-            proj = mm(normed, w_ref[:, : 4 * HEAD])
-            routes = hid[pl.ds(pair * 2, 2), :, width:].reshape(2 * seq, LANE).astype(F32)
-            gates = dense_gates(logits, chosen(routes, 0))
+            proj = mm(normed, weights[:, : 4 * HEAD])
+            gates = dense_gates(logits, chosen(jnp.concatenate(routes, axis=0).astype(F32), 0))
             gates_out[pl.ds(pair * 2, 2)] = gates.reshape(2, seq, LANE)
             gated = []
             for j in range(2):
@@ -671,16 +636,10 @@
                 qkv_out[pair * 2 + j] = jnp.concatenate(query + [key, value], axis=1)
                 gated.append(jnp.concatenate(out, axis=1))
                 gated_out[pair * 2 + j] = gated[-1]
-            branch = mm_nt(jnp.concatenate(gated, axis=0), w_ref[:, 4 * HEAD :])
-            part[pair // 2, pl.ds(lax.rem(pair, 2) * 2, 2)] = branch.astype(BF).reshape(
-                2, 2, 2, own, width
-            )
+            branch = mm_nt(jnp.concatenate(gated, axis=0), weights[:, 4 * HEAD :])
+            part[zl, pl.ds(x, 2)] = branch.astype(BF).reshape(2, 2, 2, own, width)
             for j in range(2):
                 team.swap(pair * 2 + j).start()
-
-            @pl.when(i == 0)
-            def _():
-                cot.middle()
 
             @pl.when(i > 0)
             def _():
@@ -698,52 +657,61 @@
 
         lax.fori_loop(0, 4, step, 0)
         team.last()
-        rings[0].forward()
-        cot.finish()
-        team.total(total)
+        swaps[2].finish()
+        rings[2].start()
+        swaps[3].finish()
+        rings[3].start()
+        cot.start()
+        rings[1].forward()
+        team.total1(total)
+        cot.middle()
+        team.total2(total)
         after = total[...] + own_ref[...].astype(F32)
         after_out[...] = after
         row[...] = (after * rms_scale(after) * gain_m_ref[...]).astype(BF)
-        spread = TeamSpread(row, spread_out, rest[count + 4 : count + 8])
         spread.start()
-        rings[1].forward()
         spread.middle()
+        rings[2].forward()
+        cot.finish()
         spread.finish()
+        rings[3].forward()
         team.close()
-        for ring in rings:
+        for ring in rings[1:]:
             ring.finish()
 
+    block = jax.ShapeDtypeStruct(attn_blocks.shape, BF)
+    four = jax.ShapeDtypeStruct((4,) + attn_blocks.shape, BF)
+    rows = jax.ShapeDtypeStruct((2, 4, 2, 2, own, width), BF)
     return pl.pallas_call(
         kernel,
         out_shape=[
+            four,
             jax.ShapeDtypeStruct((8, seq, width), BF),
             jax.ShapeDtypeStruct((8, seq, 4 * HEAD), BF),
             jax.ShapeDtypeStruct((8, seq, 2 * HEAD), BF),
             jax.ShapeDtypeStruct((8, seq, LANE), F32),
+            jax.ShapeDtypeStruct((8, seq, LANE), BF),
             jax.ShapeDtypeStruct((own, width), F32),
-            jax.ShapeDtypeStruct((2, 4, 2, 2, own, width), BF),
-            jax.ShapeDtypeStruct((2, 4, 2, 2, own, width), BF),
-        ]
-        + [jax.ShapeDtypeStruct((4,) + b.shape, b.dtype) for b in blocks],
-        in_specs=[ANY] * 2 + [VMEM] * 6 + [ANY] * 3,
-        out_specs=[VMEM] * 5 + [ANY] * 4,
+            rows, rows, four, four, four, block, block, block, block,
+        ],
+        in_specs=[ANY] * 6 + [VMEM] * 6,
+        out_specs=[VMEM] * 7 + [ANY] * 9,
         scratch_shapes=[
-            pltpu.VMEM(hidden.shape, BF),
-            pltpu.VMEM(weights.shape, BF),
-            pltpu.SemaphoreType.DMA((2,)),
+            pltpu.VMEM((2, 4, 2, 2, own, width + LANE), BF),
             pltpu.VMEM((2, 4, 2, 2, own, width), BF),
             pltpu.VMEM((own, width), F32),
             pltpu.VMEM((own, width), BF),
         ]
         + TeamSum.scratch(own, width)
-        + TeamSpread.sems * 2
-        + RingY.sems * 2,
+        + TeamSpread.sems * 3
+        + Swap.sems * 4
+        + RingY.sems * 4,
         name="attn_forward",
-        **settings(collective, 200 << 20, 48),
-    )(hidden, weights, gain, routers, cosines, sines, mlp_gain, hidden_own, cot_own, *blocks)
-
-
-def experts(normed, cotangent, entered, routers, weights, extra):
+        **settings(collective, 200 << 20, 56),
+    )(attn_blocks, *blocks, entering, cot_own, gain, routers, cosines, sines, mlp_gain, hidden_own)[:12]
+
+
+def experts(normed, cotangent, routes, routers, weights, extra):
     rows, width = normed.shape
     part = weights[0].shape[1]
     tile = rows // 4
@@ -789,7 +757,7 @@
         out_shape=[jax.ShapeDtypeStruct((rows, c), BF) for c in cols]
         + [jax.ShapeDtypeStruct((rows, LANE), F32)],
         in_specs=[tiled(width), tiled(width)]
-        + [pl.BlockSpec((tile, LANE), lambda i: (i, width // LANE)), whole(routers)]
+        + [tiled(LANE), whole(routers)]
         + [whole(w) for w in weights],
         out_specs=[tiled(c) for c in cols] + [tiled(LANE)],
         compiler_params=pltpu.CompilerParams(vmem_limit_bytes=48 << 20),
@@ -797,7 +765,7 @@
             flops=12 * rows * width * part, bytes_accessed=40 << 20, transcendentals=rows * part
         ),
         name="experts",
-    )(normed, cotangent, entered, routers, *weights)
+    )(normed, cotangent, routes, routers, *weights)
 
 
 def back_through_norm(total, inputs, gain, gates, normed, routers):
@@ -858,7 +826,7 @@
         x, cot, d0, d1, d2, g0, g1, part_a, part_b, load, total_a, total_b, row_a, row_b, *rest,
     ):
         loads = [
-            (part_ref, part_a), (x_ref, x), (d0_ref, d0), (d1_ref, d1), (cot_ref, cot), (d2_ref, d2), (branch_ref, part_b)
+            (x_ref, x), (d0_ref, d0), (part_ref, part_a), (branch_ref, part_b), (d1_ref, d1), (cot_ref, cot), (d2_ref, d2)
         ]
         fetches = [pltpu.make_async_copy(a, b, load.at[k]) for k, (a, b) in enumerate(loads)]
         for fetch in fetches:
@@ -880,16 +848,18 @@
             return one
 
         fetches[0].wait()
+        fetches[1].wait()
+        rings[0].start_with(product(x, d0, g0))
+        fetches[2].wait()
         team_a.swap_all()
-        fetches[1].wait()
-        fetches[2].wait()
+        fetches[3].wait()
+        team_b.swap_all()
         team_a.add_all()
-        rings[0].start_with(product(x, d0, g0))
-        fetches[3].wait()
+        fetches[4].wait()
+        rings[1].start_with(product(x, d1, g1))
         rings[0].middle()
-        rings[1].start_with(product(x, d1, g1))
         team_a.total1(total_a)
-        rings[1].middle()
+        team_b.add_all()
         after = after_ref[...]
         normed_own = (after * rms_scale(after) * gain_ref[...]).astype(BF)
         seq, quarter = own_tile()
@@ -901,23 +871,22 @@
         mid_out[...] = grad_mid
         row_a[...] = grad_mid.astype(BF)
         spread.start()
+        rings[1].middle()
         small_out[:8] = jnp.zeros((8, width), F32)
         small_out[0:1] = gain_grad
         small_out[8:] = router_grad
+        fetches[5].wait()
         fetches[6].wait()
-        team_b.swap_all()
-        spread.middle()
-        team_b.add_all()
-        fetches[4].wait()
-        fetches[5].wait()
 
         def down(block, _):
             product(cot, d2, g2)(block)
             return 0
 
         lax.fori_loop(0, 4, down, 0)
+        spread.middle()
+        team_b.total1(total_b)
         spread.finish()
-        team_b.total(total_b)
+        team_b.total2(total_b)
         row_b[...] = in_order((after + total_b[...]).astype(BF))
         out.start()
         rings[0].finish(s0)
@@ -1239,25 +1208,22 @@
     routes = [quarter_of(attn_route), no_routes, quarter_of(mlp_route)]
     routes = jnp.pad(jnp.concatenate(routes, axis=1), ((0, 0), (0, LANE - 6)))
     entering = jnp.concatenate([hidden_own, routes.astype(BF)], axis=1)
-    attn_w, _, *mlp_rows, group_in, gate_w = enter(1, attn_blocks, mlp_blocks, entering)
+    attn_w, normed_a, qkv, gated_att, gates_a, group_routes, after, normed_m, group_cot, *mlp_w = attn_forward(
+        1, attn_blocks, mlp_blocks, entering, cot_own, attn_gain, routers, cosines, sines, mlp_gain, hidden_own
+    )
     attn_w = attn_w.reshape(width, 6 * HEAD)
-    group_in = group_in.reshape(8, seq, width + LANE)
-
-    normed_a, qkv, gated_att, gates_a, after, normed_m, group_cot, *mlp_w = attn_forward(
-        2, group_in, attn_w, attn_gain, routers, cosines, sines, mlp_gain, hidden_own, cot_own, mlp_rows
-    )
-    mlp_w = [w.reshape(width, part) for w in [gate_w] + mlp_w]
+    mlp_w = [w.reshape(width, part) for w in mlp_w]
     group_cot = group_cot.reshape(group, width)
     normed_m = normed_m.reshape(group, width)
 
     h, grad_gate, grad_up, branch_m, back_m, gates_m = experts(
-        normed_m, group_cot, group_in.reshape(group, width + LANE), routers, mlp_w, 2 * part - features
+        normed_m, group_cot, group_routes.reshape(group, LANE), routers, mlp_w, 2 * part - features
     )
     grad_mid_own, small_m, grad_mid, gate_sum, up_sum, down_part, out_hidden = middle(
-        3, back_m, branch_m, normed_m, group_cot, [grad_gate, grad_up, h], after, mlp_gain, gates_m, routers, cot_own
+        2, back_m, branch_m, normed_m, group_cot, [grad_gate, grad_up, h], after, mlp_gain, gates_m, routers, cot_own
     )
     grad_in, small, *mlp_grads, attn_grads = attn_backward(
-        4, grad_mid, qkv, gated_att, normed_a, gates_a, attn_w, cosines, sines, grad_mid_own, hidden_own, attn_gain,
+        3, grad_mid, qkv, gated_att, normed_a, gates_a, attn_w, cosines, sines, grad_mid_own, hidden_own, attn_gain,
         routers, small_m, [gate_sum, up_sum], down_part,
     )
     out_hidden = out_hidden.reshape(seq, width)

time: 396 us -> 410 us (1.035)
  Pallas kernels: 345 us -> 360 us
  local copies, waits for them, and re-layouts: 38 us -> 33.6 us
    pallas_call x2 -> x1, Pallas kernels: 138 us -> 170 us  [attn_forward(): pl.pallas_call(kernel, out_shape=[four, jax.ShapeDtypeStruct((8, seq, wid...]
    pallas_call x1, Pallas kernels: 92.2 us -> 75.8 us  [middle(): pl.pallas_call(kernel, out_shape=[jax.ShapeDtypeStruct((own, width), F32)...]
    unnamed x57 -> x35, local copies, waits for them, and re-layouts: 22.3 us -> 13.8 us
where the time goes in v9:
time: 410 us; the launch traced here: 403 us
  Pallas kernels  360 us (88%)
  local copies, waits for them, and re-layouts  33.6 us (8%)
  other arithmetic  8.34 us (2%)
    pallas_call x1, Pallas kernels, attn_forward(): pl.pallas_call(kernel, out_shape=[four, jax.ShapeDtypeStruct((8, seq, wid...  170 us
    pallas_call x1, Pallas kernels, attn_backward(): pl.pallas_call(kernel, out_shape=[jax.ShapeDtypeStruct((2, 2, own, width)...  83 us
    pallas_call x1, Pallas kernels, middle(): pl.pallas_call(kernel, out_shape=[jax.ShapeDtypeStruct((own, width), F32)...  75.8 us
    pallas_call x1, Pallas kernels, experts(): pl.pallas_call(kernel, grid=(4,), out_shape=[jax.ShapeDtypeStruct((rows,...  30.6 us
    unnamed x35, local copies, waits for them, and re-layouts  13.8 us

profile of v9, /device:TPU:0, one launch (start us, length us, event | category | flops | bytes accessed | tf_op | source)
XLA Modules:
  0.0 403.0 jit_solution(9204078804123128109)
XLA Ops:
  0.7 0.1 pad.26.clone
  0.7 0.8 dynamic-slice_convert_fusion
  1.5 0.1 pad_maximum_fusion.5
  1.6 0.1 copy.59
  1.7 0.7 reshape.138
  2.4 0.6 broadcast_in_dim_reshape.6.gain_ref
  3.0 0.7 reshape.141
  3.7 0.6 broadcast_in_dim_reshape.7.gain_m_ref.gain_ref
  4.4 0.8 pad_maximum_fusion.4
  5.1 0.9 slice.76
  6.1 0.1 copy.53
  6.2 0.1 broadcast_in_dim.4
  6.4 1.0 constant_dynamic-slice_fusion
  7.4 0.1 reshape.136
  7.5 0.1 copy.60
  7.6 0.7 reshape.137.cot_ref.own_ref
  8.3 0.1 reshape.134
  8.4 0.1 copy.58
  8.5 0.1 reshape.135.own_ref.in_ref
  8.6 0.7 fusion.2.enter_ref
  9.3 0.1 reshape.129
  9.4 0.1 reshape.127
  9.5 0.5 copy_bitcast_fusion.3
  10.0 0.9 pad_maximum_fusion
  10.9 1.8 reshape.130.a_ref
  12.7 0.3 copy.62
  13.0 0.9 pad.10.router_ref
  13.9 0.3 slice_bitcast_fusion.1
  14.2 0.6 pad_maximum_fusion.3
  14.7 1.0 copy.57
  15.7 2.0 fusion.3
  17.7 0.2 copy_bitcast_fusion
  17.9 0.1 slice_bitcast_fusion.3
  18.0 0.9 pad_maximum_fusion.2
  18.9 0.1 slice_bitcast_fusion.5
  19.0 0.9 pad_maximum_fusion.1
  19.9 170.1 %attn_forward.1 = (bf16[4,8,64,768]{3,2,1,0:T(8,128)(2,1)}, bf16[8,128,2048]{2,1,0:T(8,128)(2,1)}, bf16[8,128,512]{2,1,0:T(8,128)(2,1)}, bf16[8,128,256]{2,1,0:T...) custom-call(bf16[8,64,768]{2,1,0:T(8,128)(2,1)} %reshape.130.a_ref, ...), custom_call_target="tpu_custom_call" | custom-call | bytes 209715200 | tf_op jit(solution)/shard_map/attn_forward/pallas_call | solution.py:685
  190.1 0.9 copy-done.5
  191.0 30.6 %experts.1 = (bf16[1024,768]{1,0:T(8,128)(2,1)S(1)}, bf16[1024,768]{1,0:T(8,128)(2,1)S(1)}, bf16[1024,768]{1,0:T(8,128)(2,1)S(1)}, bf16[1024,2048]{1,0:T(8,128)(...) custom-call(bf16[1024,2048]{1,0:T(8,128)(2,1)} %bitcast.93, bf16[1024,2048]{1,0:T(8,128)(2,1)} %bitcast.95, ...), custom_call_target="tpu_custom_call" | custom-call | flops 19327352832 | bytes 41943040 | tf_op jit(solution)/shard_map/experts/pallas_call | solution.py:754
  221.7 1.1 copy-done.1
  222.8 1.1 copy-done.2
  223.9 1.1 copy-done.3
  225.1 0.8 copy-done.4
  225.9 75.8 %middle.1 = (f32[32,2048]{1,0:T(8,128)}, f32[16,2048]{1,0:T(8,128)}, bf16[2,4,2,2,32,2048]{5,4,3,2,1,0:T(8,128)(2,1)}, bf16[8,64,768]{2,1,0:T(8,128)(2,1)}, bf16...) custom-call(bf16[2,4,2,2,32,2176]{5,4,3,2,1,0:T(8,128)(2,1)} %bitcast.92, ...), custom_call_target="tpu_custom_call" | custom-call | bytes 209715200 | tf_op jit(solution)/shard_map/middle/pallas_call | solution.py:898
  301.7 83.0 %attn_backward.1 = (bf16[2,2,32,2048]{3,2,1,0:T(8,128)(2,1)}, f32[16,2048]{1,0:T(8,128)}, bf16[8,64,768]{2,1,0:T(8,128)(2,1)}, bf16[8,64,768]{2,1,0:T(8,128)(2,1...) custom-call(bf16[8,128,2048]{2,1,0:T(8,128)(2,1)} %bitcast.97, bf16[2048,768]{1,0:T(8,128)(2,1)} %bitcast.102, ...), custom_call_target="tpu_custom_call" | custom-call | bytes 209715200 | tf_op jit(solution)/shard_map/attn_backward/pallas_call | solution.py:1109
  384.8 1.6 fusion.5
  386.3 1.5 slice_bitcast_fusion.9
  387.9 1.0 slice_bitcast_fusion.6
  388.9 1.0 slice_bitcast_fusion.7
  390.0 0.1 maximum_bitcast_fusion.1
  390.0 1.0 copy-done.11
  391.0 0.1 maximum_bitcast_fusion.2
  391.1 0.2 copy-done.10
  391.3 0.8 copy-done.13
  392.1 1.1 bitcast_convert_fusion
  393.2 0.1 convert_bitcast_fusion
  393.3 2.0 copy.66
  395.4 0.1 fusion.4
  395.5 1.1 copy.74
  396.6 0.2 convert_element_type.23
  396.8 1.0 maximum_bitcast_fusion
  397.8 0.2 maximum_convert_fusion
  398.0 3.8 copy.65
  401.8 0.8 copy.76
  (35 shorter events, 0.3 us)
Async XLA Ops:
  6.1 3.2 copy-start.15
  7.4 2.0 slice-start
  8.6 2.3 copy-start.8
  10.9 3.0 copy-start.9
  14.2 1.5 copy-start.6
  19.9 170.2 %copy-start = (bf16[2048,128]{1,0:T(8,128)(2,1)S(1)}, bf16[2048,128]{1,0:T(8,128)(2,1)}, u32[]{:S(2)}) copy-start(bf16[2048,128]{1,0:T(8,128)(2,1)} %pad.10.router_ref) | copy-start | bytes 1572868
  190.1 1.0 copy-start.5
  221.6 1.1 copy-start.1
  222.8 1.1 copy-start.2
  223.9 1.1 copy-start.3
  225.1 0.8 copy-start.4
  384.7 5.1 %copy-start.12 = (bf16[8,64,768]{2,1,0:T(8,128)(2,1)S(1)}, bf16[8,64,768]{2,1,0:T(8,128)(2,1)}, u32[]{:S(2)}) copy-start(bf16[8,64,768]{2,1,0:T(8,128)(2,1)} %get-tuple-element.69) | copy-start | bytes 2359300
  389.9 1.1 copy-start.11
  390.0 1.3 copy-start.10
  391.0 1.1 copy-start.13
  393.3 2.0 copy-start.7
  398.0 3.8 copy-start.14

commit v10 on v9

--- a/solution.py
+++ b/solution.py
@@ -559,23 +559,34 @@
 
 
 def attn_forward(
-    collective, attn_blocks, blocks, entering, cot_own, gain, routers, cosines, sines, mlp_gain, hidden_own
+    collective, attn_blocks, blocks, hidden, cotangent, routes, small, cosines, sines
 ):
-    own, width = hidden_own.shape
-    seq = 4 * own
+    seq, width = hidden.shape
+    own = seq // 4
+    piece = width // 8
     scale = HEAD ** (-0.5)
 
     def kernel(
-        a_ref, b0, b1, b2, enter_ref, cot_ref, gain_ref, router_ref, cos_ref, sin_ref, gain_m_ref, own_ref,
-        w_out, normed_out, qkv_out, gated_out, gates_out, routes_out, after_out,
+        a_ref, b0, b1, b2, hidden_ref, cotangent_ref, route_ref, small_ref, cos_ref, sin_ref,
+        w_out, normed_out, qkv_out, gated_out, gates_out, routes_out, after_out, enter_row, cot_row, router_ref,
         spread_out, cot_out, w0, w1, w2, a_mid, m0, m1, m2,
-        hid, part, total, row, *rest,
+        load, hid, part, total, row, *rest,
     ):
+        mine = pl.ds(pl.multiple_of((lax.axis_index("zh") * 2 + lax.axis_index("c")) * own, own), own)
+        loads = []
+        for b in range(8):
+            here, there = pl.ds(b * piece, piece), pl.ds(((b % 4) * 2 + b // 4) * piece, piece)
+            loads.append((hidden_ref.at[mine, here], enter_row.at[:, there]))
+            loads.append((cotangent_ref.at[mine, here], cot_row.at[:, there]))
+        loads.append((route_ref.at[mine], enter_row.at[:, pl.ds(width, LANE)]))
+        fetches = [pltpu.make_async_copy(a, b, load.at[k]) for k, (a, b) in enumerate(loads)]
+        for fetch in fetches:
+            fetch.start()
         meet([place(m) for m in TEAM_MOVES[1:] + [Y_MOVES[1], Y_MOVES[3]]] + [sibling()])
         n = TeamSum.count
         team, rest = TeamSum(part, rest[:n]), rest[n:]
-        enters = TeamSpread(enter_ref, hid, rest[:4])
-        cot = TeamSpread(cot_ref, cot_out, rest[4:8])
+        enters = TeamSpread(enter_row, hid, rest[:4])
+        cot = TeamSpread(cot_row, cot_out, rest[4:8])
         spread = TeamSpread(row, spread_out, rest[8:12])
         rest = rest[12:]
         swaps = [
@@ -587,7 +598,11 @@
             for k, (m, w) in enumerate(((a_mid, w_out), (m0, w0), (m1, w1), (m2, w2)))
         ]
         swaps[0].start()
+        for fetch in fetches:
+            fetch.wait()
         enters.start()
+        router_ref[...] = jnp.zeros_like(router_ref)
+        router_ref[:8] = small_ref[8:].astype(BF)
         swaps[0].finish()
         rings[0].start()
         swaps[1].start()
@@ -609,12 +624,12 @@
             for j in range(2):
                 entered = hid[zl, x + j].reshape(seq, width + LANE)
                 values = entered[:, :width].astype(F32)
-                normed_out[pair * 2 + j] = (values * rms_scale(values) * gain_ref[...]).astype(BF)
+                normed_out[pair * 2 + j] = (values * rms_scale(values) * small_ref[0:1]).astype(BF)
                 routes.append(entered[:, width:])
                 routes_out[pair * 2 + j] = routes[j]
             normed = normed_out[pl.ds(pair * 2, 2)].reshape(2 * seq, width)
             weights = w_out.reshape(width, 6 * HEAD)
-            logits = mm(normed, router_ref[...])
+            logits = mm_nt(normed, router_ref[...])
             proj = mm(normed, weights[:, : 4 * HEAD])
             gates = dense_gates(logits, chosen(jnp.concatenate(routes, axis=0).astype(F32), 0))
             gates_out[pl.ds(pair * 2, 2)] = gates.reshape(2, seq, LANE)
@@ -658,20 +673,20 @@
         lax.fori_loop(0, 4, step, 0)
         team.last()
         swaps[2].finish()
+        cot.start()
+        rings[1].forward()
         rings[2].start()
         swaps[3].finish()
-        rings[3].start()
-        cot.start()
-        rings[1].forward()
         team.total1(total)
         cot.middle()
         team.total2(total)
-        after = total[...] + own_ref[...].astype(F32)
+        after = total[...] + enter_row[:, :width].astype(F32)
         after_out[...] = after
-        row[...] = (after * rms_scale(after) * gain_m_ref[...]).astype(BF)
+        row[...] = (after * rms_scale(after) * small_ref[1:2]).astype(BF)
         spread.start()
+        rings[2].forward()
+        rings[3].start()
         spread.middle()
-        rings[2].forward()
         cot.finish()
         spread.finish()
         rings[3].forward()
@@ -692,11 +707,15 @@
             jax.ShapeDtypeStruct((8, seq, LANE), F32),
             jax.ShapeDtypeStruct((8, seq, LANE), BF),
             jax.ShapeDtypeStruct((own, width), F32),
+            jax.ShapeDtypeStruct((own, width + LANE), BF),
+            jax.ShapeDtypeStruct((own, width), BF),
+            jax.ShapeDtypeStruct((LANE, width), BF),
             rows, rows, four, four, four, block, block, block, block,
         ],
-        in_specs=[ANY] * 6 + [VMEM] * 6,
-        out_specs=[VMEM] * 7 + [ANY] * 9,
+        in_specs=[ANY] * 7 + [VMEM] * 3,
+        out_specs=[VMEM] * 10 + [ANY] * 9,
         scratch_shapes=[
+            pltpu.SemaphoreType.DMA((17,)),
             pltpu.VMEM((2, 4, 2, 2, own, width + LANE), BF),
             pltpu.VMEM((2, 4, 2, 2, own, width), BF),
             pltpu.VMEM((own, width), F32),
@@ -708,7 +727,7 @@
         + RingY.sems * 4,
         name="attn_forward",
         **settings(collective, 200 << 20, 56),
-    )(attn_blocks, *blocks, entering, cot_own, gain, routers, cosines, sines, mlp_gain, hidden_own)[:12]
+    )(attn_blocks, *blocks, hidden, cotangent, routes, small, cosines, sines)[:15]
 
 
 def experts(normed, cotangent, routes, routers, weights, extra):
@@ -720,7 +739,7 @@
         lane = EXPERTS + lax.axis_index("x")
         skip = lax.axis_index("zl") * extra
         x = x_ref[...]
-        logits = mm(x, router_ref[...])
+        logits = mm_nt(x, router_ref[...])
         index = lanes(tile)
         gates = dense_gates(logits, chosen(route_ref[...].astype(F32), EXPERTS))
         gates_out[...] = gates
@@ -771,7 +790,7 @@
 def back_through_norm(total, inputs, gain, gates, normed, routers):
     width = inputs.shape[1]
     logits_back = gates_back(gates, total[:, width:])
-    full = total[:, :width] + mm_nt(logits_back.astype(BF), routers)
+    full = total[:, :width] + mm(logits_back.astype(BF), routers)
     inner, gain_grad = norm_back(inputs, gain, full)
     return inner, gain_grad, mm_tn(logits_back.astype(BF), normed)[:8]
 
@@ -814,14 +833,14 @@
     return zl * 4 + x, zh * 2 + c
 
 
-def middle(collective, back, branch, normed, cotangent, grads, after, gain, gates, routers, cot_own):
+def middle(collective, back, branch, normed, cotangent, grads, after, small, gates, routers, cot_own):
     own, width = after.shape
     count, cols = grads[0].shape
     rows = width // 4
 
     def kernel(
         part_ref, branch_ref, x_ref, cot_ref, d0_ref, d1_ref, d2_ref,
-        after_ref, gain_ref, gates_ref, router_ref, own_ref,
+        after_ref, small_ref, gates_ref, router_ref, own_ref,
         mid_out, small_out, spread_out, s0, s1, g2, out_all,
         x, cot, d0, d1, d2, g0, g1, part_a, part_b, load, total_a, total_b, row_a, row_b, *rest,
     ):
@@ -861,11 +880,11 @@
         team_a.total1(total_a)
         team_b.add_all()
         after = after_ref[...]
-        normed_own = (after * rms_scale(after) * gain_ref[...]).astype(BF)
+        normed_own = (after * rms_scale(after) * small_ref[1:2]).astype(BF)
         seq, quarter = own_tile()
         team_a.total2(total_a)
         inner, gain_grad, router_grad = back_through_norm(
-            total_a[...], after, gain_ref[...], gates_ref[seq * 4 + quarter], normed_own, router_ref[...]
+            total_a[...], after, small_ref[1:2], gates_ref[seq * 4 + quarter], normed_own, router_ref[...]
         )
         grad_mid = own_ref[...].astype(F32) + inner
         mid_out[...] = grad_mid
@@ -933,7 +952,7 @@
         **settings(collective, 200 << 20, 58),
     )(
         back.reshape(2, 4, 2, 2, own, width + LANE), branch.reshape(2, 4, 2, 2, own, width),
-        normed, cotangent, *grads, after, gain, gates.reshape(-1, own, LANE), routers, cot_own,
+        normed, cotangent, *grads, after, small, gates.reshape(-1, own, LANE), routers, cot_own,
     )
 
 
@@ -944,9 +963,9 @@
 
 
 def attn_backward(
-    collective, grad_mid, qkv, gated, normed, gates, weights, cosines, sines, mid_own, inputs, gain, routers, small, summed, grads
+    collective, grad_mid, qkv, gated, normed, gates, weights, cosines, sines, mid_own, entered, gains, routers, small, summed, grads
 ):
-    own, width = inputs.shape
+    own, width = mid_own.shape
     seq = qkv.shape[1]
     rows, cols = grads.shape[1:]
     shard = rows // 8
@@ -956,7 +975,7 @@
     def kernel(
         gm_ref, w_ref, x_ref, g2_ref, y0, y1, qkv_ref, gated_ref, gates_ref, cos_ref, sin_ref,
         mid_ref, in_ref, gain_ref, router_ref, small_ref,
-        grad_all, small_out, s0, s1, s2, s3,
+        grad_all, gain_a, gain_m, router_a, router_m, s0, s1, s2, s3,
         gm, w, x, g2, g3, y2, y3, proj, part, load, total, row,
         acc, got, other, rest_rows, csem, ssend, srecv, *rest,
     ):
@@ -1057,15 +1076,15 @@
 
         rings[1].start_with(product)
         rings[0].middle()
-        inputs = in_ref[...].astype(F32)
-        normed_own = (inputs * rms_scale(inputs) * gain_ref[...]).astype(BF)
+        inputs = in_ref[:, :width].astype(F32)
+        normed_own = (inputs * rms_scale(inputs) * gain_ref[0:1]).astype(BF)
         own_seq, quarter = own_tile()
         gates_own = gates_ref[own_seq, pl.ds(pl.multiple_of(quarter * own, own), own)]
         team.total1(total)
         rings[1].middle()
         team.total2(total)
         inner, gain_grad, router_grad = back_through_norm(
-            total[...], inputs, gain_ref[...], gates_own, normed_own, router_ref[...]
+            total[...], inputs, gain_ref[0:1], gates_own, normed_own, router_ref[...]
         )
         row[...] = in_order((mid_ref[...] + inner).astype(BF))
         out.start()
@@ -1089,17 +1108,23 @@
             if s == 0:
                 rings[0].finish(y2)
                 swaps_back[2].start()
+            if s == 1:
+                rings[1].finish(y3)
+                last_swap.start()
             for swap in swaps:
                 swap.wait()
             acc[half] = acc[half] + got[s, 0] + got[s, 1] + got[s, 2]
         back_over = push(acc.at[half], rest_rows, csem.at[2], csem.at[3], sibling())
         back_over.start()
-        small_out[half] = in_order(acc[half])
-        rings[1].finish(y3)
-        last_swap.start()
         out.finish()
         back_over.wait()
-        small_out[rest_half] = in_order(rest_rows[...])
+        acc[rest_half] = rest_rows[...]
+        final = in_order(acc[...])
+        for ref, at in ((gain_m, 0), (gain_a, 1)):
+            for k in range(width // LANE):
+                ref[k : k + 1] = final[at : at + 1, k * LANE : (k + 1) * LANE]
+        router_a[...] = final[8 : 8 + EXPERTS]
+        router_m[...] = final[8 + EXPERTS :]
         for swap in swaps_back + [last_swap]:
             swap.finish()
         team.close()
@@ -1110,12 +1135,15 @@
         kernel,
         out_shape=[
             jax.ShapeDtypeStruct((2, 2, own, width), BF),
-            jax.ShapeDtypeStruct((16, width), F32),
+            jax.ShapeDtypeStruct((width // LANE, LANE), F32),
+            jax.ShapeDtypeStruct((width // LANE, LANE), F32),
+            jax.ShapeDtypeStruct((EXPERTS, width), F32),
+            jax.ShapeDtypeStruct((EXPERTS, width), F32),
             block, block, block,
             jax.ShapeDtypeStruct((2, heads, shard, 4 * HEAD), BF),
         ],
         in_specs=[ANY] * 6 + [VMEM] * 10,
-        out_specs=[ANY, VMEM] + [ANY] * 4,
+        out_specs=[ANY] + [VMEM] * 4 + [ANY] * 4,
         scratch_shapes=[
             pltpu.VMEM((8, seq, width), BF),
             pltpu.VMEM(weights.shape, BF),
@@ -1144,7 +1172,7 @@
         **settings(collective, 200 << 20, 58),
     )(
         grad_mid.reshape(8, seq, width), weights, normed, grads, *summed, qkv, gated, gates, cosines, sines,
-        mid_own, inputs, gain, routers, small,
+        mid_own, entered, gains, routers, small,
     )
 
 
@@ -1175,8 +1203,6 @@
     features = down_weight.shape[2]
     part = (features // LANE + 1) // 2 * LANE
     low = features - part
-    quarter = lax.axis_index("zh") * 2 + lax.axis_index("c")
-    own = seq // 4
     group = 8 * seq
     cosines, sines = rope_tables(seq)
 
@@ -1195,22 +1221,17 @@
         by_target(w) for w in (gate_up_weight[:, :, 0], gate_up_weight[:, :, 1], down_weight)
     ]
 
-    attn_gain, mlp_gain = reorder(attn_gain, 0)[None], reorder(mlp_gain, 0)[None]
-    routers = reorder(jnp.concatenate([attn_router, mlp_router], axis=1), 0)
-    routers = jnp.pad(routers, ((0, 0), (0, LANE - 2 * EXPERTS)))
-
-    def quarter_of(array):
-        return lax.dynamic_slice_in_dim(array, quarter * own, own, axis=0)
-
-    hidden_own = reorder(quarter_of(hidden), 1)
-    cot_own = reorder(quarter_of(cotangent), 1)
-    no_routes = jnp.zeros((own, 2), jnp.int32)
-    routes = [quarter_of(attn_route), no_routes, quarter_of(mlp_route)]
-    routes = jnp.pad(jnp.concatenate(routes, axis=1), ((0, 0), (0, LANE - 6)))
-    entering = jnp.concatenate([hidden_own, routes.astype(BF)], axis=1)
-    attn_w, normed_a, qkv, gated_att, gates_a, group_routes, after, normed_m, group_cot, *mlp_w = attn_forward(
-        1, attn_blocks, mlp_blocks, entering, cot_own, attn_gain, routers, cosines, sines, mlp_gain, hidden_own
-    )
+    none = jnp.zeros((6, width), F32)
+    routers = jnp.concatenate([attn_router, mlp_router], axis=1).astype(F32).T
+    small = jnp.concatenate([attn_gain[None], mlp_gain[None], none, routers], axis=0)
+    small = reorder(small, 1)
+    routes = jnp.concatenate([attn_route, jnp.zeros_like(attn_route), mlp_route], axis=1)
+    routes = jnp.pad(routes, ((0, 0), (0, LANE - 6))).astype(BF)
+
+    (
+        attn_w, normed_a, qkv, gated_att, gates_a, group_routes, after, entered, cot_own, routers,
+        normed_m, group_cot, *mlp_w,
+    ) = attn_forward(1, attn_blocks, mlp_blocks, hidden, cotangent, routes, small, cosines, sines)
     attn_w = attn_w.reshape(width, 6 * HEAD)
     mlp_w = [w.reshape(width, part) for w in mlp_w]
     group_cot = group_cot.reshape(group, width)
@@ -1220,10 +1241,10 @@
         normed_m, group_cot, group_routes.reshape(group, LANE), routers, mlp_w, 2 * part - features
     )
     grad_mid_own, small_m, grad_mid, gate_sum, up_sum, down_part, out_hidden = middle(
-        2, back_m, branch_m, normed_m, group_cot, [grad_gate, grad_up, h], after, mlp_gain, gates_m, routers, cot_own
+        2, back_m, branch_m, normed_m, group_cot, [grad_gate, grad_up, h], after, small, gates_m, routers, cot_own
     )
-    grad_in, small, *mlp_grads, attn_grads = attn_backward(
-        3, grad_mid, qkv, gated_att, normed_a, gates_a, attn_w, cosines, sines, grad_mid_own, hidden_own, attn_gain,
+    grad_in, gain_a, gain_m, router_a, router_m, *mlp_grads, attn_grads = attn_backward(
+        3, grad_mid, qkv, gated_att, normed_a, gates_a, attn_w, cosines, sines, grad_mid_own, entered, small,
         routers, small_m, [gate_sum, up_sum], down_part,
     )
     out_hidden = out_hidden.reshape(seq, width)
@@ -1243,12 +1264,12 @@
     return (
         out_hidden,
         grad_in,
-        small[1],
-        small[8 : 8 + EXPERTS].T,
+        gain_a.reshape(width),
+        router_a.T,
         qkv_grad,
         out_grad,
-        small[0],
-        small[8 + EXPERTS :].T,
+        gain_m.reshape(width),
+        router_m.T,
         jnp.stack([gate_grad, up_grad], axis=2).astype(F32),
         down_grad.astype(F32),
     )

time: 410 us -> 371 us (0.905)
  Pallas kernels: 360 us -> 323 us
    pallas_call x1, Pallas kernels: 170 us -> 137 us  [attn_forward(): pl.pallas_call(kernel, out_shape=[four, jax.ShapeDtypeStruct((8, seq, wid...]
    pallas_call x1, Pallas kernels: 83 us -> 77.6 us  [attn_backward(): pl.pallas_call(kernel, out_shape=[jax.ShapeDtypeStruct((2, 2, own, width)...]
    unnamed x35 -> x45, local copies, waits for them, and re-layouts: 13.8 us -> 16.4 us
where the time goes in v10:
time: 371 us; the launch traced here: 364 us
  Pallas kernels  323 us (87%)
  local copies, waits for them, and re-layouts  31.2 us (8%)
  other arithmetic  8.4 us (2%)
    pallas_call x1, Pallas kernels, attn_forward(): pl.pallas_call(kernel, out_shape=[four, jax.ShapeDtypeStruct((8, seq, wid...  137 us
    pallas_call x1, Pallas kernels, attn_backward(): pl.pallas_call(kernel, out_shape=[jax.ShapeDtypeStruct((2, 2, own, width)...  77.6 us
    pallas_call x1, Pallas kernels, middle(): pl.pallas_call(kernel, out_shape=[jax.ShapeDtypeStruct((own, width), F32)...  77.3 us
    pallas_call x1, Pallas kernels, experts(): pl.pallas_call(kernel, grid=(4,), out_shape=[jax.ShapeDtypeStruct((rows,...  30.8 us
    unnamed x45, local copies, waits for them, and re-layouts  16.4 us

profile of v10, /device:TPU:0, one launch (start us, length us, event | category | flops | bytes accessed | tf_op | source)
XLA Modules:
  0.0 364.1 jit_solution(9401393724866101491)
XLA Ops:
  0.6 0.0 slice-start
  0.7 0.7 convert.14
  1.4 0.7 convert.15
  2.1 0.1 pad.23.clone
  2.2 0.1 pad_maximum_fusion.4
  2.2 0.1 pad.18.clone
  2.3 0.7 concatenate.36
  3.0 0.7 concatenate.37
  3.8 0.1 copy.56
  3.9 0.6 pad.5.route_ref
  4.5 0.8 maximum_convert_fusion.1
  5.3 0.1 copy.59
  5.3 0.1 maximum_bitcast_fusion.3
  5.4 0.8 reshape.127.small_ref.gain_ref
  6.2 0.9 slice.64
  7.2 0.1 copy.51
  7.3 0.1 broadcast_in_dim.6
  7.5 0.1 reshape.122
  7.6 0.1 reshape.120
  7.6 0.5 copy_bitcast_fusion.3
  8.2 0.0 copy-start.8
  8.2 0.9 pad_maximum_fusion
  9.1 1.8 reshape.123.a_ref
  10.9 0.3 slice_bitcast_fusion.1
  11.2 0.6 pad_maximum_fusion.3
  11.7 1.0 copy.55
  12.7 2.0 fusion.1
  14.7 0.2 copy_bitcast_fusion
  14.9 0.1 slice_bitcast_fusion.3
  15.0 0.9 pad_maximum_fusion.2
  15.9 0.1 slice_bitcast_fusion.5
  16.0 0.9 pad_maximum_fusion.1
  16.9 137.3 %attn_forward.1 = (bf16[4,8,64,768]{3,2,1,0:T(8,128)(2,1)}, bf16[8,128,2048]{2,1,0:T(8,128)(2,1)}, bf16[8,128,512]{2,1,0:T(8,128)(2,1)}, bf16[8,128,256]{2,1,0:T...) custom-call(bf16[8,64,768]{2,1,0:T(8,128)(2,1)} %reshape.123.a_ref, ...), custom_call_target="tpu_custom_call" | custom-call | bytes 209715200 | tf_op jit(solution)/shard_map/attn_forward/pallas_call | solution.py:700
  154.2 1.0 copy-done
  155.3 0.9 copy-done.5
  156.2 30.8 %experts.1 = (bf16[1024,768]{1,0:T(8,128)(2,1)S(1)}, bf16[1024,768]{1,0:T(8,128)(2,1)S(1)}, bf16[1024,768]{1,0:T(8,128)(2,1)S(1)}, bf16[1024,2048]{1,0:T(8,128)(...) custom-call(bf16[1024,2048]{1,0:T(8,128)(2,1)} %bitcast.88, bf16[1024,2048]{1,0:T(8,128)(2,1)} %bitcast.90, ...), custom_call_target="tpu_custom_call" | custom-call | flops 19327352832 | bytes 41943040 | tf_op jit(solution)/shard_map/experts/pallas_call | solution.py:773
  187.0 1.1 copy-done.1
  188.2 1.1 copy-done.2
  189.3 1.1 copy-done.3
  190.4 0.8 copy-done.4
  191.2 77.3 %middle.1 = (f32[32,2048]{1,0:T(8,128)}, f32[16,2048]{1,0:T(8,128)}, bf16[2,4,2,2,32,2048]{5,4,3,2,1,0:T(8,128)(2,1)}, bf16[8,64,768]{2,1,0:T(8,128)(2,1)}, bf16...) custom-call(bf16[2,4,2,2,32,2176]{5,4,3,2,1,0:T(8,128)(2,1)} %bitcast.87, ...), custom_call_target="tpu_custom_call" | custom-call | bytes 209715200 | tf_op jit(solution)/shard_map/middle/pallas_call | solution.py:917
  268.5 77.6 %attn_backward.1 = (bf16[2,2,32,2048]{3,2,1,0:T(8,128)(2,1)}, f32[16,128]{1,0:T(8,128)}, f32[16,128]{1,0:T(8,128)}, f32[4,2048]{1,0:T(4,128)}, f32[4,2048]{1,0:T...) custom-call(bf16[8,128,2048]{2,1,0:T(8,128)(2,1)} %bitcast.92, ...), custom_call_target="tpu_custom_call" | custom-call | bytes 209715200 | tf_op jit(solution)/shard_map/attn_backward/pallas_call | solution.py:1134
  346.2 1.1 slice_bitcast_fusion.6
  347.3 1.0 slice_bitcast_fusion.7
  348.3 1.1 slice_bitcast_fusion.8
  349.4 0.1 maximum_bitcast_fusion.1
  349.5 0.0 copy-done.10
  349.5 0.1 maximum_bitcast_fusion.2
  349.6 1.0 copy-done.9
  350.6 0.1 copy-done.12
  350.7 1.1 bitcast_convert_fusion
  351.8 0.1 convert_bitcast_fusion
  351.9 2.0 copy.62
  354.0 0.1 fusion.2
  354.0 1.1 copy.70
  355.2 0.2 convert_element_type.22
  355.4 1.0 maximum_bitcast_fusion
  356.4 0.2 maximum_convert_fusion
  356.6 3.8 %copy.61 = f32[64,4,2,1408]{3,2,1,0:T(2,128)} copy(f32[64,4,2,1408]{3,0,1,2:T(8,128)S(1)} %maximum_convert_fusion) | data formatting | bytes 5767168
  360.4 0.8 copy.76
  361.2 0.6 copy.77
  361.8 0.6 copy.78
  362.4 0.6 copy.79
  363.1 0.6 copy.80
  (38 shorter events, 0.2 us)
Async XLA Ops:
  0.6 6.9 %slice-start = ((bf16[64,6,512]{2,0,1:T(8,128)(2,1)}), bf16[64,4,512]{2,0,1:T(8,128)(2,1)S(1)}, s32[]{:S(2)}) async-start(bf16[64,6,512]{2,0,1:T(8,128)(2,1)} %param.20), calls=%async_computation | async-start | bytes 524288 | tf_op jit(solution)/shard_map/slice | solution.py:1209
  0.7 6.8 %copy-start.14 = (bf16[64,4,512]{2,1,0:T(4,128)(2,1)S(1)}, bf16[64,4,512]{2,1,0:T(4,128)(2,1)}, u32[]{:S(2)}) copy-start(bf16[64,4,512]{2,1,0:T(4,128)(2,1)} %param.21) | copy-start | bytes 786436
  8.2 2.7 copy-start.8
  11.2 1.5 copy-start.6
  154.2 1.0 copy-start
  155.3 0.9 copy-start.5
  187.0 1.1 copy-start.1
  188.2 1.1 copy-start.2
  189.3 1.1 copy-start.3
  190.4 0.8 copy-start.4
  346.2 3.2 copy-start.11
  348.3 1.2 copy-start.10
  349.4 1.2 copy-start.9
  349.5 1.2 copy-start.12
  351.9 2.0 copy-start.7
  356.6 3.9 %copy-start.13 = (bf16[2,2,32,2048]{3,2,1,0:T(8,128)(2,1)S(1)}, bf16[2,2,32,2048]{3,2,1,0:T(8,128)(2,1)}, u32[]{:S(2)}) copy-start(bf16[2,2,32,2048]{3,2,1,0:T(8,128)(2,1)} %get-tuple-element.62) | copy-start | bytes 1572868
  356.6 4.6 %copy-start.18 = (f32[16,128]{1,0:T(8,128)S(1)}, f32[16,128]{1,0:T(8,128)}, u32[]{:S(2)}) copy-start(f32[16,128]{1,0:T(8,128)} %get-tuple-element.76) | copy-start | bytes 24580
  356.6 5.2 %copy-start.16 = (f32[4,2048]{1,0:T(4,128)S(1)}, f32[4,2048]{1,0:T(4,128)}, u32[]{:S(2)}) copy-start(f32[4,2048]{1,0:T(4,128)} %get-tuple-element.77) | copy-start | bytes 98308
  356.6 5.8 %copy-start.17 = (f32[16,128]{1,0:T(8,128)S(1)}, f32[16,128]{1,0:T(8,128)}, u32[]{:S(2)}) copy-start(f32[16,128]{1,0:T(8,128)} %get-tuple-element.79) | copy-start | bytes 24580
  356.6 6.4 %copy-start.15 = (f32[4,2048]{1,0:T(4,128)S(1)}, f32[4,2048]{1,0:T(4,128)}, u32[]{:S(2)}) copy-start(f32[4,2048]{1,0:T(4,128)} %get-tuple-element.80) | copy-start | bytes 98308

commit v11 on v10

--- a/solution.py
+++ b/solution.py
@@ -291,7 +291,7 @@
             self.copy(k).wait_recv()
         total = self.part[self.y].astype(F32) + self.sums[0].astype(F32) + self.sums[1].astype(F32)
         total = total.astype(BF)
-        if len(out.shape) == 3:
+        if len(out.shape) < 4:
             out[...] = total.reshape(out.shape)
         else:
             targets, count, rows, cols = out.shape
@@ -730,63 +730,6 @@
     )(attn_blocks, *blocks, hidden, cotangent, routes, small, cosines, sines)[:15]
 
 
-def experts(normed, cotangent, routes, routers, weights, extra):
-    rows, width = normed.shape
-    part = weights[0].shape[1]
-    tile = rows // 4
-
-    def kernel(x_ref, cot_ref, route_ref, router_ref, wg, wu, wd, h_out, dg_out, du_out, branch_out, back_out, gates_out):
-        lane = EXPERTS + lax.axis_index("x")
-        skip = lax.axis_index("zl") * extra
-        x = x_ref[...]
-        logits = mm_nt(x, router_ref[...])
-        index = lanes(tile)
-        gates = dense_gates(logits, chosen(route_ref[...].astype(F32), EXPERTS))
-        gates_out[...] = gates
-        valid = (lax.broadcasted_iota(jnp.int32, (1, part), 1) >= skip).astype(F32)
-        gate = pick(gates, lane) * valid
-        gate_part = mm(x, wg[...])
-        up_part = mm(x, wu[...])
-        sigma = 1.0 / (1.0 + jnp.exp(-gate_part))
-        silu = gate_part * sigma
-        activated = silu * up_part
-        h = (activated * gate).astype(BF)
-        h_out[...] = h
-        branch_out[...] = mm_nt(h, wd[...]).astype(BF)
-        cot_down = mm(cot_ref[...], wd[...])
-        dots = jnp.sum(activated * valid * cot_down, axis=1, keepdims=True)
-        grad_act = cot_down * gate
-        grad_gate = (grad_act * up_part * sigma * (1.0 + gate_part * (1.0 - sigma))).astype(BF)
-        grad_up = (grad_act * silu).astype(BF)
-        dg_out[...] = grad_gate
-        du_out[...] = grad_up
-        back_out[:, :width] = (mm_nt(grad_gate, wg[...]) + mm_nt(grad_up, wu[...])).astype(BF)
-        back_out[:, width:] = jnp.where(index == lane, dots, 0.0).astype(BF)
-
-    def tiled(cols):
-        return pl.BlockSpec((tile, cols), lambda i: (i, 0))
-
-    def whole(array):
-        return pl.BlockSpec(array.shape, lambda i: (0, 0), pipeline_mode=pl.Buffered(1))
-
-    cols = [part, part, part, width, width + LANE]
-    return pl.pallas_call(
-        kernel,
-        grid=(4,),
-        out_shape=[jax.ShapeDtypeStruct((rows, c), BF) for c in cols]
-        + [jax.ShapeDtypeStruct((rows, LANE), F32)],
-        in_specs=[tiled(width), tiled(width)]
-        + [tiled(LANE), whole(routers)]
-        + [whole(w) for w in weights],
-        out_specs=[tiled(c) for c in cols] + [tiled(LANE)],
-        compiler_params=pltpu.CompilerParams(vmem_limit_bytes=48 << 20),
-        cost_estimate=pl.CostEstimate(
-            flops=12 * rows * width * part, bytes_accessed=40 << 20, transcendentals=rows * part
-        ),
-        name="experts",
-    )(normed, cotangent, routes, routers, *weights)
-
-
 def back_through_norm(total, inputs, gain, gates, normed, routers):
     width = inputs.shape[1]
     logits_back = gates_back(gates, total[:, width:])
@@ -833,20 +776,19 @@
     return zl * 4 + x, zh * 2 + c
 
 
-def middle(collective, back, branch, normed, cotangent, grads, after, small, gates, routers, cot_own):
+def experts(collective, normed, cotangent, routes, weights, after, small, routers, cot_own, extra):
     own, width = after.shape
-    count, cols = grads[0].shape
+    count = normed.shape[0]
+    cols = weights[0].shape[1]
     rows = width // 4
+    tile = count // 4
 
     def kernel(
-        part_ref, branch_ref, x_ref, cot_ref, d0_ref, d1_ref, d2_ref,
-        after_ref, small_ref, gates_ref, router_ref, own_ref,
+        x_ref, cot_ref, wg_ref, wu_ref, wd_ref, route_ref, after_ref, small_ref, router_ref, own_ref,
         mid_out, small_out, spread_out, s0, s1, g2, out_all,
-        x, cot, d0, d1, d2, g0, g1, part_a, part_b, load, total_a, total_b, row_a, row_b, *rest,
+        x, cot, wg, wu, wd, h, dg, du, g0, gates, part_a, part_b, load, total_a, total_b, row_a, row_b, *rest,
     ):
-        loads = [
-            (x_ref, x), (d0_ref, d0), (part_ref, part_a), (branch_ref, part_b), (d1_ref, d1), (cot_ref, cot), (d2_ref, d2)
-        ]
+        loads = [(x_ref, x), (wg_ref, wg), (wu_ref, wu), (cot_ref, cot), (wd_ref, wd)]
         fetches = [pltpu.make_async_copy(a, b, load.at[k]) for k, (a, b) in enumerate(loads)]
         for fetch in fetches:
             fetch.start()
@@ -855,10 +797,71 @@
         team_a, team_b = TeamSum(part_a, rest[:n]), TeamSum(part_b, rest[n : 2 * n])
         rest = rest[2 * n :]
         n = RingSum.count
-        rings = [RingSum(g0, rest[:n]), RingSum(g1, rest[n : 2 * n])]
+        rings = [RingSum(g0, rest[:n]), RingSum(wg, rest[n : 2 * n])]
         rest = rest[2 * n :]
         spread = TeamSpread(row_a, spread_out, rest[:4])
         out = Pass(row_b, out_all, rest[4:6])
+        gate_w, up_w = wg.reshape(width, cols), wu.reshape(width, cols)
+        lane = EXPERTS + lax.axis_index("x")
+        skip = lax.axis_index("zl") * extra
+
+        def tokens(pair):
+            return pl.ds(pl.multiple_of(pair * tile, tile), tile)
+
+        def forward(pair, _):
+            at = tokens(pair)
+            x_t = x[at]
+            gates_t = dense_gates(mm_nt(x_t, router_ref[...]), chosen(route_ref[at].astype(F32), EXPERTS))
+            gates[at] = gates_t
+            valid = (lax.broadcasted_iota(jnp.int32, (1, cols), 1) >= skip).astype(F32)
+            gate = pick(gates_t, lane) * valid
+            gate_part = mm(x_t, gate_w[...])
+            up_part = mm(x_t, up_w[...])
+            sigma = 1.0 / (1.0 + jnp.exp(-gate_part))
+            silu = gate_part * sigma
+            activated = silu * up_part
+            h[at] = (activated * gate).astype(BF)
+
+            @pl.when(pair == 0)
+            def _():
+                fetches[3].wait()
+                fetches[4].wait()
+
+            cot_down = mm(cot[at], wd[...])
+            dots = jnp.sum(activated * valid * cot_down, axis=1, keepdims=True)
+            grad_act = cot_down * gate
+            dg[at] = (grad_act * up_part * sigma * (1.0 + gate_part * (1.0 - sigma))).astype(BF)
+            du[at] = (grad_act * silu).astype(BF)
+            hot = jnp.where(lanes(tile) == lane, dots, 0.0).astype(BF)
+            part_a[pair // 2, pl.ds(lax.rem(pair, 2) * 2, 2), :, :, :, width:] = hot.reshape(
+                2, 2, 2, own, LANE
+            )
+            return 0
+
+        def summed(team, columns, values):
+            def step(i, _):
+                pair = team.pair(i)
+                at = (pair // 2, pl.ds(lax.rem(pair, 2) * 2, 2), slice(None), slice(None), slice(None), columns)
+                team.part[at] = values(tokens(pair)).astype(BF).reshape(2, 2, 2, own, width)
+                for j in range(2):
+                    team.swap(pair * 2 + j).start()
+
+                @pl.when(i > 0)
+                def _():
+                    team.add_pair(i - 1)
+
+                @pl.when(i == 2)
+                def _():
+                    team.send_far_z()
+
+                @pl.when(i == 3)
+                def _():
+                    team.send_far_x()
+
+                return 0
+
+            lax.fori_loop(0, 4, step, 0)
+            team.last()
 
         def product(left, right, dst):
             def one(block):
@@ -866,25 +869,22 @@
 
             return one
 
-        fetches[0].wait()
-        fetches[1].wait()
-        rings[0].start_with(product(x, d0, g0))
-        fetches[2].wait()
-        team_a.swap_all()
-        fetches[3].wait()
-        team_b.swap_all()
-        team_a.add_all()
-        fetches[4].wait()
-        rings[1].start_with(product(x, d1, g1))
+        for fetch in fetches[:3]:
+            fetch.wait()
+        lax.fori_loop(0, 4, forward, 0)
+        rings[0].start_with(product(x, dg, g0))
+        summed(team_a, slice(0, width), lambda at: mm_nt(dg[at], gate_w[...]) + mm_nt(du[at], up_w[...]))
         rings[0].middle()
+        rings[1].start_with(product(x, du, wg))
         team_a.total1(total_a)
-        team_b.add_all()
+        summed(team_b, slice(0, width), lambda at: mm_nt(h[at], wd[...]))
         after = after_ref[...]
         normed_own = (after * rms_scale(after) * small_ref[1:2]).astype(BF)
         seq, quarter = own_tile()
+        gates_own = gates[pl.ds(pl.multiple_of((seq * 4 + quarter) * own, own), own)]
         team_a.total2(total_a)
         inner, gain_grad, router_grad = back_through_norm(
-            total_a[...], after, small_ref[1:2], gates_ref[seq * 4 + quarter], normed_own, router_ref[...]
+            total_a[...], after, small_ref[1:2], gates_own, normed_own, router_ref[...]
         )
         grad_mid = own_ref[...].astype(F32) + inner
         mid_out[...] = grad_mid
@@ -894,23 +894,29 @@
         small_out[:8] = jnp.zeros((8, width), F32)
         small_out[0:1] = gain_grad
         small_out[8:] = router_grad
-        fetches[5].wait()
-        fetches[6].wait()
 
         def down(block, _):
-            product(cot, d2, g2)(block)
+            product(cot, h, wu)(block)
             return 0
 
         lax.fori_loop(0, 4, down, 0)
+        keep = pltpu.make_async_copy(wu, g2, load.at[0])
+        keep.start()
         spread.middle()
         team_b.total1(total_b)
         spread.finish()
         team_b.total2(total_b)
         row_b[...] = in_order((after + total_b[...]).astype(BF))
         out.start()
-        rings[0].finish(s0)
-        rings[1].finish(s1)
+        stores = []
+        for ring, buffer, dst, k in ((rings[0], dg, s0, 1), (rings[1], du, s1, 2)):
+            ring.finish(buffer.at[pl.ds(0, rows)])
+            stores.append(pltpu.make_async_copy(buffer.at[pl.ds(0, rows)], dst, load.at[k]))
+            stores[-1].start()
         out.finish()
+        keep.wait()
+        for store in stores:
+            store.wait()
         team_a.close()
         team_b.close()
 
@@ -920,24 +926,27 @@
             jax.ShapeDtypeStruct((own, width), F32),
             jax.ShapeDtypeStruct((16, width), F32),
             jax.ShapeDtypeStruct((2, 4, 2, 2, own, width), BF),
-            jax.ShapeDtypeStruct((8, rows // 8, cols), BF),
-            jax.ShapeDtypeStruct((8, rows // 8, cols), BF),
+            jax.ShapeDtypeStruct((rows, cols), BF),
+            jax.ShapeDtypeStruct((rows, cols), BF),
             jax.ShapeDtypeStruct((4, rows, cols), BF),
             jax.ShapeDtypeStruct((2, 2, own, width), BF),
         ],
-        in_specs=[ANY] * 7 + [VMEM] * 5,
-        out_specs=[VMEM] * 2 + [ANY] + [VMEM] * 3 + [ANY],
+        in_specs=[ANY] * 5 + [VMEM] * 5,
+        out_specs=[VMEM] * 2 + [ANY] * 5,
         scratch_shapes=[
             pltpu.VMEM((count, width), BF),
             pltpu.VMEM((count, width), BF),
+            pltpu.VMEM((4, rows, cols), BF),
+            pltpu.VMEM((4, rows, cols), BF),
+            pltpu.VMEM((width, cols), BF),
             pltpu.VMEM((count, cols), BF),
             pltpu.VMEM((count, cols), BF),
             pltpu.VMEM((count, cols), BF),
             pltpu.VMEM((4, rows, cols), BF),
-            pltpu.VMEM((4, rows, cols), BF),
+            pltpu.VMEM((count, LANE), F32),
             pltpu.VMEM((2, 4, 2, 2, own, width + LANE), BF),
             pltpu.VMEM((2, 4, 2, 2, own, width), BF),
-            pltpu.SemaphoreType.DMA((7,)),
+            pltpu.SemaphoreType.DMA((5,)),
             pltpu.VMEM((own, width + LANE), F32),
             pltpu.VMEM((own, width), F32),
             pltpu.VMEM((own, width), BF),
@@ -948,11 +957,11 @@
         + RingSum.scratch(rows, cols) * 2
         + TeamSpread.sems
         + Pass.sems,
-        name="middle",
-        **settings(collective, 200 << 20, 58),
+        name="experts",
+        **settings(collective, 300 << 20, 61),
     )(
-        back.reshape(2, 4, 2, 2, own, width + LANE), branch.reshape(2, 4, 2, 2, own, width),
-        normed, cotangent, *grads, after, small, gates.reshape(-1, own, LANE), routers, cot_own,
+        normed, cotangent, *[w.reshape(4, rows, cols) for w in weights[:2]], weights[2], routes,
+        after, small, routers, cot_own,
     )
 
 
@@ -1237,12 +1246,11 @@
     group_cot = group_cot.reshape(group, width)
     normed_m = normed_m.reshape(group, width)
 
-    h, grad_gate, grad_up, branch_m, back_m, gates_m = experts(
-        normed_m, group_cot, group_routes.reshape(group, LANE), routers, mlp_w, 2 * part - features
+    grad_mid_own, small_m, grad_mid, gate_sum, up_sum, down_part, out_hidden = experts(
+        2, normed_m, group_cot, group_routes.reshape(group, LANE), mlp_w, after, small, routers, cot_own,
+        2 * part - features,
     )
-    grad_mid_own, small_m, grad_mid, gate_sum, up_sum, down_part, out_hidden = middle(
-        2, back_m, branch_m, normed_m, group_cot, [grad_gate, grad_up, h], after, small, gates_m, routers, cot_own
-    )
+    gate_sum, up_sum = (a.reshape(8, rows, part) for a in (gate_sum, up_sum))
     grad_in, gain_a, gain_m, router_a, router_m, *mlp_grads, attn_grads = attn_backward(
         3, grad_mid, qkv, gated_att, normed_a, gates_a, attn_w, cosines, sines, grad_mid_own, entered, small,
         routers, small_m, [gate_sum, up_sum], down_part,

time: 371 us -> 357 us (0.962)
  Pallas kernels: 323 us -> 315 us
  local copies, waits for them, and re-layouts: 31.2 us -> 25 us
    pallas_call x2 -> x1, Pallas kernels: 108 us -> 98.6 us  [experts(): pl.pallas_call(kernel, out_shape=[jax.ShapeDtypeStruct((own, width), F32)...]
    unnamed x45 -> x33, local copies, waits for them, and re-layouts: 16.4 us -> 11.2 us
where the time goes in v11:
time: 357 us; the launch traced here: 350 us
  Pallas kernels  315 us (88%)
  local copies, waits for them, and re-layouts  25 us (7%)
  other arithmetic  8.39 us (2%)
    pallas_call x1, Pallas kernels, attn_forward(): pl.pallas_call(kernel, out_shape=[four, jax.ShapeDtypeStruct((8, seq, wid...  137 us
    pallas_call x1, Pallas kernels, experts(): pl.pallas_call(kernel, out_shape=[jax.ShapeDtypeStruct((own, width), F32)...  98.6 us
    pallas_call x1, Pallas kernels, attn_backward(): pl.pallas_call(kernel, out_shape=[jax.ShapeDtypeStruct((2, 2, own, width)...  79.2 us
    unnamed x33, local copies, waits for them, and re-layouts  11.2 us

profile of v11, /device:TPU:0, one launch (start us, length us, event | category | flops | bytes accessed | tf_op | source)
XLA Modules:
  0.0 350.0 jit_solution(8577854562647169236)
XLA Ops:
  0.7 0.7 convert.14
  1.4 0.7 convert.15
  2.1 0.1 pad.23.clone
  2.1 0.1 pad_maximum_fusion.4
  2.2 0.1 pad.18.clone
  2.3 0.7 concatenate.36
  3.0 0.7 concatenate.37
  3.7 0.1 copy.56
  3.9 0.6 pad.5.route_ref
  4.5 0.8 maximum_convert_fusion.1
  5.2 0.0 slice-start
  5.3 0.1 copy.59
  5.3 0.1 maximum_bitcast_fusion.3
  5.4 0.8 reshape.118.small_ref.gain_ref
  6.2 0.9 slice.64
  7.1 0.1 copy.51
  7.3 0.1 broadcast_in_dim.6
  7.4 0.1 reshape.113
  7.6 0.1 reshape.111
  7.6 0.5 copy_bitcast_fusion.3
  8.2 0.0 copy-start.2
  8.2 0.9 pad_maximum_fusion
  9.1 1.8 reshape.114.a_ref
  10.9 0.0 copy-done.2
  10.9 0.3 slice_bitcast_fusion.1
  11.1 0.0 copy-start
  11.1 0.6 pad_maximum_fusion.3
  11.7 1.0 copy.55
  12.7 2.0 fusion.1
  14.7 0.2 copy_bitcast_fusion
  14.9 0.1 slice_bitcast_fusion.3
  14.9 0.9 pad_maximum_fusion.2
  15.9 0.1 slice_bitcast_fusion.5
  16.0 0.9 pad_maximum_fusion.1
  16.9 137.3 %attn_forward.1 = (bf16[4,8,64,768]{3,2,1,0:T(8,128)(2,1)}, bf16[8,128,2048]{2,1,0:T(8,128)(2,1)}, bf16[8,128,512]{2,1,0:T(8,128)(2,1)}, bf16[8,128,256]{2,1,0:T...) custom-call(bf16[8,64,768]{2,1,0:T(8,128)(2,1)} %reshape.114.a_ref, ...), custom_call_target="tpu_custom_call" | custom-call | bytes 209715200 | tf_op jit(solution)/shard_map/attn_forward/pallas_call | solution.py:700
  154.2 98.6 %experts.1 = (f32[32,2048]{1,0:T(8,128)}, f32[16,2048]{1,0:T(8,128)}, bf16[2,4,2,2,32,2048]{5,4,3,2,1,0:T(8,128)(2,1)}, bf16[512,768]{1,0:T(8,128)(2,1)}, bf16[5...) custom-call(bf16[1024,2048]{1,0:T(8,128)(2,1)} %bitcast.85, ...), custom_call_target="tpu_custom_call" | custom-call | bytes 314572800 | tf_op jit(solution)/shard_map/experts/pallas_call | solution.py:923
  252.8 79.2 %attn_backward.1 = (bf16[2,2,32,2048]{3,2,1,0:T(8,128)(2,1)}, f32[16,128]{1,0:T(8,128)}, f32[16,128]{1,0:T(8,128)}, f32[4,2048]{1,0:T(4,128)}, f32[4,2048]{1,0:T...) custom-call(bf16[8,128,2048]{2,1,0:T(8,128)(2,1)} %bitcast.84, ...), custom_call_target="tpu_custom_call" | custom-call | bytes 209715200 | tf_op jit(solution)/shard_map/attn_backward/pallas_call | solution.py:1143
  332.1 1.1 slice_bitcast_fusion.6
  333.1 1.0 slice_bitcast_fusion.7
  334.2 0.1 maximum_bitcast_fusion.1
  334.3 1.0 copy-done.4
  335.3 0.1 maximum_bitcast_fusion.2
  335.4 1.0 copy-done.3
  336.4 0.1 copy-done.6
  336.6 1.1 bitcast_convert_fusion
  337.7 0.1 convert_bitcast_fusion
  337.8 2.0 copy.62
  339.8 0.1 fusion.2
  339.9 1.1 copy.70
  341.0 0.2 convert_element_type.22
  341.3 1.0 maximum_bitcast_fusion
  342.2 0.2 maximum_convert_fusion
  342.4 0.0 copy-start.7
  342.4 0.0 copy-start.12
  342.5 0.0 copy-start.10
  342.5 0.0 copy-start.11
  342.5 0.0 copy-start.9
  342.5 3.8 %copy.61 = f32[64,4,2,1408]{3,2,1,0:T(2,128)} copy(f32[64,4,2,1408]{3,0,1,2:T(8,128)S(1)} %maximum_convert_fusion) | data formatting | bytes 5767168
  346.3 0.0 copy-done.7
  346.3 0.8 copy.76
  347.1 0.6 copy.77
  347.7 0.6 copy.78
  348.3 0.6 copy.79
  348.9 0.6 copy.80
  (25 shorter events, 0.2 us)
Async XLA Ops:
  0.6 6.8 %copy-start.8 = (bf16[64,4,512]{2,1,0:T(4,128)(2,1)S(1)}, bf16[64,4,512]{2,1,0:T(4,128)(2,1)}, u32[]{:S(2)}) copy-start(bf16[64,4,512]{2,1,0:T(4,128)(2,1)} %param.21) | copy-start | bytes 786436
  5.2 2.3 slice-start
  8.2 2.7 copy-start.2
  11.1 1.5 copy-start
  332.0 2.1 copy-start.5
  334.1 1.1 copy-start.4
  335.3 1.1 copy-start.3
  335.3 1.3 copy-start.6
  337.8 2.0 copy-start.1
  342.4 3.9 %copy-start.7 = (bf16[2,2,32,2048]{3,2,1,0:T(8,128)(2,1)S(1)}, bf16[2,2,32,2048]{3,2,1,0:T(8,128)(2,1)}, u32[]{:S(2)}) copy-start(bf16[2,2,32,2048]{3,2,1,0:T(8,128)(2,1)} %get-tuple-element.50) | copy-start | bytes 1572868
  342.4 4.6 %copy-start.12 = (f32[16,128]{1,0:T(8,128)S(1)}, f32[16,128]{1,0:T(8,128)}, u32[]{:S(2)}) copy-start(f32[16,128]{1,0:T(8,128)} %get-tuple-element.64) | copy-start | bytes 24580
  342.5 5.2 %copy-start.10 = (f32[4,2048]{1,0:T(4,128)S(1)}, f32[4,2048]{1,0:T(4,128)}, u32[]{:S(2)}) copy-start(f32[4,2048]{1,0:T(4,128)} %get-tuple-element.65) | copy-start | bytes 98308
  342.5 5.8 %copy-start.11 = (f32[16,128]{1,0:T(8,128)S(1)}, f32[16,128]{1,0:T(8,128)}, u32[]{:S(2)}) copy-start(f32[16,128]{1,0:T(8,128)} %get-tuple-element.67) | copy-start | bytes 24580
  342.5 6.4 %copy-start.9 = (f32[4,2048]{1,0:T(4,128)S(1)}, f32[4,2048]{1,0:T(4,128)}, u32[]{:S(2)}) copy-start(f32[4,2048]{1,0:T(4,128)} %get-tuple-element.68) | copy-start | bytes 98308

commit v12 on v11

--- a/solution.py
+++ b/solution.py
@@ -65,8 +65,8 @@
     return jnp.sum(jnp.where(lanes(values.shape[0]) == lane, values, 0.0), axis=1, keepdims=True)
 
 
-def gates_back(gates, dots):
-    return gates * (dots - jnp.sum(gates * dots, axis=1, keepdims=True))
+def gates_back(gates, gated_dots):
+    return gated_dots - gates * jnp.sum(gated_dots, axis=1, keepdims=True)
 
 
 def rope_tables(count):
@@ -180,6 +180,43 @@
         for k in range(4):
             self.copy(k).wait_send()
         self.stay.wait()
+
+    def finish_first(self):
+        for k in range(2):
+            self.copy(k).wait()
+        self.stay.wait()
+
+
+class RingRest:
+    sems = [pltpu.SemaphoreType.DMA((5,)), pltpu.SemaphoreType.DMA((2,))]
+
+    def __init__(self, src, out, sems):
+        self.y = lax.axis_index("y")
+        rows = src.shape[1] // 2
+        send, recv = sems
+        self.copies = [
+            pltpu.make_async_copy(src.at[self.line(step)], out.at[self.line(step)], send.at[2 + k])
+            for k, step in enumerate((0, 1, 3))
+        ]
+        for k in range(2):
+            here = (self.line((3, 1)[k]), pl.ds(k * rows, rows))
+            to = {"y": self.line((1, 3)[k])}
+            self.copies.append(push(src.at[here], out.at[here], send.at[k], recv.at[k], to))
+
+    def line(self, step):
+        return lax.rem(self.y + step, 4)
+
+    def start_here(self):
+        for copy in self.copies[:3]:
+            copy.start()
+
+    def start(self):
+        for copy in self.copies[3:]:
+            copy.start()
+
+    def finish(self):
+        for copy in self.copies:
+            copy.wait()
 
 
 class Swap:
@@ -212,6 +249,25 @@
     def finish(self):
         for copy in self.copies:
             copy.wait()
+
+
+class ExpertSwap(Swap):
+    def start(self):
+        me = number(place(GROUP_MOVES[0]))
+        part = self.dst.shape[2]
+        low = self.src.shape[2] - part
+        self.copies = []
+        for k, move in enumerate(GROUP_MOVES):
+            to = place(move)
+            block = self.src.at[to["x"], :, pl.ds(pl.multiple_of(to["zl"] * low, LANE), part)]
+            if k:
+                self.copies.append(
+                    push(block, self.dst.at[me], self.send.at[k], self.recv.at[k], to)
+                )
+            else:
+                self.copies.append(pltpu.make_async_copy(block, self.dst.at[me], self.send.at[0]))
+        for copy in self.copies:
+            copy.start()
 
 
 class ColumnSwap(Swap):
@@ -559,7 +615,7 @@
 
 
 def attn_forward(
-    collective, attn_blocks, blocks, hidden, cotangent, routes, small, cosines, sines
+    collective, attn_blocks, blocks, part_cols, hidden, cotangent, gains, routers, routes, cosines, sines
 ):
     seq, width = hidden.shape
     own = seq // 4
@@ -567,18 +623,18 @@
     scale = HEAD ** (-0.5)
 
     def kernel(
-        a_ref, b0, b1, b2, hidden_ref, cotangent_ref, route_ref, small_ref, cos_ref, sin_ref,
-        w_out, normed_out, qkv_out, gated_out, gates_out, routes_out, after_out, enter_row, cot_row, router_ref,
+        a_ref, b0, b1, b2, hidden_ref, cotangent_ref,
+        gain_a, gain_m, router_a, router_m, route_a, route_m, cos_ref, sin_ref,
+        w_out, normed_out, qkv_out, gated_out, gates_out, routes_out, after_out, enter_row, cot_row, router_ref, small_ref,
         spread_out, cot_out, w0, w1, w2, a_mid, m0, m1, m2,
-        load, hid, part, total, row, *rest,
+        turned, load, hid, part, total, row, *rest,
     ):
-        mine = pl.ds(pl.multiple_of((lax.axis_index("zh") * 2 + lax.axis_index("c")) * own, own), own)
+        mine = pl.ds(pl.multiple_of(own_tile()[1] * own, own), own)
         loads = []
         for b in range(8):
             here, there = pl.ds(b * piece, piece), pl.ds(((b % 4) * 2 + b // 4) * piece, piece)
             loads.append((hidden_ref.at[mine, here], enter_row.at[:, there]))
             loads.append((cotangent_ref.at[mine, here], cot_row.at[:, there]))
-        loads.append((route_ref.at[mine], enter_row.at[:, pl.ds(width, LANE)]))
         fetches = [pltpu.make_async_copy(a, b, load.at[k]) for k, (a, b) in enumerate(loads)]
         for fetch in fetches:
             fetch.start()
@@ -589,20 +645,32 @@
         cot = TeamSpread(cot_row, cot_out, rest[4:8])
         spread = TeamSpread(row, spread_out, rest[8:12])
         rest = rest[12:]
-        swaps = [
-            Swap(b, m, rest[2 * k : 2 * k + 2])
-            for k, (b, m) in enumerate(((a_ref, a_mid), (b0, m0), (b1, m1), (b2, m2)))
+        swaps = [Swap(a_ref, a_mid, rest[:2])] + [
+            ExpertSwap(b, m, rest[2 * k : 2 * k + 2])
+            for k, (b, m) in ((1, (b0, m0)), (2, (b1, m1)), (3, (b2, m2)))
         ]
         rings = [
             RingY(m, w, rest[8 + 2 * k : 10 + 2 * k])
             for k, (m, w) in enumerate(((a_mid, w_out), (m0, w0), (m1, w1), (m2, w2)))
         ]
         swaps[0].start()
+        named = [route_a[...], jnp.zeros_like(route_a), route_m[...], jnp.zeros((LANE - 6, seq), jnp.int32)]
+        turned[...] = jnp.concatenate(named, axis=0).astype(F32).T.astype(BF)
+        enter_row[:, width:] = turned[mine]
         for fetch in fetches:
             fetch.wait()
         enters.start()
+        small_ref[...] = jnp.zeros_like(small_ref)
+        for at, gain in ((0, gain_a), (1, gain_m)):
+            for b in range(8):
+                for i in range(piece // LANE):
+                    there = ((b % 4) * 2 + b // 4) * piece + i * LANE
+                    row_at = b * (piece // LANE) + i
+                    small_ref[at : at + 1, there : there + LANE] = gain[row_at : row_at + 1]
+        columns = jnp.concatenate([router_a[...].astype(F32), router_m[...].astype(F32)], axis=0)
+        columns = [columns[:, b * piece : (b + 1) * piece] for b in ((k % 2) * 4 + k // 2 for k in range(8))]
         router_ref[...] = jnp.zeros_like(router_ref)
-        router_ref[:8] = small_ref[8:].astype(BF)
+        router_ref[:8] = jnp.concatenate(columns, axis=1).astype(BF)
         swaps[0].finish()
         rings[0].start()
         swaps[1].start()
@@ -613,26 +681,34 @@
         rings[1].start()
         swaps[3].start()
         enters.finish()
-        rings[0].finish()
-        first = 2 * team.zl
-        causal = causal_mask(2, seq)
-
-        def step(i, _):
-            pair = team.pair(i)
-            zl, x = pair // 2, lax.rem(pair, 2) * 2
+
+        def ahead(pair, _):
             routes = []
             for j in range(2):
-                entered = hid[zl, x + j].reshape(seq, width + LANE)
+                entered = hid[pair // 2, lax.rem(pair, 2) * 2 + j].reshape(seq, width + LANE)
                 values = entered[:, :width].astype(F32)
                 normed_out[pair * 2 + j] = (values * rms_scale(values) * small_ref[0:1]).astype(BF)
                 routes.append(entered[:, width:])
                 routes_out[pair * 2 + j] = routes[j]
+            logits = mm_nt(normed_out[pl.ds(pair * 2, 2)].reshape(2 * seq, width), router_ref[...])
+            gates = dense_gates(logits, chosen(jnp.concatenate(routes, axis=0).astype(F32), 0))
+            gates_out[pl.ds(pair * 2, 2)] = gates.reshape(2, seq, LANE)
+            return 0
+
+        lax.fori_loop(0, 4, ahead, 0)
+        rings[0].finish()
+        swaps[2].finish()
+        rings[2].start()
+        first = 2 * team.zl
+        causal = causal_mask(2, seq)
+
+        def step(i, _):
+            pair = team.pair(i)
+            zl, x = pair // 2, lax.rem(pair, 2) * 2
             normed = normed_out[pl.ds(pair * 2, 2)].reshape(2 * seq, width)
             weights = w_out.reshape(width, 6 * HEAD)
-            logits = mm_nt(normed, router_ref[...])
             proj = mm(normed, weights[:, : 4 * HEAD])
-            gates = dense_gates(logits, chosen(jnp.concatenate(routes, axis=0).astype(F32), 0))
-            gates_out[pl.ds(pair * 2, 2)] = gates.reshape(2, seq, LANE)
+            gates = gates_out[pl.ds(pair * 2, 2)].reshape(2 * seq, LANE)
             gated = []
             for j in range(2):
                 rows = slice(j * seq, (j + 1) * seq)
@@ -663,6 +739,7 @@
             @pl.when(i == 2)
             def _():
                 team.send_far_z()
+                rings[1].forward()
 
             @pl.when(i == 3)
             def _():
@@ -672,10 +749,7 @@
 
         lax.fori_loop(0, 4, step, 0)
         team.last()
-        swaps[2].finish()
         cot.start()
-        rings[1].forward()
-        rings[2].start()
         swaps[3].finish()
         team.total1(total)
         cot.middle()
@@ -689,13 +763,15 @@
         spread.middle()
         cot.finish()
         spread.finish()
-        rings[3].forward()
         team.close()
-        for ring in rings[1:]:
+        for ring in rings[1:3]:
             ring.finish()
+        rings[3].finish_first()
 
     block = jax.ShapeDtypeStruct(attn_blocks.shape, BF)
+    block_m = jax.ShapeDtypeStruct(attn_blocks.shape[:2] + (part_cols,), BF)
     four = jax.ShapeDtypeStruct((4,) + attn_blocks.shape, BF)
+    four_m = jax.ShapeDtypeStruct((4,) + block_m.shape, BF)
     rows = jax.ShapeDtypeStruct((2, 4, 2, 2, own, width), BF)
     return pl.pallas_call(
         kernel,
@@ -710,12 +786,14 @@
             jax.ShapeDtypeStruct((own, width + LANE), BF),
             jax.ShapeDtypeStruct((own, width), BF),
             jax.ShapeDtypeStruct((LANE, width), BF),
-            rows, rows, four, four, four, block, block, block, block,
+            jax.ShapeDtypeStruct((16, width), F32),
+            rows, rows, four_m, four_m, four_m, block, block_m, block_m, block_m,
         ],
-        in_specs=[ANY] * 7 + [VMEM] * 3,
-        out_specs=[VMEM] * 10 + [ANY] * 9,
+        in_specs=[ANY] * 6 + [VMEM] * 8,
+        out_specs=[VMEM] * 11 + [ANY] * 9,
         scratch_shapes=[
-            pltpu.SemaphoreType.DMA((17,)),
+            pltpu.VMEM((seq, LANE), BF),
+            pltpu.SemaphoreType.DMA((16,)),
             pltpu.VMEM((2, 4, 2, 2, own, width + LANE), BF),
             pltpu.VMEM((2, 4, 2, 2, own, width), BF),
             pltpu.VMEM((own, width), F32),
@@ -727,7 +805,7 @@
         + RingY.sems * 4,
         name="attn_forward",
         **settings(collective, 200 << 20, 56),
-    )(attn_blocks, *blocks, hidden, cotangent, routes, small, cosines, sines)[:15]
+    )(attn_blocks, *blocks, hidden, cotangent, *gains, *routers, *routes, cosines, sines)[:16]
 
 
 def back_through_norm(total, inputs, gain, gates, normed, routers):
@@ -788,11 +866,15 @@
         mid_out, small_out, spread_out, s0, s1, g2, out_all,
         x, cot, wg, wu, wd, h, dg, du, g0, gates, part_a, part_b, load, total_a, total_b, row_a, row_b, *rest,
     ):
-        loads = [(x_ref, x), (wg_ref, wg), (wu_ref, wu), (cot_ref, cot), (wd_ref, wd)]
+        loads = [(x_ref, x), (wg_ref, wg), (wu_ref, wu), (cot_ref, cot)]
         fetches = [pltpu.make_async_copy(a, b, load.at[k]) for k, (a, b) in enumerate(loads)]
         for fetch in fetches:
             fetch.start()
+        down_rest = RingRest(wd_ref, wd, rest[:2])
+        rest = rest[2:]
+        down_rest.start_here()
         meet([place(m) for m in TEAM_MOVES[1:] + [Y_MOVES[1], Y_MOVES[3]]] + [sibling()])
+        down_rest.start()
         n = TeamSum.count
         team_a, team_b = TeamSum(part_a, rest[:n]), TeamSum(part_b, rest[n : 2 * n])
         rest = rest[2 * n :]
@@ -801,7 +883,7 @@
         rest = rest[2 * n :]
         spread = TeamSpread(row_a, spread_out, rest[:4])
         out = Pass(row_b, out_all, rest[4:6])
-        gate_w, up_w = wg.reshape(width, cols), wu.reshape(width, cols)
+        gate_w, up_w, down_w = (w.reshape(width, cols) for w in (wg, wu, wd))
         lane = EXPERTS + lax.axis_index("x")
         skip = lax.axis_index("zl") * extra
 
@@ -819,19 +901,17 @@
             up_part = mm(x_t, up_w[...])
             sigma = 1.0 / (1.0 + jnp.exp(-gate_part))
             silu = gate_part * sigma
-            activated = silu * up_part
-            h[at] = (activated * gate).astype(BF)
-
-            @pl.when(pair == 0)
-            def _():
-                fetches[3].wait()
-                fetches[4].wait()
-
-            cot_down = mm(cot[at], wd[...])
-            dots = jnp.sum(activated * valid * cot_down, axis=1, keepdims=True)
-            grad_act = cot_down * gate
-            dg[at] = (grad_act * up_part * sigma * (1.0 + gate_part * (1.0 - sigma))).astype(BF)
-            du[at] = (grad_act * silu).astype(BF)
+            h[at] = (silu * up_part * gate).astype(BF)
+            dg[at] = (up_part * sigma * (1.0 + gate_part * (1.0 - sigma)) * gate).astype(BF)
+            du[at] = (silu * gate).astype(BF)
+            return 0
+
+        def backward(pair, _):
+            at = tokens(pair)
+            cot_down = mm(cot[at], down_w[...])
+            dots = jnp.sum(h[at].astype(F32) * cot_down, axis=1, keepdims=True)
+            dg[at] = (dg[at].astype(F32) * cot_down).astype(BF)
+            du[at] = (du[at].astype(F32) * cot_down).astype(BF)
             hot = jnp.where(lanes(tile) == lane, dots, 0.0).astype(BF)
             part_a[pair // 2, pl.ds(lax.rem(pair, 2) * 2, 2), :, :, :, width:] = hot.reshape(
                 2, 2, 2, own, LANE
@@ -872,12 +952,15 @@
         for fetch in fetches[:3]:
             fetch.wait()
         lax.fori_loop(0, 4, forward, 0)
+        fetches[3].wait()
+        down_rest.finish()
+        lax.fori_loop(0, 4, backward, 0)
         rings[0].start_with(product(x, dg, g0))
         summed(team_a, slice(0, width), lambda at: mm_nt(dg[at], gate_w[...]) + mm_nt(du[at], up_w[...]))
         rings[0].middle()
         rings[1].start_with(product(x, du, wg))
         team_a.total1(total_a)
-        summed(team_b, slice(0, width), lambda at: mm_nt(h[at], wd[...]))
+        summed(team_b, slice(0, width), lambda at: mm_nt(h[at], down_w[...]))
         after = after_ref[...]
         normed_own = (after * rms_scale(after) * small_ref[1:2]).astype(BF)
         seq, quarter = own_tile()
@@ -938,7 +1021,7 @@
             pltpu.VMEM((count, width), BF),
             pltpu.VMEM((4, rows, cols), BF),
             pltpu.VMEM((4, rows, cols), BF),
-            pltpu.VMEM((width, cols), BF),
+            pltpu.VMEM((4, rows, cols), BF),
             pltpu.VMEM((count, cols), BF),
             pltpu.VMEM((count, cols), BF),
             pltpu.VMEM((count, cols), BF),
@@ -946,12 +1029,13 @@
             pltpu.VMEM((count, LANE), F32),
             pltpu.VMEM((2, 4, 2, 2, own, width + LANE), BF),
             pltpu.VMEM((2, 4, 2, 2, own, width), BF),
-            pltpu.SemaphoreType.DMA((5,)),
+            pltpu.SemaphoreType.DMA((4,)),
             pltpu.VMEM((own, width + LANE), F32),
             pltpu.VMEM((own, width), F32),
             pltpu.VMEM((own, width), BF),
             pltpu.VMEM((own, width), BF),
         ]
+        + RingRest.sems
         + TeamSum.scratch(own, width + LANE)
         + TeamSum.scratch(own, width)
         + RingSum.scratch(rows, cols) * 2
@@ -960,7 +1044,7 @@
         name="experts",
         **settings(collective, 300 << 20, 61),
     )(
-        normed, cotangent, *[w.reshape(4, rows, cols) for w in weights[:2]], weights[2], routes,
+        normed, cotangent, *[w.reshape(4, rows, cols) for w in weights], routes,
         after, small, routers, cot_own,
     )
 
@@ -1029,7 +1113,7 @@
                 )
                 gates = gates_ref[at]
                 gate = jnp.concatenate([pick(gates, first + e) for e in range(2)], axis=0)
-                each = jnp.sum(attended * grad, axis=1, keepdims=True)
+                each = jnp.sum(attended * grad, axis=1, keepdims=True) * gate
                 dots = jnp.where(lanes(seq) == first, each[:seq], 0.0)
                 dots += jnp.where(lanes(seq) == first + 1, each[seq:], 0.0)
                 grad = (grad * gate).astype(BF)
@@ -1185,12 +1269,6 @@
     )
 
 
-def reorder(array, axis):
-    shape = array.shape
-    split = shape[:axis] + (2, 4, shape[axis] // 8) + shape[axis + 1 :]
-    return jnp.swapaxes(array.reshape(split), axis, axis + 1).reshape(shape)
-
-
 def local(
     hidden,
     cotangent,
@@ -1211,7 +1289,6 @@
     rows = qkv_weight.shape[0]
     features = down_weight.shape[2]
     part = (features // LANE + 1) // 2 * LANE
-    low = features - part
     group = 8 * seq
     cosines, sines = rope_tables(seq)
 
@@ -1222,25 +1299,18 @@
     attn_blocks = jnp.concatenate([query_blocks, kv_blocks, out_blocks], axis=3)
     attn_blocks = attn_blocks.reshape(8, rows, 6 * HEAD)
 
-    def by_target(weight):
-        weight = weight.transpose(1, 0, 2)
-        return jnp.stack([weight[..., :part], weight[..., low:]], axis=0).reshape(8, rows, part)
-
     mlp_blocks = [
-        by_target(w) for w in (gate_up_weight[:, :, 0], gate_up_weight[:, :, 1], down_weight)
+        w.transpose(1, 0, 2) for w in (gate_up_weight[:, :, 0], gate_up_weight[:, :, 1], down_weight)
     ]
-
-    none = jnp.zeros((6, width), F32)
-    routers = jnp.concatenate([attn_router, mlp_router], axis=1).astype(F32).T
-    small = jnp.concatenate([attn_gain[None], mlp_gain[None], none, routers], axis=0)
-    small = reorder(small, 1)
-    routes = jnp.concatenate([attn_route, jnp.zeros_like(attn_route), mlp_route], axis=1)
-    routes = jnp.pad(routes, ((0, 0), (0, LANE - 6))).astype(BF)
+    gains = [g.reshape(width // LANE, LANE) for g in (attn_gain, mlp_gain)]
 
     (
-        attn_w, normed_a, qkv, gated_att, gates_a, group_routes, after, entered, cot_own, routers,
+        attn_w, normed_a, qkv, gated_att, gates_a, group_routes, after, entered, cot_own, routers, small,
         normed_m, group_cot, *mlp_w,
-    ) = attn_forward(1, attn_blocks, mlp_blocks, hidden, cotangent, routes, small, cosines, sines)
+    ) = attn_forward(
+        1, attn_blocks, mlp_blocks, part, hidden, cotangent, gains, [attn_router.T, mlp_router.T],
+        [attn_route.T, mlp_route.T], cosines, sines,
+    )
     attn_w = attn_w.reshape(width, 6 * HEAD)
     mlp_w = [w.reshape(width, part) for w in mlp_w]
     group_cot = group_cot.reshape(group, width)

time: 357 us -> 334 us (0.936)
  Pallas kernels: 315 us -> 300 us
  other arithmetic: 8.39 us -> 3.59 us
    pallas_call x1, Pallas kernels: 137 us -> 122 us  [attn_forward(): pl.pallas_call(kernel, out_shape=[four, jax.ShapeDtypeStruct((8, seq, wid...]
    another operation x5 -> x0, other arithmetic: 3.86 us -> none  [the longest x3 2.45 us: by_target(): jnp.stack([weight[..., :part], weight[..., low:]], axis=0)]
    unnamed x33 -> x32, local copies, waits for them, and re-layouts: 11.2 us -> 12.2 us
where the time goes in v12:
time: 334 us; the launch traced here: 328 us
  Pallas kernels  300 us (90%)
  local copies, waits for them, and re-layouts  23.6 us (7%)
  other arithmetic  3.59 us (1%)
    pallas_call x1, Pallas kernels, attn_forward(): pl.pallas_call(kernel, out_shape=[four, jax.ShapeDtypeStruct((8, seq, wid...  122 us
    pallas_call x1, Pallas kernels, experts(): pl.pallas_call(kernel, out_shape=[jax.ShapeDtypeStruct((own, width), F32)...  98 us
    pallas_call x1, Pallas kernels, attn_backward(): pl.pallas_call(kernel, out_shape=[jax.ShapeDtypeStruct((2, 2, own, width)...  79.1 us
    unnamed x32, local copies, waits for them, and re-layouts  12.2 us

profile of v12, /device:TPU:0, one launch (start us, length us, event | category | flops | bytes accessed | tf_op | source)
XLA Modules:
  0.0 328.1 jit_solution(13657143986814685724)
XLA Ops:
  0.6 0.0 slice-start
  0.7 1.0 slice.46
  1.7 0.1 copy.34
  1.8 0.1 broadcast_in_dim.2
  1.9 1.1 reshape.96
  3.0 0.0 slice-done
  3.0 0.1 reshape.94
  3.1 0.5 copy_bitcast_fusion.4
  3.6 0.0 copy-start.2
  3.6 0.9 pad_maximum_fusion
  4.5 0.0 copy-start
  4.5 1.8 reshape.97.a_ref
  6.3 0.0 copy-done.2
  6.3 0.9 copy.50
  7.2 0.0 copy-done
  7.3 2.0 fusion.1
  9.3 1.3 copy_bitcast_fusion
  10.6 122.5 %attn_forward.1 = (bf16[4,8,64,768]{3,2,1,0:T(8,128)(2,1)}, bf16[8,128,2048]{2,1,0:T(8,128)(2,1)}, bf16[8,128,512]{2,1,0:T(8,128)(2,1)}, bf16[8,128,256]{2,1,0:T...) custom-call(bf16[8,64,768]{2,1,0:T(8,128)(2,1)} %reshape.97.a_ref, ...), custom_call_target="tpu_custom_call" | custom-call | bytes 209715200 | tf_op jit(solution)/shard_map/attn_forward/pallas_call | solution.py:776
  133.0 98.0 %experts.1 = (f32[32,2048]{1,0:T(8,128)}, f32[16,2048]{1,0:T(8,128)}, bf16[2,4,2,2,32,2048]{5,4,3,2,1,0:T(8,128)(2,1)}, bf16[512,768]{1,0:T(8,128)(2,1)}, bf16[5...) custom-call(bf16[1024,2048]{1,0:T(8,128)(2,1)} %bitcast.73, ...), custom_call_target="tpu_custom_call" | custom-call | bytes 314572800 | tf_op jit(solution)/shard_map/experts/pallas_call | solution.py:1006
  231.1 79.1 %attn_backward.1 = (bf16[2,2,32,2048]{3,2,1,0:T(8,128)(2,1)}, f32[16,128]{1,0:T(8,128)}, f32[16,128]{1,0:T(8,128)}, f32[4,2048]{1,0:T(4,128)}, f32[4,2048]{1,0:T...) custom-call(bf16[8,128,2048]{2,1,0:T(8,128)(2,1)} %bitcast.72, ...), custom_call_target="tpu_custom_call" | custom-call | bytes 209715200 | tf_op jit(solution)/shard_map/attn_backward/pallas_call | solution.py:1227
  310.1 0.0 copy-start.5
  310.1 1.1 slice_bitcast_fusion
  311.2 1.0 slice_bitcast_fusion.1
  312.2 0.0 copy-done.5
  312.2 0.0 copy-start.4
  312.3 0.1 maximum_bitcast_fusion.1
  312.4 1.0 copy-done.4
  313.4 0.0 copy-start.3
  313.4 0.0 copy-start.6
  313.4 0.1 maximum_bitcast_fusion.2
  313.5 1.0 copy-done.3
  314.5 0.1 copy-done.6
  314.7 1.1 bitcast_convert_fusion
  315.8 0.1 convert_bitcast_fusion
  315.9 0.0 copy-start.1
  315.9 2.0 copy.41
  317.9 0.0 copy-done.1
  317.9 0.1 fusion.2
  318.0 1.1 copy.51
  319.1 0.2 convert_element_type.20
  319.4 1.0 maximum_bitcast_fusion
  320.3 0.2 maximum_convert_fusion
  320.5 0.0 copy-start.7
  320.5 0.0 copy-start.11
  320.6 0.0 copy-start.9
  320.6 0.0 copy-start.10
  320.6 0.0 copy-start.8
  320.6 3.8 %copy.40 = f32[64,4,2,1408]{3,2,1,0:T(2,128)} copy(f32[64,4,2,1408]{3,0,1,2:T(8,128)S(1)} %maximum_convert_fusion) | data formatting | bytes 5767168
  324.4 0.0 copy-done.7
  324.4 0.8 copy.57
  325.2 0.0 copy-done.11
  325.2 0.6 copy.58
  325.8 0.0 copy-done.9
  325.8 0.6 copy.59
  326.4 0.0 copy-done.10
  326.4 0.6 copy.60
  327.0 0.0 copy-done.8
  327.0 0.6 copy.61
  (6 shorter events, 0.2 us)
Async XLA Ops:
  0.6 2.4 slice-start
  3.6 2.7 copy-start.2
  4.5 2.7 copy-start
  310.1 2.1 copy-start.5
  312.2 1.1 copy-start.4
  313.4 1.1 copy-start.3
  313.4 1.3 copy-start.6
  315.9 2.0 copy-start.1
  320.5 3.9 %copy-start.7 = (bf16[2,2,32,2048]{3,2,1,0:T(8,128)(2,1)S(1)}, bf16[2,2,32,2048]{3,2,1,0:T(8,128)(2,1)}, u32[]{:S(2)}) copy-start(bf16[2,2,32,2048]{3,2,1,0:T(8,128)(2,1)} %get-tuple-element.52) | copy-start | bytes 1572868
  320.5 4.6 %copy-start.11 = (f32[16,128]{1,0:T(8,128)S(1)}, f32[16,128]{1,0:T(8,128)}, u32[]{:S(2)}) copy-start(f32[16,128]{1,0:T(8,128)} %get-tuple-element.66) | copy-start | bytes 24580
  320.6 5.2 %copy-start.9 = (f32[4,2048]{1,0:T(4,128)S(1)}, f32[4,2048]{1,0:T(4,128)}, u32[]{:S(2)}) copy-start(f32[4,2048]{1,0:T(4,128)} %get-tuple-element.67) | copy-start | bytes 98308
  320.6 5.8 %copy-start.10 = (f32[16,128]{1,0:T(8,128)S(1)}, f32[16,128]{1,0:T(8,128)}, u32[]{:S(2)}) copy-start(f32[16,128]{1,0:T(8,128)} %get-tuple-element.69) | copy-start | bytes 24580
  320.6 6.4 %copy-start.8 = (f32[4,2048]{1,0:T(4,128)S(1)}, f32[4,2048]{1,0:T(4,128)}, u32[]{:S(2)}) copy-start(f32[4,2048]{1,0:T(4,128)} %get-tuple-element.70) | copy-start | bytes 98308

commit v13 on v12

--- a/solution.py
+++ b/solution.py
@@ -326,11 +326,17 @@
             self.copy(k).start()
 
     def start_with(self, product):
+        self.begin_with(product)
+        self.go_on_with(product)
+
+    def begin_with(self, product):
         product(self.line(2))
         self.copy(0).start()
         self.copy(1).start()
         product(self.line(1))
         self.copy(2).start()
+
+    def go_on_with(self, product):
         product(self.line(3))
         self.copy(3).start()
         product(self.y)
@@ -955,8 +961,9 @@
         fetches[3].wait()
         down_rest.finish()
         lax.fori_loop(0, 4, backward, 0)
-        rings[0].start_with(product(x, dg, g0))
+        rings[0].begin_with(product(x, dg, g0))
         summed(team_a, slice(0, width), lambda at: mm_nt(dg[at], gate_w[...]) + mm_nt(du[at], up_w[...]))
+        rings[0].go_on_with(product(x, dg, g0))
         rings[0].middle()
         rings[1].start_with(product(x, du, wg))
         team_a.total1(total_a)
@@ -980,12 +987,16 @@
 
         def down(block, _):
             product(cot, h, wu)(block)
+
+            @pl.when(block == 1)
+            def _():
+                spread.middle()
+
             return 0
 
         lax.fori_loop(0, 4, down, 0)
         keep = pltpu.make_async_copy(wu, g2, load.at[0])
         keep.start()
-        spread.middle()
         team_b.total1(total_b)
         spread.finish()
         team_b.total2(total_b)
@@ -1292,12 +1303,15 @@
     group = 8 * seq
     cosines, sines = rope_tables(seq)
 
-    query_blocks = qkv_weight[:, :EXPERTS].reshape(rows, 2, 2, 4, HEAD).transpose(1, 3, 0, 2, 4)
-    kv_blocks = qkv_weight[:, EXPERTS:].reshape(rows, 2, 4, HEAD).transpose(2, 0, 1, 3)
-    kv_blocks = jnp.broadcast_to(kv_blocks[None], (2,) + kv_blocks.shape)
-    out_blocks = out_weight.reshape(rows, 2, 2, 4, HEAD).transpose(1, 3, 0, 2, 4)
-    attn_blocks = jnp.concatenate([query_blocks, kv_blocks, out_blocks], axis=3)
-    attn_blocks = attn_blocks.reshape(8, rows, 6 * HEAD)
+    qkv_rows, out_rows = qkv_weight.transpose(1, 0, 2), out_weight.transpose(1, 0, 2)
+
+    def target(zl, x):
+        head = slice(x * HEAD, (x + 1) * HEAD)
+        first = 2 * zl
+        pieces = [qkv_rows[n, :, head] for n in (first, first + 1, EXPERTS, EXPERTS + 1)]
+        return jnp.concatenate(pieces + [out_rows[n, :, head] for n in (first, first + 1)], axis=1)
+
+    attn_blocks = jnp.stack([target(zl, x) for zl in range(2) for x in range(4)], axis=0)
 
     mlp_blocks = [
         w.transpose(1, 0, 2) for w in (gate_up_weight[:, :, 0], gate_up_weight[:, :, 1], down_weight)
@@ -1339,6 +1353,8 @@
         return jnp.concatenate([grad[0], grad[1, ..., 2 * part - features :]], axis=-1).transpose(1, 0, 2)
 
     gate_grad, up_grad, down_grad = [placed_back(g) for g in mlp_grads]
+    gate_up_grad = jnp.stack([gate_grad, up_grad], axis=2)
+    gate_up_grad, down_grad = lax.optimization_barrier((gate_up_grad, down_grad))
     return (
         out_hidden,
         grad_in,
@@ -1348,7 +1364,7 @@
         out_grad,
         gain_m.reshape(width),
         router_m.T,
-        jnp.stack([gate_grad, up_grad], axis=2).astype(F32),
+        gate_up_grad.astype(F32),
         down_grad.astype(F32),
     )
 

time: 334 us -> 328 us (0.982)
    unnamed x32 -> x47, local copies, waits for them, and re-layouts: 12.2 us -> 15.2 us
where the time goes in v13:
time: 328 us; the launch traced here: 323 us
  Pallas kernels  297 us (91%)
  local copies, waits for them, and re-layouts  21.9 us (7%)
    pallas_call x1, Pallas kernels, attn_forward(): pl.pallas_call(kernel, out_shape=[four, jax.ShapeDtypeStruct((8, seq, wid...  123 us
    pallas_call x1, Pallas kernels, experts(): pl.pallas_call(kernel, out_shape=[jax.ShapeDtypeStruct((own, width), F32)...  95.2 us
    pallas_call x1, Pallas kernels, attn_backward(): pl.pallas_call(kernel, out_shape=[jax.ShapeDtypeStruct((2, 2, own, width)...  79.3 us
    unnamed x47, local copies, waits for them, and re-layouts  15.2 us

profile of v13, /device:TPU:0, one launch (start us, length us, event | category | flops | bytes accessed | tf_op | source)
XLA Modules:
  0.0 322.9 jit_solution(17201100636497423354)
XLA Ops:
  0.6 0.0 copy-start.8
  0.7 1.0 copy.40
  1.7 2.0 copy.38
  3.7 0.0 copy-done.8
  3.8 0.0 copy-start
  3.8 0.1 constant_dynamic-update-slice_fusion.46
  4.0 0.1 constant_dynamic-update-slice_fusion.43
  4.0 0.1 constant_dynamic-update-slice_fusion.42
  4.2 0.9 copy-done
  5.1 0.0 copy-start.2
  5.1 2.0 fusion.1
  7.1 0.0 copy-done.2
  7.2 1.3 copy_bitcast_fusion
  8.5 122.5 %attn_forward.1 = (bf16[4,8,64,768]{3,2,1,0:T(8,128)(2,1)}, bf16[8,128,2048]{2,1,0:T(8,128)(2,1)}, bf16[8,128,512]{2,1,0:T(8,128)(2,1)}, bf16[8,128,256]{2,1,0:T...) custom-call(bf16[8,64,768]{2,1,0:T(8,128)(2,1)} %copy-done.2, ...), custom_call_target="tpu_custom_call" | custom-call | bytes 209715200 | tf_op jit(solution)/shard_map/attn_forward/pallas_call | solution.py:782
  131.0 95.2 %experts.1 = (f32[32,2048]{1,0:T(8,128)}, f32[16,2048]{1,0:T(8,128)}, bf16[2,4,2,2,32,2048]{5,4,3,2,1,0:T(8,128)(2,1)}, bf16[512,768]{1,0:T(8,128)(2,1)}, bf16[5...) custom-call(bf16[1024,2048]{1,0:T(8,128)(2,1)} %bitcast.260, ...), custom_call_target="tpu_custom_call" | custom-call | bytes 314572800 | tf_op jit(solution)/shard_map/experts/pallas_call | solution.py:1017
  226.2 79.3 %attn_backward.1 = (bf16[2,2,32,2048]{3,2,1,0:T(8,128)(2,1)}, f32[16,128]{1,0:T(8,128)}, f32[16,128]{1,0:T(8,128)}, f32[4,2048]{1,0:T(4,128)}, f32[4,2048]{1,0:T...) custom-call(bf16[8,128,2048]{2,1,0:T(8,128)(2,1)} %bitcast.259, ...), custom_call_target="tpu_custom_call" | custom-call | bytes 209715200 | tf_op jit(solution)/shard_map/attn_backward/pallas_call | solution.py:1238
  305.5 0.0 copy-start.5
  305.5 1.1 slice_bitcast_fusion
  306.6 1.0 slice_bitcast_fusion.1
  307.6 0.0 copy-done.5
  307.6 0.0 copy-start.4
  307.7 0.1 maximum_bitcast_fusion.1
  307.7 1.0 copy-done.4
  308.8 0.1 maximum_bitcast_fusion.2
  308.8 0.0 copy-start.3
  308.8 0.1 pad_maximum_fusion
  309.0 1.0 copy-done.3
  310.0 0.0 copy-start.6
  310.0 0.0 copy-start.1
  310.0 0.1 maximum_bitcast_fusion.3
  310.1 0.9 copy-done.6
  311.0 1.1 bitcast_convert_fusion
  312.1 0.0 copy-done.1
  312.1 0.1 fusion.2
  312.2 1.1 copy.39
  313.3 0.2 convert_element_type.17
  313.6 0.9 maximum_bitcast_fusion
  314.5 3.1 copy.29
  317.6 0.0 copy-start.7
  317.6 0.0 copy-start.12
  317.6 0.0 copy-start.10
  317.6 0.0 copy-start.11
  317.6 0.0 copy-start.9
  317.6 1.7 copy.30
  319.3 0.0 copy-done.7
  319.3 0.8 copy.93
  320.1 0.0 copy-done.12
  320.1 0.6 copy.94
  320.7 0.0 copy-done.10
  320.7 0.6 copy.95
  321.3 0.0 copy-done.11
  321.3 0.6 copy.96
  321.9 0.0 copy-done.9
  321.9 0.6 copy.97
  (16 shorter events, 0.3 us)
Async XLA Ops:
  0.6 3.1 copy-start.8
  3.8 1.4 copy-start
  5.1 2.0 copy-start.2
  305.5 2.1 copy-start.5
  307.6 1.1 copy-start.4
  308.8 1.1 copy-start.3
  310.0 1.0 copy-start.6
  310.0 2.1 copy-start.1
  317.6 1.7 copy-start.7
  317.6 2.5 copy-start.12
  317.6 3.1 copy-start.10
  317.6 3.7 %copy-start.11 = (f32[16,128]{1,0:T(8,128)S(1)}, f32[16,128]{1,0:T(8,128)}, u32[]{:S(2)}) copy-start(f32[16,128]{1,0:T(8,128)} %get-tuple-element.71) | copy-start | bytes 24580
  317.6 4.3 %copy-start.9 = (f32[4,2048]{1,0:T(4,128)S(1)}, f32[4,2048]{1,0:T(4,128)}, u32[]{:S(2)}) copy-start(f32[4,2048]{1,0:T(4,128)} %get-tuple-element.72) | copy-start | bytes 98308
